TPU v7x, 32 devices: a whole 2x2x4 slice. The times are simulated.
32 devices in a mesh: section: 2 (over x), tensor: 2 (over y), batch: 8 (over z, core).
Axes of the slice: x: 2, y: 2, z: 4, core: 2. Of those that a mesh axis runs over, the one named last changes fastest.
Arguments:
- tokens: bfloat16 [2, 8, 512, 768], P(None, 'batch', 'tensor'), may hold values from -6 to 6
- block_place: int32 [2, 8], P(None, 'batch'), may hold values from 0 to 3, as said below
- cotangent: bfloat16 [2, 8, 512, 768], P(None, 'batch', 'tensor'), may hold values from -6 to 6
- norm_gains: float32 [2, 2, 768], P('section'), may hold values from 0.5 to 1.5
- norm_biases: float32 [2, 2, 768], P('section'), may hold values from -1.2 to 1.2
- query_key: bfloat16 [2, 768, 2, 768], P('section', None, None, 'tensor'), may hold values from -0.21875 to 0.21875
- query_bias: float32 [2, 768], P('section', 'tensor'), may hold values from -1.8 to 1.8
- value_own: bfloat16 [2, 768, 384], P('section', None, 'tensor'), may hold values from -0.21875 to 0.21875
- value_bias: float32 [2, 384], P('section', 'tensor'), may hold values from -0.3 to 0.3
- value_extra: bfloat16 [768, 384], P(None, 'tensor'), may hold values from -0.21875 to 0.21875
- out_weight: bfloat16 [2, 768, 768], P('section', 'tensor'), may hold values from -1.75 to 1.75
- out_bias: float32 [2, 768], P('section'), may hold values from -1.8 to 1.8
- up_weight: bfloat16 [2, 768, 3072], P('section', None, 'tensor'), may hold values from -0.21875 to 0.21875
- up_bias: float32 [2, 3072], P('section', 'tensor'), may hold values from -1.8 to 1.8
- down_weight: bfloat16 [2, 3072, 768], P('section', 'tensor'), may hold values from -0.109375 to 0.109375
- down_bias: float32 [2, 768], P('section'), may hold values from -1.8 to 1.8
Outputs:
- layer_outputs: bfloat16 [2, 2, 8, 512, 768], P('section', None, 'batch', 'tensor')
- input_grads: float32 [2, 2, 8, 512, 768], P('section', None, 'batch', 'tensor')
- norm_gains_grad: float32 [2, 2, 768], P('section')
- norm_biases_grad: float32 [2, 2, 768], P('section')
- query_key_grad: float32 [2, 768, 2, 768], P('section', None, None, 'tensor')
- query_bias_grad: float32 [2, 768], P('section', 'tensor')
- value_own_grad: float32 [2, 768, 384], P('section', None, 'tensor')
- value_bias_grad: float32 [2, 384], P('section', 'tensor')
- value_extra_grad: float32 [768, 384], P('section', 'tensor')
- out_weight_grad: float32 [2, 768, 768], P('section', 'tensor')
- out_bias_grad: float32 [2, 768], P('section')
- up_weight_grad: float32 [2, 768, 3072], P('section', None, 'tensor')
- up_bias_grad: float32 [2, 3072], P('section', 'tensor')
- down_weight_grad: float32 [2, 3072, 768], P('section', 'tensor')
- down_bias_grad: float32 [2, 768], P('section')
Inputs may be any that keep to these rules, and one draw needn't show every extreme that they name: `block_place`: in each micro-batch, sequences of 2 or 4 blocks lie one after another along the 8 blocks: block 0 has value 0, and a block with value p > 0 continues the sequence of the block before it, whose value is p - 1. A third of each micro-batch's sequences hold 4 blocks, the others 2.
All inputs are finite; a program needn't handle non-finite values.
Results may differ from a plain program's by a relative error of at most 0.028.
Values may be sent and summed in bfloat16 or wider, within the bound.
No kernel may reach another device: no remote copies, remote signals or barrier semaphores. Data moves between devices by JAX's collectives and lax.ppermute only.
A program may use at most 256 MiB of HBM per device.

v0:
```python
import jax
import jax.numpy as jnp
from jax import lax
from jax.sharding import PartitionSpec as P

HEAD = 64


def shifted(value, axis, steps):
    count = lax.axis_size(axis)
    initial, last = (max(0, -steps), min(count, count - steps))
    return lax.ppermute(value, axis, [(source, source + steps) for source in range(initial, last)])


def for_sending(x):
    return jax.tree.map(lambda a: a.astype(jnp.bfloat16) if a.dtype == jnp.float32 else a, x)


def norm_rows(values, scales, shifts):
    centred = values - jnp.mean(values, axis=-1, keepdims=True)
    spread = jnp.mean(centred * centred, axis=-1, keepdims=True)
    return centred * lax.rsqrt(spread + 1e-05) * scales + shifts


def gelu_tanh(values):
    return jax.nn.gelu(values, approximate=True)


def guarded(predicate, action, *operands):
    computed = action(*operands)
    return jax.tree.map(
        lambda member: jnp.where(predicate, member, jnp.zeros_like(member)), computed
    )


def store_row(storage, new_row, micro_index, is_valid):
    old_row = lax.dynamic_index_in_dim(storage, micro_index, 0, keepdims=False)
    return lax.dynamic_update_index_in_dim(
        storage, jnp.where(is_valid, new_row, old_row), micro_index, 0
    )


def key_mask(position, length):
    row_index = lax.broadcasted_iota(jnp.int32, (length, 4 * length), 0)
    column_index = lax.broadcasted_iota(jnp.int32, (length, 4 * length), 1)
    offset = 3 - column_index // length
    return (offset <= position) & ((offset > 0) | (column_index % length <= row_index))


def head_pair(values, first_lane):
    return lax.dynamic_slice_in_dim(values, first_lane, 2 * HEAD, 1).reshape(
        values.shape[0], 2, HEAD
    )


def softmax_rows(queries, key_matrix, allowed):
    scores = jnp.einsum(
        "qhd,khd->hqk", queries, key_matrix, preferred_element_type=jnp.float32
    ) * HEAD ** (-0.5)
    scores = jnp.where(allowed[None], scores, -1e30)
    row_top = jnp.max(scores, axis=-1, keepdims=True)
    weights = jnp.exp(scores - row_top)
    return weights / jnp.sum(weights, axis=-1, keepdims=True)


def attend_forward(queries, key_matrix, values, allowed):

    def pair_step(number, output):
        first_lane = number * 2 * HEAD
        attention = softmax_rows(
            head_pair(queries, first_lane), head_pair(key_matrix, first_lane), allowed
        )
        result = jnp.einsum(
            "hqk,khd->qhd",
            attention.astype(jnp.bfloat16),
            head_pair(values, first_lane),
            preferred_element_type=jnp.float32,
        )
        return lax.dynamic_update_slice_in_dim(
            output, result.reshape(queries.shape[0], 2 * HEAD), first_lane, 1
        )

    return lax.fori_loop(
        0, queries.shape[1] // (2 * HEAD), pair_step, jnp.zeros(queries.shape, jnp.float32)
    )


def attend_backward(queries, key_matrix, values, grad_output, allowed):
    factor = HEAD ** (-0.5)

    def pair_step(number, carried):
        query_total, key_total, value_total = carried
        first_lane = number * 2 * HEAD
        query_pair = head_pair(queries, first_lane)
        key_pair = head_pair(key_matrix, first_lane)
        value_pair = head_pair(values, first_lane)
        grad_pair = head_pair(grad_output, first_lane)
        attention = softmax_rows(query_pair, key_pair, allowed)
        value_grad = jnp.einsum(
            "hqk,qhd->khd",
            attention.astype(jnp.bfloat16),
            grad_pair,
            preferred_element_type=jnp.float32,
        )
        weight_grad = jnp.einsum(
            "qhd,khd->hqk", grad_pair, value_pair, preferred_element_type=jnp.float32
        )
        row_inner = jnp.sum(weight_grad * attention, axis=-1, keepdims=True)
        score_grad = (attention * (weight_grad - row_inner)).astype(jnp.bfloat16)
        query_grad = (
            jnp.einsum("hqk,khd->qhd", score_grad, key_pair, preferred_element_type=jnp.float32)
            * factor
        )
        key_grad = (
            jnp.einsum("hqk,qhd->khd", score_grad, query_pair, preferred_element_type=jnp.float32)
            * factor
        )
        query_total = lax.dynamic_update_slice_in_dim(
            query_total, query_grad.reshape(query_total.shape[0], 2 * HEAD), first_lane, 1
        )
        key_total = lax.dynamic_update_slice_in_dim(
            key_total, key_grad.reshape(key_total.shape[0], 2 * HEAD), first_lane, 1
        )
        value_total = lax.dynamic_update_slice_in_dim(
            value_total, value_grad.reshape(value_total.shape[0], 2 * HEAD), first_lane, 1
        )
        return (query_total, key_total, value_total)

    initial = (
        jnp.zeros(queries.shape, jnp.float32),
        jnp.zeros(key_matrix.shape, jnp.float32),
        jnp.zeros(values.shape, jnp.float32),
    )
    return lax.fori_loop(0, queries.shape[1] // (2 * HEAD), pair_step, initial)


def collect(values):
    return lax.all_gather(values, "tensor", axis=0, tiled=True)


def spread_sum(action, row_count):
    return lax.psum_scatter(
        action(jnp.int32(0), row_count * lax.axis_size("tensor")).astype(jnp.bfloat16),
        "tensor",
        scatter_dimension=0,
        tiled=True,
    ).astype(jnp.float32)


def collect_grad(values):
    return lax.all_gather(values, "tensor", axis=0, tiled=True)


def spread_grad(action, row_count):
    return lax.psum_scatter(
        action(jnp.int32(0), row_count * lax.axis_size("tensor")).astype(jnp.bfloat16),
        "tensor",
        scatter_dimension=0,
        tiled=True,
    ).astype(jnp.float32)


def pass_keys(key_matrix, values):
    earlier = [shifted((key_matrix, values), "batch", offset) for offset in (3, 2, 1)]
    key_window = jnp.concatenate([couple[0] for couple in earlier] + [key_matrix], axis=0)
    value_window = jnp.concatenate([couple[1] for couple in earlier] + [values], axis=0)
    return (key_window, value_window)


def return_keys(key_grads, value_grads, length):

    def window_rows(grads, number):
        return lax.slice_in_dim(grads, number * length, (number + 1) * length, axis=0)

    key_total = window_rows(key_grads, 3)
    value_total = window_rows(value_grads, 3)
    for offset in (1, 2, 3):
        arrived = (
            shifted(
                window_rows(key_grads, 3 - offset).astype(jnp.bfloat16), "batch", -offset
            ).astype(jnp.float32),
            shifted(
                window_rows(value_grads, 3 - offset).astype(jnp.bfloat16), "batch", -offset
            ).astype(jnp.float32),
        )
        key_total = key_total + arrived[0]
        value_total = value_total + arrived[1]
    return (key_total, value_total)


def layer_forward(residual, position, reused, params, is_first, is_valid):
    (
        norm_scale,
        norm_shift,
        query_key,
        query_bias,
        value_own,
        value_bias,
        value_extra,
        out_weight,
        out_bias,
        up_weight,
        up_bias,
        down_weight,
        down_bias,
    ) = params
    row_count = residual.shape[0]
    features = residual.shape[1]
    head_width = query_bias.shape[0]
    normed = collect(norm_rows(residual, norm_scale[0], norm_shift[0]).astype(jnp.bfloat16))
    length = normed.shape[0]

    def project_in(normed):
        combined = jnp.dot(
            normed, query_key.reshape(features, 2 * head_width), preferred_element_type=jnp.float32
        )
        queries = (combined[:, :head_width] + query_bias).astype(jnp.bfloat16)
        key_matrix = combined[:, head_width:].astype(jnp.bfloat16)
        own_values = (
            jnp.dot(normed, value_own, preferred_element_type=jnp.float32) + value_bias
        ).astype(jnp.bfloat16)
        other_values = lax.cond(
            is_first,
            lambda: jnp.dot(normed, value_extra, preferred_element_type=jnp.float32).astype(
                jnp.bfloat16
            ),
            lambda: reused,
        )
        return (queries, key_matrix, jnp.concatenate([own_values, other_values], axis=1))

    queries, key_matrix, values = guarded(is_valid, project_in, normed)
    key_window, value_window = pass_keys(key_matrix, values)
    allowed = key_mask(position, length)
    attended = guarded(is_valid, attend_forward, queries, key_window, value_window, allowed).astype(
        jnp.bfloat16
    )

    def out_rows(first_row, amount):
        return guarded(
            is_valid,
            lambda sliced: jnp.dot(sliced, out_weight, preferred_element_type=jnp.float32),
            attended,
        )

    hidden = residual + spread_sum(out_rows, row_count) + out_bias
    mlp_in = collect(norm_rows(hidden, norm_scale[1], norm_shift[1]).astype(jnp.bfloat16))

    def project_up(mlp_in):
        up_values = jnp.dot(mlp_in, up_weight, preferred_element_type=jnp.float32) + up_bias
        return (up_values, gelu_tanh(up_values).astype(jnp.bfloat16))

    up_values, active = guarded(is_valid, project_up, mlp_in)

    def down_rows(first_row, amount):
        return guarded(
            is_valid,
            lambda sliced: jnp.dot(sliced, down_weight, preferred_element_type=jnp.float32),
            active,
        )

    result = hidden + spread_sum(down_rows, row_count) + down_bias
    stored = (
        normed,
        queries,
        key_window,
        value_window,
        attended,
        hidden,
        mlp_in,
        up_values,
        active,
    )
    return (result, values[:, : value_own.shape[1]], stored)


def layer_backward(residual, position, params, stored, upstream, returned, is_first, is_valid):
    (
        norm_scale,
        norm_shift,
        query_key,
        query_bias,
        value_own,
        value_bias,
        value_extra,
        out_weight,
        out_bias,
        up_weight,
        up_bias,
        down_weight,
        down_bias,
    ) = params
    normed, queries, key_window, value_window, attended, hidden, mlp_in, up_values, active = stored
    row_count = residual.shape[0]
    features = residual.shape[1]
    length = normed.shape[0]
    own_width = value_own.shape[1]
    grad_full = collect_grad(upstream.astype(jnp.bfloat16))

    def down_back(grad_full):
        grad_active = jnp.einsum(
            "rd,fd->rf", grad_full, down_weight, preferred_element_type=jnp.float32
        )
        return jax.vjp(gelu_tanh, up_values)[1](grad_active)[0].astype(jnp.bfloat16)

    grad_up = guarded(is_valid, down_back, grad_full)

    def up_rows(first_row, amount):
        return guarded(
            is_valid,
            lambda sliced: jnp.einsum(
                "rf,df->rd", sliced, up_weight, preferred_element_type=jnp.float32
            ),
            grad_up,
        )

    mlp_back = jax.vjp(norm_rows, hidden, norm_scale[1], norm_shift[1])[1](
        spread_grad(up_rows, row_count)
    )
    grad_hidden = upstream + mlp_back[0]
    grad_hidden_full = collect_grad(grad_hidden.astype(jnp.bfloat16))

    def out_back(grad_hidden_full):
        return jnp.einsum(
            "rd,hd->rh", grad_hidden_full, out_weight, preferred_element_type=jnp.float32
        ).astype(jnp.bfloat16)

    grad_attended = guarded(is_valid, out_back, grad_hidden_full)
    window_grads = guarded(
        is_valid,
        attend_backward,
        queries,
        key_window,
        value_window,
        grad_attended,
        key_mask(position, length),
    )
    key_grads, value_grads = return_keys(window_grads[1], window_grads[2], length)
    query_low = window_grads[0].astype(jnp.bfloat16)
    key_low = key_grads.astype(jnp.bfloat16)
    own_low = (value_grads[:, :own_width] + returned).astype(jnp.bfloat16)
    other_grads = value_grads[:, own_width:]
    other_low = other_grads.astype(jnp.bfloat16)
    pair_low = jnp.concatenate([query_low, key_low], axis=1)

    def input_rows(first_row, amount):

        def compute(pair_rows, own_rows, other_rows):
            summed = jnp.einsum(
                "rh,dh->rd",
                pair_rows,
                query_key.reshape(features, -1),
                preferred_element_type=jnp.float32,
            )
            summed = summed + jnp.einsum(
                "rh,dh->rd", own_rows, value_own, preferred_element_type=jnp.float32
            )
            return summed + lax.cond(
                is_first,
                lambda: jnp.einsum(
                    "rh,dh->rd", other_rows, value_extra, preferred_element_type=jnp.float32
                ),
                lambda: jnp.zeros(summed.shape, jnp.float32),
            )

        return guarded(is_valid, compute, *[source for source in (pair_low, own_low, other_low)])

    norm_back = jax.vjp(norm_rows, residual, norm_scale[0], norm_shift[0])[1](
        spread_grad(input_rows, row_count)
    )
    grad_residual = grad_hidden + norm_back[0]

    def matrix_grads():
        grad_query_key = jnp.einsum(
            "rd,rh->dh", normed, pair_low, preferred_element_type=jnp.float32
        ).reshape(query_key.shape)
        grad_value_own = jnp.einsum(
            "rd,rh->dh", normed, own_low, preferred_element_type=jnp.float32
        )
        grad_value_extra = lax.cond(
            is_first,
            lambda: jnp.einsum("rd,rh->dh", normed, other_low, preferred_element_type=jnp.float32),
            lambda: jnp.zeros(value_extra.shape, jnp.float32),
        )
        grad_out_weight = jnp.einsum(
            "rh,rd->hd", attended, grad_hidden_full, preferred_element_type=jnp.float32
        )
        grad_up_weight = jnp.einsum(
            "rd,rf->df", mlp_in, grad_up, preferred_element_type=jnp.float32
        )
        grad_down_weight = jnp.einsum(
            "rf,rd->fd", active, grad_full, preferred_element_type=jnp.float32
        )
        return (
            grad_query_key,
            grad_value_own,
            grad_value_extra,
            grad_out_weight,
            grad_up_weight,
            grad_down_weight,
        )

    (
        grad_query_key,
        grad_value_own,
        grad_value_extra,
        grad_out_weight,
        grad_up_weight,
        grad_down_weight,
    ) = guarded(is_valid, matrix_grads)
    layer_grads = (
        jnp.stack([norm_back[1], mlp_back[1]]),
        jnp.stack([norm_back[2], mlp_back[2]]),
        grad_query_key,
        jnp.sum(query_low.astype(jnp.float32), axis=0),
        grad_value_own,
        jnp.sum(own_low.astype(jnp.float32), axis=0),
        grad_value_extra,
        grad_out_weight,
        jnp.sum(grad_hidden, axis=0),
        grad_up_weight,
        jnp.sum(grad_up.astype(jnp.float32), axis=0),
        grad_down_weight,
        jnp.sum(upstream, axis=0),
    )
    return (grad_residual, other_grads, layer_grads)


def local(
    tokens,
    block_place,
    cotangent,
    norm_gains,
    norm_biases,
    query_key,
    query_bias,
    value_own,
    value_bias,
    value_extra,
    out_weight,
    out_bias,
    up_weight,
    up_bias,
    down_weight,
    down_bias,
):
    micro_count = tokens.shape[0]
    half_rows = tokens.shape[2]
    features = tokens.shape[3]
    length = half_rows * lax.axis_size("tensor")
    own_width = value_own.shape[2]
    section_index = lax.axis_index("section")
    is_first = section_index == 0
    params = (
        norm_gains[0],
        norm_biases[0],
        query_key[0],
        query_bias[0],
        value_own[0],
        value_bias[0],
        value_extra,
        out_weight[0],
        out_bias[0],
        up_weight[0],
        up_bias[0],
        down_weight[0],
        down_bias[0],
    )
    inbound = jnp.zeros((half_rows, features), jnp.bfloat16)
    inbound_values = jnp.zeros((length, own_width), jnp.bfloat16)
    inputs_kept = jnp.zeros((micro_count, half_rows, features), jnp.bfloat16)
    values_kept = jnp.zeros((micro_count, length, own_width), jnp.bfloat16)
    outputs = jnp.zeros((micro_count, half_rows, features), jnp.bfloat16)
    for moment in range(micro_count + 1):
        micro_index = moment - section_index
        is_valid = (micro_index >= 0) & (micro_index < micro_count)
        micro_index = jnp.clip(micro_index, 0, micro_count - 1)
        source = jnp.where(is_first, tokens[micro_index, 0], inbound)
        inputs_kept = store_row(inputs_kept, source, micro_index, is_valid)
        values_kept = store_row(values_kept, inbound_values, micro_index, is_valid)
        result, shared, stored = layer_forward(
            source.astype(jnp.float32),
            block_place[micro_index, 0],
            inbound_values,
            params,
            is_first,
            is_valid,
        )
        rounded = result.astype(jnp.bfloat16)
        outputs = store_row(outputs, rounded, micro_index, is_valid)
        inbound, inbound_values = shifted((rounded, shared), "section", 1)
    grad_inbound = jnp.zeros((half_rows, features), jnp.float32)
    returned = jnp.zeros((length, own_width), jnp.float32)
    input_grads = jnp.zeros((micro_count, half_rows, features), jnp.float32)
    totals = None
    for moment in range(micro_count + 1):
        micro_index = moment - 1 + section_index
        is_valid = (micro_index >= 0) & (micro_index < micro_count)
        micro_index = jnp.clip(micro_index, 0, micro_count - 1)
        source = lax.dynamic_index_in_dim(inputs_kept, micro_index, 0, keepdims=False).astype(
            jnp.float32
        )
        reused = lax.dynamic_index_in_dim(values_kept, micro_index, 0, keepdims=False)
        position = block_place[micro_index, 0]
        upstream = jnp.where(
            is_first,
            grad_inbound.astype(jnp.bfloat16).astype(jnp.float32),
            cotangent[micro_index, 0].astype(jnp.float32),
        )
        upstream = jnp.where(is_valid, upstream, 0.0)
        stored = layer_forward(source, position, reused, params, is_first, is_valid)[2]
        grad_residual, other_grads, layer_grads = layer_backward(
            source, position, params, stored, upstream, returned, is_first, is_valid
        )
        totals = layer_grads if totals is None else jax.tree.map(jnp.add, totals, layer_grads)
        input_grads = store_row(input_grads, grad_residual, micro_index, is_valid)
        grad_inbound, returned = (
            shifted(grad_residual.astype(jnp.bfloat16), "section", -1).astype(grad_residual.dtype),
            shifted(for_sending(other_grads), "section", -1).astype(other_grads.dtype),
        )
    (
        grad_norm_gains,
        grad_norm_biases,
        grad_query_key,
        grad_query_bias,
        grad_value_own,
        grad_value_bias,
        grad_value_extra,
        grad_out_weight,
        grad_out_bias,
        grad_up_weight,
        grad_up_bias,
        grad_down_weight,
        grad_down_bias,
    ) = totals
    summed = lax.psum(
        (
            grad_query_key,
            grad_query_bias,
            grad_value_own,
            grad_value_bias,
            grad_out_weight,
            grad_up_weight,
            grad_up_bias,
            grad_down_weight,
            grad_value_extra,
        ),
        "batch",
    )
    shared_sums = lax.psum(
        (grad_norm_gains, grad_norm_biases, grad_out_bias, grad_down_bias), ("tensor", "batch")
    )
    extra_rows = lax.psum_scatter(
        summed[8].astype(jnp.bfloat16), "section", scatter_dimension=0, tiled=True
    ).astype(jnp.float32)
    return (
        outputs.reshape(1, micro_count, 1, half_rows, features),
        input_grads.reshape(1, micro_count, 1, half_rows, features),
        shared_sums[0][None],
        shared_sums[1][None],
        summed[0][None],
        summed[1][None],
        summed[2][None],
        summed[3][None],
        extra_rows,
        summed[4][None],
        shared_sums[2][None],
        summed[5][None],
        summed[6][None],
        summed[7][None],
        shared_sums[3][None],
    )


def solution(mesh):
    return jax.shard_map(
        local,
        mesh=mesh,
        in_specs=(
            P(None, "batch", "tensor", None),
            P(None, "batch"),
            P(None, "batch", "tensor", None),
            P("section", None, None),
            P("section", None, None),
            P("section", None, None, "tensor"),
            P("section", "tensor"),
            P("section", None, "tensor"),
            P("section", "tensor"),
            P(None, "tensor"),
            P("section", "tensor", None),
            P("section", None),
            P("section", None, "tensor"),
            P("section", "tensor"),
            P("section", "tensor", None),
            P("section", None),
        ),
        out_specs=(
            P("section", None, "batch", "tensor", None),
            P("section", None, "batch", "tensor", None),
            P("section", None, None),
            P("section", None, None),
            P("section", None, None, "tensor"),
            P("section", "tensor"),
            P("section", None, "tensor"),
            P("section", "tensor"),
            P("section", "tensor"),
            P("section", "tensor", None),
            P("section", None),
            P("section", None, "tensor"),
            P("section", "tensor"),
            P("section", "tensor", None),
            P("section", None),
        ),
        check_vma=False,
    )
```

profile of v0, /device:TPU:0, one launch (start us, length us, event | category | flops | bytes accessed | tf_op | source)
XLA Modules:
  0.0 2019.1 jit_solution(3533743056050270631)
XLA Ops:
  11.9 12.8 all_gather.54
  70.5 58.0 %while.156 = (s32[]{:T(128)}, bf16[512,384]{0,1:T(8,128)(2,1)}, bf16[2048,384]{0,1:T(8,128)(2,1)}, bf16[512,384]{0,1:T(8,128)(2,1)}, bf16[2048,384]{0,1:T(8,128)...) while((s32[]{:T(128)}, bf16[512,384]{0,1:T(8,128)(2,1)}, ...), condition=%wide.region_7.8_spmd.clone, body=%wide.region_4.7_spmd.clone.sunk | while | flops 557844480 | bytes 22851796 | solution.py:83
  132.1 36.8 %reduce-scatter.19.cloned.1.call-done = bf16[256,768]{1,0:T(8,128)(2,1)} async-done(((bf16[512,768]{1,0:T(8,128)(2,1)}), bf16[256,768]{1,0:T(8,128)(2,1)}) %reduce-scatter.19.cloned.1.call-update) | async-done | bytes 393232 | tf_op jit(solution)/shard_map/reduce_scatter | solution.py:142
  191.7 16.3 reduce-scatter.21.cloned.1.call-done
  279.5 62.9 %while.157 = (s32[]{:T(128)}, bf16[512,384]{0,1:T(8,128)(2,1)}, bf16[2048,384]{0,1:T(8,128)(2,1)}, bf16[512,384]{0,1:T(8,128)(2,1)}, bf16[2048,384]{0,1:T(8,128)...) while((s32[]{:T(128)}, bf16[512,384]{0,1:T(8,128)(2,1)}, ...), condition=%wide.region_19.20_spmd.clone, body=%wide.region_16.19_spmd.clone.sunk | while | flops 557844480 | bytes 22851796 | solution.py:83
  345.5 33.0 %reduce-scatter.23.cloned.1.call-done = bf16[256,768]{1,0:T(8,128)(2,1)} async-done(((bf16[512,768]{1,0:T(8,128)(2,1)}), bf16[256,768]{1,0:T(8,128)(2,1)}) %reduce-scatter.23.cloned.1.call-update) | async-done | bytes 393232 | tf_op jit(solution)/shard_map/reduce_scatter | solution.py:142
  486.8 61.2 %while.159 = (s32[]{:T(128)}, bf16[512,384]{0,1:T(8,128)(2,1)}, bf16[2048,384]{0,1:T(8,128)(2,1)}, bf16[512,384]{0,1:T(8,128)(2,1)}, bf16[2048,384]{0,1:T(8,128)...) while((s32[]{:T(128)}, bf16[512,384]{0,1:T(8,128)(2,1)}, ...), condition=%wide.region_43.44_spmd.clone, body=%wide.region_40.43_spmd.clone.sunk | while | flops 557844480 | bytes 22851796 | solution.py:83
  561.0 26.1 %reduce-scatter.31.cloned.1.call-done = bf16[256,768]{1,0:T(8,128)(2,1)} async-done(((bf16[512,768]{1,0:T(8,128)(2,1)}), bf16[256,768]{1,0:T(8,128)(2,1)}) %reduce-scatter.31.cloned.1.call-update) | async-done | bytes 393232 | tf_op jit(solution)/shard_map/reduce_scatter | solution.py:142
  612.7 19.9 reduce-scatter.33.cloned.1.call-done
  689.4 59.0 %while.161 = (s32[]{:T(128)}, bf16[512,384]{0,1:T(8,128)(2,1)}, bf16[2048,384]{0,1:T(8,128)(2,1)}, bf16[512,384]{0,1:T(8,128)(2,1)}, bf16[2048,384]{0,1:T(8,128)...) while((s32[]{:T(128)}, bf16[512,384]{0,1:T(8,128)(2,1)}, ...), condition=%wide.region_67.68_spmd.clone, body=%wide.region_64.67_spmd.clone.sunk | while | flops 557844480 | bytes 22851796 | solution.py:83
  751.2 36.9 %reduce-scatter.37.cloned.1.call-done = bf16[256,768]{1,0:T(8,128)(2,1)} async-done(((bf16[512,768]{1,0:T(8,128)(2,1)}), bf16[256,768]{1,0:T(8,128)(2,1)}) %reduce-scatter.37.cloned.1.call-update) | async-done | bytes 393232 | tf_op jit(solution)/shard_map/reduce_scatter | solution.py:142
  812.0 79.3 %while.160 = (s32[]{:T(128)}, bf16[512,384]{0,1:T(8,128)(2,1)}, f32[2048,384]{0,1:T(8,128)}, f32[2048,384]{0,1:T(8,128)}, bf16[2048,384]{0,1:T(8,128)(2,1)}, /*i...) while((s32[]{:T(128)}, bf16[512,384]{0,1:T(8,128)(2,1)}, ...), condition=%wide.region_54.55_spmd.clone, body=%wide.region_50.54_spmd.clone.sunk | while | flops 1378223104 | bytes 101642528 | solution.py:134
  918.7 13.6 collective-permute-done.29
  946.5 25.2 %reduce-scatter.35.cloned.1.call-done = bf16[256,768]{1,0:T(8,128)(2,1)} async-done(((bf16[512,768]{1,0:T(8,128)(2,1)}), bf16[256,768]{1,0:T(8,128)(2,1)}) %reduce-scatter.35.cloned.1.call-update) | async-done | bytes 393232 | tf_op jit(solution)/shard_map/reduce_scatter | solution.py:155
  1062.0 58.0 %while.158 = (s32[]{:T(128)}, bf16[512,384]{0,1:T(8,128)(2,1)}, bf16[2048,384]{0,1:T(8,128)(2,1)}, bf16[512,384]{0,1:T(8,128)(2,1)}, bf16[2048,384]{0,1:T(8,128)...) while((s32[]{:T(128)}, bf16[512,384]{0,1:T(8,128)(2,1)}, ...), condition=%wide.region_31.32_spmd.clone, body=%wide.region_28.31_spmd.clone.sunk | while | flops 557844480 | bytes 22851796 | solution.py:83
  1125.9 19.4 all_gather.64
  1161.7 58.2 %while.163 = (s32[]{:T(128)}, bf16[512,384]{0,1:T(8,128)(2,1)}, bf16[2048,384]{0,1:T(8,128)(2,1)}, bf16[512,384]{0,1:T(8,128)(2,1)}, bf16[2048,384]{0,1:T(8,128)...) while((s32[]{:T(128)}, bf16[512,384]{0,1:T(8,128)(2,1)}, ...), condition=%wide.region_91.92_spmd.clone, body=%wide.region_88.91_spmd.clone.sunk | while | flops 557844480 | bytes 22851796 | solution.py:83
  1263.4 77.1 %while.162 = (s32[]{:T(128)}, bf16[512,384]{0,1:T(8,128)(2,1)S(1)}, f32[2048,384]{0,1:T(8,128)}, f32[2048,384]{0,1:T(8,128)}, bf16[2048,384]{0,1:T(8,128)(2,1)},...) while((s32[]{:T(128)}, bf16[512,384]{0,1:T(8,128)(2,1)S(1)}, ...), condition=%wide.region_78.79_spmd.clone, body=%wide.region_74.78_spmd.clone.sunk | while | flops 1378223104 | bytes 101642528 | solution.py:134
  1408.2 12.9 reduce-scatter.41.cloned.1.call-done
  1430.7 12.2 all_gather.70
  1509.8 77.4 %while.164 = (s32[]{:T(128)}, bf16[512,384]{0,1:T(8,128)(2,1)S(1)}, f32[2048,384]{0,1:T(8,128)}, f32[2048,384]{0,1:T(8,128)}, bf16[2048,384]{0,1:T(8,128)(2,1)},...) while((s32[]{:T(128)}, bf16[512,384]{0,1:T(8,128)(2,1)S(1)}, ...), condition=%wide.region_102.103_spmd.clone, body=%wide.region_98.102_spmd.clone.sunk | while | flops 1378223104 | bytes 101642528 | solution.py:134
  1621.2 47.3 %all-reduce.7 = (f32[1,384]{1,0:T(1,128)}, f32[1,192]{1,0:T(1,128)}, bf16[768,192]{0,1:T(8,128)(2,1)}, f32[1,1536]{1,0:T(1,128)}) all-reduce(f32[1,384]{1,0:T(1,128)S(1)} %broadcast_in_dim.520, f32[1,192]{1,0:T(1,128)S(1)} %bitcast.884, ...), channel_id=1, replica_groups=mesh['section'=2,'tensor'=2,'batch'=8] {'batch'}, use_global_device_ids=true, to_apply=%region_126.127 | all-reduce | flops 149568 | bytes 901632 | tf_op jit(solution)/shard_map/psum | solution.py:535
  1740.9 62.5 %all-reduce = (f32[1,2,768]{2,1,0:T(2,128)}, f32[1,2,768]{2,1,0:T(2,128)}, f32[1,768]{1,0:T(1,128)}, f32[1,768]{1,0:T(1,128)}) all-reduce(f32[1,2,768]{2,1,0:T(2,128)S(1)} %fusion.492, f32[1,2,768]{2,1,0:T(2,128)S(1)} %fusion.494, ...), channel_id=1, replica_groups=mesh['section'=2,'tensor'=2,'batch'=8] {'tensor','batch'}, use_global_device_ids=true, to_apply=%region_114.115 | all-reduce | flops 4608 | bytes 36864 | tf_op jit(solution)/shard_map/psum | solution.py:549
  1806.2 194.5 %all-reduce.6.cloned.1.call-done = (f32[1,768,2,384]{3,2,1,0:T(2,128)}, f32[1,768,192]{1,2,0:T(8,128)}, f32[1,384,768]{2,1,0:T(8,128)}, f32[1,768,1536]{2,1,0:T(8,128)}, f32[1,1536,768]{2,1,0:T(8,128)}) async-done(((f32[1,768,2,384]{3,2,1,0:T(2,128)}, f32[1,768,192]{1,2,0:T(8,128)}, f32[1,384,768]{2,1,0:T(8,128)}, f32[1,768,1536]{2,1,0:T(8,128)}, f32[1,1536,768]{2,1,0:T(8,128)}), ...) | async-done | bytes 13565968 | tf_op jit(solution)/shard_map/psum | solution.py:535
  (1164 shorter events, 1450.1 us)
Async XLA Ops:
  7.2 161.7 %reduce-scatter.19.cloned.1.call-start = ((), (), s32[]{:S(2)}) async-start(), calls=%async_computation.16 | async-start | bytes 1179648 | tf_op jit(solution)/shard_map/reduce_scatter | solution.py:142
  131.3 76.6 %reduce-scatter.21.cloned.1.call-start = ((), (), s32[]{:S(2)}) async-start(), calls=%async_computation.17 | async-start | bytes 1179648 | tf_op jit(solution)/shard_map/reduce_scatter | solution.py:142
  190.3 188.3 %reduce-scatter.23.cloned.1.call-start = ((), (), s32[]{:S(2)}) async-start(), calls=%async_computation.18 | async-start | bytes 1179648 | tf_op jit(solution)/shard_map/reduce_scatter | solution.py:142
  345.1 72.1 %reduce-scatter.25.cloned.1.call-start = ((), (), s32[]{:S(2)}) async-start(), calls=%async_computation.19 | async-start | bytes 1179648 | tf_op jit(solution)/shard_map/reduce_scatter | solution.py:142
  399.6 187.5 %reduce-scatter.31.cloned.1.call-start = ((), (), s32[]{:S(2)}) async-start(), calls=%async_computation.22 | async-start | bytes 1179648 | tf_op jit(solution)/shard_map/reduce_scatter | solution.py:142
  550.7 81.9 %reduce-scatter.33.cloned.1.call-start = ((), (), s32[]{:S(2)}) async-start(), calls=%async_computation.23 | async-start | bytes 1179648 | tf_op jit(solution)/shard_map/reduce_scatter | solution.py:155
  612.6 175.5 %reduce-scatter.37.cloned.1.call-start = ((), (), s32[]{:S(2)}) async-start(), calls=%async_computation.25 | async-start | bytes 1179648 | tf_op jit(solution)/shard_map/reduce_scatter | solution.py:142
  751.1 220.6 %reduce-scatter.35.cloned.1.call-start = ((), (), s32[]{:S(2)}) async-start(), calls=%async_computation.24 | async-start | bytes 1179648 | tf_op jit(solution)/shard_map/reduce_scatter | solution.py:155
  942.3 289.8 %reduce-scatter.27.cloned.1.call-start = ((), (), s32[]{:S(2)}) async-start(), calls=%async_computation.20 | async-start | bytes 1179648 | tf_op jit(solution)/shard_map/reduce_scatter | solution.py:142
  1044.7 106.8 %collective-permute-start.52 = (bf16[512,384]{0,1:T(8,128)(2,1)}, bf16[512,384]{0,1:T(8,128)(2,1)}, u32[]{:S(2)}, u32[]{:S(2)}) collective-permute-start(bf16[512,384]{0,1:T(8,128)(2,1)} %get-tuple-element.2550), channel_id=1, source_target_pairs={{0,3},{1,4},{2,5},{3,6},{4,7},{8,11},{9,12},{10,13},{11,14},{12,15... | collective-permute-start | bytes 1179656 | tf_op jit(solution)/shard_map/ppermute | solution.py:12
  1046.9 108.7 %collective-permute-start.53 = (bf16[512,384]{0,1:T(8,128)(2,1)}, bf16[512,384]{0,1:T(8,128)(2,1)}, u32[]{:S(2)}, u32[]{:S(2)}) collective-permute-start(bf16[512,384]{0,1:T(8,128)(2,1)} %get-tuple-element.2550), channel_id=1, source_target_pairs={{0,2},{1,3},{2,4},{3,5},{4,6},{5,7},{8,10},{9,11},{10,12},{11,13},... | collective-permute-start | bytes 1179656 | tf_op jit(solution)/shard_map/ppermute | solution.py:12
  1052.9 102.7 %collective-permute-start.54 = (bf16[512,384]{0,1:T(8,128)(2,1)}, bf16[512,384]{0,1:T(8,128)(2,1)}, u32[]{:S(2)}, u32[]{:S(2)}) collective-permute-start(bf16[512,384]{0,1:T(8,128)(2,1)} %get-tuple-element.2550), channel_id=1, source_target_pairs={{0,1},{1,2},{2,3},{3,4},{4,5},{5,6},{6,7},{8,9},{9,10},{10,11},{11... | collective-permute-start | bytes 1179656 | tf_op jit(solution)/shard_map/ppermute | solution.py:12
  1055.1 103.3 %collective-permute-start.49 = (bf16[512,384]{0,1:T(8,128)(2,1)}, bf16[512,384]{0,1:T(8,128)(2,1)}, u32[]{:S(2)}, u32[]{:S(2)}) collective-permute-start(bf16[512,384]{0,1:T(8,128)(2,1)} %maximum_select_fusion.5), channel_id=1, source_target_pairs={{0,3},{1,4},{2,5},{3,6},{4,7},{8,11},{9,12},{10,13},{11,14},{12,15... | collective-permute-start | bytes 1179656 | tf_op jit(solution)/shard_map/ppermute | solution.py:12
  1057.1 65.6 %collective-permute-start.34 = (bf16[256,768]{1,0:T(8,128)(2,1)}, bf16[256,768]{1,0:T(8,128)(2,1)}, u32[]{:S(2)}, u32[]{:S(2)}) collective-permute-start(bf16[256,768]{1,0:T(8,128)(2,1)} %get-tuple-element.2479), channel_id=1, source_target_pairs={{16,0},{17,1},{18,2},{19,3},{20,4},{21,5},{22,6},{23,7},{24,8},{25... | collective-permute-start | bytes 1179656 | tf_op jit(solution)/shard_map/ppermute | solution.py:12
  1122.7 109.4 %reduce-scatter.39.cloned.1.call-start = ((), (), s32[]{:S(2)}) async-start(), calls=%async_computation.26 | async-start | bytes 1179648 | tf_op jit(solution)/shard_map/reduce_scatter | solution.py:155
  1155.2 85.1 %reduce-scatter.43.cloned.1.call-start = ((), (), s32[]{:S(2)}) async-start(), calls=%async_computation.28 | async-start | bytes 1179648 | tf_op jit(solution)/shard_map/reduce_scatter | solution.py:142
  1222.7 198.4 %reduce-scatter.41.cloned.1.call-start = ((), (), s32[]{:S(2)}) async-start(), calls=%async_computation.27 | async-start | bytes 1179648 | tf_op jit(solution)/shard_map/reduce_scatter | solution.py:155
  1393.2 91.8 %reduce-scatter.45.cloned.1.call-start = ((), (), s32[]{:S(2)}) async-start(), calls=%async_computation.29 | async-start | bytes 1179648 | tf_op jit(solution)/shard_map/reduce_scatter | solution.py:155
  1465.7 264.5 %reduce-scatter.49.cloned.1.call-start = ((), (), s32[]{:S(2)}) async-start(), calls=%async_computation.31 | async-start | bytes 589824
  1474.3 145.0 %collective-permute-start.61 = (bf16[512,192]{0,1:T(8,128)(2,1)}, bf16[512,192]{0,1:T(8,128)(2,1)}, u32[]{:S(2)}, u32[]{:S(2)}) collective-permute-start(bf16[512,192]{0,1:T(8,128)(2,1)} %slice.398), channel_id=1, source_target_pairs={{16,0},{17,1},{18,2},{19,3},{20,4},{21,5},{22,6},{23,7},{24,8},{25... | collective-permute-start | bytes 589832 | tf_op jit(solution)/shard_map/ppermute | solution.py:12
  1598.2 87.5 %collective-permute-start.55 = (bf16[512,384]{0,1:T(8,128)(2,1)}, bf16[512,384]{0,1:T(8,128)(2,1)}, u32[]{:S(2)}, u32[]{:S(2)}) collective-permute-start(bf16[512,384]{0,1:T(8,128)(2,1)} %get-tuple-element.2538), channel_id=1, source_target_pairs={{1,0},{2,1},{3,2},{4,3},{5,4},{6,5},{7,6},{9,8},{10,9},{11,10},{12... | collective-permute-start | bytes 1179656 | tf_op jit(solution)/shard_map/ppermute | solution.py:12
  1611.5 74.2 %collective-permute-start.56 = (bf16[512,384]{0,1:T(8,128)(2,1)}, bf16[512,384]{0,1:T(8,128)(2,1)}, u32[]{:S(2)}, u32[]{:S(2)}) collective-permute-start(bf16[512,384]{0,1:T(8,128)(2,1)} %get-tuple-element.2540), channel_id=1, source_target_pairs={{2,0},{3,1},{4,2},{5,3},{6,4},{7,5},{10,8},{11,9},{12,10},{13,11},... | collective-permute-start | bytes 1179656 | tf_op jit(solution)/shard_map/ppermute | solution.py:12
  1612.8 72.9 %collective-permute-start.57 = (bf16[512,384]{0,1:T(8,128)(2,1)}, bf16[512,384]{0,1:T(8,128)(2,1)}, u32[]{:S(2)}, u32[]{:S(2)}) collective-permute-start(bf16[512,384]{0,1:T(8,128)(2,1)} %get-tuple-element.2539), channel_id=1, source_target_pairs={{3,0},{4,1},{5,2},{6,3},{7,4},{11,8},{12,9},{13,10},{14,11},{15,12... | collective-permute-start | bytes 1179656 | tf_op jit(solution)/shard_map/ppermute | solution.py:12
  1691.8 308.8 %all-reduce.6.cloned.1.call-start = ((), (), s32[]{:S(2)}) async-start(), calls=%async_computation.32 | async-start | bytes 27131904 | tf_op jit(solution)/shard_map/psum | solution.py:535
  (280 other events, 4536.9 us)
Sparse Core Ops, SparseCore 0:
  131.5 37.3 reduce-scatter.18
  190.4 17.4 reduce-scatter.20
  345.2 33.3 reduce-scatter.22
  399.7 17.4 reduce-scatter.24
  550.8 36.3 reduce-scatter.30
  612.7 19.7 reduce-scatter.32
  751.2 36.8 reduce-scatter.36
  942.4 29.2 reduce-scatter.34
  1122.8 23.5 reduce-scatter.26
  1155.3 16.3 reduce-scatter.38
  1222.8 17.4 reduce-scatter.42
  1393.3 27.6 reduce-scatter.40
  1465.8 16.4 reduce-scatter.44
  1670.5 11.1 reduce-scatter.48
  1683.8 17.4 reduce-scatter.28
  1703.5 17.4 reduce-scatter.46
  1724.7 275.9 all-reduce.5
where the time goes:
time: 2040 us; the launch traced here: 2020 us
  matrix products  531 us (26%)
  waiting for transfers between devices  520 us (25%)
  blocking collectives  320 us (16%)
  other arithmetic  260 us (13%)
  local copies, waits for them, and re-layouts  226 us (11%)
  starting transfers between devices  144 us (7%)
    sub x27, matrix products, softmax_rows(): weights = jnp.exp(scores - row_top)  198 us
    psum x1, waiting for transfers between devices, local(): lax.psum((grad_query_key, grad_query_bias, grad_value_own, grad_value_bia...  194 us
    reduce_scatter x9, waiting for transfers between devices, spread_sum(): lax.psum_scatter(action(jnp.int32(0), row_count * lax.axis_size('tensor')...  154 us
    ppermute x62, starting transfers between devices, shifted(): lax.ppermute(value, axis, [(source, source + steps) for source in range(i...  142 us
    all_gather x12, blocking collectives, collect(): return lax.all_gather(values, 'tensor', axis=0, tiled=True)  137 us
    ppermute x62, waiting for transfers between devices, shifted(): lax.ppermute(value, axis, [(source, source + steps) for source in range(i...  113 us
    dynamic_slice x72, local copies, waits for them, and re-layouts, head_pair(): lax.dynamic_slice_in_dim(values, first_lane, 2 * HEAD, 1)  95.7 us
    dot_general x18, matrix products, pair_step(): jnp.einsum('hqk,khd->qhd', attention.astype(jnp.bfloat16), head_pair(valu...  88.6 us
  transfers between devices with their start and end apart: 79, of which 29 were waited for; matrix products, arithmetic and copies ran while one was open for 22% of the time, Pallas kernels for 0%

commit v1 on v0

v1 whole, which is shorter than its diff:
```python
import jax
import jax.numpy as jnp
from jax import lax
from jax.experimental import pallas as pl
from jax.experimental.pallas import tpu as pltpu
from jax.sharding import PartitionSpec as P

F32 = jnp.float32
BF = jnp.bfloat16
NEG=-1e30
def dot_nt(a,b): return lax.dot_general(a,b,(((1,),(1,)),((),())),preferred_element_type=F32)
def dot_nn(a,b): return lax.dot_general(a,b,(((1,),(0,)),((),())),preferred_element_type=F32)
def dot_tn(a,b): return lax.dot_general(a,b,(((0,),(0,)),((),())),preferred_element_type=F32)

def lane_low(shape):
    return lax.broadcasted_iota(jnp.int32, shape, 1) < 64

def head_of(pair, sub, fill):
    low = lane_low(pair.shape)
    keep = low if sub==0 else ~low
    return jnp.where(keep, pair, jnp.full_like(pair, fill))

def fwd_local_kernel(flag_ref, q_ref, k_ref, v_ref, pk_ref, pv_ref, o_ref, l_ref, m_ref):
    pairs = q_ref.shape[1]//128
    n = q_ref.shape[0]; half = n//2
    def run(with_partner):
        for c in range(2):
            rows = pl.ds(c*half, half)
            nk = (c+1)*half
            row = lax.broadcasted_iota(jnp.int32,(half,nk),0)+c*half
            col = lax.broadcasted_iota(jnp.int32,(half,nk),1)
            ok = col<=row
            for p in range(pairs):
                ls = slice(p*128,(p+1)*128)
                qp = q_ref[rows, ls]
                kp = k_ref[0:nk, ls]; vp = v_ref[0:nk, ls]
                outs=[]
                for sub in range(2):
                    s = dot_nt(qp, head_of(kp, sub, 0))
                    s = jnp.where(ok, s, NEG)
                    m = jnp.max(s,axis=1,keepdims=True)
                    if with_partner:
                        s2 = dot_nt(qp, head_of(pk_ref[:, ls], sub, 0))
                        m = jnp.maximum(m, jnp.max(s2,axis=1,keepdims=True))
                    e = jnp.exp(s-m).astype(BF)
                    o = dot_nn(e, head_of(vp, sub, 1))
                    if with_partner:
                        e2 = jnp.exp(s2-m).astype(BF)
                        o = o + dot_nn(e2, head_of(pv_ref[:, ls], sub, 1))
                    outs.append(o)
                    m_ref[rows, 2*p+sub:2*p+sub+1] = m
                low = lane_low(outs[0].shape)
                o_ref[rows, ls] = jnp.where(low, outs[0], outs[1])
                l_ref[rows, ls] = pltpu.roll(jnp.where(low, outs[1], outs[0]), 64, 1)
    @pl.when(flag_ref[0]==1)
    def _(): run(True)
    @pl.when(flag_ref[0]==0)
    def _(): run(False)

def fwd_cross_kernel(flag_ref, q_ref, k_ref, v_ref, o_ref, l_ref, m_ref, out_ref, lse_ref, scr):
    pairs = q_ref.shape[1]//128
    n = q_ref.shape[0]; half=n//2
    @pl.when(flag_ref[1]==0)
    def _():
        out_ref[...] = (o_ref[...]/l_ref[...]).astype(BF)
        for p in range(pairs):
            for sub in range(2):
                h=2*p+sub
                scr[:,h:h+1] = m_ref[:,h:h+1] + jnp.log(l_ref[:,h*64:h*64+1])
    @pl.when(flag_ref[1]==1)
    def _():
        for c in range(2):
            rows = pl.ds(c*half, half)
            for p in range(pairs):
                ls = slice(p*128,(p+1)*128)
                qp = q_ref[rows, ls]
                outs=[]; als=[]; ms=[]
                for sub in range(2):
                    h=2*p+sub
                    s = dot_nt(qp, head_of(k_ref[:, ls], sub, 0))
                    m0 = m_ref[rows,h:h+1]
                    m = jnp.maximum(m0, jnp.max(s,axis=1,keepdims=True))
                    e = jnp.exp(s-m).astype(BF)
                    outs.append(dot_nn(e, head_of(v_ref[:, ls], sub, 1)))
                    als.append(jnp.exp(m0-m)); ms.append(m)
                low = lane_low(outs[0].shape)
                al = jnp.where(low, als[0], als[1])
                o = o_ref[rows, ls]*al + jnp.where(low, outs[0], outs[1])
                l = l_ref[rows, ls]*al + pltpu.roll(jnp.where(low, outs[1], outs[0]), 64, 1)
                out_ref[rows, ls] = (o/l).astype(BF)
                lg = jnp.log(l)
                scr[rows, 2*p:2*p+1] = ms[0] + lg[:,0:1]
                scr[rows, 2*p+1:2*p+2] = ms[1] + lg[:,64:65]
    lse_ref[...] = jnp.transpose(scr[...])[0:8,:]

VM = pl.BlockSpec(memory_space=pltpu.VMEM)
SM = pl.BlockSpec(memory_space=pltpu.SMEM)
PAR = pltpu.CompilerParams(vmem_limit_bytes=48*1024*1024)
def S(shape,d): return jax.ShapeDtypeStruct(shape,d)
def attend_local(flags,q,k,v,pk,pv):
    n,w=q.shape
    return pl.pallas_call(fwd_local_kernel,out_shape=[S((n,w),F32),S((n,w),F32),S((n,128),F32)],in_specs=[SM]+[VM]*5,out_specs=[VM]*3,compiler_params=PAR)(flags,q,k,v,pk,pv)
def attend_cross(flags,q,k,v,o,l,m):
    n,w=q.shape
    return pl.pallas_call(fwd_cross_kernel,out_shape=[S((n,w),BF),S((8,n),F32)],in_specs=[SM]+[VM]*6,out_specs=[VM]*2,scratch_shapes=[pltpu.VMEM((n,128),F32)],compiler_params=PAR)(flags,q,k,v,o,l,m)

def bwd_tile(qp, kh, vh, dop, lse_row, del_row, ok):
    st = dot_nt(kh, qp)
    pt = jnp.exp(st - lse_row)
    if ok is not None: pt = jnp.where(ok, pt, 0.0)
    dpt = dot_nt(vh, dop)
    dst = (pt*(dpt-del_row)).astype(BF)
    return pt.astype(BF), dst

def deltas(do_ref, at_ref, scr, del_ref):
    pairs = do_ref.shape[1]//128
    for p in range(pairs):
        ls = slice(p*128,(p+1)*128)
        pr = do_ref[:,ls].astype(F32)*at_ref[:,ls].astype(F32)
        low = lane_low(pr.shape)
        scr[:,2*p:2*p+1] = jnp.sum(jnp.where(low,pr,0.0),axis=1,keepdims=True)
        scr[:,2*p+1:2*p+2] = jnp.sum(jnp.where(low,0.0,pr),axis=1,keepdims=True)
    del_ref[...] = jnp.transpose(scr[...])[0:8,:]

def bwd_cross_kernel(flag_ref, q_ref, do_ref, at_ref, lse_ref, k_ref, v_ref, dq_ref, dk_ref, dv_ref, del_ref, scr):
    deltas(do_ref, at_ref, scr, del_ref)
    pairs = q_ref.shape[1]//128
    nk = k_ref.shape[0]; kc=256
    @pl.when(flag_ref[1]==0)
    def _():
        dq_ref[...]=jnp.zeros_like(dq_ref); dk_ref[...]=jnp.zeros_like(dk_ref); dv_ref[...]=jnp.zeros_like(dv_ref)
    @pl.when(flag_ref[1]==1)
    def _():
        for p in range(pairs):
            ls = slice(p*128,(p+1)*128)
            qp=q_ref[:,ls]; dop=do_ref[:,ls]
            dqs=[None,None]
            low = lane_low((kc,128))
            for j in range(nk//kc):
                ks=pl.ds(j*kc,kc)
                kp=k_ref[ks,ls]; vp=v_ref[ks,ls]
                r=[]
                for sub in range(2):
                    h=2*p+sub
                    kh=head_of(kp,sub,0); vh=head_of(vp,sub,0)
                    pt,dst=bwd_tile(qp,kh,vh,dop,lse_ref[h:h+1,:],del_ref[h:h+1,:],None)
                    r.append((dot_nn(pt,dop), dot_nn(dst,qp)))
                    d=dot_tn(dst,kh)
                    dqs[sub]= d if dqs[sub] is None else dqs[sub]+d
                dv_ref[ks,ls]=jnp.where(low,r[0][0],r[1][0]).astype(BF)
                dk_ref[ks,ls]=jnp.where(low,r[0][1],r[1][1]).astype(BF)
            dq_ref[:,ls]=dqs[0]+dqs[1]

def bwd_local_kernel(flag_ref, q_ref, do_ref, lse_ref, del_ref, k_ref, v_ref, pk_ref, pv_ref, dqc_ref, dq_ref, dk_ref, dv_ref, dpk_ref, dpv_ref):
    pairs = q_ref.shape[1]//128
    n=q_ref.shape[0]; half=n//2; kc=half
    def tile_pair(p, ks, kr, vr, qoff, ok):
        ls = slice(p*128,(p+1)*128)
        qp=q_ref[qoff:,ls]; dop=do_ref[qoff:,ls]
        kp=kr[ks,ls]; vp=vr[ks,ls]
        low = lane_low((kc,128)); r=[]; dq=None
        for sub in range(2):
            h=2*p+sub
            kh=head_of(kp,sub,0); vh=head_of(vp,sub,0)
            pt,dst=bwd_tile(qp,kh,vh,dop,lse_ref[h:h+1,qoff:],del_ref[h:h+1,qoff:],ok)
            r.append((dot_nn(pt,dop), dot_nn(dst,qp)))
            d=dot_tn(dst,kh)
            dq = d if dq is None else dq+d
        return dq, jnp.where(low,r[0][1],r[1][1]), jnp.where(low,r[0][0],r[1][0])
    def mask(j):
        key=lax.broadcasted_iota(jnp.int32,(kc,n-j*kc),0); qq=lax.broadcasted_iota(jnp.int32,(kc,n-j*kc),1)
        return key<=qq
    for p in range(pairs):
        ls = slice(p*128,(p+1)*128)
        for j in range(2):
            ks=pl.ds(j*kc,kc)
            dq,dk,dv=tile_pair(p,ks,k_ref,v_ref,j*kc,mask(j))
            dk_ref[ks,ls]=dk; dv_ref[ks,ls]=dv
            if j==0: dq_ref[:,ls]=dqc_ref[:,ls]+dq
            else: dq_ref[kc:,ls]=dq_ref[kc:,ls]+dq
    @pl.when(flag_ref[0]==1)
    def _():
        for p in range(pairs):
            ls = slice(p*128,(p+1)*128)
            acc=dq_ref[:,ls]
            for j in range(2):
                ks=pl.ds(j*kc,kc)
                dq,dk,dv=tile_pair(p,ks,pk_ref,pv_ref,0,None)
                dpk_ref[ks,ls]=dk.astype(BF); dpv_ref[ks,ls]=dv.astype(BF)
                acc=acc+dq
            dq_ref[:,ls]=acc
    @pl.when(flag_ref[0]==0)
    def _():
        dpk_ref[...]=jnp.zeros_like(dpk_ref); dpv_ref[...]=jnp.zeros_like(dpv_ref)

def attend_cross_back(flags,q,do,at,lse,k,v):
    n,w=q.shape; nk=k.shape[0]
    return pl.pallas_call(bwd_cross_kernel,out_shape=[S((n,w),F32),S((nk,w),BF),S((nk,w),BF),S((8,n),F32)],in_specs=[SM]+[VM]*6,out_specs=[VM]*4,scratch_shapes=[pltpu.VMEM((n,128),F32)],compiler_params=PAR)(flags,q,do,at,lse,k,v)
def attend_local_back(flags,q,do,lse,dl,k,v,pk,pv,dqc):
    n,w=q.shape
    return pl.pallas_call(bwd_local_kernel,out_shape=[S((n,w),F32),S((n,w),F32),S((n,w),F32),S((n,w),BF),S((n,w),BF)],in_specs=[SM]+[VM]*9,out_specs=[VM]*5,compiler_params=PAR)(flags,q,do,lse,dl,k,v,pk,pv,dqc)


def swap(value, axis, bit=0):
    count = lax.axis_size(axis)
    return lax.ppermute(value, axis, [(i, i ^ (1 << bit)) for i in range(count)])


def shift(value, steps):
    count = lax.axis_size("batch")
    first, last = max(0, -steps), min(count, count - steps)
    return lax.ppermute(value, "batch", [(i, i + steps) for i in range(first, last)])


def after(value, *earlier):
    return lax.optimization_barrier((value,) + earlier)[0]


def matmul(left, right):
    return jnp.dot(left, right, preferred_element_type=F32)


def matmul_nt(left, right):
    return lax.dot_general(left, right, (((1,), (1,)), ((), ())), preferred_element_type=F32)


def matmul_tn(left, right):
    return lax.dot_general(left, right, (((0,), (0,)), ((), ())), preferred_element_type=F32)


def norm_rows(values, scales, shifts):
    centred = values - jnp.mean(values, axis=-1, keepdims=True)
    spread = jnp.mean(centred * centred, axis=-1, keepdims=True)
    return centred * lax.rsqrt(spread + 1e-05) * scales + shifts


def norm_back(values, scales, grad):
    centred = values - jnp.mean(values, axis=-1, keepdims=True)
    spread = jnp.mean(centred * centred, axis=-1, keepdims=True)
    rate = lax.rsqrt(spread + 1e-05)
    unit = centred * rate
    scaled = grad * scales
    inner = jnp.mean(scaled * unit, axis=-1, keepdims=True)
    result = rate * (scaled - jnp.mean(scaled, axis=-1, keepdims=True) - unit * inner)
    return result, jnp.sum(grad * unit, axis=0), jnp.sum(grad, axis=0)


def gelu_both(u):
    factor = 0.7978845608028654
    square = u * u
    t = jnp.tanh(factor * u * (1.0 + 0.044715 * square))
    value = 0.5 * u * (1.0 + t)
    slope = 0.5 * (1.0 + t) + 0.5 * u * (1.0 - t * t) * factor * (1.0 + 3 * 0.044715 * square)
    return value, slope


def tensor_sum(make_part, count, rows):
    size = rows // count
    sums = []
    for i in range(count):
        part = make_part(i * size, size).astype(BF)
        sums.append(part.astype(F32) + swap(part, "tensor").astype(F32))
    return jnp.concatenate(sums, axis=0)


CHUNKS = 2


def forward_layer(x, layer, flags, carried_values):
    rows = x.shape[0]
    normed = norm_rows(x, layer["gains"][0], layer["biases"][0]).astype(BF)
    queries = ((matmul(normed, layer["wq"]) + layer["bq"]).astype(BF) * 0.125).astype(BF)
    keys = matmul(normed, layer["wk"]).astype(BF)
    own = (matmul(normed, layer["wvo"]) + layer["bv"]).astype(BF)
    if carried_values is None:
        values = jnp.concatenate([own, matmul(normed, layer["wvx"]).astype(BF)], axis=1)
        sent = values
    else:
        sent = own
    prior_k = shift(keys, 2)
    prior_v = shift(sent, 2)
    part_k, part_v = swap(keys, "batch"), swap(sent, "batch")
    prior_k = jnp.concatenate([prior_k, swap(prior_k, "batch")], axis=0)
    prior_v = jnp.concatenate([prior_v, swap(prior_v, "batch")], axis=0)
    if carried_values is not None:
        width = own.shape[1]
        values, part_v, prior_v = [
            jnp.concatenate([a, b[:, :width]], axis=1)
            for a, b in zip((own, part_v, prior_v), carried_values)
        ]
    out, total, top = attend_local(flags, queries, keys, values, part_k, part_v)
    attended, lse = attend_cross(flags, queries, prior_k, prior_v, out, total, top)

    hidden = x + layer["bo"] + tensor_sum(
        lambda start, size: matmul(attended[start : start + size], layer["wo"]), CHUNKS, rows
    )
    mlp_in = norm_rows(hidden, layer["gains"][1], layer["biases"][1]).astype(BF)
    pieces = []

    def down(start, size):
        active, slope = gelu_both(matmul(mlp_in[start : start + size], layer["wup"]) + layer["bup"])
        active = active.astype(BF)
        pieces.append((active, slope.astype(BF)))
        return matmul(active, layer["wdown"])

    y = hidden + layer["bdown"] + tensor_sum(down, CHUNKS, rows)
    active = jnp.concatenate([p[0] for p in pieces], axis=0)
    slope = jnp.concatenate([p[1] for p in pieces], axis=0)
    stored = dict(
        x=x, normed=normed, queries=queries, keys=keys, values=values, part_k=part_k, part_v=part_v,
        prior_k=prior_k, prior_v=prior_v, attended=attended, lse=lse, hidden=hidden, mlp_in=mlp_in,
        active=active, slope=slope,
    )
    return y, (values, part_v, prior_v), stored


def backward_layer(dy, layer, kept, flags, returned):
    rows = dy.shape[0]
    dy_low = dy.astype(BF)
    pieces = []

    def up_back(start, size):
        d_active = matmul_nt(dy_low[start : start + size], layer["wdown"])
        d_up = (d_active * kept["slope"][start : start + size].astype(F32)).astype(BF)
        pieces.append(d_up)
        return matmul_nt(d_up, layer["wup"])

    d_mlp_in = tensor_sum(up_back, CHUNKS, rows)
    d_up = jnp.concatenate(pieces, axis=0)
    back, d_gain1, d_bias1 = norm_back(kept["hidden"], layer["gains"][1], d_mlp_in)
    dh = dy + back
    dh_low = dh.astype(BF)
    d_attended = matmul_nt(dh_low, layer["wo"]).astype(BF)
    width = layer["wvo"].shape[1]
    dq_cross, d_prior_k, d_prior_v, delta = attend_cross_back(
        flags, kept["queries"], d_attended, kept["attended"], kept["lse"], kept["prior_k"], kept["prior_v"]
    )
    if returned is None:
        send_v = d_prior_v[:, :width]
    else:
        send_v = jnp.concatenate(
            [
                (d_prior_v[:, :width].astype(F32) + returned[2].astype(F32)).astype(BF),
                d_prior_v[:, width:],
            ],
            axis=1,
        )

    def home(grads):
        return shift(
            (grads[:rows].astype(F32) + swap(grads[rows:], "batch").astype(F32)).astype(BF), -2
        ).astype(F32)

    far_k, far_v = home(d_prior_k), home(send_v)
    dq, dk, dv, d_part_k, d_part_v = attend_local_back(
        flags, kept["queries"], d_attended, kept["lse"], delta, kept["keys"], kept["values"],
        kept["part_k"], kept["part_v"], dq_cross,
    )
    dk = dk + swap(d_part_k, "batch").astype(F32) + far_k
    dv_own, dv_other = dv[:, :width], dv[:, width:]
    if returned is None:
        back_values = (dv_other, d_part_v[:, width:], d_prior_v[:, width:])
        dv_low = (
            dv_own + swap(d_part_v[:, :width], "batch").astype(F32) + far_v
        ).astype(BF)
    else:
        back_values = None
        near = jnp.concatenate(
            [
                (d_part_v[:, :width].astype(F32) + returned[1].astype(F32)).astype(BF),
                d_part_v[:, width:],
            ],
            axis=1,
        )
        arrived = swap(near, "batch").astype(F32) + far_v
        dv_low = jnp.concatenate(
            [dv_own + returned[0] + arrived[:, :width], dv_other + arrived[:, width:]], axis=1
        ).astype(BF)
    dq_low = (dq * 0.125).astype(BF)
    dk_low = dk.astype(BF)

    def input_part(start, size):
        cut = slice(start, start + size)
        part = matmul_nt(dq_low[cut], layer["wq"]) + matmul_nt(dk_low[cut], layer["wk"])
        part = part + matmul_nt(dv_low[cut, :width], layer["wvo"])
        if returned is not None:
            part = part + matmul_nt(dv_low[cut, width:], layer["wvx"])
        return part

    d_normed = tensor_sum(input_part, CHUNKS, rows)
    back, d_gain0, d_bias0 = norm_back(kept["x"], layer["gains"][0], d_normed)
    dx = dh + back

    half = layer["wdown"].shape[1]
    up_cols = d_up.shape[1]
    d_down = matmul_tn(kept["active"], dy_low).astype(BF)
    d_ups = [
        matmul_tn(kept["mlp_in"], d_up[:, i : i + half]).astype(BF) for i in range(0, up_cols, half)
    ]
    d_out = matmul_tn(kept["attended"], dh_low).astype(BF)
    d_qk = matmul_tn(kept["normed"], jnp.concatenate([dq_low, dk_low], axis=1)).astype(BF)
    d_v = matmul_tn(kept["normed"], dv_low).astype(BF)
    if returned is None:
        d_v = jnp.concatenate([d_v, jnp.zeros_like(d_v)], axis=1)
    small = jnp.concatenate(
        [
            d_gain0, d_gain1, d_bias0, d_bias1, jnp.sum(dh, axis=0), jnp.sum(dy, axis=0),
            jnp.sum(dq_low.astype(F32), axis=0), jnp.sum(dv_low[:, :width].astype(F32), axis=0),
            jnp.sum(d_up.astype(F32), axis=0),
        ]
    )
    mlp = jnp.concatenate(
        [d.reshape(2, 2, -1, half) for d in [d_down] + d_ups], axis=2
    )
    features = half
    v_rows = features // 4
    v_packed = jnp.concatenate(
        [d_v.reshape(2, 2, 2, v_rows // 2, 2 * width)[:, :, i] for i in range(2)], axis=3
    )
    pad = 4 * SMALL_ROWS * features - small.shape[0]
    small_packed = jnp.pad(small, (0, pad)).astype(BF).reshape(2, 2, SMALL_ROWS, features)
    attn = jnp.concatenate(
        [d_qk.reshape(2, 2, -1, features), d_out.reshape(2, 2, -1, features), v_packed, small_packed],
        axis=2,
    )
    return dx, back_values, mlp, attn


SMALL_ROWS = 32


def scatter_sum(parts):
    core = lax.axis_index("batch") % 2
    section = lax.axis_index("section")
    take = lambda a, i, axis: lax.dynamic_index_in_dim(a, i, axis, keepdims=False)
    near = take(parts, core, 1).astype(F32) + swap(take(parts, 1 - core, 1), "batch").astype(F32)
    near = near.astype(BF)
    mine = take(near, section, 0).astype(F32) + swap(take(near, 1 - section, 0), "section").astype(F32)
    return all_sum(mine.astype(BF))


def all_sum(part):
    bits = (lax.axis_size("batch") // 2).bit_length() - 1
    index = lax.axis_index("batch")
    for bit in range(1, bits + 1):
        side = (index >> bit) & 1
        halves = part.reshape((2, part.shape[0] // 2) + part.shape[1:])
        keep = lax.dynamic_index_in_dim(halves, side, 0, keepdims=False)
        send = lax.dynamic_index_in_dim(halves, 1 - side, 0, keepdims=False)
        part = (keep.astype(F32) + swap(send, "batch", bit).astype(F32)).astype(BF)
    for bit in range(bits, 0, -1):
        side = (index >> bit) & 1
        part = paired(part, swap(part, "batch", bit), side).reshape((2 * part.shape[0],) + part.shape[1:])
    return part


def paired(mine, other, side):
    first = jnp.where(side == 0, mine, other)
    second = jnp.where(side == 0, other, mine)
    return jnp.stack([first, second])


def fetch_weights(values):
    core = lax.axis_index("batch") % 2
    halves = [v.reshape((2, v.shape[0] // 2) + v.shape[1:]) for v in values]
    sent = [lax.dynamic_index_in_dim(h, core, 0, keepdims=False) for h in halves]
    got = swap(sent, "section")
    other = swap(got, "batch")
    return [
        paired(a, b, core).reshape(v.shape) for a, b, v in zip(got, other, values)
    ]


def local(
    tokens, block_place, cotangent, norm_gains, norm_biases, query_key, query_bias, value_own, value_bias,
    value_extra, out_weight, out_bias, up_weight, up_bias, down_weight, down_bias,
):
    section = lax.axis_index("section")
    tensor = lax.axis_index("tensor")
    core = lax.axis_index("batch") % 2
    features = tokens.shape[3]
    half_rows = tokens.shape[2]
    head_width = query_bias.shape[1]
    width = value_own.shape[2]
    micros = tokens.shape[0]
    assert micros == 2 and lax.axis_size("section") == 2 and lax.axis_size("tensor") == 2

    def micro(array):
        return lax.dynamic_index_in_dim(array, section, 0, keepdims=False)[0]

    my_tokens = micro(tokens)
    my_cotangent = micro(cotangent)
    place = micro(block_place)
    flags = jnp.stack([place & 1, place >> 1]).astype(jnp.int32)

    small_sizes = [2 * features, 2 * features, head_width, width, features, up_bias.shape[1], features]
    small = jnp.concatenate(
        [a.reshape(-1) for a in (norm_gains, norm_biases, query_bias, value_bias, out_bias, up_bias, down_bias)]
    )
    wqk = query_key[0].reshape(features, 2 * head_width)
    first_own = [wqk, value_own[0]]
    x_rows = paired(my_tokens, swap(my_tokens, "tensor"), tensor).reshape(2 * half_rows, features)
    small_other = swap(small, "section")
    first_other = fetch_weights(first_own)
    second_own = [out_weight[0], up_weight[0]]
    held = lax.optimization_barrier(tuple(second_own) + tuple(first_other))
    second_other = fetch_weights(list(held[:2]))
    first_other = list(held[2:])
    held = lax.optimization_barrier((down_weight[0],) + tuple(second_other))
    third_other = fetch_weights([held[0]])
    second_other = list(held[1:])
    owns = first_own + second_own + [down_weight[0]]
    others = first_other + second_other + third_other

    layers = []
    for number in range(2):
        mine = section == number
        picked = [jnp.where(mine, a, b) for a, b in zip(owns, others)]
        numbers = jnp.where(mine, small, small_other)
        cuts = []
        start = 0
        for size in small_sizes:
            cuts.append(numbers[start : start + size])
            start += size
        layers.append(
            dict(
                gains=cuts[0].reshape(2, features), biases=cuts[1].reshape(2, features), bq=cuts[2], bv=cuts[3],
                bo=cuts[4], bup=cuts[5], bdown=cuts[6], wq=picked[0][:, :head_width], wk=picked[0][:, head_width:],
                wvo=picked[1], wvx=value_extra, wo=picked[2], wup=picked[3], wdown=picked[4],
            )
        )

    y0, carried, kept0 = forward_layer(x_rows.astype(F32), layers[0], flags, None)
    y0_low = y0.astype(BF)
    y1, ignored, kept1 = forward_layer(y0_low.astype(F32), layers[1], flags, carried)
    y1_low = y1.astype(BF)

    def my_half(rows):
        return lax.dynamic_slice_in_dim(rows, tensor * half_rows, half_rows, 0)

    def by_section(first, second, low):
        mine = jnp.where(section == 0, first, second)
        other = swap(jnp.where(section == 0, second, first).astype(low), "section").astype(mine.dtype)
        return paired(mine, other, section)

    outputs = by_section(my_half(y0_low), my_half(y1_low), BF)

    dy1 = paired(my_cotangent, swap(my_cotangent, "tensor"), tensor).reshape(2 * half_rows, features)
    dx1, back_values, mlp1, attn1 = backward_layer(dy1.astype(F32), layers[1], kept1, flags, None)
    mlp1, attn1 = scatter_sum(mlp1), scatter_sum(attn1)
    dx0, ignored, mlp0, attn0 = backward_layer(
        dx1.astype(BF).astype(F32), layers[0], kept0, flags, back_values
    )
    mlp0, attn0 = scatter_sum(mlp0), scatter_sum(attn0)
    input_grads = by_section(my_half(dx0), my_half(dx1), BF)

    def gathered(first, second):
        mine = jnp.where(section == 0, first, second)
        other = swap(jnp.where(section == 0, second, first), "section")
        both = paired(mine, other, section)
        return jnp.moveaxis(paired(both, swap(both, "batch"), core), 0, 1)

    mlp = gathered(mlp0, mlp1)
    attn = gathered(attn0, attn1)
    v_rows = features // 4

    def v_unpacked(packed):
        return jnp.stack([packed[..., : 2 * width], packed[..., 2 * width :]], axis=-3)

    qk_rows, out_rows = features // 4, head_width // 4
    v_start = qk_rows + out_rows
    v_end = v_start + v_rows // 2
    extra_mine = attn0[v_start:v_end]
    extra_mine = v_unpacked(extra_mine).reshape(v_rows, 2 * width)[:, width:]
    extra = paired(extra_mine, swap(extra_mine, "batch"), core).reshape(2 * v_rows, width).astype(F32)

    d_qk = attn[:, :, :qk_rows].reshape(features, 2, head_width).astype(F32)
    d_out = attn[:, :, qk_rows:v_start].reshape(head_width, features).astype(F32)
    d_v = v_unpacked(attn[:, :, v_start:v_end]).reshape(features, 2 * width)[:, :width].astype(F32)
    numbers = attn[:, :, v_end:].reshape(-1).astype(F32)
    d_down = mlp[:, :, : down_weight.shape[1] // 4].reshape(-1, features).astype(F32)
    pieces = []
    start = down_weight.shape[1] // 4
    for i in range(up_weight.shape[2] // features):
        pieces.append(mlp[:, :, start : start + features // 4].reshape(features, features))
        start += features // 4
    d_up = jnp.concatenate(pieces, axis=1).astype(F32)
    cuts = []
    start = 0
    for size in [features] * 6 + [head_width, width, up_bias.shape[1]]:
        cuts.append(numbers[start : start + size])
        start += size
    return (
        outputs.reshape(1, micros, 1, half_rows, features),
        input_grads.reshape(1, micros, 1, half_rows, features),
        jnp.stack(cuts[0:2])[None],
        jnp.stack(cuts[2:4])[None],
        d_qk[None],
        cuts[6][None],
        d_v[None],
        cuts[7][None],
        extra,
        d_out[None],
        cuts[4][None],
        d_up[None],
        cuts[8][None],
        d_down[None],
        cuts[5][None],
    )


def solution(mesh):
    return jax.shard_map(
        local,
        mesh=mesh,
        in_specs=(
            P(None, "batch", "tensor", None),
            P(None, "batch"),
            P(None, "batch", "tensor", None),
            P("section", None, None),
            P("section", None, None),
            P("section", None, None, "tensor"),
            P("section", "tensor"),
            P("section", None, "tensor"),
            P("section", "tensor"),
            P(None, "tensor"),
            P("section", "tensor", None),
            P("section", None),
            P("section", None, "tensor"),
            P("section", "tensor"),
            P("section", "tensor", None),
            P("section", None),
        ),
        out_specs=(
            P("section", None, "batch", "tensor", None),
            P("section", None, "batch", "tensor", None),
            P("section", None, None),
            P("section", None, None),
            P("section", None, None, "tensor"),
            P("section", "tensor"),
            P("section", None, "tensor"),
            P("section", "tensor"),
            P("section", "tensor"),
            P("section", "tensor", None),
            P("section", None),
            P("section", None, "tensor"),
            P("section", "tensor"),
            P("section", "tensor", None),
            P("section", None),
        ),
        check_vma=False,
    )
```

time: 2040 us -> 658 us (0.32)
  matrix products: 531 us -> 52.6 us
  blocking collectives: 320 us -> 0 us
  waiting for transfers between devices: 520 us -> 315 us
  other arithmetic: 260 us -> 82 us
  local copies, waits for them, and re-layouts: 226 us -> 61.3 us
  starting transfers between devices: 144 us -> 96.8 us
  Pallas kernels: 0 us -> 36.7 us
    dot_general x120 -> x55, matrix products: 333 us -> 52.6 us  [the longest x24 18.9 us: matmul_nt(): lax.dot_general(left, right, (((1,), (1,)), ((), ())), preferred_element_...]
    reduce_scatter x15 -> x0, waiting for transfers between devices: 212 us -> none  [the longest x9 154 us: spread_sum(): lax.psum_scatter(action(jnp.int32(0), row_count * lax.axis_size('tensor')...]
    all_gather x18 -> x0, blocking collectives: 211 us -> none  [the longest x12 137 us: collect(): return lax.all_gather(values, 'tensor', axis=0, tiled=True)]
    ppermute x62 -> x84, waiting for transfers between devices: 113 us -> 315 us  [the longest x76 267 us: swap(): return lax.ppermute(value, axis, [(i, i ^ 1 << bit) for i in range(count)])]
    sub x27 -> x0, matrix products: 198 us -> none  [softmax_rows(): weights = jnp.exp(scores - row_top)]
    psum x1 -> x0, waiting for transfers between devices: 194 us -> none  [local(): lax.psum((grad_query_key, grad_query_bias, grad_value_own, grad_value_bia...]
    psum x2 -> x0, blocking collectives: 110 us -> none  [the longest x1 62.5 us: local(): lax.psum((grad_norm_gains, grad_norm_biases, grad_out_bias, grad_down_bia...]
    dynamic_slice x81 -> x4, local copies, waits for them, and re-layouts: 104 us -> 0.54 us  [the longest x1 0.31 us: fetch_weights(): lax.dynamic_index_in_dim(h, core, 0, keepdims=False)]
  transfers between devices with their start and end apart: 79 -> 84, of which waited for: 29 -> 43; matrix products, arithmetic and copies ran while one was open for 22% -> 22% of each run, Pallas kernels for 0% -> 5%
where the time goes in v1:
time: 658 us; the launch traced here: 648 us
  waiting for transfers between devices  315 us (48%)
  starting transfers between devices  96.8 us (15%)
  other arithmetic  82 us (12%)
  local copies, waits for them, and re-layouts  61.3 us (9%)
  matrix products  52.6 us (8%)
  Pallas kernels  36.7 us (6%)
    ppermute x76, waiting for transfers between devices, swap(): return lax.ppermute(value, axis, [(i, i ^ 1 << bit) for i in range(count)])  267 us
    ppermute x76, starting transfers between devices, swap(): return lax.ppermute(value, axis, [(i, i ^ 1 << bit) for i in range(count)])  77.1 us
    ppermute x8, waiting for transfers between devices, shift(): lax.ppermute(value, 'batch', [(i, i + steps) for i in range(first, last)])  48 us
    unnamed x228, local copies, waits for them, and re-layouts  26.1 us
    ppermute x8, starting transfers between devices, shift(): lax.ppermute(value, 'batch', [(i, i + steps) for i in range(first, last)])  19.7 us
    dot_general x24, matrix products, matmul_nt(): lax.dot_general(left, right, (((1,), (1,)), ((), ())), preferred_element_...  18.9 us
    dot_general x12, matrix products, matmul_tn(): lax.dot_general(left, right, (((0,), (0,)), ((), ())), preferred_element_...  17.6 us
    dot_general x19, matrix products, matmul(): return jnp.dot(left, right, preferred_element_type=F32)  16.1 us
  transfers between devices with their start and end apart: 84, of which 43 were waited for; matrix products, arithmetic and copies ran while one was open for 22% of the time, Pallas kernels for 5%

profile of v1, /device:TPU:0, one launch (start us, length us, event | category | flops | bytes accessed | tf_op | source)
XLA Modules:
  0.0 647.9 jit_solution(14737064123582253634)
XLA Ops:
  23.0 7.8 %collective-permute-done.4 = bf16[384,192]{0,1:T(8,128)(2,1)S(1)} collective-permute-done((bf16[384,192]{0,1:T(8,128)(2,1)}, bf16[384,192]{0,1:T(8,128)(2,1)S(1)}, u32[]{:S(2)}, u32[]{:S(2)}) %collective-permute-start.4) | collective-permute-done | bytes 147488 | tf_op jit(solution)/shard_map/ppermute | solution.py:206
  50.6 22.5 %collective-permute-done.14 = bf16[384,1536]{1,0:T(8,128)(2,1)S(1)} collective-permute-done((bf16[384,1536]{1,0:T(8,128)(2,1)S(1)}, bf16[384,1536]{1,0:T(8,128)(2,1)S(1)}, u32[]{:S(2)}, u32[]{:S(2)}) %collective-permute-start.14) | collective-permute-done | bytes 1179680 | tf_op jit(solution)/shard_map/ppermute | solution.py:206
  82.0 9.3 %shard_map.272 = (bf16[512,384]{1,0:T(8,128)(2,1)S(1)}, f32[8,512]{1,0:T(8,128)S(1)}) custom-call(s32[2]{0:T(128)S(1)} %pad_add_fusion.flag_ref, bf16[512,384]{1,0:T(8,128)(2,1)S(1)} %fusion.102.q_ref, bf16[1024,384]{1,0:T(8,128)(2,1)S(1)} %constant_dynamic-update-slice_fusion.k_ref, bf16[1024,384]{1,0:T(8,128)(2,1)S(1)} %constant_dynamic-update-slice_fusion.2.v_ref, ...), custom_call_target="tpu_custom_call" | custom-call | tf_op jit(solution)/shard_map/pallas_call | solution.py:105
  96.9 7.9 %collective-permute-done.17 = bf16[256,768]{1,0:T(8,128)(2,1)S(1)} collective-permute-done((bf16[256,768]{1,0:T(8,128)(2,1)S(1)}, bf16[256,768]{1,0:T(8,128)(2,1)S(1)}, u32[]{:S(2)}, u32[]{:S(2)}) %collective-permute-start.17) | collective-permute-done | bytes 393248 | tf_op jit(solution)/shard_map/ppermute | solution.py:206
  104.9 8.3 %collective-permute-done.16 = bf16[256,768]{1,0:T(8,128)(2,1)S(1)} collective-permute-done((bf16[256,768]{1,0:T(8,128)(2,1)S(1)}, bf16[256,768]{1,0:T(8,128)(2,1)S(1)}, u32[]{:S(2)}, u32[]{:S(2)}) %collective-permute-start.16) | collective-permute-done | bytes 393248 | tf_op jit(solution)/shard_map/ppermute | solution.py:206
  114.0 10.5 %collective-permute-done.18 = bf16[768,768]{1,0:T(8,128)(2,1)S(1)} collective-permute-done((bf16[768,768]{1,0:T(8,128)(2,1)S(1)}, bf16[768,768]{1,0:T(8,128)(2,1)S(1)}, u32[]{:S(2)}, u32[]{:S(2)}) %collective-permute-start.18) | collective-permute-done | bytes 1179680 | tf_op jit(solution)/shard_map/ppermute | solution.py:206
  183.6 9.6 %collective-permute-done.29 = bf16[256,768]{1,0:T(8,128)(2,1)S(1)} collective-permute-done((bf16[256,768]{1,0:T(8,128)(2,1)S(1)}, bf16[256,768]{1,0:T(8,128)(2,1)S(1)}, u32[]{:S(2)}, u32[]{:S(2)}) %collective-permute-start.29) | collective-permute-done | bytes 393248 | tf_op jit(solution)/shard_map/ppermute | solution.py:206
  193.3 8.0 %collective-permute-done.28 = bf16[256,768]{1,0:T(8,128)(2,1)S(1)} collective-permute-done((bf16[256,768]{1,0:T(8,128)(2,1)S(1)}, bf16[256,768]{1,0:T(8,128)(2,1)S(1)}, u32[]{:S(2)}, u32[]{:S(2)}) %collective-permute-start.28) | collective-permute-done | bytes 393248 | tf_op jit(solution)/shard_map/ppermute | solution.py:206
  224.8 18.5 %collective-permute-done.35 = bf16[256,768]{1,0:T(8,128)(2,1)S(1)} collective-permute-done((bf16[256,768]{1,0:T(8,128)(2,1)S(1)}, bf16[256,768]{1,0:T(8,128)(2,1)S(1)}, u32[]{:S(2)}, u32[]{:S(2)}) %collective-permute-start.35) | collective-permute-done | bytes 393248 | tf_op jit(solution)/shard_map/ppermute | solution.py:206
  281.8 21.0 %collective-permute-done.41 = bf16[512,192]{1,0:T(8,128)(2,1)S(1)} collective-permute-done((bf16[512,192]{1,0:T(8,128)(2,1)S(1)}, bf16[512,192]{1,0:T(8,128)(2,1)S(1)}, u32[]{:S(2)}, u32[]{:S(2)}) %collective-permute-start.41) | collective-permute-done | bytes 196640 | tf_op jit(solution)/shard_map/ppermute | solution.py:212
  319.0 7.6 %collective-permute-done.43 = bf16[256,768]{1,0:T(8,128)(2,1)S(1)} collective-permute-done((bf16[256,768]{1,0:T(8,128)(2,1)S(1)}, bf16[256,768]{1,0:T(8,128)(2,1)S(1)}, u32[]{:S(2)}, u32[]{:S(2)}) %collective-permute-start.43) | collective-permute-done | bytes 393248 | tf_op jit(solution)/shard_map/ppermute | solution.py:206
  396.6 9.8 %collective-permute-done.51 = bf16[512,384]{1,0:T(8,128)(2,1)S(1)} collective-permute-done((bf16[512,384]{1,0:T(8,128)(2,1)S(1)}, bf16[512,384]{1,0:T(8,128)(2,1)S(1)}, u32[]{:S(2)}, u32[]{:S(2)}) %collective-permute-start.51) | collective-permute-done | bytes 393248 | tf_op jit(solution)/shard_map/ppermute | solution.py:212
  409.6 9.1 %collective-permute-done.48 = bf16[512,384]{1,0:T(8,128)(2,1)S(1)} collective-permute-done((bf16[512,384]{1,0:T(8,128)(2,1)S(1)}, bf16[512,384]{1,0:T(8,128)(2,1)S(1)}, u32[]{:S(2)}, u32[]{:S(2)}) %collective-permute-start.48) | collective-permute-done | bytes 393248 | tf_op jit(solution)/shard_map/ppermute | solution.py:212
  428.2 8.2 %collective-permute-start.62 = (bf16[416,768]{1,0:T(8,128)(2,1)}, bf16[416,768]{1,0:T(8,128)(2,1)}, u32[]{:S(2)}, u32[]{:S(2)}) collective-permute-start(bf16[416,768]{1,0:T(8,128)(2,1)} %dynamic-slice_bitcast_fusion.8), channel_id=1, source_target_pairs={{0,16},{16,0},{1,17},{17,1},{2,18},{18,2},{3,19},{19,3},{4,20},{20... | collective-permute-start | bytes 1916936 | tf_op jit(solution)/shard_map/ppermute | solution.py:206
  440.8 8.4 %collective-permute-start.54 = (bf16[256,768]{1,0:T(8,128)(2,1)}, bf16[256,768]{1,0:T(8,128)(2,1)}, u32[]{:S(2)}, u32[]{:S(2)}) collective-permute-start(bf16[256,768]{1,0:T(8,128)(2,1)} %get-tuple-element.176), channel_id=1, source_target_pairs={{0,16},{16,0},{1,17},{17,1},{2,18},{18,2},{3,19},{19,3},{4,20},{20... | collective-permute-start | bytes 1179656 | tf_op jit(solution)/shard_map/ppermute | solution.py:206
  472.5 7.7 %collective-permute-done.65 = bf16[104,768]{1,0:T(8,128)(2,1)S(1)} collective-permute-done((bf16[104,768]{1,0:T(8,128)(2,1)S(1)}, bf16[104,768]{1,0:T(8,128)(2,1)S(1)}, u32[]{:S(2)}, u32[]{:S(2)}) %collective-permute-start.65) | collective-permute-done | bytes 159776 | tf_op jit(solution)/shard_map/ppermute | solution.py:206
  489.1 13.5 %collective-permute-done.79 = bf16[192,768]{1,0:T(8,128)(2,1)S(1)} collective-permute-done((bf16[192,768]{1,0:T(8,128)(2,1)S(1)}, bf16[192,768]{1,0:T(8,128)(2,1)S(1)}, u32[]{:S(2)}, u32[]{:S(2)}) %collective-permute-start.79) | collective-permute-done | bytes 294944 | tf_op jit(solution)/shard_map/ppermute | solution.py:206
  511.8 8.1 %collective-permute-done.57 = bf16[208,768]{1,0:T(8,128)(2,1)S(1)} collective-permute-done((bf16[208,768]{1,0:T(8,128)(2,1)S(1)}, bf16[208,768]{1,0:T(8,128)(2,1)S(1)}, u32[]{:S(2)}, u32[]{:S(2)}) %collective-permute-start.57) | collective-permute-done | bytes 319520 | tf_op jit(solution)/shard_map/ppermute | solution.py:206
  521.0 16.4 %collective-permute-done.72 = bf16[384,768]{1,0:T(8,128)(2,1)S(1)} collective-permute-done((bf16[384,768]{1,0:T(8,128)(2,1)S(1)}, bf16[384,768]{1,0:T(8,128)(2,1)S(1)}, u32[]{:S(2)}, u32[]{:S(2)}) %collective-permute-start.72) | collective-permute-done | bytes 589856 | tf_op jit(solution)/shard_map/ppermute | solution.py:206
  537.7 9.7 %collective-permute-done.81 = bf16[384,768]{1,0:T(8,128)(2,1)S(1)} collective-permute-done((bf16[384,768]{1,0:T(8,128)(2,1)S(1)}, bf16[384,768]{1,0:T(8,128)(2,1)S(1)}, u32[]{:S(2)}, u32[]{:S(2)}) %collective-permute-start.81) | collective-permute-done | bytes 589856 | tf_op jit(solution)/shard_map/ppermute | solution.py:206
  549.4 9.8 %collective-permute-done.73 = bf16[192,768]{1,0:T(8,128)(2,1)S(1)} collective-permute-done((bf16[192,768]{1,0:T(8,128)(2,1)S(1)}, bf16[192,768]{1,0:T(8,128)(2,1)S(1)}, u32[]{:S(2)}, u32[]{:S(2)}) %collective-permute-start.73) | collective-permute-done | bytes 294944 | tf_op jit(solution)/shard_map/ppermute | solution.py:206
  563.3 7.6 %collective-permute-done.74 = bf16[192,768]{1,0:T(8,128)(2,1)S(1)} collective-permute-done((bf16[192,768]{1,0:T(8,128)(2,1)S(1)}, bf16[192,768]{1,0:T(8,128)(2,1)S(1)}, u32[]{:S(2)}, u32[]{:S(2)}) %collective-permute-start.74) | collective-permute-done | bytes 294944 | tf_op jit(solution)/shard_map/ppermute | solution.py:206
  577.6 9.9 %collective-permute-done.75 = bf16[384,768]{1,0:T(8,128)(2,1)S(1)} collective-permute-done((bf16[384,768]{1,0:T(8,128)(2,1)S(1)}, bf16[384,768]{1,0:T(8,128)(2,1)S(1)}, u32[]{:S(2)}, u32[]{:S(2)}) %collective-permute-start.75) | collective-permute-done | bytes 589856 | tf_op jit(solution)/shard_map/ppermute | solution.py:206
  595.7 19.6 %collective-permute-done.82 = bf16[768,768]{1,0:T(8,128)(2,1)S(1)} collective-permute-done((bf16[768,768]{1,0:T(8,128)(2,1)S(1)}, bf16[768,768]{1,0:T(8,128)(2,1)S(1)}, u32[]{:S(2)}, u32[]{:S(2)}) %collective-permute-start.82) | collective-permute-done | bytes 1179680 | tf_op jit(solution)/shard_map/ppermute | solution.py:206
  (686 shorter events, 375.4 us)
Async XLA Ops:
  20.2 52.9 %collective-permute-start.33 = (bf16[256,768]{1,0:T(8,128)(2,1)}, bf16[256,768]{1,0:T(8,128)(2,1)}, u32[]{:S(2)}, u32[]{:S(2)}) collective-permute-start(bf16[256,768]{1,0:T(8,128)(2,1)} %dynamic-slice_bitcast_fusion.13), channel_id=1, source_target_pairs={{0,8},{8,0},{1,9},{9,1},{2,10},{10,2},{3,11},{11,3},{4,12},{12,4},... | collective-permute-start | bytes 1179656 | tf_op jit(solution)/shard_map/ppermute | solution.py:206
  38.7 37.2 %collective-permute-start.12 = (bf16[192,768]{1,0:T(8,128)(2,1)S(1)}, bf16[192,768]{1,0:T(8,128)(2,1)S(1)}, u32[]{:S(2)}, u32[]{:S(2)}) collective-permute-start(bf16[192,768]{1,0:T(8,128)(2,1)S(1)} %dynamic-slice_bitcast_fusion.19), channel_id=1, source_target_pairs={{0,16},{16,0},{1,17},{17,1},{2,18},{18,2},{3,19},{19,3},{4,20},{20... | collective-permute-start | bytes 884744 | tf_op jit(solution)/shard_map/ppermute | solution.py:206
  40.3 32.8 %collective-permute-start.14 = (bf16[384,1536]{1,0:T(8,128)(2,1)S(1)}, bf16[384,1536]{1,0:T(8,128)(2,1)S(1)}, u32[]{:S(2)}, u32[]{:S(2)}) collective-permute-start(bf16[384,1536]{1,0:T(8,128)(2,1)S(1)} %dynamic-slice_bitcast_fusion.7), channel_id=1, source_target_pairs={{0,16},{16,0},{1,17},{17,1},{2,18},{18,2},{3,19},{19,3},{4,20},{20... | collective-permute-start | bytes 3538952 | tf_op jit(solution)/shard_map/ppermute | solution.py:206
  42.8 33.2 %collective-permute-start.6 = (bf16[512,384]{1,0:T(8,128)(2,1)S(1)}, bf16[512,384]{1,0:T(8,128)(2,1)S(1)}, u32[]{:S(2)}, u32[]{:S(2)}) collective-permute-start(bf16[512,384]{1,0:T(8,128)(2,1)S(1)} %convolution_convert_fusion.22.k_ref), channel_id=1, source_target_pairs={{0,2},{1,3},{2,4},{3,5},{4,6},{5,7},{8,10},{9,11},{10,12},{11,13},... | collective-permute-start | bytes 1179656 | tf_op jit(solution)/shard_map/ppermute | solution.py:212
  47.1 29.9 %collective-permute-start.8 = (bf16[512,384]{1,0:T(8,128)(2,1)S(1)}, bf16[512,384]{1,0:T(8,128)(2,1)S(1)}, u32[]{:S(2)}, u32[]{:S(2)}) collective-permute-start(bf16[512,384]{1,0:T(8,128)(2,1)S(1)} %pad_maximum_fusion.29.v_ref), channel_id=1, source_target_pairs={{0,2},{1,3},{2,4},{3,5},{4,6},{5,7},{8,10},{9,11},{10,12},{11,13},... | collective-permute-start | bytes 1179656 | tf_op jit(solution)/shard_map/ppermute | solution.py:212
  96.5 27.9 %collective-permute-start.18 = (bf16[768,768]{1,0:T(8,128)(2,1)S(1)}, bf16[768,768]{1,0:T(8,128)(2,1)S(1)}, u32[]{:S(2)}, u32[]{:S(2)}) collective-permute-start(bf16[768,768]{1,0:T(8,128)(2,1)S(1)} %dynamic-slice_bitcast_fusion.6), channel_id=1, source_target_pairs={{0,16},{16,0},{1,17},{17,1},{2,18},{18,2},{3,19},{19,3},{4,20},{20... | collective-permute-start | bytes 3538952 | tf_op jit(solution)/shard_map/ppermute | solution.py:206
  214.2 52.1 %collective-permute-start.31 = (bf16[256,768]{1,0:T(8,128)(2,1)}, bf16[256,768]{1,0:T(8,128)(2,1)}, u32[]{:S(2)}, u32[]{:S(2)}) collective-permute-start(bf16[256,768]{1,0:T(8,128)(2,1)} %convolution_convert_fusion.17), channel_id=1, source_target_pairs={{0,8},{8,0},{1,9},{9,1},{2,10},{10,2},{3,11},{11,3},{4,12},{12,4},... | collective-permute-start | bytes 1179656 | tf_op jit(solution)/shard_map/ppermute | solution.py:206
  217.3 51.6 %collective-permute-start.30 = (bf16[256,768]{1,0:T(8,128)(2,1)}, bf16[256,768]{1,0:T(8,128)(2,1)}, u32[]{:S(2)}, u32[]{:S(2)}) collective-permute-start(bf16[256,768]{1,0:T(8,128)(2,1)} %convolution_convert_fusion.18), channel_id=1, source_target_pairs={{0,8},{8,0},{1,9},{9,1},{2,10},{10,2},{3,11},{11,3},{4,12},{12,4},... | collective-permute-start | bytes 1179656 | tf_op jit(solution)/shard_map/ppermute | solution.py:206
  219.3 31.1 %collective-permute-start.34 = (bf16[256,768]{1,0:T(8,128)(2,1)S(1)}, bf16[256,768]{1,0:T(8,128)(2,1)S(1)}, u32[]{:S(2)}, u32[]{:S(2)}) collective-permute-start(bf16[256,768]{1,0:T(8,128)(2,1)S(1)} %convolution_convert_fusion.16), channel_id=1, source_target_pairs={{0,8},{8,0},{1,9},{9,1},{2,10},{10,2},{3,11},{11,3},{4,12},{12,4},... | collective-permute-start | bytes 1179656 | tf_op jit(solution)/shard_map/ppermute | solution.py:206
  224.8 165.3 %collective-permute-start.76 = (bf16[2,768,768]{2,1,0:T(8,128)(2,1)}, bf16[2,768,768]{2,1,0:T(8,128)(2,1)}, u32[]{:S(2)}, u32[]{:S(2)}) collective-permute-start(bf16[2,768,768]{2,1,0:T(8,128)(2,1)} %dynamic-slice_bitcast_fusion), channel_id=1, source_target_pairs={{0,1},{1,0},{2,3},{3,2},{4,5},{5,4},{6,7},{7,6},{8,9},{9,8},{10,11... | collective-permute-start | bytes 7077896 | tf_op jit(solution)/shard_map/ppermute | solution.py:206
  271.3 37.8 %collective-permute-start.32 = (bf16[256,768]{1,0:T(8,128)(2,1)}, bf16[256,768]{1,0:T(8,128)(2,1)}, u32[]{:S(2)}, u32[]{:S(2)}) collective-permute-start(bf16[256,768]{1,0:T(8,128)(2,1)} %get-tuple-element.179), channel_id=1, source_target_pairs={{0,16},{16,0},{1,17},{17,1},{2,18},{18,2},{3,19},{19,3},{4,20},{20... | collective-permute-start | bytes 1179656 | tf_op jit(solution)/shard_map/ppermute | solution.py:206
  277.2 35.3 %collective-permute-start.36 = (bf16[512,384]{1,0:T(8,128)(2,1)}, bf16[512,384]{1,0:T(8,128)(2,1)}, u32[]{:S(2)}, u32[]{:S(2)}) collective-permute-start(bf16[512,384]{1,0:T(8,128)(2,1)} %get-tuple-element.70), channel_id=1, source_target_pairs={{0,1},{1,0},{2,3},{3,2},{4,5},{5,4},{6,7},{7,6},{8,9},{9,8},{10,11... | collective-permute-start | bytes 1179656 | tf_op jit(solution)/shard_map/ppermute | solution.py:206
  280.4 32.1 %collective-permute-start.38 = (bf16[512,384]{1,0:T(8,128)(2,1)}, bf16[512,384]{1,0:T(8,128)(2,1)}, u32[]{:S(2)}, u32[]{:S(2)}) collective-permute-start(bf16[512,384]{1,0:T(8,128)(2,1)} %add_convert_fusion.12), channel_id=1, source_target_pairs={{2,0},{3,1},{4,2},{5,3},{6,4},{7,5},{10,8},{11,9},{12,10},{13,11},... | collective-permute-start | bytes 1179656 | tf_op jit(solution)/shard_map/ppermute | solution.py:212
  358.4 67.3 %collective-permute-start.61 = (bf16[2,416,768]{2,1,0:T(8,128)(2,1)}, bf16[2,416,768]{2,1,0:T(8,128)(2,1)}, u32[]{:S(2)}, u32[]{:S(2)}) collective-permute-start(bf16[2,416,768]{2,1,0:T(8,128)(2,1)} %dynamic-slice_bitcast_fusion.2), channel_id=1, source_target_pairs={{0,1},{1,0},{2,3},{3,2},{4,5},{5,4},{6,7},{7,6},{8,9},{9,8},{10,11... | collective-permute-start | bytes 3833864 | tf_op jit(solution)/shard_map/ppermute | solution.py:206
  363.6 105.9 %collective-permute-start.70 = (bf16[2,768,768]{2,1,0:T(8,128)(2,1)}, bf16[2,768,768]{2,1,0:T(8,128)(2,1)}, u32[]{:S(2)}, u32[]{:S(2)}) collective-permute-start(bf16[2,768,768]{2,1,0:T(8,128)(2,1)} %dynamic-slice_bitcast_fusion.1), channel_id=1, source_target_pairs={{0,1},{1,0},{2,3},{3,2},{4,5},{5,4},{6,7},{7,6},{8,9},{9,8},{10,11... | collective-permute-start | bytes 7077896 | tf_op jit(solution)/shard_map/ppermute | solution.py:206
  396.2 65.2 %collective-permute-start.77 = (bf16[768,768]{1,0:T(8,128)(2,1)}, bf16[768,768]{1,0:T(8,128)(2,1)}, u32[]{:S(2)}, u32[]{:S(2)}) collective-permute-start(bf16[768,768]{1,0:T(8,128)(2,1)} %dynamic-slice_bitcast_fusion.4), channel_id=1, source_target_pairs={{0,16},{16,0},{1,17},{17,1},{2,18},{18,2},{3,19},{19,3},{4,20},{20... | collective-permute-start | bytes 3538952 | tf_op jit(solution)/shard_map/ppermute | solution.py:206
  440.8 47.0 %collective-permute-start.54 = (bf16[256,768]{1,0:T(8,128)(2,1)}, bf16[256,768]{1,0:T(8,128)(2,1)}, u32[]{:S(2)}, u32[]{:S(2)}) collective-permute-start(bf16[256,768]{1,0:T(8,128)(2,1)} %get-tuple-element.176), channel_id=1, source_target_pairs={{0,16},{16,0},{1,17},{17,1},{2,18},{18,2},{3,19},{19,3},{4,20},{20... | collective-permute-start | bytes 1179656 | tf_op jit(solution)/shard_map/ppermute | solution.py:206
  455.6 30.2 %collective-permute-start.55 = (bf16[2,416,768]{2,1,0:T(8,128)(2,1)S(1)}, bf16[2,416,768]{2,1,0:T(8,128)(2,1)S(1)}, u32[]{:S(2)}, u32[]{:S(2)}) collective-permute-start(bf16[2,416,768]{2,1,0:T(8,128)(2,1)S(1)} %dynamic-slice_bitcast_fusion.3), channel_id=1, source_target_pairs={{0,1},{1,0},{2,3},{3,2},{4,5},{5,4},{6,7},{7,6},{8,9},{9,8},{10,11... | collective-permute-start | bytes 3833864 | tf_op jit(solution)/shard_map/ppermute | solution.py:206
  471.8 37.4 %collective-permute-start.71 = (bf16[768,768]{1,0:T(8,128)(2,1)S(1)}, bf16[768,768]{1,0:T(8,128)(2,1)S(1)}, u32[]{:S(2)}, u32[]{:S(2)}) collective-permute-start(bf16[768,768]{1,0:T(8,128)(2,1)S(1)} %dynamic-slice_bitcast_fusion.5), channel_id=1, source_target_pairs={{0,16},{16,0},{1,17},{17,1},{2,18},{18,2},{3,19},{19,3},{4,20},{20... | collective-permute-start | bytes 3538952 | tf_op jit(solution)/shard_map/ppermute | solution.py:206
  509.5 27.8 %collective-permute-start.72 = (bf16[384,768]{1,0:T(8,128)(2,1)S(1)}, bf16[384,768]{1,0:T(8,128)(2,1)S(1)}, u32[]{:S(2)}, u32[]{:S(2)}) collective-permute-start(bf16[384,768]{1,0:T(8,128)(2,1)S(1)} %dynamic-slice_bitcast_fusion.11), channel_id=1, source_target_pairs={{0,2},{1,3},{2,0},{3,1},{4,6},{5,7},{6,4},{7,5},{8,10},{9,11},{10,... | collective-permute-start | bytes 1769480 | tf_op jit(solution)/shard_map/ppermute | solution.py:206
  511.1 36.3 %collective-permute-start.81 = (bf16[384,768]{1,0:T(8,128)(2,1)S(1)}, bf16[384,768]{1,0:T(8,128)(2,1)S(1)}, u32[]{:S(2)}, u32[]{:S(2)}) collective-permute-start(bf16[384,768]{1,0:T(8,128)(2,1)S(1)} %bitcast.452), channel_id=1, source_target_pairs={{0,2},{1,3},{2,0},{3,1},{4,6},{5,7},{6,4},{7,5},{8,10},{9,11},{10,... | collective-permute-start | bytes 1769480 | tf_op jit(solution)/shard_map/ppermute | solution.py:206
  520.0 27.5 %collective-permute-start.58 = (bf16[104,768]{1,0:T(8,128)(2,1)S(1)}, bf16[104,768]{1,0:T(8,128)(2,1)S(1)}, u32[]{:S(2)}, u32[]{:S(2)}) collective-permute-start(bf16[104,768]{1,0:T(8,128)(2,1)S(1)} %dynamic-slice_bitcast_fusion.21), channel_id=1, source_target_pairs={{0,4},{1,5},{2,6},{3,7},{4,0},{5,1},{6,2},{7,3},{8,12},{9,13},{10,... | collective-permute-start | bytes 479240 | tf_op jit(solution)/shard_map/ppermute | solution.py:206
  587.8 27.5 %collective-permute-start.82 = (bf16[768,768]{1,0:T(8,128)(2,1)S(1)}, bf16[768,768]{1,0:T(8,128)(2,1)S(1)}, u32[]{:S(2)}, u32[]{:S(2)}) collective-permute-start(bf16[768,768]{1,0:T(8,128)(2,1)S(1)} %bitcast.478), channel_id=1, source_target_pairs={{0,16},{16,0},{1,17},{17,1},{2,18},{18,2},{3,19},{19,3},{4,20},{20... | collective-permute-start | bytes 3538952 | tf_op jit(solution)/shard_map/ppermute | solution.py:206
  592.4 27.4 %collective-permute-start.68 = (bf16[2,416,768]{2,1,0:T(8,128)(2,1)}, bf16[2,416,768]{2,1,0:T(8,128)(2,1)}, u32[]{:S(2)}, u32[]{:S(2)}) collective-permute-start(bf16[2,416,768]{2,1,0:T(8,128)(2,1)} %pad_maximum_fusion.11), channel_id=1, source_target_pairs={{0,1},{1,0},{2,3},{3,2},{4,5},{5,4},{6,7},{7,6},{8,9},{9,8},{10,11... | collective-permute-start | bytes 3833864 | tf_op jit(solution)/shard_map/ppermute | solution.py:206
  (171 other events, 2014.4 us)

commit v2 on v1

v2 whole, which is shorter than its diff:
```python
import jax
import jax.numpy as jnp
from jax import lax
from jax.experimental import pallas as pl
from jax.experimental.pallas import tpu as pltpu
from jax.sharding import PartitionSpec as P

F32 = jnp.float32
BF = jnp.bfloat16
LOW = -1e30
HEAD = 64
CHUNKS = 2

GAIN0, GAIN1, BIAS0, BIAS1, BO, BDOWN, BQ, BKV, BUP = range(9)
TABLE = 16

WHOLE = pl.BlockSpec(memory_space=pltpu.VMEM)
SCALARS = pl.BlockSpec(memory_space=pltpu.SMEM)
FAR_OFF = pl.BlockSpec(memory_space=pltpu.HBM)


def dot_nn(a, b):
    return lax.dot_general(a, b, (((1,), (0,)), ((), ())), preferred_element_type=F32)


def dot_nt(a, b):
    return lax.dot_general(a, b, (((1,), (1,)), ((), ())), preferred_element_type=F32)


def dot_tn(a, b):
    return lax.dot_general(a, b, (((0,), (0,)), ((), ())), preferred_element_type=F32)


class Late:
    def __init__(self, array):
        self.array = array


def call(inner_body, outs, scalars, blocks, remote=(), scratch=(), us=1.0, limit=16):
    shapes = [jax.ShapeDtypeStruct(shape, kind) for shape, kind in outs]
    late = [i for i, b in enumerate(blocks) if isinstance(b, Late)]
    blocks = [b.array if isinstance(b, Late) else b for b in blocks]
    n_in, n_out = 1 + len(blocks) + len(remote), len(outs)
    staged = [pltpu.VMEM(blocks[i].shape, blocks[i].dtype) for i in late]
    sems = [pltpu.SemaphoreType.DMA((len(late),))] if late else []

    def body(*refs):
        refs = list(refs)
        if not late:
            return inner_body(*refs)
        first = n_in + n_out
        stage, sem, own = refs[first : first + len(late)], refs[first + len(late)], refs[first + len(late) + 1 :]
        copies = [pltpu.make_async_copy(refs[1 + i], v, sem.at[k]) for k, (i, v) in enumerate(zip(late, stage))]
        for copy in copies:
            copy.start()
        for copy in copies:
            copy.wait()
        for i, v in zip(late, stage):
            refs[1 + i] = v
        return inner_body(*refs[:first], *own)

    return pl.pallas_call(
        body,
        out_shape=shapes,
        in_specs=[SCALARS] + [FAR_OFF if i in late else WHOLE for i in range(len(blocks))] + [FAR_OFF] * len(remote),
        out_specs=[WHOLE] * len(outs),
        scratch_shapes=staged + sems + list(scratch),
        compiler_params=pltpu.CompilerParams(vmem_limit_bytes=limit * 1024 * 1024),
        cost_estimate=pl.CostEstimate(flops=int(us * 2.3e9), bytes_accessed=int(us * 4e6), transcendentals=0),
    )(scalars, *blocks, *remote)


def fetch_start(scalars, layer, own, got, other, held, sem):
    half = held.shape[0] // 2

    @pl.when(scalars[2] == layer)
    def _():
        pltpu.make_async_copy(own, held, sem).start()

    @pl.when(scalars[2] != layer)
    def _():
        mine = pl.multiple_of(scalars[3] * half, half)
        rest = pl.multiple_of((1 - scalars[3]) * half, half)
        pltpu.make_async_copy(got, held.at[pl.ds(mine, half)], sem).start()
        pltpu.make_async_copy(other, held.at[pl.ds(rest, half)], sem).start()


def fetch_wait(own, held, sem):
    pltpu.make_async_copy(own, held, sem).wait()


def held_like(*weights):
    return [pltpu.VMEM(w[0].shape, BF) for w in weights] + [pltpu.SemaphoreType.DMA] * len(weights)


def norm_parts(v):
    centred = v - jnp.mean(v, axis=-1, keepdims=True)
    rate = lax.rsqrt(jnp.mean(centred * centred, axis=-1, keepdims=True) + 1e-05)
    return centred * rate, rate


def norm_grad(v, gain, grad):
    unit, rate = norm_parts(v)
    scaled = grad * gain
    inner = jnp.mean(scaled * unit, axis=-1, keepdims=True)
    result = rate * (scaled - jnp.mean(scaled, axis=-1, keepdims=True) - unit * inner)
    return result, jnp.sum(grad * unit, axis=0, keepdims=True), jnp.sum(grad, axis=0, keepdims=True)


def gelu_both(u):
    factor = 0.7978845608028654
    square = u * u
    t = jnp.tanh(factor * u * (1.0 + 0.044715 * square))
    half = 0.5 * (1.0 + t)
    slope = half + (0.5 * factor) * u * (1.0 - t * t) * (1.0 + (3 * 0.044715) * square)
    return u * half, slope


def project(scalars, layer, weights, table, x=None, ahead=None, carried=None):
    if ahead is None:
        rows, features = x[0].shape
        blocks = [table, *x]
    else:
        rows, features = ahead[0][1].shape
        blocks = [table, ahead[0][0], Late(carried)]
        for chunk in ahead:
            blocks.extend(chunk[1:])
    width = weights[0].shape[1] // 3

    def body(scal, tab, *refs):
        given = refs[: len(blocks) - 1]
        own, got, other = refs[len(blocks) - 1 : len(blocks) + 2]
        outs = refs[len(blocks) + 2 : -2]
        held, sem = refs[-2:]
        fetch_start(scal, layer, own, got, other, held, sem)
        for c in range(CHUNKS):
            at = slice(c * rows, (c + 1) * rows)
            if ahead is None:
                v = given[c][...].astype(F32)
            else:
                before, carry = given[:2]
                hid, mine, came = given[2 + 3 * c : 5 + 3 * c]
                y = hid[...] + before[BDOWN : BDOWN + 1] + mine[...].astype(F32) + came[...].astype(F32)
                low = y.astype(BF)
                outs[5 + c][...] = low
                v = low.astype(F32)
            unit, _ = norm_parts(v)
            normed = (unit * tab[GAIN0 : GAIN0 + 1] + tab[BIAS0 : BIAS0 + 1]).astype(BF)
            outs[c][...] = normed
            if c == 0:
                fetch_wait(own, held, sem)
            q = dot_nn(normed, held[:, :width]) + tab[BQ : BQ + 1, :width]
            outs[2 + c][...] = (q.astype(BF).astype(F32) * 0.125).astype(BF)
            kv = dot_nn(normed, held[:, width:]) + tab[BKV : BKV + 1]
            if ahead is not None:
                rolled = pltpu.roll(carry[at, :].astype(F32), width // 2, 1)
                lane = lax.broadcasted_iota(jnp.int32, kv.shape, 1)
                kv = jnp.where(lane >= width + width // 2, rolled, kv)
            outs[4][at, :] = kv.astype(BF)

    outs = [((rows, features), BF)] * 2 + [((rows, width), BF)] * 2 + [((2 * rows, 2 * width), BF)]
    if ahead is not None:
        outs += [((rows, features), BF)] * 2
    r = call(body, outs, scalars, blocks, weights, held_like(weights), us=2.5)
    return list(x) if ahead is None else r[5:], r[:2], r[2:4], r[4]


def low_lanes(shape):
    return lax.broadcasted_iota(jnp.int32, shape, 1) < HEAD


def head_of(pair, sub, fill):
    keep = low_lanes(pair.shape)
    return jnp.where(keep if sub == 0 else ~keep, pair, jnp.full_like(pair, fill))


def halves_of(ref, size):
    return tuple(ref.at[i * size : (i + 1) * size] for i in range(ref.shape[0] // size))


def spans(p, width):
    return slice(p * 128, (p + 1) * 128), slice(width + p * 128, width + (p + 1) * 128)


def scored(q, tiles, p, width, masks):
    ks, vs = spans(p, width)
    tops, outs = [], []
    for sub in range(2):
        scores = [dot_nt(q, head_of(t[:, ks], sub, 0)) for t in tiles]
        scores = [s if m is None else jnp.where(m, s, LOW) for s, m in zip(scores, masks)]
        top = scores[0].max(axis=1, keepdims=True)
        for s in scores[1:]:
            top = jnp.maximum(top, s.max(axis=1, keepdims=True))
        total = None
        for s, t in zip(scores, tiles):
            part = dot_nn(jnp.exp(s - top).astype(BF), head_of(t[:, vs], sub, 1))
            total = part if total is None else total + part
        tops.append(top)
        outs.append(total)
    low = low_lanes(outs[0].shape)
    value = jnp.where(low, outs[0], outs[1])
    amount = pltpu.roll(jnp.where(low, outs[1], outs[0]), HEAD, 1)
    return tops, value, amount


def attend_local(scalars, q, kv, near):
    size, width = q[0].shape
    rows = size * CHUNKS

    def body(scal, q0, q1, k_all, n_all, out, amount, tops):
        own = halves_of(k_all, size)
        row = lax.broadcasted_iota(jnp.int32, (size, size), 0)
        col = lax.broadcasted_iota(jnp.int32, (size, size), 1)
        causal = col <= row

        def run(extra):
            for c, q_ref in enumerate((q0, q1)):
                at = slice(c * size, (c + 1) * size)
                tiles = list(extra) + [own[i] for i in range(c + 1)]
                masks = [None] * (len(tiles) - 1) + [causal]
                for p in range(width // 128):
                    span = slice(p * 128, (p + 1) * 128)
                    top, value, total = scored(q_ref[:, span], tiles, p, width, masks)
                    out[at, span] = value
                    amount[at, span] = total
                    tops[at, 2 * p : 2 * p + 1] = top[0]
                    tops[at, 2 * p + 1 : 2 * p + 2] = top[1]

        @pl.when(scal[0] == 1)
        def _():
            run(halves_of(n_all, size))

        @pl.when(scal[0] == 0)
        def _():
            run(())

    outs = [((rows, width), F32), ((rows, width), F32), ((rows, 128), F32)]
    return call(body, outs, scalars, [*q, kv, near], us=5)


def attend_far(scalars, layer, c, q, far, out, amount, tops, weights):
    size, width = q.shape
    features = weights[0].shape[1]

    def body(scal, q_ref, fa, fb, out_ref, amount_ref, tops_ref, own, got, other, att, lse, part, stats, held, sem):
        fetch_start(scal, layer, own, got, other, held, sem)
        at = slice(c * size, (c + 1) * size)
        stats[...] = jnp.zeros_like(stats)

        def finish(p, value, total, top0, top1):
            span = slice(p * 128, (p + 1) * 128)
            att[:, span] = (value / total).astype(BF)
            logs = jnp.log(total)
            stats[:, 2 * p : 2 * p + 1] = top0 + logs[:, 0:1]
            stats[:, 2 * p + 1 : 2 * p + 2] = top1 + logs[:, HEAD : HEAD + 1]

        @pl.when(scal[1] == 0)
        def _():
            for p in range(width // 128):
                span = slice(p * 128, (p + 1) * 128)
                finish(p, out_ref[at, span], amount_ref[at, span], tops_ref[at, 2 * p : 2 * p + 1], tops_ref[at, 2 * p + 1 : 2 * p + 2])

        @pl.when(scal[1] == 1)
        def _():
            for p in range(width // 128):
                span = slice(p * 128, (p + 1) * 128)
                new, value, total = scored(q_ref[:, span], halves_of(fa, size) + halves_of(fb, size), p, width, [None] * 4)
                tops_all, olds, news = [], [], []
                for sub in range(2):
                    before = tops_ref[at, 2 * p + sub : 2 * p + sub + 1]
                    top = jnp.maximum(before, new[sub])
                    tops_all.append(top)
                    olds.append(jnp.exp(before - top))
                    news.append(jnp.exp(new[sub] - top))
                low = low_lanes(value.shape)
                keep = jnp.where(low, olds[0], olds[1])
                take = jnp.where(low, news[0], news[1])
                finish(p, out_ref[at, span] * keep + value * take, amount_ref[at, span] * keep + total * take, *tops_all)

        lse[...] = jnp.transpose(stats[...])[0:8, :]
        fetch_wait(own, held, sem)
        part[...] = dot_nn(att[...], held[...]).astype(BF)

    outs = [((size, width), BF), ((8, size), F32), ((size, features), BF)]
    scratch = [pltpu.VMEM((size, 128), F32)] + held_like(weights)
    return call(body, outs, scalars, [q, *far, out, amount, tops], weights, scratch, us=4.5)


def back_tile(p, width, q, do, lse, delta, kv, mask):
    ks, vs = spans(p, width)
    dq, dks, dvs = None, [], []
    for sub in range(2):
        h = 2 * p + sub
        key = head_of(kv[:, ks], sub, 0)
        scores = dot_nt(key, q)
        weight = jnp.exp(scores - lse[h : h + 1, :])
        if mask is not None:
            weight = jnp.where(mask, weight, 0.0)
        d_weight = dot_nt(head_of(kv[:, vs], sub, 0), do)
        d_score = (weight * (d_weight - delta[h : h + 1, :])).astype(BF)
        dvs.append(dot_nn(weight.astype(BF), do))
        dks.append(dot_nn(d_score, q))
        d = dot_tn(d_score, key)
        dq = d if dq is None else dq + d
    low = low_lanes(dks[0].shape)
    return dq, jnp.where(low, dks[0], dks[1]), jnp.where(low, dvs[0], dvs[1])


def attend_others_back(scalars, q, do, lse, delta, far, near):
    size, width = q[0].shape
    rows = size * CHUNKS

    def body(scal, q0, q1, o0, o1, l0, l1, d0, d1, fa, fb, n_all, dq_out, mine, crossing):
        queries, grads, lses, deltas = (q0, q1), (o0, o1), (l0, l1), (d0, d1)
        dq_out[...] = jnp.zeros_like(dq_out)

        def run(sources):
            for p in range(width // 128):
                ks, vs = spans(p, width)
                total = [dq_out[c * size : (c + 1) * size, ks] for c in range(CHUNKS)]
                for source, ref, start in sources:
                    for i in range(CHUNKS):
                        tile = source.at[i * size : (i + 1) * size]
                        at = slice(start + i * size, start + (i + 1) * size)
                        dk = dv = None
                        for c in range(CHUNKS):
                            dq, k, v = back_tile(p, width, queries[c][:, ks], grads[c][:, ks], lses[c], deltas[c], tile, None)
                            total[c] = total[c] + dq
                            dk, dv = (k, v) if dk is None else (dk + k, dv + v)
                        ref[at, ks] = dk.astype(BF)
                        ref[at, vs] = dv.astype(BF)
                for c in range(CHUNKS):
                    dq_out[c * size : (c + 1) * size, ks] = total[c]

        @pl.when(scal[0] == 1)
        def _():
            run([(n_all, crossing, rows)])

        @pl.when(scal[0] == 0)
        def _():
            crossing[rows:, :] = jnp.zeros((rows, 2 * width), BF)

        @pl.when(scal[1] == 1)
        def _():
            run([(fb, crossing, 0), (fa, mine, 0)])

        @pl.when(scal[1] == 0)
        def _():
            mine[...] = jnp.zeros_like(mine)
            crossing[:rows, :] = jnp.zeros((rows, 2 * width), BF)

    outs = [((rows, width), F32), ((rows, 2 * width), BF), ((2 * rows, 2 * width), BF)]
    blocks = [*map(Late, q), *do, *map(Late, lse), *delta, *map(Late, far), Late(near)]
    return call(body, outs, scalars, blocks, us=16)


def attend_own_back(scalars, q, do, lse, delta, kv, dq_before):
    size, width = q[0].shape

    def body(scal, q0, q1, o0, o1, l0, l1, d0, d1, k_all, before, dq0, dq1, dk0, dk1):
        queries, grads, lses, deltas = (q0, q1), (o0, o1), (l0, l1), (d0, d1)
        key = lax.broadcasted_iota(jnp.int32, (size, size), 0)
        query = lax.broadcasted_iota(jnp.int32, (size, size), 1)
        causal = key <= query
        for p in range(width // 128):
            ks, vs = spans(p, width)
            total = [before[c * size : (c + 1) * size, ks] for c in range(CHUNKS)]
            for j, (source, ref) in enumerate(zip(halves_of(k_all, size), (dk0, dk1))):
                dk = dv = None
                for c in range(j, CHUNKS):
                    mask = causal if c == j else None
                    dq, k, v = back_tile(p, width, queries[c][:, ks], grads[c][:, ks], lses[c], deltas[c], source, mask)
                    total[c] = total[c] + dq
                    dk, dv = (k, v) if dk is None else (dk + k, dv + v)
                ref[:, ks] = dk
                ref[:, vs] = dv
            for c, ref in enumerate((dq0, dq1)):
                ref[:, ks] = (total[c] * 0.125).astype(BF)

    outs = [((size, width), BF)] * 2 + [((size, 2 * width), F32)] * 2
    blocks = [*map(Late, q), *do, *map(Late, lse), *delta, Late(kv), dq_before]
    return call(body, outs, scalars, blocks, us=6)


def feed_forward(scalars, layer, table, x, mine, came, up, down):
    rows, features = x.shape
    inner = up[0].shape[1]

    def body(scal, tab, x_ref, mine_ref, came_ref, u_own, u_got, u_other, d_own, d_got, d_other,
             hidden, mlp_in, active, slope, part, up_held, down_held, up_sem, down_sem):
        fetch_start(scal, layer, u_own, u_got, u_other, up_held, up_sem)
        fetch_start(scal, layer, d_own, d_got, d_other, down_held, down_sem)
        h = x_ref[...].astype(F32) + (mine_ref[...].astype(F32) + came_ref[...].astype(F32)) + tab[BO : BO + 1]
        hidden[...] = h
        unit, _ = norm_parts(h)
        low = (unit * tab[GAIN1 : GAIN1 + 1] + tab[BIAS1 : BIAS1 + 1]).astype(BF)
        mlp_in[...] = low
        fetch_wait(u_own, up_held, up_sem)
        for j in range(inner // features):
            cols = slice(j * features, (j + 1) * features)
            value, grad = gelu_both(dot_nn(low, up_held[:, cols]) + tab[BUP + j : BUP + j + 1])
            active[:, cols] = value.astype(BF)
            slope[:, cols] = grad.astype(BF)
        fetch_wait(d_own, down_held, down_sem)
        part[...] = dot_nn(active[...], down_held[...]).astype(BF)

    outs = [((rows, features), F32), ((rows, features), BF), ((rows, inner), BF), ((rows, inner), BF), ((rows, features), BF)]
    return call(body, outs, scalars, [table, Late(x), mine, came], [*up, *down], held_like(up, down), us=4, limit=24)


def feed_back(scalars, layer, dy, slope, up, down):
    rows, features = dy.shape
    inner = up[0].shape[1]

    def body(scal, dy_ref, slope_ref, u_own, u_got, u_other, d_own, d_got, d_other,
             d_up, part, sums, up_held, down_held, up_sem, down_sem):
        fetch_start(scal, layer, d_own, d_got, d_other, down_held, down_sem)
        fetch_start(scal, layer, u_own, u_got, u_other, up_held, up_sem)
        sums[...] = jnp.zeros_like(sums)
        fetch_wait(d_own, down_held, down_sem)
        for j in range(inner // features):
            cols = slice(j * features, (j + 1) * features)
            grad = (dot_nt(dy_ref[...], down_held[cols, :]) * slope_ref[:, cols].astype(F32)).astype(BF)
            d_up[:, cols] = grad
            sums[j : j + 1, :] = jnp.sum(grad.astype(F32), axis=0, keepdims=True)
        fetch_wait(u_own, up_held, up_sem)
        part[...] = dot_nt(d_up[...], up_held[...]).astype(BF)

    outs = [((rows, inner), BF), ((rows, features), BF), ((8, features), F32)]
    return call(body, outs, scalars, [dy, Late(slope)], [*up, *down], held_like(up, down), us=4.5, limit=24)


def middle_back(scalars, layer, table, hidden, mine, came, dy, attended, weights):
    rows, features = hidden.shape
    width = attended.shape[1]

    def body(scal, tab, hid, mine_ref, came_ref, dy_ref, att, own, got, other, dh_ref, low_ref, da_ref, delta, sums, stats, held, sem):
        fetch_start(scal, layer, own, got, other, held, sem)
        grad = mine_ref[...].astype(F32) + came_ref[...].astype(F32)
        back, d_gain, d_bias = norm_grad(hid[...], tab[GAIN1 : GAIN1 + 1], grad)
        up = dy_ref[...].astype(F32)
        dh = up + back
        dh_ref[...] = dh
        low = dh.astype(BF)
        low_ref[...] = low
        sums[...] = jnp.zeros_like(sums)
        sums[0:1, :] = d_gain
        sums[1:2, :] = d_bias
        sums[2:3, :] = jnp.sum(dh, axis=0, keepdims=True)
        sums[3:4, :] = jnp.sum(up, axis=0, keepdims=True)
        stats[...] = jnp.zeros_like(stats)
        fetch_wait(own, held, sem)
        da = dot_nt(low, held[...]).astype(BF)
        da_ref[...] = da
        for p in range(width // 128):
            span = slice(p * 128, (p + 1) * 128)
            product = da[:, span].astype(F32) * att[:, span].astype(F32)
            first = low_lanes(product.shape)
            stats[:, 2 * p : 2 * p + 1] = jnp.sum(jnp.where(first, product, 0.0), axis=1, keepdims=True)
            stats[:, 2 * p + 1 : 2 * p + 2] = jnp.sum(jnp.where(first, 0.0, product), axis=1, keepdims=True)
        delta[...] = jnp.transpose(stats[...])[0:8, :]

    outs = [((rows, features), F32), ((rows, features), BF), ((rows, width), BF), ((8, rows), F32), ((8, features), F32)]
    scratch = [pltpu.VMEM((rows, 128), F32)] + held_like(weights)
    return call(body, outs, scalars, [table, Late(hidden), mine, came, dy, Late(attended)], weights, scratch, us=2.8)


def project_back(scalars, layer, c, dq, dkv, near, far, returned, weights):
    rows, width = dq.shape
    features = weights[0].shape[0]

    def body(scal, dq_ref, dkv_ref, near_ref, far_ref, *rest):
        back_ref = rest[0] if returned is not None else None
        own, got, other = rest[-9:-6] if returned is None else rest[-8:-5]
        outs = rest[-6:-2] if returned is None else rest[-5:-2]
        held, sem = rest[-2:]
        fetch_start(scal, layer, own, got, other, held, sem)
        at = slice(c * rows, (c + 1) * rows)
        total = dkv_ref[...] + near_ref[at, :].astype(F32) + far_ref[at, :].astype(F32)
        if returned is None:
            outs[3][...] = total
        else:
            rolled = pltpu.roll(back_ref[...], 2 * width - width // 2, 1)
            lane = lax.broadcasted_iota(jnp.int32, total.shape, 1)
            total = total + jnp.where((lane >= width) & (lane < width + width // 2), rolled, 0.0)
        low = total.astype(BF)
        outs[0][...] = low
        sums = outs[2]
        sums[...] = jnp.zeros_like(sums)
        sums[0:1, :width] = jnp.sum(dq_ref[...].astype(F32), axis=0, keepdims=True)
        sums[1:2, :] = jnp.sum(low.astype(F32), axis=0, keepdims=True)
        fetch_wait(own, held, sem)
        outs[1][...] = (dot_nt(dq_ref[...], held[:, :width]) + dot_nt(low, held[:, width:])).astype(BF)

    outs = [((rows, 2 * width), BF), ((rows, features), BF), ((8, features), F32)]
    blocks = [dq, dkv, near, far]
    if returned is None:
        outs.append(((rows, 2 * width), F32))
    else:
        blocks.append(returned)
    return call(body, outs, scalars, blocks, weights, held_like(weights), us=2.7)


def last_back(scalars, table, x, mine, came, dh):
    rows, features = x.shape

    def body(scal, tab, x_ref, mine_ref, came_ref, dh_ref, dx_ref, low_ref, sums):
        grad = mine_ref[...].astype(F32) + came_ref[...].astype(F32)
        back, d_gain, d_bias = norm_grad(x_ref[...].astype(F32), tab[GAIN0 : GAIN0 + 1], grad)
        dx = dh_ref[...] + back
        dx_ref[...] = dx
        low_ref[...] = dx.astype(BF)
        sums[...] = jnp.zeros_like(sums)
        sums[0:1, :] = d_gain
        sums[1:2, :] = d_bias

    outs = [((rows, features), F32), ((rows, features), BF), ((8, features), F32)]
    return call(body, outs, scalars, [table, Late(x), mine, came, Late(dh)], us=1.5)


def both_chunks(left, left_span, right, right_span):
    total = None
    for a, b in zip(left, right):
        d = dot_tn(a[:, left_span], b[:, right_span])
        total = d if total is None else total + d
    return total


def wide_grads(scalars, active, dy, mlp_in, d_up):
    features = dy[0].shape[1]
    inner = active[0].shape[1]
    a, half = inner // 4, features // 2
    size = a + half

    def body(scal, a0, a1, y0, y1, m0, m1, u0, u1, packed):
        for k in range(4):
            span = slice(k * a, (k + 1) * a)
            packed[k, :a, :] = both_chunks((a0, a1), span, (y0, y1), slice(None)).astype(BF)
            for i in range(2):
                part = both_chunks((m0, m1), slice(i * half, (i + 1) * half), (u0, u1), span)
                packed[k, a:, i * a : (i + 1) * a] = part.astype(BF)

    blocks = [*map(Late, active), *dy, *map(Late, mlp_in), *d_up]
    return call(body, [((4, size, features), BF)], scalars, blocks, us=3.7)[0]


def narrow_grads(scalars, normed, dq, dkv, attended, dh_low):
    features = normed[0].shape[1]
    width = dq[0].shape[1]
    rows = features // 4
    half, c = rows // 2, width // 4
    size = rows + half + c

    def body(scal, n0, n1, q0, q1, k0, k1, t0, t1, h0, h1, packed):
        every = slice(None)
        for x in range(2):
            span = slice(2 * x * rows, 2 * (x + 1) * rows)
            first = both_chunks((n0, n1), span, (q0, q1), every).astype(BF)
            second = both_chunks((n0, n1), span, (k0, k1), every).astype(BF)
            for core in range(2):
                k, at = 2 * core + x, core * rows
                packed[k, :rows, :width] = first[at : at + rows, :]
                packed[k, :rows, width:] = second[at : at + rows, :width]
                packed[k, rows : rows + half, :width] = second[at : at + half, width:]
                packed[k, rows : rows + half, width:] = second[at + half : at + rows, width:]
        out = both_chunks((t0, t1), every, (h0, h1), every).astype(BF)
        for k in range(4):
            packed[k, rows + half :, :] = out[k * c : (k + 1) * c, :]

    blocks = [*map(Late, normed), *dq, *dkv, *map(Late, attended), *map(Late, dh_low)]
    return call(body, [((4, size, features), BF)], scalars, blocks, us=2.1)[0]


def collect(scal, refs, held, sem):
    copies = []
    for i, ref in enumerate(refs):
        core = scal[3] if i < 2 else 1 - scal[3]
        section = scal[2] if i % 2 == 0 else 1 - scal[2]
        copies.append(pltpu.make_async_copy(ref, held.at[2 * core + section], sem.at[i]))
    for copy in copies:
        copy.start()
    for copy in copies:
        copy.wait()


def wide_unpack(scalars, parts, inner):
    size, features = parts[0].shape
    a, half = inner // 4, features // 2

    def body(scal, p0, p1, p2, p3, down, up, held, sem):
        collect(scal, (p0, p1, p2, p3), held, sem)
        for k in range(4):
            down[k * a : (k + 1) * a, :] = held[k, :a, :].astype(F32)
            for i in range(2):
                up[i * half : (i + 1) * half, k * a : (k + 1) * a] = held[k, a:, i * a : (i + 1) * a].astype(F32)

    outs = [((inner, features), F32), ((features, inner), F32)]
    scratch = [pltpu.VMEM((4, size, features), BF), pltpu.SemaphoreType.DMA((4,))]
    return call(body, outs, scalars, [], parts, scratch, us=5)


def narrow_unpack(scalars, parts, extras, width):
    size, features = parts[0].shape
    rows = features // 4
    half, c, own = rows // 2, width // 4, width // 2

    def body(scal, p0, p1, p2, p3, e0, e1, query, key, value, extra, out, held, pair, sem, pair_sem):
        last = [pltpu.make_async_copy(e, pair.at[i if i == 0 else 1], pair_sem.at[i]) for i, e in enumerate((e0, e1))]
        for copy in last:
            copy.start()
        collect(scal, (p0, p1, p2, p3), held, sem)
        for copy in last:
            copy.wait()
        for x in range(2):
            for core in range(2):
                k, at = 2 * core + x, (2 * x + core) * rows
                query[at : at + rows, :] = held[k, :rows, :width].astype(F32)
                key[at : at + rows, :] = held[k, :rows, width:].astype(F32)
                value[at : at + half, :] = held[k, rows : rows + half, :own].astype(F32)
                value[at + half : at + rows, :] = held[k, rows : rows + half, width : width + own].astype(F32)
        for k in range(4):
            out[k * c : (k + 1) * c, :] = held[k, rows + half :, :].astype(F32)
        for i in range(2):
            core = scal[3] if i == 0 else 1 - scal[3]
            at = pl.multiple_of(core * rows, rows)
            cut = pair[i].astype(F32)
            left = pltpu.roll(cut[:, :width], own, 1)
            right = pltpu.roll(cut[:, width:], own, 1)
            extra[pl.ds(at, half), :] = left[:, :own]
            extra[pl.ds(pl.multiple_of(at + half, 8), half), :] = right[:, :own]

    outs = [((features, width), F32)] * 2 + [((features, own), F32), ((2 * rows, own), F32), ((width, features), F32)]
    scratch = [
        pltpu.VMEM((4, size, features), BF), pltpu.VMEM((2, half, features), BF),
        pltpu.SemaphoreType.DMA((4,)), pltpu.SemaphoreType.DMA((2,)),
    ]
    return call(body, outs, scalars, [], list(parts) + list(extras), scratch, us=3)


def swap(value, axis, bits=1):
    count = lax.axis_size(axis)
    return lax.ppermute(value, axis, [(i, i ^ bits) for i in range(count)])


def shift(value, steps):
    count = lax.axis_size("batch")
    first, last = max(0, -steps), min(count, count - steps)
    return lax.ppermute(value, "batch", [(i, i + steps) for i in range(first, last)])


def after(value, *earlier):
    return lax.optimization_barrier((value,) + earlier)[0]


def take(array, index, axis=0):
    return lax.dynamic_index_in_dim(array, index, axis, keepdims=False)


def paired(mine, other, side):
    return jnp.where(side == 0, mine, other), jnp.where(side == 0, other, mine)


class Reduction:
    def __init__(self, parts):
        self.core = lax.axis_index("batch") % 2
        self.section = lax.axis_index("section")
        self.parts = parts.reshape((2, 2) + parts.shape[1:])

    def over_cores(self):
        self.near = swap(take(self.parts, 1 - self.core), "batch")
        return self.near

    def prepare(self):
        mine = take(self.parts, self.core)
        other = 1 - self.section
        self.sent = (take(mine, other).astype(F32) + take(self.near, other).astype(F32)).astype(BF)
        self.kept = (take(mine, self.section).astype(F32) + take(self.near, self.section).astype(F32)).astype(BF)

    def over_sections(self):
        self.came = swap(self.sent, "section")

    def scatter(self):
        self.bits = list(range(1, lax.axis_size("batch").bit_length() - 1))
        index = lax.axis_index("batch")
        part = (self.kept.astype(F32) + self.came.astype(F32)).astype(BF)
        for bit in self.bits[:-1]:
            side = (index >> bit) & 1
            cut = part.reshape((2, part.shape[0] // 2) + part.shape[1:])
            if bit > 1:
                cut = lax.optimization_barrier(cut)
            got = swap(take(cut, 1 - side), "batch", 1 << bit)
            part = (take(cut, side), got)
            if bit != self.bits[-2]:
                part = (part[0].astype(F32) + part[1].astype(F32)).astype(BF)
        self.part = part
        return part

    def exchange(self):
        part = self.part
        self.part = (part[0].astype(F32) + part[1].astype(F32)).astype(BF)
        self.over = swap(self.part, "batch", 1 << self.bits[-1])

    def gather(self):
        part = (self.part.astype(F32) + self.over.astype(F32)).astype(BF)
        index = lax.axis_index("batch")
        for bit in reversed(self.bits[:-1]):
            got = swap(part, "batch", 1 << bit)
            self.pair = (part, got, (index >> bit) & 1)
            part = jnp.concatenate(paired(*self.pair), axis=0)
        return part

    def finish(self):
        self.quarter = jnp.concatenate(paired(*self.pair), axis=0)


def tie(value, *others):
    return lax.optimization_barrier((value,) + others)


def forward_layer(scalars, layer, table, w, x=None, ahead=None, carried=None, hooks=None):
    hooks = hooks or {}
    nothing = lambda value: value
    x, normed, q, kv = project(scalars, layer, w["qkv"], table, x=x, ahead=ahead, carried=carried)
    if "projected" in hooks:
        kv = hooks["projected"](kv, q)
    far = shift(kv, 2)
    near = swap(kv, "batch")
    out, amount, tops = attend_local(scalars, q, kv, near)
    far = hooks.get("arrived", nothing)(after(far, out))
    far = [far, swap(far, "batch")]
    att, lse, parts, came = [], [], [], []
    for c in range(CHUNKS):
        a, l, part = attend_far(scalars, layer, c, q[c], far, out, amount, tops, w["out"])
        att.append(a)
        lse.append(l)
        parts.append(part)
        came.append(swap(part, "tensor"))
    came[0] = hooks.get("far", lambda came, part: came)(came[0], parts[-1])
    hidden, mlp_in, active, slope, results = [], [], [], [], []
    for c in range(CHUNKS):
        h, m, a, s, part = feed_forward(scalars, layer, table, x[c], parts[c], came[c], w["up"], w["down"])
        hidden.append(h)
        mlp_in.append(m)
        active.append(a)
        slope.append(s)
        results.append((table, h, part))
    kept = dict(x=x, normed=normed, q=q, kv=kv, near=near, far=far, att=att, lse=lse, hidden=hidden,
                mlp_in=mlp_in, active=active, slope=slope)
    return results, kept


def backward_layer(scalars, layer, table, w, kept, dy, returned, steps):
    rows = CHUNKS * dy[0].shape[0]
    dy = steps("start", dy)
    d_up, parts, up_sums = [], [], []
    for c in range(CHUNKS):
        grad, part, sums = feed_back(scalars, layer, dy[c], kept["slope"][c], w["up"], w["down"])
        d_up.append(grad)
        up_sums.append(sums)
        parts.append((part, swap(part, "tensor")))
    wide = Reduction(wide_grads(scalars, kept["active"], dy, kept["mlp_in"], d_up))
    parts = steps("fed", parts, wide)
    dh, dh_low, d_att, delta, mid_sums = [], [], [], [], []
    for c in range(CHUNKS):
        r = middle_back(scalars, layer, table, kept["hidden"][c], *parts[c], dy[c], kept["att"][c], w["out"])
        for held, value in zip((dh, dh_low, d_att, delta, mid_sums), r):
            held.append(value)
    d_att = steps("mid", d_att, wide)
    dq, mine, crossing = attend_others_back(
        scalars, kept["q"], d_att, kept["lse"], delta, kept["far"], kept["near"]
    )
    came = swap(crossing, "batch")
    total, near = (mine.astype(F32) + came[:rows].astype(F32)).astype(BF), came[rows:]
    total, dq = steps("far", (total, dq), wide)
    home = shift(total, -2)
    dq0, dq1, dk0, dk1 = attend_own_back(scalars, kept["q"], d_att, kept["lse"], delta, kept["kv"], dq)
    dq, dkv = [dq0, dq1], [dk0, dk1]
    home, dq = steps("near", (home, dq), wide)
    dkv_low, parts, in_sums, back = [], [], [], []
    for c in range(CHUNKS):
        again = None if returned is None else returned[c]
        r = project_back(scalars, layer, c, dq[c], dkv[c], near, home, again, w["qkv"])
        dkv_low.append(r[0])
        parts.append((r[1], swap(r[1], "tensor")))
        in_sums.append(r[2])
        back.extend(r[3:])
    narrow = Reduction(narrow_grads(scalars, kept["normed"], dq, dkv_low, kept["att"], dh_low))
    parts = steps("proj", parts, wide, narrow)
    dx, dx_low, last_sums = [], [], []
    for c in range(CHUNKS):
        r = last_back(scalars, table, kept["x"][c], *parts[c], dh[c])
        dx.append(r[0])
        dx_low.append(r[1])
        last_sums.append(r[2])
    up, mid, last, inn = [a + b for a, b in (up_sums, mid_sums, last_sums, in_sums)]
    blank = jnp.zeros((TABLE - BUP - 2, up.shape[1]), F32)
    small = jnp.concatenate(
        [last[0:1], mid[0:1], last[1:2], mid[1:2], mid[2:4], inn[0:2], up[0:2], blank], axis=0
    )
    return dx, dx_low, back, wide, narrow, small


def local(
    tokens, block_place, cotangent, norm_gains, norm_biases, query_key, query_bias, value_own, value_bias,
    value_extra, out_weight, out_bias, up_weight, up_bias, down_weight, down_bias,
):
    section = lax.axis_index("section")
    tensor = lax.axis_index("tensor")
    core = lax.axis_index("batch") % 2
    micros, _, half_rows, features = tokens.shape
    width = query_bias.shape[1]
    own_width = value_own.shape[2]
    inner = up_weight.shape[2]
    assert micros == 2 and lax.axis_size("section") == 2 and lax.axis_size("tensor") == 2
    assert 2 * own_width == width and 2 * width == features and inner == 2 * features

    place = take(block_place, section)[0]
    scalars = jnp.stack([place & 1, place >> 1, section, core]).astype(jnp.int32)

    my_tokens = take(tokens, section)[0]
    x = paired(my_tokens, swap(my_tokens, "tensor"), tensor)

    def row(*pieces):
        flat = jnp.concatenate([p.reshape(-1) for p in pieces])
        return jnp.pad(flat, (0, features - flat.shape[0]))[None]

    blank = jnp.zeros((width,), F32)
    own_table = jnp.concatenate(
        [norm_gains[0], norm_biases[0], out_bias, down_bias, row(query_bias[0]), row(blank, value_bias[0]),
         up_bias[0].reshape(2, features), jnp.zeros((TABLE - BUP - 2, features), F32)], axis=0
    )
    extra = jnp.where(section == 0, value_extra, jnp.zeros_like(value_extra))
    pieces = [query_key[0].reshape(features, 2 * width), value_own[0], extra]

    def half_of(weight):
        return take(weight.reshape((2, weight.shape[0] // 2) + weight.shape[1:]), core)

    qkv_half = jnp.concatenate([half_of(p) for p in pieces], axis=1)
    qkv = jnp.concatenate(pieces, axis=1)
    other_table = swap(own_table, "section")
    qkv_got = swap(qkv_half, "section")
    out_got = swap(half_of(out_weight[0]), "section")
    tables = paired(own_table, other_table, section)
    qkv_got, out_got, qkv, scalars, *rest = tie(qkv_got, out_got, qkv, scalars, *tables, *x)
    tables, x = rest[:2], rest[2:]
    qkv_other = swap(qkv_got, "batch")
    w = dict(qkv=(qkv, qkv_got, qkv_other))
    late = {}

    def on_projected(kv, q):
        up, down, mine, kv = tie(half_of(up_weight[0]), half_of(down_weight[0]), take(cotangent, section)[0], kv)
        late["up"], late["down"] = swap(up, "section"), swap(down, "section")
        late["dy"] = mine, swap(mine, "tensor")
        w["out"] = (out_weight[0], out_got, swap(after(out_got, kv), "batch"))
        return kv

    def on_arrived(far):
        mine, other = late["dy"]
        far, got, other = tie(far, late["up"], other)
        late["dy"] = paired(mine, other, tensor)
        w["up"] = (up_weight[0], got, swap(got, "batch"))
        return far

    def on_far(came, part):
        came, got = tie(came, late["down"], part)[:2]
        w["down"] = (down_weight[0], got, swap(got, "batch"))
        return came

    first, kept0 = forward_layer(
        scalars, 0, tables[0], w, x=x, hooks=dict(projected=on_projected, arrived=on_arrived, far=on_far)
    )
    first = [r + (swap(r[2], "tensor"),) for r in first]
    second, kept1 = forward_layer(scalars, 1, tables[1], w, ahead=first, carried=kept0["kv"])
    y0 = kept1["x"]

    def my_half(chunks):
        return jnp.where(tensor == 0, chunks[0], chunks[1])

    def by_section(mine0, mine1, kind):
        mine = jnp.where(section == 0, mine0, mine1)
        other = swap(jnp.where(section == 0, mine1, mine0).astype(kind), "section")
        return mine, other

    def steps1(number, values, wide=None, narrow=None):
        leaves, tree = jax.tree.flatten(values)
        if number == "fed":
            *leaves, wide.parts = tie(*leaves, wide.parts)
            wide.over_cores()
        if number == "mid":
            *leaves, wide.near = tie(*leaves, wide.near)
            wide.prepare()
            *leaves, wide.sent = tie(*leaves, wide.sent)
            wide.over_sections()
        if number == "near":
            *leaves, wide.came = tie(*leaves, wide.came)
            wide.scatter()
        if number == "proj":
            *leaves, narrow.parts = tie(*leaves, narrow.parts)
            narrow.over_cores()
        return jax.tree.unflatten(tree, leaves)

    dx1, dx1_low, back, wide1, narrow1, small1 = backward_layer(scalars, 1, tables[1], w, kept1, late["dy"], None, steps1)

    def steps0(number, values, wide=None, narrow=None):
        leaves, tree = jax.tree.flatten(values)
        if number == "start":
            kept, got = wide1.part
            *leaves, got, narrow1.near = tie(*leaves, got, narrow1.near)
            wide1.part = kept, got
            wide1.exchange()
            narrow1.prepare()
            narrow1.over_sections()
        if number == "fed":
            *leaves, wide.parts, narrow1.came = tie(*leaves, wide.parts, narrow1.came)
            wide.over_cores()
            narrow1.scatter()
        if number == "mid":
            *leaves, wide.near, wide1.over = tie(*leaves, wide.near, wide1.over)
            wide1.gather()
            wide.prepare()
            *leaves, wide.sent = tie(*leaves, wide.sent)
            wide.over_sections()
        if number == "far":
            mine, got, side = wide1.pair
            kept, came = narrow1.part
            *leaves, got, came = tie(*leaves, got, came)
            wide1.pair = mine, got, side
            narrow1.part = kept, came
        if number == "near":
            *leaves, wide.came = tie(*leaves, wide.came)
            wide.scatter()
            narrow1.exchange()
        if number == "proj":
            kept, got = wide.part
            *leaves, narrow.parts, got = tie(*leaves, narrow.parts, got)
            wide.part = kept, got
            narrow.over_cores()
            wide.exchange()
            narrow.prepare()
            narrow.over_sections()
        return jax.tree.unflatten(tree, leaves)

    dx0, dx0_low, _, wide0, narrow0, small0 = backward_layer(scalars, 0, tables[0], w, kept0, dx1_low, back, steps0)
    came = [swap(after(r[2], dx0_low[0]), "tensor") for r in second]
    y1 = my_half(
        [(r[1] + r[0][BDOWN : BDOWN + 1] + r[2].astype(F32) + c.astype(F32)).astype(BF) for r, c in zip(second, came)]
    )
    outputs = jnp.stack(paired(*by_section(my_half(y0), y1, BF), section))
    narrow1.gather()
    narrow0.scatter()
    wide0.gather()
    narrow0.exchange()
    narrow0.gather()
    for work in (wide0, wide1, narrow0, narrow1):
        work.finish()
    input_grads = paired(*[a.astype(F32) for a in by_section(my_half(dx0), my_half(dx1), BF)], section)
    input_grads = jnp.stack(input_grads)

    sums = jnp.stack([small0, small1])
    sums = sums + swap(sums, "batch")
    table = take(sums, section) + swap(take(sums, 1 - section), "section")
    for bit in range(1, lax.axis_size("batch").bit_length() - 1):
        table = table + swap(table, "batch", 1 << bit)

    def gathered(first, second):
        mine = jnp.where(section == 0, first, second)
        other = swap(jnp.where(section == 0, second, first), "section")
        return mine, other, swap(mine, "batch"), swap(other, "batch")

    d_down, d_up = wide_unpack(scalars, gathered(wide0.quarter, wide1.quarter), inner)
    rows = features // 4
    extra = narrow0.quarter[rows : rows + rows // 2]
    extras = (extra, swap(extra, "batch"))
    d_q, d_k, d_v, d_extra, d_out = narrow_unpack(
        scalars, gathered(narrow0.quarter, narrow1.quarter), extras, width
    )
    d_qk = jnp.stack([d_q, d_k], axis=1)
    return (
        outputs.reshape(1, micros, 1, half_rows, features),
        input_grads.reshape(1, micros, 1, half_rows, features),
        table[GAIN0 : GAIN1 + 1][None],
        table[BIAS0 : BIAS1 + 1][None],
        d_qk.reshape(1, features, 2, width),
        table[BQ : BQ + 1, :width],
        d_v[None],
        table[BKV : BKV + 1, width : width + own_width],
        d_extra,
        d_out[None],
        table[BO : BO + 1],
        d_up[None],
        table[BUP : BUP + 2].reshape(1, inner),
        d_down[None],
        table[BDOWN : BDOWN + 1],
    )


def solution(mesh):
    return jax.shard_map(
        local,
        mesh=mesh,
        in_specs=(
            P(None, "batch", "tensor", None),
            P(None, "batch"),
            P(None, "batch", "tensor", None),
            P("section", None, None),
            P("section", None, None),
            P("section", None, None, "tensor"),
            P("section", "tensor"),
            P("section", None, "tensor"),
            P("section", "tensor"),
            P(None, "tensor"),
            P("section", "tensor", None),
            P("section", None),
            P("section", None, "tensor"),
            P("section", "tensor"),
            P("section", "tensor", None),
            P("section", None),
        ),
        out_specs=(
            P("section", None, "batch", "tensor", None),
            P("section", None, "batch", "tensor", None),
            P("section", None, None),
            P("section", None, None),
            P("section", None, None, "tensor"),
            P("section", "tensor"),
            P("section", None, "tensor"),
            P("section", "tensor"),
            P("section", "tensor"),
            P("section", "tensor", None),
            P("section", None),
            P("section", None, "tensor"),
            P("section", "tensor"),
            P("section", "tensor", None),
            P("section", None),
        ),
        check_vma=False,
    )
```

time: 658 us -> 627 us (0.953)
  Pallas kernels: 36.7 us -> 127 us
  matrix products: 52.6 us -> 0 us
  other arithmetic: 82 us -> 34.3 us
  waiting for transfers between devices: 315 us -> 279 us
  local copies, waits for them, and re-layouts: 61.3 us -> 84.7 us
  starting transfers between devices: 96.8 us -> 89.5 us
    pallas_call x8 -> x38, Pallas kernels: 36.7 us -> 127 us  [call(): pl.pallas_call(body, out_shape=shapes, in_specs=[SCALARS] + [FAR_OFF if i...]
    dot_general x55 -> x0, matrix products: 52.6 us -> none  [the longest x24 18.9 us: matmul_nt(): lax.dot_general(left, right, (((1,), (1,)), ((), ())), preferred_element_...]
    ppermute x76 -> x66, waiting for transfers between devices: 267 us -> 227 us  [swap(): return lax.ppermute(value, axis, [(i, i ^ bits) for i in range(count)])]
    unnamed x228 -> x499, local copies, waits for them, and re-layouts: 26.1 us -> 59.7 us
    another operation x42 -> x4, other arithmetic: 15.7 us -> 0.92 us  [the longest x1 0.72 us: local(): jnp.stack([place & 1, place >> 1, section, core]).astype(jnp.int32)]
    reduce_sum x31 -> x0, other arithmetic: 14.7 us -> none  [the longest x11 5.63 us: norm_back(): return (result, jnp.sum(grad * unit, axis=0), jnp.sum(grad, axis=0))]
    ppermute x8 -> x4, starting transfers between devices: 19.7 us -> 11 us  [shift(): lax.ppermute(value, 'batch', [(i, i + steps) for i in range(first, last)])]
    convert_element_type x35 -> x19, other arithmetic: 27.7 us -> 19.1 us  [the longest x4 6.59 us: scatter(): part = (self.kept.astype(F32) + self.came.astype(F32)).astype(BF)]
  transfers between devices with their start and end apart: 84 -> 70, of which waited for: 43 -> 40; matrix products, arithmetic and copies ran while one was open for 22% -> 7% of each run, Pallas kernels for 5% -> 15%
where the time goes in v2:
time: 627 us; the launch traced here: 619 us
  waiting for transfers between devices  279 us (44%)
  Pallas kernels  127 us (20%)
  starting transfers between devices  89.5 us (14%)
  local copies, waits for them, and re-layouts  84.7 us (14%)
  other arithmetic  34.3 us (5%)
    ppermute x66, waiting for transfers between devices, swap(): return lax.ppermute(value, axis, [(i, i ^ bits) for i in range(count)])  227 us
    pallas_call x38, Pallas kernels, call(): pl.pallas_call(body, out_shape=shapes, in_specs=[SCALARS] + [FAR_OFF if i...  127 us
    ppermute x66, starting transfers between devices, swap(): return lax.ppermute(value, axis, [(i, i ^ bits) for i in range(count)])  78.5 us
    unnamed x499, local copies, waits for them, and re-layouts  59.7 us
    ppermute x4, waiting for transfers between devices, shift(): lax.ppermute(value, 'batch', [(i, i + steps) for i in range(first, last)])  52.4 us
  transfers between devices with their start and end apart: 70, of which 40 were waited for; matrix products, arithmetic and copies ran while one was open for 7% of the time, Pallas kernels for 15%

profile of v2, /device:TPU:0, one launch (start us, length us, event | category | flops | bytes accessed | tf_op | source)
XLA Modules:
  0.0 619.3 jit_solution(134545783824643291)
XLA Ops:
  56.9 11.7 %collective-permute-done.5.refs_2_.refs_9_ = bf16[512,768]{1,0:T(8,128)(2,1)S(1)} collective-permute-done((bf16[512,768]{1,0:T(8,128)(2,1)S(1)}, bf16[512,768]{1,0:T(8,128)(2,1)S(1)}, u32[]{:S(2)}, u32[]{:S(2)}) %collective-permute-start.5) | collective-permute-done | bytes 786464 | tf_op jit(solution)/shard_map/ppermute | solution.py:648
  83.9 19.2 %collective-permute-done.12.refs_9_.refs_7_ = bf16[768,768]{1,0:T(8,128)(2,1)S(1)} collective-permute-done((bf16[768,768]{1,0:T(8,128)(2,1)S(1)}, bf16[768,768]{1,0:T(8,128)(2,1)S(1)}, u32[]{:S(2)}, u32[]{:S(2)}) %collective-permute-start.12) | collective-permute-done | bytes 1179680 | tf_op jit(solution)/shard_map/ppermute | solution.py:642
  105.4 9.7 %collective-permute-done.16.refs_4_ = bf16[256,768]{1,0:T(8,128)(2,1)S(1)} collective-permute-done((bf16[256,768]{1,0:T(8,128)(2,1)S(1)}, bf16[256,768]{1,0:T(8,128)(2,1)S(1)}, u32[]{:S(2)}, u32[]{:S(2)}) %collective-permute-start.16) | collective-permute-done | bytes 393248 | tf_op jit(solution)/shard_map/ppermute | solution.py:642
  133.1 7.3 %collective-permute-done.15.refs_6_ = bf16[256,768]{1,0:T(8,128)(2,1)S(1)} collective-permute-done((bf16[256,768]{1,0:T(8,128)(2,1)S(1)}, bf16[256,768]{1,0:T(8,128)(2,1)S(1)}, u32[]{:S(2)}, u32[]{:S(2)}) %collective-permute-start.15) | collective-permute-done | bytes 393248 | tf_op jit(solution)/shard_map/ppermute | solution.py:642
  154.3 10.4 %collective-permute-done.18.refs_2_.refs_9_ = bf16[512,768]{1,0:T(8,128)(2,1)} collective-permute-done((bf16[512,768]{1,0:T(8,128)(2,1)S(1)}, bf16[512,768]{1,0:T(8,128)(2,1)}, u32[]{:S(2)}, u32[]{:S(2)}) %collective-permute-start.18) | collective-permute-done | bytes 786464 | tf_op jit(solution)/shard_map/ppermute | solution.py:648
  236.7 7.4 %collective-permute-start.26 = (bf16[1024,768]{1,0:T(8,128)(2,1)S(1)}, bf16[1024,768]{1,0:T(8,128)(2,1)S(1)}, u32[]{:S(2)}, u32[]{:S(2)}) collective-permute-start(bf16[1024,768]{1,0:T(8,128)(2,1)S(1)} %get-tuple-element.290), channel_id=1, source_target_pairs={{0,1},{1,0},{2,3},{3,2},{4,5},{5,4},{6,7},{7,6},{8,9},{9,8},{10,11... | collective-permute-start | bytes 4718600 | tf_op jit(solution)/shard_map/ppermute | solution.py:642
  249.1 6.4 %shard_map.289 = (bf16[256,384]{1,0:T(8,128)(2,1)S(1)}, bf16[256,384]{1,0:T(8,128)(2,1)S(1)}, f32[256,768]{1,0:T(8,128)S(1)}, f32[256,768]{1,0:T(8,128)S(1)}) custom-call(s32[4]{0:T(128)S(1)} %pad_add_fusion.refs_0_, bf16[256,384]{1,0:T(8,128)(2,1)S(1)} %copy-done.183, bf16[256,384]{1,0:T(8,128)(2,1)S(1)} %copy-done.186, ...), custom_call_target="tpu_custom_call" | custom-call | flops 13799999488 | bytes 24000000 | tf_op jit(solution)/shard_map/pallas_call | solution.py:62
  255.6 16.4 %collective-permute-done.28 = bf16[768,768]{1,0:T(8,128)(2,1)S(1)} collective-permute-done((bf16[768,768]{1,0:T(8,128)(2,1)S(1)}, bf16[768,768]{1,0:T(8,128)(2,1)S(1)}, u32[]{:S(2)}, u32[]{:S(2)}) %collective-permute-start.28) | collective-permute-done | bytes 1179680 | tf_op jit(solution)/shard_map/ppermute | solution.py:642
  272.0 14.0 %collective-permute-done.27.refs_4_ = bf16[512,768]{1,0:T(8,128)(2,1)S(1)} collective-permute-done((bf16[512,768]{1,0:T(8,128)(2,1)S(1)}, bf16[512,768]{1,0:T(8,128)(2,1)S(1)}, u32[]{:S(2)}, u32[]{:S(2)}) %collective-permute-start.27) | collective-permute-done | bytes 786464 | tf_op jit(solution)/shard_map/ppermute | solution.py:648
  302.0 7.2 %collective-permute-done.30.refs_4_ = bf16[256,768]{1,0:T(8,128)(2,1)S(1)} collective-permute-done((bf16[256,768]{1,0:T(8,128)(2,1)S(1)}, bf16[256,768]{1,0:T(8,128)(2,1)S(1)}, u32[]{:S(2)}, u32[]{:S(2)}) %collective-permute-start.30) | collective-permute-done | bytes 393248 | tf_op jit(solution)/shard_map/ppermute | solution.py:642
  323.7 8.5 %collective-permute-done.31 = bf16[384,768]{1,0:T(8,128)(2,1)S(1)} collective-permute-done((bf16[384,768]{1,0:T(8,128)(2,1)S(1)}, bf16[384,768]{1,0:T(8,128)(2,1)S(1)}, u32[]{:S(2)}, u32[]{:S(2)}) %collective-permute-start.31) | collective-permute-done | bytes 589856 | tf_op jit(solution)/shard_map/ppermute | solution.py:642
  375.5 15.4 %collective-permute-done.37 = bf16[384,768]{1,0:T(8,128)(2,1)S(1)} collective-permute-done((bf16[384,768]{1,0:T(8,128)(2,1)S(1)}, bf16[384,768]{1,0:T(8,128)(2,1)S(1)}, u32[]{:S(2)}, u32[]{:S(2)}) %collective-permute-start.37) | collective-permute-done | bytes 589856 | tf_op jit(solution)/shard_map/ppermute | solution.py:642
  394.3 9.5 %shard_map.300 = (f32[512,384]{1,0:T(8,128)S(1)}, bf16[512,768]{1,0:T(8,128)(2,1)S(1)}, bf16[1024,768]{1,0:T(8,128)(2,1)}) custom-call(s32[4]{0:T(128)S(1)} %pad_add_fusion.refs_0_, bf16[256,384]{1,0:T(8,128)(2,1)S(1)} %copy-done.196, bf16[256,384]{1,0:T(8,128)(2,1)S(1)} %copy-done.199, bf16[256,384]{1,0:T(8,128)(2,1)S(1)} %get-tuple-element.344.refs_3_, ...), custom_call_target="tpu_custom_call" | custom-call | flops 36800000000 | bytes 64000000 | tf_op jit(solution)/shard_map/pallas_call | solution.py:62
  405.6 6.4 %collective-permute-start.38 = (bf16[1024,768]{1,0:T(8,128)(2,1)}, bf16[1024,768]{1,0:T(8,128)(2,1)}, u32[]{:S(2)}, u32[]{:S(2)}) collective-permute-start(bf16[1024,768]{1,0:T(8,128)(2,1)} %get-tuple-element.351), channel_id=1, source_target_pairs={{0,1},{1,0},{2,3},{3,2},{4,5},{5,4},{6,7},{7,6},{8,9},{9,8},{10,11... | collective-permute-start | bytes 4718600 | tf_op jit(solution)/shard_map/ppermute | solution.py:642
  428.4 15.6 %collective-permute-done.40 = bf16[192,768]{1,0:T(8,128)(2,1)S(1)} collective-permute-done((bf16[192,768]{1,0:T(8,128)(2,1)S(1)}, bf16[192,768]{1,0:T(8,128)(2,1)S(1)}, u32[]{:S(2)}, u32[]{:S(2)}) %collective-permute-start.40) | collective-permute-done | bytes 294944 | tf_op jit(solution)/shard_map/ppermute | solution.py:642
  446.2 6.4 %shard_map.301 = (bf16[256,384]{1,0:T(8,128)(2,1)S(1)}, bf16[256,384]{1,0:T(8,128)(2,1)S(1)}, f32[256,768]{1,0:T(8,128)S(1)}, f32[256,768]{1,0:T(8,128)S(1)}) custom-call(s32[4]{0:T(128)S(1)} %pad_add_fusion.refs_0_, bf16[256,384]{1,0:T(8,128)(2,1)S(1)} %copy-done.197, bf16[256,384]{1,0:T(8,128)(2,1)S(1)} %copy-done.200, bf16[256,384]{1,0:T(8,128)(2,1)S(1)} %copy-done.202, ...), custom_call_target="tpu_custom_call" | custom-call | flops 13799999488 | bytes 24000000 | tf_op jit(solution)/shard_map/pallas_call | solution.py:62
  454.9 16.3 %collective-permute-done.41.refs_4_ = bf16[512,768]{1,0:T(8,128)(2,1)S(1)} collective-permute-done((bf16[512,768]{1,0:T(8,128)(2,1)S(1)}, bf16[512,768]{1,0:T(8,128)(2,1)S(1)}, u32[]{:S(2)}, u32[]{:S(2)}) %collective-permute-start.41) | collective-permute-done | bytes 786464 | tf_op jit(solution)/shard_map/ppermute | solution.py:648
  480.0 7.0 %collective-permute-start.45 = (bf16[384,768]{1,0:T(8,128)(2,1)S(1)}, bf16[384,768]{1,0:T(8,128)(2,1)S(1)}, u32[]{:S(2)}, u32[]{:S(2)}) collective-permute-start(bf16[384,768]{1,0:T(8,128)(2,1)S(1)} %dynamic-slice_bitcast_fusion.6), channel_id=1, source_target_pairs={{0,2},{1,3},{2,0},{3,1},{4,6},{5,7},{6,4},{7,5},{8,10},{9,11},{10,... | collective-permute-start | bytes 1769480 | tf_op jit(solution)/shard_map/ppermute | solution.py:642
  521.6 9.1 %collective-permute-done.52 = f32[16,768]{1,0:T(8,128)S(1)} collective-permute-done((f32[16,768]{1,0:T(8,128)S(1)}, f32[16,768]{1,0:T(8,128)S(1)}, u32[]{:S(2)}, u32[]{:S(2)}) %collective-permute-start.52) | collective-permute-done | bytes 49184 | tf_op jit(solution)/shard_map/ppermute | solution.py:642
  535.4 8.2 %collective-permute-done.65 = bf16[384,768]{1,0:T(8,128)(2,1)S(1)} collective-permute-done((bf16[384,768]{1,0:T(8,128)(2,1)S(1)}, bf16[384,768]{1,0:T(8,128)(2,1)S(1)}, u32[]{:S(2)}, u32[]{:S(2)}) %collective-permute-start.65) | collective-permute-done | bytes 589856 | tf_op jit(solution)/shard_map/ppermute | solution.py:642
  551.1 9.0 %collective-permute-done.66 = bf16[384,768]{1,0:T(8,128)(2,1)S(1)} collective-permute-done((bf16[384,768]{1,0:T(8,128)(2,1)S(1)}, bf16[384,768]{1,0:T(8,128)(2,1)S(1)}, u32[]{:S(2)}, u32[]{:S(2)}) %collective-permute-start.66) | collective-permute-done | bytes 589856 | tf_op jit(solution)/shard_map/ppermute | solution.py:642
  567.1 10.9 %collective-permute-done.57 = bf16[192,768]{1,0:T(8,128)(2,1)S(1)} collective-permute-done((bf16[192,768]{1,0:T(8,128)(2,1)S(1)}, bf16[192,768]{1,0:T(8,128)(2,1)S(1)}, u32[]{:S(2)}, u32[]{:S(2)}) %collective-permute-start.57) | collective-permute-done | bytes 294944 | tf_op jit(solution)/shard_map/ppermute | solution.py:642
  579.0 7.5 %collective-permute-done.67.refs_2_ = bf16[768,768]{1,0:T(8,128)(2,1)S(1)} collective-permute-done((bf16[768,768]{1,0:T(8,128)(2,1)S(1)}, bf16[768,768]{1,0:T(8,128)(2,1)S(1)}, u32[]{:S(2)}, u32[]{:S(2)}) %collective-permute-start.67) | collective-permute-done | bytes 1179680 | tf_op jit(solution)/shard_map/ppermute | solution.py:642
  596.5 8.6 %collective-permute-done.61.refs_2_ = bf16[384,768]{1,0:T(8,128)(2,1)S(1)} collective-permute-done((bf16[384,768]{1,0:T(8,128)(2,1)S(1)}, bf16[384,768]{1,0:T(8,128)(2,1)S(1)}, u32[]{:S(2)}, u32[]{:S(2)}) %collective-permute-start.61) | collective-permute-done | bytes 589856 | tf_op jit(solution)/shard_map/ppermute | solution.py:642
  (747 shorter events, 366.8 us)
Async XLA Ops:
  9.9 29.7 %collective-permute-start = (bf16[384,1152]{1,0:T(8,128)(2,1)}, bf16[384,1152]{1,0:T(8,128)(2,1)}, u32[]{:S(2)}, u32[]{:S(2)}) collective-permute-start(bf16[384,1152]{1,0:T(8,128)(2,1)} %concatenate.32), channel_id=1, source_target_pairs={{0,16},{16,0},{1,17},{17,1},{2,18},{18,2},{3,19},{19,3},{4,20},{20... | collective-permute-start | bytes 2654216 | tf_op jit(solution)/shard_map/ppermute | solution.py:642
  46.3 28.3 %collective-permute-start.7 = (bf16[384,1536]{1,0:T(8,128)(2,1)S(1)}, bf16[384,1536]{1,0:T(8,128)(2,1)S(1)}, u32[]{:S(2)}, u32[]{:S(2)}) collective-permute-start(bf16[384,1536]{1,0:T(8,128)(2,1)S(1)} %dynamic-slice_bitcast_fusion.5), channel_id=1, source_target_pairs={{0,16},{16,0},{1,17},{17,1},{2,18},{18,2},{3,19},{19,3},{4,20},{20... | collective-permute-start | bytes 3538952 | tf_op jit(solution)/shard_map/ppermute | solution.py:642
  48.2 20.5 %collective-permute-start.5 = (bf16[512,768]{1,0:T(8,128)(2,1)S(1)}, bf16[512,768]{1,0:T(8,128)(2,1)S(1)}, u32[]{:S(2)}, u32[]{:S(2)}) collective-permute-start(bf16[512,768]{1,0:T(8,128)(2,1)S(1)} %get-tuple-element.224.refs_3_.refs_9_), channel_id=1, source_target_pairs={{0,2},{1,3},{2,4},{3,5},{4,6},{5,7},{8,10},{9,11},{10,12},{11,13},... | collective-permute-start | bytes 2359304 | tf_op jit(solution)/shard_map/ppermute | solution.py:648
  75.2 27.9 %collective-permute-start.12 = (bf16[768,768]{1,0:T(8,128)(2,1)S(1)}, bf16[768,768]{1,0:T(8,128)(2,1)S(1)}, u32[]{:S(2)}, u32[]{:S(2)}) collective-permute-start(bf16[768,768]{1,0:T(8,128)(2,1)S(1)} %dynamic-slice_bitcast_fusion.4), channel_id=1, source_target_pairs={{0,16},{16,0},{1,17},{17,1},{2,18},{18,2},{3,19},{19,3},{4,20},{20... | collective-permute-start | bytes 3538952 | tf_op jit(solution)/shard_map/ppermute | solution.py:642
  76.9 38.2 %collective-permute-start.13 = (bf16[384,1536]{1,0:T(8,128)(2,1)S(1)}, bf16[384,1536]{1,0:T(8,128)(2,1)S(1)}, u32[]{:S(2)}, u32[]{:S(2)}) collective-permute-start(bf16[384,1536]{1,0:T(8,128)(2,1)S(1)} %collective-permute-done.7.refs_6_.refs_4_), channel_id=1, source_target_pairs={{0,1},{1,0},{2,3},{3,2},{4,5},{5,4},{6,7},{7,6},{8,9},{9,8},{10,11... | collective-permute-start | bytes 3538952 | tf_op jit(solution)/shard_map/ppermute | solution.py:642
  79.5 23.6 %collective-permute-start.11 = (bf16[256,768]{1,0:T(8,128)(2,1)S(1)}, bf16[256,768]{1,0:T(8,128)(2,1)S(1)}, u32[]{:S(2)}, u32[]{:S(2)}) collective-permute-start(bf16[256,768]{1,0:T(8,128)(2,1)S(1)} %get-tuple-element.236.refs_3_), channel_id=1, source_target_pairs={{0,8},{8,0},{1,9},{9,1},{2,10},{10,2},{3,11},{11,3},{4,12},{12,4},... | collective-permute-start | bytes 1179656 | tf_op jit(solution)/shard_map/ppermute | solution.py:642
  143.7 20.9 %collective-permute-start.18 = (bf16[512,768]{1,0:T(8,128)(2,1)S(1)}, bf16[512,768]{1,0:T(8,128)(2,1)}, u32[]{:S(2)}, u32[]{:S(2)}) collective-permute-start(bf16[512,768]{1,0:T(8,128)(2,1)S(1)} %get-tuple-element.249.refs_3_.refs_9_), channel_id=1, source_target_pairs={{0,2},{1,3},{2,4},{3,5},{4,6},{5,7},{8,10},{9,11},{10,12},{11,13},... | collective-permute-start | bytes 2359304 | tf_op jit(solution)/shard_map/ppermute | solution.py:648
  244.0 28.0 %collective-permute-start.28 = (bf16[768,768]{1,0:T(8,128)(2,1)S(1)}, bf16[768,768]{1,0:T(8,128)(2,1)S(1)}, u32[]{:S(2)}, u32[]{:S(2)}) collective-permute-start(bf16[768,768]{1,0:T(8,128)(2,1)S(1)} %fusion.3), channel_id=1, source_target_pairs={{0,16},{16,0},{1,17},{17,1},{2,18},{18,2},{3,19},{19,3},{4,20},{20... | collective-permute-start | bytes 3538952 | tf_op jit(solution)/shard_map/ppermute | solution.py:642
  247.3 38.7 %collective-permute-start.27 = (bf16[512,768]{1,0:T(8,128)(2,1)S(1)}, bf16[512,768]{1,0:T(8,128)(2,1)S(1)}, u32[]{:S(2)}, u32[]{:S(2)}) collective-permute-start(bf16[512,768]{1,0:T(8,128)(2,1)S(1)} %add_convert_fusion.3), channel_id=1, source_target_pairs={{2,0},{3,1},{4,2},{5,3},{6,4},{7,5},{10,8},{11,9},{12,10},{13,11},... | collective-permute-start | bytes 2359304 | tf_op jit(solution)/shard_map/ppermute | solution.py:648
  310.4 21.8 %collective-permute-start.32 = (bf16[2,384,768]{2,1,0:T(8,128)(2,1)}, bf16[2,384,768]{2,1,0:T(8,128)(2,1)}, u32[]{:S(2)}, u32[]{:S(2)}) collective-permute-start(bf16[2,384,768]{2,1,0:T(8,128)(2,1)} %dynamic-slice_bitcast_fusion.3), channel_id=1, source_target_pairs={{0,1},{1,0},{2,3},{3,2},{4,5},{5,4},{6,7},{7,6},{8,9},{9,8},{10,11... | collective-permute-start | bytes 3538952 | tf_op jit(solution)/shard_map/ppermute | solution.py:642
  360.1 30.8 %collective-permute-start.36 = (bf16[2,768,768]{2,1,0:T(8,128)(2,1)}, bf16[2,768,768]{2,1,0:T(8,128)(2,1)}, u32[]{:S(2)}, u32[]{:S(2)}) collective-permute-start(bf16[2,768,768]{2,1,0:T(8,128)(2,1)} %dynamic-slice_bitcast_fusion), channel_id=1, source_target_pairs={{0,1},{1,0},{2,3},{3,2},{4,5},{5,4},{6,7},{7,6},{8,9},{9,8},{10,11... | collective-permute-start | bytes 7077896 | tf_op jit(solution)/shard_map/ppermute | solution.py:642
  361.7 29.3 %collective-permute-start.37 = (bf16[384,768]{1,0:T(8,128)(2,1)S(1)}, bf16[384,768]{1,0:T(8,128)(2,1)S(1)}, u32[]{:S(2)}, u32[]{:S(2)}) collective-permute-start(bf16[384,768]{1,0:T(8,128)(2,1)S(1)} %fusion.8), channel_id=1, source_target_pairs={{0,4},{1,5},{2,6},{3,7},{4,0},{5,1},{6,2},{7,3},{8,12},{9,13},{10,... | collective-permute-start | bytes 1769480 | tf_op jit(solution)/shard_map/ppermute | solution.py:642
  405.6 21.3 %collective-permute-start.38 = (bf16[1024,768]{1,0:T(8,128)(2,1)}, bf16[1024,768]{1,0:T(8,128)(2,1)}, u32[]{:S(2)}, u32[]{:S(2)}) collective-permute-start(bf16[1024,768]{1,0:T(8,128)(2,1)} %get-tuple-element.351), channel_id=1, source_target_pairs={{0,1},{1,0},{2,3},{3,2},{4,5},{5,4},{6,7},{7,6},{8,9},{9,8},{10,11... | collective-permute-start | bytes 4718600 | tf_op jit(solution)/shard_map/ppermute | solution.py:642
  418.1 25.9 %collective-permute-start.39 = (bf16[384,768]{1,0:T(8,128)(2,1)S(1)}, bf16[384,768]{1,0:T(8,128)(2,1)S(1)}, u32[]{:S(2)}, u32[]{:S(2)}) collective-permute-start(bf16[384,768]{1,0:T(8,128)(2,1)S(1)} %add_convert_fusion.7), channel_id=1, source_target_pairs={{0,2},{1,3},{2,0},{3,1},{4,6},{5,7},{6,4},{7,5},{8,10},{9,11},{10,... | collective-permute-start | bytes 1769480 | tf_op jit(solution)/shard_map/ppermute | solution.py:642
  426.9 28.0 %collective-permute-start.42 = (bf16[768,768]{1,0:T(8,128)(2,1)S(1)}, bf16[768,768]{1,0:T(8,128)(2,1)S(1)}, u32[]{:S(2)}, u32[]{:S(2)}) collective-permute-start(bf16[768,768]{1,0:T(8,128)(2,1)S(1)} %copy-done.228), channel_id=1, source_target_pairs={{0,16},{16,0},{1,17},{17,1},{2,18},{18,2},{3,19},{19,3},{4,20},{20... | collective-permute-start | bytes 3538952 | tf_op jit(solution)/shard_map/ppermute | solution.py:642
  444.8 62.1 %collective-permute-start.59 = (bf16[192,768]{1,0:T(8,128)(2,1)}, bf16[192,768]{1,0:T(8,128)(2,1)}, u32[]{:S(2)}, u32[]{:S(2)}) collective-permute-start(bf16[192,768]{1,0:T(8,128)(2,1)} %fusion.12), channel_id=1, source_target_pairs={{0,4},{1,5},{2,6},{3,7},{4,0},{5,1},{6,2},{7,3},{8,12},{9,13},{10,... | collective-permute-start | bytes 884744 | tf_op jit(solution)/shard_map/ppermute | solution.py:642
  444.8 26.3 %collective-permute-start.41 = (bf16[512,768]{1,0:T(8,128)(2,1)S(1)}, bf16[512,768]{1,0:T(8,128)(2,1)S(1)}, u32[]{:S(2)}, u32[]{:S(2)}) collective-permute-start(bf16[512,768]{1,0:T(8,128)(2,1)S(1)} %add_convert_fusion.2), channel_id=1, source_target_pairs={{2,0},{3,1},{4,2},{5,3},{6,4},{7,5},{10,8},{11,9},{12,10},{13,11},... | collective-permute-start | bytes 2359304 | tf_op jit(solution)/shard_map/ppermute | solution.py:648
  506.4 25.9 %collective-permute-start.54 = (bf16[2,384,768]{2,1,0:T(8,128)(2,1)S(1)}, bf16[2,384,768]{2,1,0:T(8,128)(2,1)S(1)}, u32[]{:S(2)}, u32[]{:S(2)}) collective-permute-start(bf16[2,384,768]{2,1,0:T(8,128)(2,1)S(1)} %dynamic-slice_bitcast_fusion.2), channel_id=1, source_target_pairs={{0,1},{1,0},{2,3},{3,2},{4,5},{5,4},{6,7},{7,6},{8,9},{9,8},{10,11... | collective-permute-start | bytes 3538952 | tf_op jit(solution)/shard_map/ppermute | solution.py:642
  513.6 30.0 %collective-permute-start.65 = (bf16[384,768]{1,0:T(8,128)(2,1)S(1)}, bf16[384,768]{1,0:T(8,128)(2,1)S(1)}, u32[]{:S(2)}, u32[]{:S(2)}) collective-permute-start(bf16[384,768]{1,0:T(8,128)(2,1)S(1)} %fusion.4), channel_id=1, source_target_pairs={{0,4},{1,5},{2,6},{3,7},{4,0},{5,1},{6,2},{7,3},{8,12},{9,13},{10,... | collective-permute-start | bytes 1769480 | tf_op jit(solution)/shard_map/ppermute | solution.py:642
  519.5 58.7 %collective-permute-start.46 = (bf16[256,768]{1,0:T(8,128)(2,1)S(1)}, bf16[256,768]{1,0:T(8,128)(2,1)S(1)}, u32[]{:S(2)}, u32[]{:S(2)}) collective-permute-start(bf16[256,768]{1,0:T(8,128)(2,1)S(1)} %copy-done.35), channel_id=1, source_target_pairs={{0,8},{8,0},{1,9},{9,1},{2,10},{10,2},{3,11},{11,3},{4,12},{12,4},... | collective-permute-start | bytes 1179656 | tf_op jit(solution)/shard_map/ppermute | solution.py:642
  520.4 57.8 %collective-permute-start.47 = (bf16[256,768]{1,0:T(8,128)(2,1)S(1)}, bf16[256,768]{1,0:T(8,128)(2,1)S(1)}, u32[]{:S(2)}, u32[]{:S(2)}) collective-permute-start(bf16[256,768]{1,0:T(8,128)(2,1)S(1)} %copy-done.37), channel_id=1, source_target_pairs={{0,8},{8,0},{1,9},{9,1},{2,10},{10,2},{3,11},{11,3},{4,12},{12,4},... | collective-permute-start | bytes 1179656 | tf_op jit(solution)/shard_map/ppermute | solution.py:642
  544.2 43.4 %collective-permute-start.49 = (bf16[256,768]{1,0:T(8,128)(2,1)S(1)}, bf16[256,768]{1,0:T(8,128)(2,1)S(1)}, u32[]{:S(2)}, u32[]{:S(2)}) collective-permute-start(bf16[256,768]{1,0:T(8,128)(2,1)S(1)} %get-tuple-element.432), channel_id=1, source_target_pairs={{0,16},{16,0},{1,17},{17,1},{2,18},{18,2},{3,19},{19,3},{4,20},{20... | collective-permute-start | bytes 1179656 | tf_op jit(solution)/shard_map/ppermute | solution.py:642
  560.7 25.8 %collective-permute-start.67 = (bf16[768,768]{1,0:T(8,128)(2,1)S(1)}, bf16[768,768]{1,0:T(8,128)(2,1)S(1)}, u32[]{:S(2)}, u32[]{:S(2)}) collective-permute-start(bf16[768,768]{1,0:T(8,128)(2,1)S(1)} %get-tuple-element.438), channel_id=1, source_target_pairs={{0,16},{16,0},{1,17},{17,1},{2,18},{18,2},{3,19},{19,3},{4,20},{20... | collective-permute-start | bytes 3538952 | tf_op jit(solution)/shard_map/ppermute | solution.py:642
  578.9 26.2 %collective-permute-start.68 = (bf16[768,768]{1,0:T(8,128)(2,1)S(1)}, bf16[768,768]{1,0:T(8,128)(2,1)S(1)}, u32[]{:S(2)}, u32[]{:S(2)}) collective-permute-start(bf16[768,768]{1,0:T(8,128)(2,1)S(1)} %get-tuple-element.439.refs_1_), channel_id=1, source_target_pairs={{0,1},{1,0},{2,3},{3,2},{4,5},{5,4},{6,7},{7,6},{8,9},{9,8},{10,11... | collective-permute-start | bytes 3538952 | tf_op jit(solution)/shard_map/ppermute | solution.py:642
  (292 other events, 3345.7 us)

commit v3 on v2

--- a/solution.py
+++ b/solution.py
@@ -306,80 +306,107 @@
     return dq, jnp.where(low, dks[0], dks[1]), jnp.where(low, dvs[0], dvs[1])
 
 
-def attend_others_back(scalars, q, do, lse, delta, far, near):
+def staged(size, width):
+    rows = size * CHUNKS
+    return [pltpu.VMEM((rows, width), BF), pltpu.VMEM((rows, width), BF), pltpu.VMEM((8, rows), F32), pltpu.VMEM((8, rows), F32)]
+
+
+def stage(size, given, held):
+    for k, ref in enumerate(held):
+        for c in range(CHUNKS):
+            at = slice(c * size, (c + 1) * size)
+            if k < 2:
+                ref[at, :] = given[2 * k + c][...]
+            else:
+                ref[:, at] = given[2 * k + c][...]
+
+
+def back_over(held, width, size, sources, dq_ref):
+    q, do, lse, delta = held
+    for p in range(width // 128):
+        ks, vs = spans(p, width)
+        total = dq_ref[:, ks]
+        for source, ref, start in sources:
+            for i in range(CHUNKS):
+                at = slice(start + i * size, start + (i + 1) * size)
+                tile = source.at[i * size : (i + 1) * size]
+                dq, dk, dv = back_tile(p, width, q[:, ks], do[:, ks], lse, delta, tile, None)
+                total = total + dq
+                ref[at, ks] = dk.astype(BF)
+                ref[at, vs] = dv.astype(BF)
+        dq_ref[:, ks] = total
+
+
+def attend_far_back(scalars, q, do, lse, delta, far):
     size, width = q[0].shape
     rows = size * CHUNKS
 
-    def body(scal, q0, q1, o0, o1, l0, l1, d0, d1, fa, fb, n_all, dq_out, mine, crossing):
-        queries, grads, lses, deltas = (q0, q1), (o0, o1), (l0, l1), (d0, d1)
+    def body(scal, q0, q1, o0, o1, l0, l1, d0, d1, fa, fb, dq_out, mine, others, *held):
         dq_out[...] = jnp.zeros_like(dq_out)
 
-        def run(sources):
-            for p in range(width // 128):
-                ks, vs = spans(p, width)
-                total = [dq_out[c * size : (c + 1) * size, ks] for c in range(CHUNKS)]
-                for source, ref, start in sources:
-                    for i in range(CHUNKS):
-                        tile = source.at[i * size : (i + 1) * size]
-                        at = slice(start + i * size, start + (i + 1) * size)
-                        dk = dv = None
-                        for c in range(CHUNKS):
-                            dq, k, v = back_tile(p, width, queries[c][:, ks], grads[c][:, ks], lses[c], deltas[c], tile, None)
-                            total[c] = total[c] + dq
-                            dk, dv = (k, v) if dk is None else (dk + k, dv + v)
-                        ref[at, ks] = dk.astype(BF)
-                        ref[at, vs] = dv.astype(BF)
-                for c in range(CHUNKS):
-                    dq_out[c * size : (c + 1) * size, ks] = total[c]
+        @pl.when(scal[1] == 1)
+        def _():
+            stage(size, (q0, q1, o0, o1, l0, l1, d0, d1), held)
+            back_over(held, width, size, [(fb, others, 0), (fa, mine, 0)], dq_out)
+
+        @pl.when(scal[1] == 0)
+        def _():
+            mine[...] = jnp.zeros_like(mine)
+            others[...] = jnp.zeros_like(others)
+
+    outs = [((rows, width), F32), ((rows, 2 * width), BF), ((rows, 2 * width), BF)]
+    blocks = [*map(Late, q), *do, *map(Late, lse), *delta, *map(Late, far)]
+    return call(body, outs, scalars, blocks, (), staged(size, width), us=12)
+
+
+def attend_near_back(scalars, q, do, lse, delta, near, dq_before, others):
+    size, width = q[0].shape
+    rows = size * CHUNKS
+
+    def body(scal, q0, q1, o0, o1, l0, l1, d0, d1, n_all, before, passed, dq_out, crossing, *held):
+        dq_out[...] = before[...]
+        crossing[:rows, :] = passed[...]
 
         @pl.when(scal[0] == 1)
         def _():
-            run([(n_all, crossing, rows)])
+            stage(size, (q0, q1, o0, o1, l0, l1, d0, d1), held)
+            back_over(held, width, size, [(n_all, crossing, rows)], dq_out)
 
         @pl.when(scal[0] == 0)
         def _():
             crossing[rows:, :] = jnp.zeros((rows, 2 * width), BF)
 
-        @pl.when(scal[1] == 1)
-        def _():
-            run([(fb, crossing, 0), (fa, mine, 0)])
-
-        @pl.when(scal[1] == 0)
-        def _():
-            mine[...] = jnp.zeros_like(mine)
-            crossing[:rows, :] = jnp.zeros((rows, 2 * width), BF)
-
-    outs = [((rows, width), F32), ((rows, 2 * width), BF), ((2 * rows, 2 * width), BF)]
-    blocks = [*map(Late, q), *do, *map(Late, lse), *delta, *map(Late, far), Late(near)]
-    return call(body, outs, scalars, blocks, us=16)
+    outs = [((rows, width), F32), ((2 * rows, 2 * width), BF)]
+    blocks = [*map(Late, q), *do, *map(Late, lse), *delta, Late(near), dq_before, others]
+    return call(body, outs, scalars, blocks, (), staged(size, width), us=6)
 
 
 def attend_own_back(scalars, q, do, lse, delta, kv, dq_before):
     size, width = q[0].shape
-
-    def body(scal, q0, q1, o0, o1, l0, l1, d0, d1, k_all, before, dq0, dq1, dk0, dk1):
-        queries, grads, lses, deltas = (q0, q1), (o0, o1), (l0, l1), (d0, d1)
-        key = lax.broadcasted_iota(jnp.int32, (size, size), 0)
-        query = lax.broadcasted_iota(jnp.int32, (size, size), 1)
+    rows = size * CHUNKS
+
+    def body(scal, q0, q1, o0, o1, l0, l1, d0, d1, k_all, before, dq0, dq1, dk0, dk1, *held):
+        stage(size, (q0, q1, o0, o1, l0, l1, d0, d1), held)
+        qs, dos, lses, deltas = held
+        key = lax.broadcasted_iota(jnp.int32, (size, rows), 0)
+        query = lax.broadcasted_iota(jnp.int32, (size, rows), 1)
         causal = key <= query
         for p in range(width // 128):
             ks, vs = spans(p, width)
-            total = [before[c * size : (c + 1) * size, ks] for c in range(CHUNKS)]
-            for j, (source, ref) in enumerate(zip(halves_of(k_all, size), (dk0, dk1))):
-                dk = dv = None
-                for c in range(j, CHUNKS):
-                    mask = causal if c == j else None
-                    dq, k, v = back_tile(p, width, queries[c][:, ks], grads[c][:, ks], lses[c], deltas[c], source, mask)
-                    total[c] = total[c] + dq
-                    dk, dv = (k, v) if dk is None else (dk + k, dv + v)
-                ref[:, ks] = dk
-                ref[:, vs] = dv
-            for c, ref in enumerate((dq0, dq1)):
-                ref[:, ks] = (total[c] * 0.125).astype(BF)
+            k0, k1 = halves_of(k_all, size)
+            first, dk, dv = back_tile(p, width, qs[:, ks], dos[:, ks], lses, deltas, k0, causal)
+            dk0[:, ks] = dk
+            dk0[:, vs] = dv
+            late = [ref.at[:, size:rows] for ref in (lses, deltas)]
+            second, dk, dv = back_tile(p, width, qs[size:, ks], dos[size:, ks], *late, k1, causal[:, :size])
+            dk1[:, ks] = dk
+            dk1[:, vs] = dv
+            dq0[:, ks] = ((before[:size, ks] + first[:size]) * 0.125).astype(BF)
+            dq1[:, ks] = ((before[size:, ks] + first[size:] + second) * 0.125).astype(BF)
 
     outs = [((size, width), BF)] * 2 + [((size, 2 * width), F32)] * 2
     blocks = [*map(Late, q), *do, *map(Late, lse), *delta, Late(kv), dq_before]
-    return call(body, outs, scalars, blocks, us=6)
+    return call(body, outs, scalars, blocks, (), staged(size, width), us=6)
 
 
 def feed_forward(scalars, layer, table, x, mine, came, up, down):
@@ -766,9 +793,9 @@
         for held, value in zip((dh, dh_low, d_att, delta, mid_sums), r):
             held.append(value)
     d_att = steps("mid", d_att, wide)
-    dq, mine, crossing = attend_others_back(
-        scalars, kept["q"], d_att, kept["lse"], delta, kept["far"], kept["near"]
-    )
+    dq, mine, others = attend_far_back(scalars, kept["q"], d_att, kept["lse"], delta, kept["far"])
+    dq = steps("between", dq, wide)
+    dq, crossing = attend_near_back(scalars, kept["q"], d_att, kept["lse"], delta, kept["near"], dq, others)
     came = swap(crossing, "batch")
     total, near = (mine.astype(F32) + came[:rows].astype(F32)).astype(BF), came[rows:]
     total, dq = steps("far", (total, dq), wide)
@@ -788,6 +815,8 @@
     parts = steps("proj", parts, wide, narrow)
     dx, dx_low, last_sums = [], [], []
     for c in range(CHUNKS):
+        if c == 1:
+            parts[1] = steps("last", parts[1], wide, narrow)
         r = last_back(scalars, table, kept["x"][c], *parts[c], dh[c])
         dx.append(r[0])
         dx_low.append(r[1])
@@ -845,11 +874,13 @@
     tables, x = rest[:2], rest[2:]
     qkv_other = swap(qkv_got, "batch")
     w = dict(qkv=(qkv, qkv_got, qkv_other))
-    late = {}
+    late = dict(
+        up=swap(after(half_of(up_weight[0]), qkv_got), "section"),
+        down=swap(after(half_of(down_weight[0]), qkv_got), "section"),
+    )
 
     def on_projected(kv, q):
-        up, down, mine, kv = tie(half_of(up_weight[0]), half_of(down_weight[0]), take(cotangent, section)[0], kv)
-        late["up"], late["down"] = swap(up, "section"), swap(down, "section")
+        mine, kv = tie(take(cotangent, section)[0], kv)
         late["dy"] = mine, swap(mine, "tensor")
         w["out"] = (out_weight[0], out_got, swap(after(out_got, kv), "batch"))
         return kv
@@ -895,8 +926,12 @@
             *leaves, wide.came = tie(*leaves, wide.came)
             wide.scatter()
         if number == "proj":
-            *leaves, narrow.parts = tie(*leaves, narrow.parts)
+            kept, got = wide.part
+            *leaves, narrow.parts, got = tie(*leaves, narrow.parts, got)
+            wide.part = kept, got
             narrow.over_cores()
+        if number == "last":
+            *leaves, narrow.near = tie(*leaves, narrow.near)
         return jax.tree.unflatten(tree, leaves)
 
     dx1, dx1_low, back, wide1, narrow1, small1 = backward_layer(scalars, 1, tables[1], w, kept1, late["dy"], None, steps1)
@@ -904,23 +939,22 @@
     def steps0(number, values, wide=None, narrow=None):
         leaves, tree = jax.tree.flatten(values)
         if number == "start":
-            kept, got = wide1.part
-            *leaves, got, narrow1.near = tie(*leaves, got, narrow1.near)
-            wide1.part = kept, got
             wide1.exchange()
             narrow1.prepare()
+            *leaves, wide1.part, narrow1.sent = tie(*leaves, wide1.part, narrow1.sent)
+            wide1.over = swap(wide1.part, "batch", 1 << wide1.bits[-1])
             narrow1.over_sections()
         if number == "fed":
-            *leaves, wide.parts, narrow1.came = tie(*leaves, wide.parts, narrow1.came)
+            *leaves, wide.parts, narrow1.came, wide1.over = tie(*leaves, wide.parts, narrow1.came, wide1.over)
             wide.over_cores()
             narrow1.scatter()
+            wide1.gather()
         if number == "mid":
-            *leaves, wide.near, wide1.over = tie(*leaves, wide.near, wide1.over)
-            wide1.gather()
+            *leaves, wide.near = tie(*leaves, wide.near)
             wide.prepare()
             *leaves, wide.sent = tie(*leaves, wide.sent)
             wide.over_sections()
-        if number == "far":
+        if number == "between":
             mine, got, side = wide1.pair
             kept, came = narrow1.part
             *leaves, got, came = tie(*leaves, got, came)
@@ -929,45 +963,62 @@
         if number == "near":
             *leaves, wide.came = tie(*leaves, wide.came)
             wide.scatter()
-            narrow1.exchange()
         if number == "proj":
             kept, got = wide.part
             *leaves, narrow.parts, got = tie(*leaves, narrow.parts, got)
             wide.part = kept, got
             narrow.over_cores()
             wide.exchange()
+        if number == "last":
+            *leaves, narrow.near = tie(*leaves, narrow.near)
             narrow.prepare()
-            narrow.over_sections()
         return jax.tree.unflatten(tree, leaves)
 
     dx0, dx0_low, _, wide0, narrow0, small0 = backward_layer(scalars, 0, tables[0], w, kept0, dx1_low, back, steps0)
-    came = [swap(after(r[2], dx0_low[0]), "tensor") for r in second]
-    y1 = my_half(
-        [(r[1] + r[0][BDOWN : BDOWN + 1] + r[2].astype(F32) + c.astype(F32)).astype(BF) for r, c in zip(second, came)]
-    )
-    outputs = jnp.stack(paired(*by_section(my_half(y0), y1, BF), section))
-    narrow1.gather()
+    sums = jnp.stack([small0, small1])
+    y_parts = [r[2] for r in second]
+    grads = [my_half(dx0), my_half(dx1)]
+    sums, narrow0.sent, *y_parts = tie(sums, narrow0.sent, *y_parts)
+    narrow0.over_sections()
+    narrow1.exchange()
+    y_came = [swap(y, "tensor") for y in y_parts]
+    sums = sums + swap(sums, "batch")
+    sums, narrow0.came, wide0.over = tie(sums, narrow0.came, wide0.over)
     narrow0.scatter()
     wide0.gather()
+    mine, got, side = wide0.pair
+    kept, came = narrow0.part
+    mine_grads, other_grads = by_section(*grads, BF)
+    table = take(sums, section) + swap(take(sums, 1 - section), "section")
+    narrow1.gather()
+    table, got, came, other_grads, *y_came = tie(table, got, came, other_grads, *y_came)
+    wide0.pair = mine, got, side
+    narrow0.part = kept, came
     narrow0.exchange()
-    narrow0.gather()
-    for work in (wide0, wide1, narrow0, narrow1):
-        work.finish()
-    input_grads = paired(*[a.astype(F32) for a in by_section(my_half(dx0), my_half(dx1), BF)], section)
-    input_grads = jnp.stack(input_grads)
-
-    sums = jnp.stack([small0, small1])
-    sums = sums + swap(sums, "batch")
-    table = take(sums, section) + swap(take(sums, 1 - section), "section")
+    wide0.finish()
+    wide1.finish()
+    y1 = my_half(
+        [(r[1] + r[0][BDOWN : BDOWN + 1] + r[2].astype(F32) + c.astype(F32)).astype(BF) for r, c in zip(second, y_came)]
+    )
+    mine_out, other_out = by_section(my_half(y0), y1, BF)
     for bit in range(1, lax.axis_size("batch").bit_length() - 1):
         table = table + swap(table, "batch", 1 << bit)
+    wide_mine = jnp.where(section == 0, wide0.quarter, wide1.quarter)
+    wide_other = swap(jnp.where(section == 0, wide1.quarter, wide0.quarter), "section")
+    narrow0.over, table, other_out = tie(narrow0.over, table, other_out)
+    narrow0.gather()
+    narrow0.finish()
+    narrow1.finish()
+    outputs = jnp.stack(paired(mine_out, other_out, section))
+    input_grads = jnp.stack(paired(mine_grads.astype(F32), other_grads.astype(F32), section))
 
     def gathered(first, second):
         mine = jnp.where(section == 0, first, second)
         other = swap(jnp.where(section == 0, second, first), "section")
         return mine, other, swap(mine, "batch"), swap(other, "batch")
 
-    d_down, d_up = wide_unpack(scalars, gathered(wide0.quarter, wide1.quarter), inner)
+    wide_all = (wide_mine, wide_other, swap(wide_mine, "batch"), swap(wide_other, "batch"))
+    d_down, d_up = wide_unpack(scalars, wide_all, inner)
     rows = features // 4
     extra = narrow0.quarter[rows : rows + rows // 2]
     extras = (extra, swap(extra, "batch"))

time: 627 us -> 597 us (0.952)
  local copies, waits for them, and re-layouts: 84.7 us -> 70.8 us
  waiting for transfers between devices: 279 us -> 267 us
  starting transfers between devices: 89.5 us -> 82.4 us
    ppermute x4, waiting for transfers between devices: 52.4 us -> 22.5 us  [shift(): lax.ppermute(value, 'batch', [(i, i + steps) for i in range(first, last)])]
    ppermute x66, waiting for transfers between devices: 227 us -> 245 us  [swap(): return lax.ppermute(value, axis, [(i, i ^ bits) for i in range(count)])]
    unnamed x499 -> x475, local copies, waits for them, and re-layouts: 59.7 us -> 50.9 us
    pallas_call x38 -> x40, Pallas kernels: 127 us -> 128 us  [call(): pl.pallas_call(body, out_shape=shapes, in_specs=[SCALARS] + [FAR_OFF if i...]
  transfers between devices with their start and end apart: 70 -> 70, of which waited for: 40 -> 33; matrix products, arithmetic and copies ran while one was open for 7% -> 8% of each run, Pallas kernels for 15% -> 15%
where the time goes in v3:
time: 597 us; the launch traced here: 590 us
  waiting for transfers between devices  267 us (45%)
  Pallas kernels  128 us (21%)
  starting transfers between devices  82.4 us (14%)
  local copies, waits for them, and re-layouts  70.8 us (12%)
  other arithmetic  37.2 us (6%)
    ppermute x66, waiting for transfers between devices, swap(): return lax.ppermute(value, axis, [(i, i ^ bits) for i in range(count)])  245 us
    pallas_call x40, Pallas kernels, call(): pl.pallas_call(body, out_shape=shapes, in_specs=[SCALARS] + [FAR_OFF if i...  128 us
    ppermute x66, starting transfers between devices, swap(): return lax.ppermute(value, axis, [(i, i ^ bits) for i in range(count)])  72.7 us
    unnamed x475, local copies, waits for them, and re-layouts  50.9 us
    ppermute x4, waiting for transfers between devices, shift(): lax.ppermute(value, 'batch', [(i, i + steps) for i in range(first, last)])  22.5 us
  transfers between devices with their start and end apart: 70, of which 33 were waited for; matrix products, arithmetic and copies ran while one was open for 8% of the time, Pallas kernels for 15%

profile of v3, /device:TPU:0, one launch (start us, length us, event | category | flops | bytes accessed | tf_op | source)
XLA Modules:
  0.0 589.6 jit_solution(69571732441164665)
XLA Ops:
  25.8 6.9 %collective-permute-done.2 = f32[16,768]{1,0:T(8,128)S(1)} collective-permute-done((f32[16,768]{1,0:T(8,128)S(1)}, f32[16,768]{1,0:T(8,128)S(1)}, u32[]{:S(2)}, u32[]{:S(2)}) %collective-permute-start.2) | collective-permute-done | bytes 49184 | tf_op jit(solution)/shard_map/ppermute | solution.py:669
  55.5 11.2 %collective-permute-done.5.refs_2_.refs_9_ = bf16[512,768]{1,0:T(8,128)(2,1)S(1)} collective-permute-done((bf16[512,768]{1,0:T(8,128)(2,1)S(1)}, bf16[512,768]{1,0:T(8,128)(2,1)S(1)}, u32[]{:S(2)}, u32[]{:S(2)}) %collective-permute-start.5) | collective-permute-done | bytes 786464 | tf_op jit(solution)/shard_map/ppermute | solution.py:675
  66.7 6.0 %collective-permute-done.7.refs_6_.refs_4_ = bf16[384,1536]{1,0:T(8,128)(2,1)S(1)} collective-permute-done((bf16[384,1536]{1,0:T(8,128)(2,1)S(1)}, bf16[384,1536]{1,0:T(8,128)(2,1)S(1)}, u32[]{:S(2)}, u32[]{:S(2)}) %collective-permute-start.7) | collective-permute-done | bytes 1179680 | tf_op jit(solution)/shard_map/ppermute | solution.py:669
  81.3 20.1 %collective-permute-done.12.refs_9_.refs_7_ = bf16[768,768]{1,0:T(8,128)(2,1)S(1)} collective-permute-done((bf16[768,768]{1,0:T(8,128)(2,1)S(1)}, bf16[768,768]{1,0:T(8,128)(2,1)S(1)}, u32[]{:S(2)}, u32[]{:S(2)}) %collective-permute-start.12) | collective-permute-done | bytes 1179680 | tf_op jit(solution)/shard_map/ppermute | solution.py:669
  103.8 9.7 %collective-permute-done.16.refs_4_ = bf16[256,768]{1,0:T(8,128)(2,1)S(1)} collective-permute-done((bf16[256,768]{1,0:T(8,128)(2,1)S(1)}, bf16[256,768]{1,0:T(8,128)(2,1)S(1)}, u32[]{:S(2)}, u32[]{:S(2)}) %collective-permute-start.16) | collective-permute-done | bytes 393248 | tf_op jit(solution)/shard_map/ppermute | solution.py:669
  125.4 6.0 %collective-permute-done.17.refs_9_ = bf16[256,768]{1,0:T(8,128)(2,1)S(1)} collective-permute-done((bf16[256,768]{1,0:T(8,128)(2,1)S(1)}, bf16[256,768]{1,0:T(8,128)(2,1)S(1)}, u32[]{:S(2)}, u32[]{:S(2)}) %collective-permute-start.17) | collective-permute-done | bytes 393248 | tf_op jit(solution)/shard_map/ppermute | solution.py:669
  131.4 7.3 %collective-permute-done.15.refs_6_ = bf16[256,768]{1,0:T(8,128)(2,1)S(1)} collective-permute-done((bf16[256,768]{1,0:T(8,128)(2,1)S(1)}, bf16[256,768]{1,0:T(8,128)(2,1)S(1)}, u32[]{:S(2)}, u32[]{:S(2)}) %collective-permute-start.15) | collective-permute-done | bytes 393248 | tf_op jit(solution)/shard_map/ppermute | solution.py:669
  153.2 11.2 %collective-permute-done.18.refs_2_.refs_9_ = bf16[512,768]{1,0:T(8,128)(2,1)S(1)} collective-permute-done((bf16[512,768]{1,0:T(8,128)(2,1)S(1)}, bf16[512,768]{1,0:T(8,128)(2,1)S(1)}, u32[]{:S(2)}, u32[]{:S(2)}) %collective-permute-start.18) | collective-permute-done | bytes 786464 | tf_op jit(solution)/shard_map/ppermute | solution.py:675
  177.8 6.0 %collective-permute-done.21.refs_4_ = bf16[256,768]{1,0:T(8,128)(2,1)S(1)} collective-permute-done((bf16[256,768]{1,0:T(8,128)(2,1)S(1)}, bf16[256,768]{1,0:T(8,128)(2,1)S(1)}, u32[]{:S(2)}, u32[]{:S(2)}) %collective-permute-start.21) | collective-permute-done | bytes 393248 | tf_op jit(solution)/shard_map/ppermute | solution.py:669
  235.5 8.9 %shard_map.289 = (f32[512,384]{1,0:T(8,128)S(1)}, bf16[1024,768]{1,0:T(8,128)(2,1)}) custom-call(s32[4]{0:T(128)S(1)} %pad_add_fusion.refs_0_, bf16[256,384]{1,0:T(8,128)(2,1)S(1)} %copy-done.162, bf16[256,384]{1,0:T(8,128)(2,1)S(1)} %copy-done.166, bf16[256,384]{1,0:T(8,128)(2,1)S(1)} %get-tuple-element.306.refs_3_, ...), custom_call_target="tpu_custom_call" | custom-call | flops 13799999488 | bytes 24000000 | tf_op jit(solution)/shard_map/pallas_call | solution.py:62
  263.1 15.5 %collective-permute-done.28 = bf16[768,768]{1,0:T(8,128)(2,1)S(1)} collective-permute-done((bf16[768,768]{1,0:T(8,128)(2,1)}, bf16[768,768]{1,0:T(8,128)(2,1)S(1)}, u32[]{:S(2)}, u32[]{:S(2)}) %collective-permute-start.28) | collective-permute-done | bytes 1179680 | tf_op jit(solution)/shard_map/ppermute | solution.py:669
  298.7 6.3 %collective-permute-done.30.refs_4_ = bf16[256,768]{1,0:T(8,128)(2,1)S(1)} collective-permute-done((bf16[256,768]{1,0:T(8,128)(2,1)S(1)}, bf16[256,768]{1,0:T(8,128)(2,1)S(1)}, u32[]{:S(2)}, u32[]{:S(2)}) %collective-permute-start.30) | collective-permute-done | bytes 393248 | tf_op jit(solution)/shard_map/ppermute | solution.py:669
  326.6 8.6 %collective-permute-start.36 = (bf16[384,768]{1,0:T(8,128)(2,1)S(1)}, bf16[384,768]{1,0:T(8,128)(2,1)S(1)}, u32[]{:S(2)}, u32[]{:S(2)}) collective-permute-start(bf16[384,768]{1,0:T(8,128)(2,1)S(1)} %fusion.9), channel_id=1, source_target_pairs={{0,4},{1,5},{2,6},{3,7},{4,0},{5,1},{6,2},{7,3},{8,12},{9,13},{10,... | collective-permute-start | bytes 1769480 | tf_op jit(solution)/shard_map/ppermute | solution.py:669
  340.4 20.5 %collective-permute-done.36 = bf16[384,768]{1,0:T(8,128)(2,1)S(1)} collective-permute-done((bf16[384,768]{1,0:T(8,128)(2,1)S(1)}, bf16[384,768]{1,0:T(8,128)(2,1)S(1)}, u32[]{:S(2)}, u32[]{:S(2)}) %collective-permute-start.36) | collective-permute-done | bytes 589856 | tf_op jit(solution)/shard_map/ppermute | solution.py:669
  376.2 8.5 %collective-permute-done.38 = bf16[384,768]{1,0:T(8,128)(2,1)S(1)} collective-permute-done((bf16[384,768]{1,0:T(8,128)(2,1)S(1)}, bf16[384,768]{1,0:T(8,128)(2,1)S(1)}, u32[]{:S(2)}, u32[]{:S(2)}) %collective-permute-start.38) | collective-permute-done | bytes 589856 | tf_op jit(solution)/shard_map/ppermute | solution.py:669
  404.2 17.5 %collective-permute-done.42 = bf16[768,768]{1,0:T(8,128)(2,1)S(1)} collective-permute-done((bf16[768,768]{1,0:T(8,128)(2,1)}, bf16[768,768]{1,0:T(8,128)(2,1)S(1)}, u32[]{:S(2)}, u32[]{:S(2)}) %collective-permute-start.42) | collective-permute-done | bytes 1179680 | tf_op jit(solution)/shard_map/ppermute | solution.py:669
  438.1 6.5 %collective-permute-done.44.refs_4_ = bf16[256,768]{1,0:T(8,128)(2,1)S(1)} collective-permute-done((bf16[256,768]{1,0:T(8,128)(2,1)S(1)}, bf16[256,768]{1,0:T(8,128)(2,1)S(1)}, u32[]{:S(2)}, u32[]{:S(2)}) %collective-permute-start.44) | collective-permute-done | bytes 393248 | tf_op jit(solution)/shard_map/ppermute | solution.py:669
  466.4 18.4 %collective-permute-done.49 = bf16[384,768]{1,0:T(8,128)(2,1)} collective-permute-done((bf16[384,768]{1,0:T(8,128)(2,1)}, bf16[384,768]{1,0:T(8,128)(2,1)}, u32[]{:S(2)}, u32[]{:S(2)}) %collective-permute-start.49) | collective-permute-done | bytes 589856 | tf_op jit(solution)/shard_map/ppermute | solution.py:669
  493.5 7.9 %collective-permute-done.55 = bf16[256,768]{1,0:T(8,128)(2,1)S(1)} collective-permute-done((bf16[256,768]{1,0:T(8,128)(2,1)S(1)}, bf16[256,768]{1,0:T(8,128)(2,1)S(1)}, u32[]{:S(2)}, u32[]{:S(2)}) %collective-permute-start.55) | collective-permute-done | bytes 393248 | tf_op jit(solution)/shard_map/ppermute | solution.py:669
  501.4 8.7 %collective-permute-done.52 = bf16[192,768]{1,0:T(8,128)(2,1)S(1)} collective-permute-done((bf16[192,768]{1,0:T(8,128)(2,1)S(1)}, bf16[192,768]{1,0:T(8,128)(2,1)S(1)}, u32[]{:S(2)}, u32[]{:S(2)}) %collective-permute-start.52) | collective-permute-done | bytes 294944 | tf_op jit(solution)/shard_map/ppermute | solution.py:669
  520.3 8.9 %collective-permute-done.58 = f32[16,768]{1,0:T(8,128)S(1)} collective-permute-done((f32[16,768]{1,0:T(8,128)S(1)}, f32[16,768]{1,0:T(8,128)S(1)}, u32[]{:S(2)}, u32[]{:S(2)}) %collective-permute-start.58) | collective-permute-done | bytes 49184 | tf_op jit(solution)/shard_map/ppermute | solution.py:669
  531.2 6.2 %collective-permute-done.60 = bf16[192,768]{1,0:T(8,128)(2,1)S(1)} collective-permute-done((bf16[192,768]{1,0:T(8,128)(2,1)S(1)}, bf16[192,768]{1,0:T(8,128)(2,1)S(1)}, u32[]{:S(2)}, u32[]{:S(2)}) %collective-permute-start.60) | collective-permute-done | bytes 294944 | tf_op jit(solution)/shard_map/ppermute | solution.py:669
  540.8 28.8 %collective-permute-done.63.refs_2_ = bf16[384,768]{1,0:T(8,128)(2,1)S(1)} collective-permute-done((bf16[384,768]{1,0:T(8,128)(2,1)S(1)}, bf16[384,768]{1,0:T(8,128)(2,1)S(1)}, u32[]{:S(2)}, u32[]{:S(2)}) %collective-permute-start.63) | collective-permute-done | bytes 589856 | tf_op jit(solution)/shard_map/ppermute | solution.py:669
  582.4 7.0 %shard_map.310 = (f32[1536,768]{1,0:T(8,128)}, f32[768,1536]{1,0:T(8,128)}) custom-call(s32[4]{0:T(128)S(1)} %pad_add_fusion.refs_0_, bf16[768,768]{1,0:T(8,128)(2,1)S(1)} %get-tuple-element.485.refs_1_, bf16[768,768]{1,0:T(8,128)(2,1)S(1)} %collective-permute-done.67.refs_2_, bf16[768,768]{1,0:T(8,128)(2,1)} %collective-permute-done.68.refs_3_, ...), custom_call_target="tpu_custom_call" | custom-call | flops 11500000256 | bytes 20000000 | tf_op jit(solution)/shard_map/pallas_call | solution.py:62
  (727 shorter events, 322.8 us)
Async XLA Ops:
  9.0 29.6 %collective-permute-start = (bf16[384,1152]{1,0:T(8,128)(2,1)}, bf16[384,1152]{1,0:T(8,128)(2,1)}, u32[]{:S(2)}, u32[]{:S(2)}) collective-permute-start(bf16[384,1152]{1,0:T(8,128)(2,1)} %concatenate.32), channel_id=1, source_target_pairs={{0,16},{16,0},{1,17},{17,1},{2,18},{18,2},{3,19},{19,3},{4,20},{20... | collective-permute-start | bytes 2654216 | tf_op jit(solution)/shard_map/ppermute | solution.py:669
  44.6 28.1 %collective-permute-start.7 = (bf16[384,1536]{1,0:T(8,128)(2,1)S(1)}, bf16[384,1536]{1,0:T(8,128)(2,1)S(1)}, u32[]{:S(2)}, u32[]{:S(2)}) collective-permute-start(bf16[384,1536]{1,0:T(8,128)(2,1)S(1)} %dynamic-slice_bitcast_fusion.5), channel_id=1, source_target_pairs={{0,16},{16,0},{1,17},{17,1},{2,18},{18,2},{3,19},{19,3},{4,20},{20... | collective-permute-start | bytes 3538952 | tf_op jit(solution)/shard_map/ppermute | solution.py:669
  50.0 22.7 %collective-permute-start.8 = (bf16[256,768]{1,0:T(8,128)(2,1)S(1)}, bf16[256,768]{1,0:T(8,128)(2,1)S(1)}, u32[]{:S(2)}, u32[]{:S(2)}) collective-permute-start(bf16[256,768]{1,0:T(8,128)(2,1)S(1)} %dynamic-slice_bitcast_fusion.9), channel_id=1, source_target_pairs={{0,8},{8,0},{1,9},{9,1},{2,10},{10,2},{3,11},{11,3},{4,12},{12,4},... | collective-permute-start | bytes 1179656 | tf_op jit(solution)/shard_map/ppermute | solution.py:669
  73.8 27.6 %collective-permute-start.12 = (bf16[768,768]{1,0:T(8,128)(2,1)S(1)}, bf16[768,768]{1,0:T(8,128)(2,1)S(1)}, u32[]{:S(2)}, u32[]{:S(2)}) collective-permute-start(bf16[768,768]{1,0:T(8,128)(2,1)S(1)} %dynamic-slice_bitcast_fusion.4), channel_id=1, source_target_pairs={{0,16},{16,0},{1,17},{17,1},{2,18},{18,2},{3,19},{19,3},{4,20},{20... | collective-permute-start | bytes 3538952 | tf_op jit(solution)/shard_map/ppermute | solution.py:669
  75.6 37.9 %collective-permute-start.13 = (bf16[384,1536]{1,0:T(8,128)(2,1)S(1)}, bf16[384,1536]{1,0:T(8,128)(2,1)S(1)}, u32[]{:S(2)}, u32[]{:S(2)}) collective-permute-start(bf16[384,1536]{1,0:T(8,128)(2,1)S(1)} %collective-permute-done.7.refs_6_.refs_4_), channel_id=1, source_target_pairs={{0,1},{1,0},{2,3},{3,2},{4,5},{5,4},{6,7},{7,6},{8,9},{9,8},{10,11... | collective-permute-start | bytes 3538952 | tf_op jit(solution)/shard_map/ppermute | solution.py:669
  77.7 23.7 %collective-permute-start.11 = (bf16[256,768]{1,0:T(8,128)(2,1)S(1)}, bf16[256,768]{1,0:T(8,128)(2,1)S(1)}, u32[]{:S(2)}, u32[]{:S(2)}) collective-permute-start(bf16[256,768]{1,0:T(8,128)(2,1)S(1)} %get-tuple-element.259.refs_3_), channel_id=1, source_target_pairs={{0,8},{8,0},{1,9},{9,1},{2,10},{10,2},{3,11},{11,3},{4,12},{12,4},... | collective-permute-start | bytes 1179656 | tf_op jit(solution)/shard_map/ppermute | solution.py:669
  250.5 28.1 %collective-permute-start.28 = (bf16[768,768]{1,0:T(8,128)(2,1)}, bf16[768,768]{1,0:T(8,128)(2,1)S(1)}, u32[]{:S(2)}, u32[]{:S(2)}) collective-permute-start(bf16[768,768]{1,0:T(8,128)(2,1)} %fusion.3), channel_id=1, source_target_pairs={{0,16},{16,0},{1,17},{17,1},{2,18},{18,2},{3,19},{19,3},{4,20},{20... | collective-permute-start | bytes 3538952 | tf_op jit(solution)/shard_map/ppermute | solution.py:669
  255.3 23.2 %collective-permute-start.27 = (bf16[512,768]{1,0:T(8,128)(2,1)S(1)}, bf16[512,768]{1,0:T(8,128)(2,1)S(1)}, u32[]{:S(2)}, u32[]{:S(2)}) collective-permute-start(bf16[512,768]{1,0:T(8,128)(2,1)S(1)} %add_convert_fusion.3), channel_id=1, source_target_pairs={{2,0},{3,1},{4,2},{5,3},{6,4},{7,5},{10,8},{11,9},{12,10},{13,11},... | collective-permute-start | bytes 2359304 | tf_op jit(solution)/shard_map/ppermute | solution.py:675
  280.8 24.3 %collective-permute-start.31 = (bf16[384,768]{1,0:T(8,128)(2,1)S(1)}, bf16[384,768]{1,0:T(8,128)(2,1)S(1)}, u32[]{:S(2)}, u32[]{:S(2)}) collective-permute-start(bf16[384,768]{1,0:T(8,128)(2,1)S(1)} %dynamic-slice_bitcast_fusion.7), channel_id=1, source_target_pairs={{0,2},{1,3},{2,0},{3,1},{4,6},{5,7},{6,4},{7,5},{8,10},{9,11},{10,... | collective-permute-start | bytes 1769480 | tf_op jit(solution)/shard_map/ppermute | solution.py:669
  326.6 34.3 %collective-permute-start.36 = (bf16[384,768]{1,0:T(8,128)(2,1)S(1)}, bf16[384,768]{1,0:T(8,128)(2,1)S(1)}, u32[]{:S(2)}, u32[]{:S(2)}) collective-permute-start(bf16[384,768]{1,0:T(8,128)(2,1)S(1)} %fusion.9), channel_id=1, source_target_pairs={{0,4},{1,5},{2,6},{3,7},{4,0},{5,1},{6,2},{7,3},{8,12},{9,13},{10,... | collective-permute-start | bytes 1769480 | tf_op jit(solution)/shard_map/ppermute | solution.py:669
  363.6 21.2 %collective-permute-start.38 = (bf16[384,768]{1,0:T(8,128)(2,1)S(1)}, bf16[384,768]{1,0:T(8,128)(2,1)S(1)}, u32[]{:S(2)}, u32[]{:S(2)}) collective-permute-start(bf16[384,768]{1,0:T(8,128)(2,1)S(1)} %add_convert_fusion.7), channel_id=1, source_target_pairs={{0,2},{1,3},{2,0},{3,1},{4,6},{5,7},{6,4},{7,5},{8,10},{9,11},{10,... | collective-permute-start | bytes 1769480 | tf_op jit(solution)/shard_map/ppermute | solution.py:669
  393.6 28.2 %collective-permute-start.42 = (bf16[768,768]{1,0:T(8,128)(2,1)}, bf16[768,768]{1,0:T(8,128)(2,1)S(1)}, u32[]{:S(2)}, u32[]{:S(2)}) collective-permute-start(bf16[768,768]{1,0:T(8,128)(2,1)} %fusion.1), channel_id=1, source_target_pairs={{0,16},{16,0},{1,17},{17,1},{2,18},{18,2},{3,19},{19,3},{4,20},{20... | collective-permute-start | bytes 3538952 | tf_op jit(solution)/shard_map/ppermute | solution.py:669
  396.4 25.3 %collective-permute-start.41 = (bf16[512,768]{1,0:T(8,128)(2,1)S(1)}, bf16[512,768]{1,0:T(8,128)(2,1)S(1)}, u32[]{:S(2)}, u32[]{:S(2)}) collective-permute-start(bf16[512,768]{1,0:T(8,128)(2,1)S(1)} %add_convert_fusion.2), channel_id=1, source_target_pairs={{2,0},{3,1},{4,2},{5,3},{6,4},{7,5},{10,8},{11,9},{12,10},{13,11},... | collective-permute-start | bytes 2359304 | tf_op jit(solution)/shard_map/ppermute | solution.py:675
  448.5 36.3 %collective-permute-start.49 = (bf16[384,768]{1,0:T(8,128)(2,1)}, bf16[384,768]{1,0:T(8,128)(2,1)}, u32[]{:S(2)}, u32[]{:S(2)}) collective-permute-start(bf16[384,768]{1,0:T(8,128)(2,1)} %fusion.5), channel_id=1, source_target_pairs={{0,4},{1,5},{2,6},{3,7},{4,0},{5,1},{6,2},{7,3},{8,12},{9,13},{10,... | collective-permute-start | bytes 1769480 | tf_op jit(solution)/shard_map/ppermute | solution.py:669
  460.5 24.4 %collective-permute-start.48 = (bf16[384,768]{1,0:T(8,128)(2,1)}, bf16[384,768]{1,0:T(8,128)(2,1)S(1)}, u32[]{:S(2)}, u32[]{:S(2)}) collective-permute-start(bf16[384,768]{1,0:T(8,128)(2,1)} %fusion.6), channel_id=1, source_target_pairs={{0,16},{16,0},{1,17},{17,1},{2,18},{18,2},{3,19},{19,3},{4,20},{20... | collective-permute-start | bytes 1769480 | tf_op jit(solution)/shard_map/ppermute | solution.py:669
  462.8 28.0 %collective-permute-start.61 = (bf16[192,768]{1,0:T(8,128)(2,1)S(1)}, bf16[192,768]{1,0:T(8,128)(2,1)S(1)}, u32[]{:S(2)}, u32[]{:S(2)}) collective-permute-start(bf16[192,768]{1,0:T(8,128)(2,1)S(1)} %fusion.12), channel_id=1, source_target_pairs={{0,4},{1,5},{2,6},{3,7},{4,0},{5,1},{6,2},{7,3},{8,12},{9,13},{10,... | collective-permute-start | bytes 884744 | tf_op jit(solution)/shard_map/ppermute | solution.py:669
  464.7 27.2 %collective-permute-start.53 = (bf16[256,768]{1,0:T(8,128)(2,1)S(1)}, bf16[256,768]{1,0:T(8,128)(2,1)S(1)}, u32[]{:S(2)}, u32[]{:S(2)}) collective-permute-start(bf16[256,768]{1,0:T(8,128)(2,1)S(1)} %get-tuple-element.481), channel_id=1, source_target_pairs={{0,16},{16,0},{1,17},{17,1},{2,18},{18,2},{3,19},{19,3},{4,20},{20... | collective-permute-start | bytes 1179656 | tf_op jit(solution)/shard_map/ppermute | solution.py:669
  465.6 27.8 %collective-permute-start.54 = (bf16[256,768]{1,0:T(8,128)(2,1)S(1)}, bf16[256,768]{1,0:T(8,128)(2,1)S(1)}, u32[]{:S(2)}, u32[]{:S(2)}) collective-permute-start(bf16[256,768]{1,0:T(8,128)(2,1)S(1)} %copy-done.27), channel_id=1, source_target_pairs={{0,8},{8,0},{1,9},{9,1},{2,10},{10,2},{3,11},{11,3},{4,12},{12,4},... | collective-permute-start | bytes 1179656 | tf_op jit(solution)/shard_map/ppermute | solution.py:669
  487.5 22.6 %collective-permute-start.51 = (bf16[384,768]{1,0:T(8,128)(2,1)S(1)}, bf16[384,768]{1,0:T(8,128)(2,1)S(1)}, u32[]{:S(2)}, u32[]{:S(2)}) collective-permute-start(bf16[384,768]{1,0:T(8,128)(2,1)S(1)} %add_convert_fusion.5), channel_id=1, source_target_pairs={{0,2},{1,3},{2,0},{3,1},{4,6},{5,7},{6,4},{7,5},{8,10},{9,11},{10,... | collective-permute-start | bytes 1769480 | tf_op jit(solution)/shard_map/ppermute | solution.py:669
  492.0 28.3 %collective-permute-start.62 = (bf16[192,768]{1,0:T(8,128)(2,1)S(1)}, bf16[192,768]{1,0:T(8,128)(2,1)S(1)}, u32[]{:S(2)}, u32[]{:S(2)}) collective-permute-start(bf16[192,768]{1,0:T(8,128)(2,1)S(1)} %add_convert_fusion.10), channel_id=1, source_target_pairs={{0,2},{1,3},{2,0},{3,1},{4,6},{5,7},{6,4},{7,5},{8,10},{9,11},{10,... | collective-permute-start | bytes 884744 | tf_op jit(solution)/shard_map/ppermute | solution.py:669
  529.9 39.8 %collective-permute-start.67 = (bf16[768,768]{1,0:T(8,128)(2,1)S(1)}, bf16[768,768]{1,0:T(8,128)(2,1)S(1)}, u32[]{:S(2)}, u32[]{:S(2)}) collective-permute-start(bf16[768,768]{1,0:T(8,128)(2,1)S(1)} %get-tuple-element.484), channel_id=1, source_target_pairs={{0,16},{16,0},{1,17},{17,1},{2,18},{18,2},{3,19},{19,3},{4,20},{20... | collective-permute-start | bytes 3538952 | tf_op jit(solution)/shard_map/ppermute | solution.py:669
  537.7 32.0 %collective-permute-start.63 = (bf16[384,768]{1,0:T(8,128)(2,1)S(1)}, bf16[384,768]{1,0:T(8,128)(2,1)S(1)}, u32[]{:S(2)}, u32[]{:S(2)}) collective-permute-start(bf16[384,768]{1,0:T(8,128)(2,1)S(1)} %get-tuple-element.492), channel_id=1, source_target_pairs={{0,16},{16,0},{1,17},{17,1},{2,18},{18,2},{3,19},{19,3},{4,20},{20... | collective-permute-start | bytes 1769480 | tf_op jit(solution)/shard_map/ppermute | solution.py:669
  538.9 43.5 %collective-permute-start.68 = (bf16[768,768]{1,0:T(8,128)(2,1)S(1)}, bf16[768,768]{1,0:T(8,128)(2,1)}, u32[]{:S(2)}, u32[]{:S(2)}) collective-permute-start(bf16[768,768]{1,0:T(8,128)(2,1)S(1)} %get-tuple-element.485.refs_1_), channel_id=1, source_target_pairs={{0,1},{1,0},{2,3},{3,2},{4,5},{5,4},{6,7},{7,6},{8,9},{9,8},{10,11... | collective-permute-start | bytes 3538952 | tf_op jit(solution)/shard_map/ppermute | solution.py:669
  540.3 34.0 %collective-permute-start.64 = (bf16[384,768]{1,0:T(8,128)(2,1)S(1)}, bf16[384,768]{1,0:T(8,128)(2,1)S(1)}, u32[]{:S(2)}, u32[]{:S(2)}) collective-permute-start(bf16[384,768]{1,0:T(8,128)(2,1)S(1)} %get-tuple-element.493.refs_1_), channel_id=1, source_target_pairs={{0,1},{1,0},{2,3},{3,2},{4,5},{5,4},{6,7},{7,6},{8,9},{9,8},{10,11... | collective-permute-start | bytes 1769480 | tf_op jit(solution)/shard_map/ppermute | solution.py:669
  (282 other events, 2839.0 us)

commit v4 on v3

--- a/solution.py
+++ b/solution.py
@@ -36,37 +36,69 @@
         self.array = array
 
 
-def call(inner_body, outs, scalars, blocks, remote=(), scratch=(), us=1.0, limit=16):
-    shapes = [jax.ShapeDtypeStruct(shape, kind) for shape, kind in outs]
+def in_hbm(array):
+    return pltpu.with_memory_space_constraint(array, pltpu.HBM)
+
+
+FLUSH = []
+
+
+def flush(*refs):
+    for ref in refs:
+        for k, (held, copy, started) in enumerate(FLUSH[-1]):
+            if held is ref and not started:
+                copy.start()
+                FLUSH[-1][k] = (held, copy, True)
+
+
+LATER, RAW = 1, 2
+
+
+def call(inner_body, outs, scalars, blocks, remote=(), scratch=(), us=1.0, limit=48):
+    shapes = [pltpu.HBM(o[0], o[1]) if len(o) > 2 else jax.ShapeDtypeStruct(o[0], o[1]) for o in outs]
+    kinds = [o[2] if len(o) > 2 else 0 for o in outs]
     late = [i for i, b in enumerate(blocks) if isinstance(b, Late)]
-    blocks = [b.array if isinstance(b, Late) else b for b in blocks]
+    blocks = [in_hbm(b.array) if isinstance(b, Late) else b for b in blocks]
+    remote = [in_hbm(r) for r in remote]
     n_in, n_out = 1 + len(blocks) + len(remote), len(outs)
-    staged = [pltpu.VMEM(blocks[i].shape, blocks[i].dtype) for i in late]
-    sems = [pltpu.SemaphoreType.DMA((len(late),))] if late else []
+    later = [i for i, kind in enumerate(kinds) if kind == LATER]
+    spare = [pltpu.VMEM(blocks[i].shape, blocks[i].dtype) for i in late]
+    spare += [pltpu.VMEM(shapes[i].shape, shapes[i].dtype) for i in later]
+    sems = [pltpu.SemaphoreType.DMA((max(len(late), 1),)), pltpu.SemaphoreType.DMA((max(len(later), 1),))]
 
     def body(*refs):
         refs = list(refs)
-        if not late:
-            return inner_body(*refs)
         first = n_in + n_out
-        stage, sem, own = refs[first : first + len(late)], refs[first + len(late)], refs[first + len(late) + 1 :]
-        copies = [pltpu.make_async_copy(refs[1 + i], v, sem.at[k]) for k, (i, v) in enumerate(zip(late, stage))]
+        n_spare = len(spare)
+        held, (sem, out_sem), own = refs[first : first + n_spare], refs[first + n_spare : first + n_spare + 2], refs[first + n_spare + 2 :]
+        copies = [pltpu.make_async_copy(refs[1 + i], v, sem.at[k]) for k, (i, v) in enumerate(zip(late, held))]
+        back = [
+            pltpu.make_async_copy(v, refs[n_in + i], out_sem.at[k])
+            for k, (i, v) in enumerate(zip(later, held[len(late) :]))
+        ]
         for copy in copies:
             copy.start()
         for copy in copies:
             copy.wait()
-        for i, v in zip(late, stage):
+        for i, v in zip(late, held):
             refs[1 + i] = v
-        return inner_body(*refs[:first], *own)
+        for i, v in zip(later, held[len(late) :]):
+            refs[n_in + i] = v
+        FLUSH.append([(held[len(late) + k], copy, False) for k, copy in enumerate(back)])
+        inner_body(*refs[:first], *own)
+        flush(*held[len(late) :])
+        FLUSH.pop()
+        for copy in back:
+            copy.wait()
 
     return pl.pallas_call(
         body,
         out_shape=shapes,
         in_specs=[SCALARS] + [FAR_OFF if i in late else WHOLE for i in range(len(blocks))] + [FAR_OFF] * len(remote),
-        out_specs=[WHOLE] * len(outs),
-        scratch_shapes=staged + sems + list(scratch),
+        out_specs=[FAR_OFF if kind else WHOLE for kind in kinds],
+        scratch_shapes=spare + sems + list(scratch),
         compiler_params=pltpu.CompilerParams(vmem_limit_bytes=limit * 1024 * 1024),
-        cost_estimate=pl.CostEstimate(flops=int(us * 2.3e9), bytes_accessed=int(us * 4e6), transcendentals=0),
+        cost_estimate=pl.CostEstimate(flops=int(us * 1.2e8), bytes_accessed=int(us * 2e5), transcendentals=0),
     )(scalars, *blocks, *remote)
 
 
@@ -124,7 +156,7 @@
         rows, features = ahead[0][1].shape
         blocks = [table, ahead[0][0], Late(carried)]
         for chunk in ahead:
-            blocks.extend(chunk[1:])
+            blocks.extend([Late(chunk[1]), *chunk[2:]])
     width = weights[0].shape[1] // 3
 
     def body(scal, tab, *refs):
@@ -158,9 +190,9 @@
                 kv = jnp.where(lane >= width + width // 2, rolled, kv)
             outs[4][at, :] = kv.astype(BF)
 
-    outs = [((rows, features), BF)] * 2 + [((rows, width), BF)] * 2 + [((2 * rows, 2 * width), BF)]
+    outs = [((rows, features), BF, LATER)] * 2 + [((rows, width), BF)] * 2 + [((2 * rows, 2 * width), BF)]
     if ahead is not None:
-        outs += [((rows, features), BF)] * 2
+        outs += [((rows, features), BF, LATER)] * 2
     r = call(body, outs, scalars, blocks, weights, held_like(weights), us=2.5)
     return list(x) if ahead is None else r[5:], r[:2], r[2:4], r[4]
 
@@ -278,10 +310,11 @@
                 finish(p, out_ref[at, span] * keep + value * take, amount_ref[at, span] * keep + total * take, *tops_all)
 
         lse[...] = jnp.transpose(stats[...])[0:8, :]
+        flush(att, lse)
         fetch_wait(own, held, sem)
         part[...] = dot_nn(att[...], held[...]).astype(BF)
 
-    outs = [((size, width), BF), ((8, size), F32), ((size, features), BF)]
+    outs = [((size, width), BF, LATER), ((8, size), F32, LATER), ((size, features), BF)]
     scratch = [pltpu.VMEM((size, 128), F32)] + held_like(weights)
     return call(body, outs, scalars, [q, *far, out, amount, tops], weights, scratch, us=4.5)
 
@@ -359,26 +392,25 @@
     return call(body, outs, scalars, blocks, (), staged(size, width), us=12)
 
 
-def attend_near_back(scalars, q, do, lse, delta, near, dq_before, others):
+def attend_near_back(scalars, q, do, lse, delta, near, dq_before):
     size, width = q[0].shape
     rows = size * CHUNKS
 
-    def body(scal, q0, q1, o0, o1, l0, l1, d0, d1, n_all, before, passed, dq_out, crossing, *held):
+    def body(scal, q0, q1, o0, o1, l0, l1, d0, d1, n_all, before, dq_out, crossing, *held):
         dq_out[...] = before[...]
-        crossing[:rows, :] = passed[...]
 
         @pl.when(scal[0] == 1)
         def _():
             stage(size, (q0, q1, o0, o1, l0, l1, d0, d1), held)
-            back_over(held, width, size, [(n_all, crossing, rows)], dq_out)
+            back_over(held, width, size, [(n_all, crossing, 0)], dq_out)
 
         @pl.when(scal[0] == 0)
         def _():
-            crossing[rows:, :] = jnp.zeros((rows, 2 * width), BF)
-
-    outs = [((rows, width), F32), ((2 * rows, 2 * width), BF)]
-    blocks = [*map(Late, q), *do, *map(Late, lse), *delta, Late(near), dq_before, others]
-    return call(body, outs, scalars, blocks, (), staged(size, width), us=6)
+            crossing[...] = jnp.zeros_like(crossing)
+
+    outs = [((rows, width), F32), ((rows, 2 * width), BF)]
+    blocks = [*map(Late, q), *do, *map(Late, lse), *delta, Late(near), dq_before]
+    return call(body, outs, scalars, blocks, (), staged(size, width), us=0.2)
 
 
 def attend_own_back(scalars, q, do, lse, delta, kv, dq_before):
@@ -406,7 +438,7 @@
 
     outs = [((size, width), BF)] * 2 + [((size, 2 * width), F32)] * 2
     blocks = [*map(Late, q), *do, *map(Late, lse), *delta, Late(kv), dq_before]
-    return call(body, outs, scalars, blocks, (), staged(size, width), us=6)
+    return call(body, outs, scalars, blocks, (), staged(size, width), us=0.2)
 
 
 def feed_forward(scalars, layer, table, x, mine, came, up, down):
@@ -422,17 +454,19 @@
         unit, _ = norm_parts(h)
         low = (unit * tab[GAIN1 : GAIN1 + 1] + tab[BIAS1 : BIAS1 + 1]).astype(BF)
         mlp_in[...] = low
+        flush(hidden, mlp_in)
         fetch_wait(u_own, up_held, up_sem)
         for j in range(inner // features):
             cols = slice(j * features, (j + 1) * features)
             value, grad = gelu_both(dot_nn(low, up_held[:, cols]) + tab[BUP + j : BUP + j + 1])
             active[:, cols] = value.astype(BF)
             slope[:, cols] = grad.astype(BF)
+        flush(active, slope)
         fetch_wait(d_own, down_held, down_sem)
         part[...] = dot_nn(active[...], down_held[...]).astype(BF)
 
-    outs = [((rows, features), F32), ((rows, features), BF), ((rows, inner), BF), ((rows, inner), BF), ((rows, features), BF)]
-    return call(body, outs, scalars, [table, Late(x), mine, came], [*up, *down], held_like(up, down), us=4, limit=24)
+    outs = [((rows, features), F32, LATER), ((rows, features), BF, LATER), ((rows, inner), BF, LATER), ((rows, inner), BF, LATER), ((rows, features), BF)]
+    return call(body, outs, scalars, [table, Late(x), mine, came], [*up, *down], held_like(up, down), us=4)
 
 
 def feed_back(scalars, layer, dy, slope, up, down):
@@ -454,7 +488,7 @@
         part[...] = dot_nt(d_up[...], up_held[...]).astype(BF)
 
     outs = [((rows, inner), BF), ((rows, features), BF), ((8, features), F32)]
-    return call(body, outs, scalars, [dy, Late(slope)], [*up, *down], held_like(up, down), us=4.5, limit=24)
+    return call(body, outs, scalars, [dy, Late(slope)], [*up, *down], held_like(up, down), us=1.0)
 
 
 def middle_back(scalars, layer, table, hidden, mine, came, dy, attended, weights):
@@ -470,6 +504,7 @@
         dh_ref[...] = dh
         low = dh.astype(BF)
         low_ref[...] = low
+        flush(dh_ref, low_ref)
         sums[...] = jnp.zeros_like(sums)
         sums[0:1, :] = d_gain
         sums[1:2, :] = d_bias
@@ -487,7 +522,7 @@
             stats[:, 2 * p + 1 : 2 * p + 2] = jnp.sum(jnp.where(first, 0.0, product), axis=1, keepdims=True)
         delta[...] = jnp.transpose(stats[...])[0:8, :]
 
-    outs = [((rows, features), F32), ((rows, features), BF), ((rows, width), BF), ((8, rows), F32), ((8, features), F32)]
+    outs = [((rows, features), F32, LATER), ((rows, features), BF, LATER), ((rows, width), BF), ((8, rows), F32), ((8, features), F32)]
     scratch = [pltpu.VMEM((rows, 128), F32)] + held_like(weights)
     return call(body, outs, scalars, [table, Late(hidden), mine, came, dy, Late(attended)], weights, scratch, us=2.8)
 
@@ -522,9 +557,9 @@
     outs = [((rows, 2 * width), BF), ((rows, features), BF), ((8, features), F32)]
     blocks = [dq, dkv, near, far]
     if returned is None:
-        outs.append(((rows, 2 * width), F32))
+        outs.append(((rows, 2 * width), F32, LATER))
     else:
-        blocks.append(returned)
+        blocks.append(Late(returned))
     return call(body, outs, scalars, blocks, weights, held_like(weights), us=2.7)
 
 
@@ -541,8 +576,8 @@
         sums[0:1, :] = d_gain
         sums[1:2, :] = d_bias
 
-    outs = [((rows, features), F32), ((rows, features), BF), ((8, features), F32)]
-    return call(body, outs, scalars, [table, Late(x), mine, came, Late(dh)], us=1.5)
+    outs = [((rows, features), F32, LATER), ((rows, features), BF), ((8, features), F32)]
+    return call(body, outs, scalars, [table, Late(x), mine, came, Late(dh)], us=0.5)
 
 
 def both_chunks(left, left_span, right, right_span):
@@ -553,22 +588,36 @@
     return total
 
 
+def hand_out(scal, packed, send, mine, sem):
+    copies = [
+        pltpu.make_async_copy(packed.at[pl.ds(2 * (1 - scal[3]), 2)], send, sem.at[0]),
+        pltpu.make_async_copy(packed.at[pl.ds(2 * scal[3], 2)], mine, sem.at[1]),
+    ]
+    for copy in copies:
+        copy.start()
+    for copy in copies:
+        copy.wait()
+
+
 def wide_grads(scalars, active, dy, mlp_in, d_up):
     features = dy[0].shape[1]
     inner = active[0].shape[1]
     a, half = inner // 4, features // 2
     size = a + half
 
-    def body(scal, a0, a1, y0, y1, m0, m1, u0, u1, packed):
+    def body(scal, a0, a1, y0, y1, m0, m1, u0, u1, send, mine, packed, sem):
         for k in range(4):
             span = slice(k * a, (k + 1) * a)
             packed[k, :a, :] = both_chunks((a0, a1), span, (y0, y1), slice(None)).astype(BF)
             for i in range(2):
                 part = both_chunks((m0, m1), slice(i * half, (i + 1) * half), (u0, u1), span)
                 packed[k, a:, i * a : (i + 1) * a] = part.astype(BF)
+        hand_out(scal, packed, send, mine, sem)
 
     blocks = [*map(Late, active), *dy, *map(Late, mlp_in), *d_up]
-    return call(body, [((4, size, features), BF)], scalars, blocks, us=3.7)[0]
+    outs = [((2, size, features), BF, RAW)] * 2
+    scratch = [pltpu.VMEM((4, size, features), BF), pltpu.SemaphoreType.DMA((2,))]
+    return call(body, outs, scalars, blocks, (), scratch, us=3.7)
 
 
 def narrow_grads(scalars, normed, dq, dkv, attended, dh_low):
@@ -578,7 +627,7 @@
     half, c = rows // 2, width // 4
     size = rows + half + c
 
-    def body(scal, n0, n1, q0, q1, k0, k1, t0, t1, h0, h1, packed):
+    def body(scal, n0, n1, q0, q1, k0, k1, t0, t1, h0, h1, send, mine, packed, sem):
         every = slice(None)
         for x in range(2):
             span = slice(2 * x * rows, 2 * (x + 1) * rows)
@@ -593,49 +642,56 @@
         out = both_chunks((t0, t1), every, (h0, h1), every).astype(BF)
         for k in range(4):
             packed[k, rows + half :, :] = out[k * c : (k + 1) * c, :]
+        hand_out(scal, packed, send, mine, sem)
 
     blocks = [*map(Late, normed), *dq, *dkv, *map(Late, attended), *map(Late, dh_low)]
-    return call(body, [((4, size, features), BF)], scalars, blocks, us=2.1)[0]
-
-
-def collect(scal, refs, held, sem):
+    outs = [((2, size, features), BF, RAW)] * 2
+    scratch = [pltpu.VMEM((4, size, features), BF), pltpu.SemaphoreType.DMA((2,))]
+    return call(body, outs, scalars, blocks, (), scratch, us=2.1)
+
+
+def collect(scal, parts, held, sem):
     copies = []
-    for i, ref in enumerate(refs):
+    for i, refs in enumerate(parts):
         core = scal[3] if i < 2 else 1 - scal[3]
         section = scal[2] if i % 2 == 0 else 1 - scal[2]
-        copies.append(pltpu.make_async_copy(ref, held.at[2 * core + section], sem.at[i]))
+        size = held.shape[1] // len(refs)
+        for j, ref in enumerate(refs):
+            place = held.at[2 * core + section, j * size : (j + 1) * size]
+            copies.append(pltpu.make_async_copy(ref, place, sem.at[len(copies)]))
     for copy in copies:
         copy.start()
     for copy in copies:
         copy.wait()
 
 
-def wide_unpack(scalars, parts, inner):
-    size, features = parts[0].shape
+def wide_unpack(scalars, mine, mine2, other, other2, inner):
+    size, features = mine.shape
     a, half = inner // 4, features // 2
 
-    def body(scal, p0, p1, p2, p3, down, up, held, sem):
-        collect(scal, (p0, p1, p2, p3), held, sem)
+    def body(scal, p0, p1a, p1b, p2, p3a, p3b, down, up, token, held, sem):
+        collect(scal, ((p0,), (p1a, p1b), (p2,), (p3a, p3b)), held, sem)
         for k in range(4):
             down[k * a : (k + 1) * a, :] = held[k, :a, :].astype(F32)
             for i in range(2):
                 up[i * half : (i + 1) * half, k * a : (k + 1) * a] = held[k, a:, i * a : (i + 1) * a].astype(F32)
-
-    outs = [((inner, features), F32), ((features, inner), F32)]
-    scratch = [pltpu.VMEM((4, size, features), BF), pltpu.SemaphoreType.DMA((4,))]
-    return call(body, outs, scalars, [], parts, scratch, us=5)
-
-
-def narrow_unpack(scalars, parts, extras, width):
+        token[...] = jnp.zeros_like(token)
+
+    outs = [((inner, features), F32), ((features, inner), F32), ((8, 128), F32)]
+    scratch = [pltpu.VMEM((4, size, features), BF), pltpu.SemaphoreType.DMA((6,))]
+    return call(body, outs, scalars, [], [mine, *other, mine2, *other2], scratch, us=5)
+
+
+def narrow_unpack(scalars, parts, extras, width, token):
     size, features = parts[0].shape
     rows = features // 4
     half, c, own = rows // 2, width // 4, width // 2
 
-    def body(scal, p0, p1, p2, p3, e0, e1, query, key, value, extra, out, held, pair, sem, pair_sem):
+    def body(scal, _, p0, p1, p2, p3, e0, e1, query, key, value, extra, out, held, pair, sem, pair_sem):
         last = [pltpu.make_async_copy(e, pair.at[i if i == 0 else 1], pair_sem.at[i]) for i, e in enumerate((e0, e1))]
         for copy in last:
             copy.start()
-        collect(scal, (p0, p1, p2, p3), held, sem)
+        collect(scal, ((p0,), (p1,), (p2,), (p3,)), held, sem)
         for copy in last:
             copy.wait()
         for x in range(2):
@@ -661,7 +717,7 @@
         pltpu.VMEM((4, size, features), BF), pltpu.VMEM((2, half, features), BF),
         pltpu.SemaphoreType.DMA((4,)), pltpu.SemaphoreType.DMA((2,)),
     ]
-    return call(body, outs, scalars, [], list(parts) + list(extras), scratch, us=3)
+    return call(body, outs, scalars, [token], list(parts) + list(extras), scratch, us=3)
 
 
 def swap(value, axis, bits=1):
@@ -688,56 +744,66 @@
 
 
 class Reduction:
-    def __init__(self, parts):
-        self.core = lax.axis_index("batch") % 2
+    def __init__(self, grads, pieces):
         self.section = lax.axis_index("section")
-        self.parts = parts.reshape((2, 2) + parts.shape[1:])
+        self.send, self.mine = grads
+        self.pieces = pieces
 
     def over_cores(self):
-        self.near = swap(take(self.parts, 1 - self.core), "batch")
-        return self.near
+        self.near = swap(self.send, "batch")
+
+    def pair_sum(self, section, start, size):
+        cut = [lax.dynamic_slice(a, (section, start, 0), (1, size, a.shape[2]))[0] for a in (self.mine, self.near)]
+        return cut[0].astype(F32) + cut[1].astype(F32)
 
     def prepare(self):
-        mine = take(self.parts, self.core)
-        other = 1 - self.section
-        self.sent = (take(mine, other).astype(F32) + take(self.near, other).astype(F32)).astype(BF)
-        self.kept = (take(mine, self.section).astype(F32) + take(self.near, self.section).astype(F32)).astype(BF)
-
-    def over_sections(self):
-        self.came = swap(self.sent, "section")
-
-    def scatter(self):
-        self.bits = list(range(1, lax.axis_size("batch").bit_length() - 1))
+        size = self.mine.shape[1] // self.pieces
+        self.sent = [self.pair_sum(1 - self.section, i * size, size).astype(BF) for i in range(self.pieces)]
+
+    def over_sections(self, i=0):
+        if i == 0:
+            self.came = []
+        self.came.append(swap(self.sent[i], "section"))
+
+    def scatter_send(self):
         index = lax.axis_index("batch")
-        part = (self.kept.astype(F32) + self.came.astype(F32)).astype(BF)
-        for bit in self.bits[:-1]:
-            side = (index >> bit) & 1
-            cut = part.reshape((2, part.shape[0] // 2) + part.shape[1:])
-            if bit > 1:
-                cut = lax.optimization_barrier(cut)
-            got = swap(take(cut, 1 - side), "batch", 1 << bit)
-            part = (take(cut, side), got)
-            if bit != self.bits[-2]:
-                part = (part[0].astype(F32) + part[1].astype(F32)).astype(BF)
-        self.part = part
-        return part
-
-    def exchange(self):
-        part = self.part
-        self.part = (part[0].astype(F32) + part[1].astype(F32)).astype(BF)
-        self.over = swap(self.part, "batch", 1 << self.bits[-1])
-
-    def gather(self):
-        part = (self.part.astype(F32) + self.over.astype(F32)).astype(BF)
+        half = self.mine.shape[1] // 2
+        came = self.came if self.pieces == 2 else [self.came[0][:half], self.came[0][half:]]
+        cut = [(self.pair_sum(self.section, i * half, half) + came[i].astype(F32)).astype(BF) for i in range(2)]
+        *first, near, far = chip_bits()
+        for bit in first:
+            keep, send = paired(*cut, (index >> bit) & 1)
+            total = (keep.astype(F32) + swap(send, "batch", 1 << bit).astype(F32)).astype(BF)
+            cut = jnp.split(total, 2, axis=0)
+        self.keep, send = paired(*cut, (index >> near) & 1)
+        return send
+
+    def exchange_send(self, got):
+        self.part = (self.keep.astype(F32) + got.astype(F32)).astype(BF)
+        return self.part
+
+    def gather_send(self, got):
+        self.part = (self.part.astype(F32) + got.astype(F32)).astype(BF)
+        return self.part
+
+    def finish(self, got):
         index = lax.axis_index("batch")
-        for bit in reversed(self.bits[:-1]):
-            got = swap(part, "batch", 1 << bit)
-            self.pair = (part, got, (index >> bit) & 1)
-            part = jnp.concatenate(paired(*self.pair), axis=0)
-        return part
-
-    def finish(self):
-        self.quarter = jnp.concatenate(paired(*self.pair), axis=0)
+        *first, near, far = chip_bits()
+        part = jnp.concatenate(paired(self.part, got, (index >> near) & 1), axis=0)
+        for bit in reversed(first):
+            part = jnp.concatenate(paired(part, swap(part, "batch", 1 << bit), (index >> bit) & 1), axis=0)
+        self.quarter = part
+
+
+def chip_bits():
+    return list(range(1, lax.axis_size("batch").bit_length() - 1))
+
+
+def swap_all(values, place):
+    sizes = [v.shape[0] for v in values]
+    got = swap(jnp.concatenate(values, axis=0) if len(values) > 1 else values[0], "batch", 1 << chip_bits()[place])
+    ends = [sum(sizes[: i + 1]) for i in range(len(sizes))]
+    return [got[end - size : end] for size, end in zip(sizes, ends)]
 
 
 def tie(value, *others):
@@ -762,7 +828,7 @@
         lse.append(l)
         parts.append(part)
         came.append(swap(part, "tensor"))
-    came[0] = hooks.get("far", lambda came, part: came)(came[0], parts[-1])
+    came = hooks.get("far", nothing)(came)
     hidden, mlp_in, active, slope, results = [], [], [], [], []
     for c in range(CHUNKS):
         h, m, a, s, part = feed_forward(scalars, layer, table, x[c], parts[c], came[c], w["up"], w["down"])
@@ -778,14 +844,16 @@
 
 def backward_layer(scalars, layer, table, w, kept, dy, returned, steps):
     rows = CHUNKS * dy[0].shape[0]
-    dy = steps("start", dy)
+    dy = list(steps("start", dy))
     d_up, parts, up_sums = [], [], []
     for c in range(CHUNKS):
+        if c == 1:
+            dy[1] = steps("half", after(dy[1], parts[0][0]))
         grad, part, sums = feed_back(scalars, layer, dy[c], kept["slope"][c], w["up"], w["down"])
         d_up.append(grad)
         up_sums.append(sums)
         parts.append((part, swap(part, "tensor")))
-    wide = Reduction(wide_grads(scalars, kept["active"], dy, kept["mlp_in"], d_up))
+    wide = Reduction(wide_grads(scalars, kept["active"], dy, kept["mlp_in"], d_up), 2)
     parts = steps("fed", parts, wide)
     dh, dh_low, d_att, delta, mid_sums = [], [], [], [], []
     for c in range(CHUNKS):
@@ -794,12 +862,12 @@
             held.append(value)
     d_att = steps("mid", d_att, wide)
     dq, mine, others = attend_far_back(scalars, kept["q"], d_att, kept["lse"], delta, kept["far"])
+    total = (mine.astype(F32) + swap(others, "batch").astype(F32)).astype(BF)
+    dq = steps("turn", after(dq, total), wide)
+    home = shift(total, -2)
+    dq, crossing = attend_near_back(scalars, kept["q"], d_att, kept["lse"], delta, kept["near"], dq)
+    near = swap(crossing, "batch")
     dq = steps("between", dq, wide)
-    dq, crossing = attend_near_back(scalars, kept["q"], d_att, kept["lse"], delta, kept["near"], dq, others)
-    came = swap(crossing, "batch")
-    total, near = (mine.astype(F32) + came[:rows].astype(F32)).astype(BF), came[rows:]
-    total, dq = steps("far", (total, dq), wide)
-    home = shift(total, -2)
     dq0, dq1, dk0, dk1 = attend_own_back(scalars, kept["q"], d_att, kept["lse"], delta, kept["kv"], dq)
     dq, dkv = [dq0, dq1], [dk0, dk1]
     home, dq = steps("near", (home, dq), wide)
@@ -811,12 +879,11 @@
         parts.append((r[1], swap(r[1], "tensor")))
         in_sums.append(r[2])
         back.extend(r[3:])
-    narrow = Reduction(narrow_grads(scalars, kept["normed"], dq, dkv_low, kept["att"], dh_low))
+    narrow = Reduction(narrow_grads(scalars, kept["normed"], dq, dkv_low, kept["att"], dh_low), 1)
     parts = steps("proj", parts, wide, narrow)
+    parts = steps("last", parts, wide, narrow)
     dx, dx_low, last_sums = [], [], []
     for c in range(CHUNKS):
-        if c == 1:
-            parts[1] = steps("last", parts[1], wide, narrow)
         r = last_back(scalars, table, kept["x"][c], *parts[c], dh[c])
         dx.append(r[0])
         dx_low.append(r[1])
@@ -892,8 +959,8 @@
         w["up"] = (up_weight[0], got, swap(got, "batch"))
         return far
 
-    def on_far(came, part):
-        came, got = tie(came, late["down"], part)[:2]
+    def on_far(came):
+        *came, got = tie(*came, late["down"])
         w["down"] = (down_weight[0], got, swap(got, "batch"))
         return came
 
@@ -915,115 +982,131 @@
     def steps1(number, values, wide=None, narrow=None):
         leaves, tree = jax.tree.flatten(values)
         if number == "fed":
-            *leaves, wide.parts = tie(*leaves, wide.parts)
+            *leaves, wide.send = tie(*leaves, wide.send)
             wide.over_cores()
         if number == "mid":
             *leaves, wide.near = tie(*leaves, wide.near)
             wide.prepare()
-            *leaves, wide.sent = tie(*leaves, wide.sent)
-            wide.over_sections()
+            *leaves, wide.sent[0], wide.sent[1] = tie(*leaves, *wide.sent)
+            wide.over_sections(0)
+        if number == "between":
+            *leaves, wide.came[0], wide.sent[1] = tie(*leaves, wide.came[0], wide.sent[1])
+            wide.over_sections(1)
         if number == "near":
-            *leaves, wide.came = tie(*leaves, wide.came)
-            wide.scatter()
+            *leaves, wide.came[1] = tie(*leaves, wide.came[1])
+            late["a1"] = swap_all([wide.scatter_send()], -2)[0]
         if number == "proj":
-            kept, got = wide.part
-            *leaves, narrow.parts, got = tie(*leaves, narrow.parts, got)
-            wide.part = kept, got
+            *leaves, narrow.send, got = tie(*leaves, narrow.send, late["a1"])
             narrow.over_cores()
-        if number == "last":
-            *leaves, narrow.near = tie(*leaves, narrow.near)
-        return jax.tree.unflatten(tree, leaves)
-
-    dx1, dx1_low, back, wide1, narrow1, small1 = backward_layer(scalars, 1, tables[1], w, kept1, late["dy"], None, steps1)
-
-    def steps0(number, values, wide=None, narrow=None):
-        leaves, tree = jax.tree.flatten(values)
-        if number == "start":
-            wide1.exchange()
-            narrow1.prepare()
-            *leaves, wide1.part, narrow1.sent = tie(*leaves, wide1.part, narrow1.sent)
-            wide1.over = swap(wide1.part, "batch", 1 << wide1.bits[-1])
-            narrow1.over_sections()
-        if number == "fed":
-            *leaves, wide.parts, narrow1.came, wide1.over = tie(*leaves, wide.parts, narrow1.came, wide1.over)
-            wide.over_cores()
-            narrow1.scatter()
-            wide1.gather()
-        if number == "mid":
-            *leaves, wide.near = tie(*leaves, wide.near)
-            wide.prepare()
-            *leaves, wide.sent = tie(*leaves, wide.sent)
-            wide.over_sections()
-        if number == "between":
-            mine, got, side = wide1.pair
-            kept, came = narrow1.part
-            *leaves, got, came = tie(*leaves, got, came)
-            wide1.pair = mine, got, side
-            narrow1.part = kept, came
-        if number == "near":
-            *leaves, wide.came = tie(*leaves, wide.came)
-            wide.scatter()
-        if number == "proj":
-            kept, got = wide.part
-            *leaves, narrow.parts, got = tie(*leaves, narrow.parts, got)
-            wide.part = kept, got
-            narrow.over_cores()
-            wide.exchange()
+            sent = wide.exchange_send(got)
+            *leaves, sent = tie(*leaves, sent)
+            late["b1"] = swap_all([sent], -1)[0]
         if number == "last":
             *leaves, narrow.near = tie(*leaves, narrow.near)
             narrow.prepare()
+            *leaves, narrow.sent[0] = tie(*leaves, narrow.sent[0])
+            narrow.over_sections()
+        return jax.tree.unflatten(tree, leaves)
+
+    dx1, dx1_low, back, wide1, narrow1, small1 = backward_layer(scalars, 1, tables[1], w, kept1, late["dy"], None, steps1)
+
+    def steps0(number, values, wide=None, narrow=None):
+        leaves, tree = jax.tree.flatten(values)
+        if number == "half":
+            *leaves, narrow1.came[0], got = tie(*leaves, narrow1.came[0], late["b1"])
+            sent = [wide1.gather_send(got), narrow1.scatter_send()]
+            *leaves, sent[0], sent[1] = tie(*leaves, *sent)
+            late["c1"] = swap_all(sent, -2)
+        if number == "fed":
+            *leaves, wide.send, got, narrow_got = tie(*leaves, wide.send, *late["c1"])
+            wide.over_cores()
+            wide1.finish(got)
+            sent = narrow1.exchange_send(narrow_got)
+            *leaves, sent = tie(*leaves, sent)
+            late["d1"] = swap_all([sent], -1)[0]
+        if number == "mid":
+            *leaves, wide.near, got = tie(*leaves, wide.near, late["d1"])
+            wide.prepare()
+            *leaves, wide.sent[0], wide.sent[1] = tie(*leaves, *wide.sent)
+            wide.over_sections(0)
+            late["e1"] = narrow1.gather_send(got)
+        if number == "between":
+            *leaves, wide.came[0], wide.sent[1] = tie(*leaves, wide.came[0], wide.sent[1])
+            wide.over_sections(1)
+        if number == "near":
+            *leaves, wide.came[1] = tie(*leaves, wide.came[1])
+            late["a0"] = swap_all([wide.scatter_send(), late["e1"]], -2)
+        if number == "proj":
+            *leaves, narrow.send, got, narrow_got = tie(*leaves, narrow.send, *late["a0"])
+            narrow1.finish(narrow_got)
+            narrow.over_cores()
+            sent = wide.exchange_send(got)
+            *leaves, sent = tie(*leaves, sent)
+            late["b0"] = swap_all([sent], -1)[0]
+            *leaves, narrow.near = tie(*leaves, narrow.near)
+            narrow.prepare()
+            *leaves, narrow.sent[0] = tie(*leaves, narrow.sent[0])
+            narrow.over_sections()
+            late["y1"] = [swap(after(r[2], leaves[0]), "tensor") for r in second]
+        if number == "last":
+            *leaves, narrow.came[0] = tie(*leaves, narrow.came[0])
         return jax.tree.unflatten(tree, leaves)
 
     dx0, dx0_low, _, wide0, narrow0, small0 = backward_layer(scalars, 0, tables[0], w, kept0, dx1_low, back, steps0)
     sums = jnp.stack([small0, small1])
-    y_parts = [r[2] for r in second]
-    grads = [my_half(dx0), my_half(dx1)]
-    sums, narrow0.sent, *y_parts = tie(sums, narrow0.sent, *y_parts)
-    narrow0.over_sections()
-    narrow1.exchange()
-    y_came = [swap(y, "tensor") for y in y_parts]
     sums = sums + swap(sums, "batch")
-    sums, narrow0.came, wide0.over = tie(sums, narrow0.came, wide0.over)
-    narrow0.scatter()
-    wide0.gather()
-    mine, got, side = wide0.pair
-    kept, came = narrow0.part
+    got, sums, *rest = tie(late["b0"], sums, *late["y1"], my_half(dx0), my_half(dx1))
+    y_came, grads = rest[:2], rest[2:]
+    sent = [narrow0.scatter_send(), wide0.gather_send(got)]
+    sent[0], sent[1], sums, grads[0], grads[1] = tie(*sent, sums, *grads)
+    late["c0"] = swap_all(sent, -2)
+    table = take(sums, section) + swap(take(sums, 1 - section), "section")
     mine_grads, other_grads = by_section(*grads, BF)
-    table = take(sums, section) + swap(take(sums, 1 - section), "section")
-    narrow1.gather()
-    table, got, came, other_grads, *y_came = tie(table, got, came, other_grads, *y_came)
-    wide0.pair = mine, got, side
-    narrow0.part = kept, came
-    narrow0.exchange()
-    wide0.finish()
-    wide1.finish()
     y1 = my_half(
         [(r[1] + r[0][BDOWN : BDOWN + 1] + r[2].astype(F32) + c.astype(F32)).astype(BF) for r, c in zip(second, y_came)]
     )
     mine_out, other_out = by_section(my_half(y0), y1, BF)
-    for bit in range(1, lax.axis_size("batch").bit_length() - 1):
+
+    narrow0_got, wide0_got, table, other_grads, other_out = tie(
+        *late["c0"], table, other_grads, other_out
+    )
+    sent = narrow0.exchange_send(narrow0_got)
+    wide0.finish(wide0_got)
+    wide_mine = jnp.where(section == 0, wide0.quarter, wide1.quarter)
+    wide_sent = jnp.split(jnp.where(section == 0, wide1.quarter, wide0.quarter), 2, axis=0)
+    sent, wide_sent[0] = tie(sent, wide_sent[0])
+    got = swap_all([sent], -1)[0]
+    wide_other = [swap(wide_sent[0], "section")]
+    for bit in chip_bits()[:-1]:
         table = table + swap(table, "batch", 1 << bit)
-    wide_mine = jnp.where(section == 0, wide0.quarter, wide1.quarter)
-    wide_other = swap(jnp.where(section == 0, wide1.quarter, wide0.quarter), "section")
-    narrow0.over, table, other_out = tie(narrow0.over, table, other_out)
-    narrow0.gather()
-    narrow0.finish()
-    narrow1.finish()
+
+    got, table, wide_other[0], wide_sent[1] = tie(got, table, wide_other[0], wide_sent[1])
+    sent = narrow0.gather_send(got)
+    got = swap_all([sent], -2)[0]
+    wide_mine2, wide_other2 = swap(wide_mine, "batch"), swap(wide_other[0], "batch")
+    table = table + swap(table, "batch", 1 << chip_bits()[-1])
+    wide_other.append(swap(wide_sent[1], "section"))
+
+    got, wide_other[1], table = tie(got, wide_other[1], table)
+    narrow0.finish(got)
     outputs = jnp.stack(paired(mine_out, other_out, section))
     input_grads = jnp.stack(paired(mine_grads.astype(F32), other_grads.astype(F32), section))
 
     def gathered(first, second):
         mine = jnp.where(section == 0, first, second)
         other = swap(jnp.where(section == 0, second, first), "section")
-        return mine, other, swap(mine, "batch"), swap(other, "batch")
-
-    wide_all = (wide_mine, wide_other, swap(wide_mine, "batch"), swap(wide_other, "batch"))
-    d_down, d_up = wide_unpack(scalars, wide_all, inner)
+        mine2 = swap(mine, "batch")
+        other, mine2 = tie(other, mine2, token)[:2]
+        return mine, other, mine2, swap(other, "batch")
+
+    d_down, d_up, token = wide_unpack(
+        scalars, wide_mine, wide_mine2, wide_other, [wide_other2, swap(wide_other[1], "batch")], inner
+    )
     rows = features // 4
     extra = narrow0.quarter[rows : rows + rows // 2]
     extras = (extra, swap(extra, "batch"))
     d_q, d_k, d_v, d_extra, d_out = narrow_unpack(
-        scalars, gathered(narrow0.quarter, narrow1.quarter), extras, width
+        scalars, gathered(narrow0.quarter, narrow1.quarter), extras, width, token
     )
     d_qk = jnp.stack([d_q, d_k], axis=1)
     return (

time: 597 us -> 554 us (0.928)
  Pallas kernels: 128 us -> 176 us
  waiting for transfers between devices: 267 us -> 226 us
  local copies, waits for them, and re-layouts: 70.8 us -> 37 us
  other arithmetic: 37.2 us -> 24.4 us
    pallas_call x40, Pallas kernels: 128 us -> 176 us  [call(): pl.pallas_call(body, out_shape=shapes, in_specs=[SCALARS] + [FAR_OFF if i...]
    ppermute x66 -> x69, waiting for transfers between devices: 245 us -> 201 us  [swap(): return lax.ppermute(value, axis, [(i, i ^ bits) for i in range(count)])]
    unnamed x475 -> x175, local copies, waits for them, and re-layouts: 50.9 us -> 23.5 us
    convert_element_type x18 -> x14, other arithmetic: 24.1 us -> 8.19 us  [the longest x4 3.89 us: prepare(): self.pair_sum(1 - self.section, i * size, size).astype(BF)]
    ppermute x66 -> x69, starting transfers between devices: 72.7 us -> 68.3 us  [swap(): return lax.ppermute(value, axis, [(i, i ^ bits) for i in range(count)])]
  transfers between devices with their start and end apart: 70 -> 73, of which waited for: 33 -> 38; matrix products, arithmetic and copies ran while one was open for 8% -> 6% of each run, Pallas kernels for 15% -> 28%
where the time goes in v4:
time: 554 us; the launch traced here: 546 us
  waiting for transfers between devices  226 us (41%)
  Pallas kernels  176 us (32%)
  starting transfers between devices  78.3 us (14%)
  local copies, waits for them, and re-layouts  37 us (7%)
  other arithmetic  24.4 us (4%)
    ppermute x69, waiting for transfers between devices, swap(): return lax.ppermute(value, axis, [(i, i ^ bits) for i in range(count)])  201 us
    pallas_call x40, Pallas kernels, call(): pl.pallas_call(body, out_shape=shapes, in_specs=[SCALARS] + [FAR_OFF if i...  176 us
    ppermute x69, starting transfers between devices, swap(): return lax.ppermute(value, axis, [(i, i ^ bits) for i in range(count)])  68.3 us
    ppermute x4, waiting for transfers between devices, shift(): lax.ppermute(value, 'batch', [(i, i + steps) for i in range(first, last)])  25.4 us
    unnamed x175, local copies, waits for them, and re-layouts  23.5 us
  transfers between devices with their start and end apart: 73, of which 38 were waited for; matrix products, arithmetic and copies ran while one was open for 6% of the time, Pallas kernels for 28%

profile of v4, /device:TPU:0, one launch (start us, length us, event | category | flops | bytes accessed | tf_op | source)
XLA Modules:
  0.0 545.8 jit_solution(16674207857249286371)
XLA Ops:
  23.3 8.1 %collective-permute-done.2 = f32[16,768]{1,0:T(8,128)S(1)} collective-permute-done((f32[16,768]{1,0:T(8,128)S(1)}, f32[16,768]{1,0:T(8,128)S(1)}, u32[]{:S(2)}, u32[]{:S(2)}) %collective-permute-start.2) | collective-permute-done | bytes 49184 | tf_op jit(solution)/shard_map/ppermute | solution.py:725
  55.0 11.7 %collective-permute-done.5.refs_2_.refs_9_ = bf16[512,768]{1,0:T(8,128)(2,1)S(1)} collective-permute-done((bf16[512,768]{1,0:T(8,128)(2,1)S(1)}, bf16[512,768]{1,0:T(8,128)(2,1)S(1)}, u32[]{:S(2)}, u32[]{:S(2)}) %collective-permute-start.5) | collective-permute-done | bytes 786464 | tf_op jit(solution)/shard_map/ppermute | solution.py:731
  77.4 18.4 %collective-permute-done.13.refs_9_.refs_7_ = bf16[768,768]{1,0:T(8,128)(2,1)S(1)} collective-permute-done((bf16[768,768]{1,0:T(8,128)(2,1)S(1)}, bf16[768,768]{1,0:T(8,128)(2,1)S(1)}, u32[]{:S(2)}, u32[]{:S(2)}) %collective-permute-start.13) | collective-permute-done | bytes 1179680 | tf_op jit(solution)/shard_map/ppermute | solution.py:725
  118.3 7.9 %collective-permute-done.16.refs_6_ = bf16[256,768]{1,0:T(8,128)(2,1)S(1)} collective-permute-done((bf16[256,768]{1,0:T(8,128)(2,1)S(1)}, bf16[256,768]{1,0:T(8,128)(2,1)S(1)}, u32[]{:S(2)}, u32[]{:S(2)}) %collective-permute-start.16) | collective-permute-done | bytes 393248 | tf_op jit(solution)/shard_map/ppermute | solution.py:725
  140.0 13.7 %collective-permute-done.18.refs_2_.refs_9_ = bf16[512,768]{1,0:T(8,128)(2,1)S(1)} collective-permute-done((bf16[512,768]{1,0:T(8,128)(2,1)S(1)}, bf16[512,768]{1,0:T(8,128)(2,1)S(1)}, u32[]{:S(2)}, u32[]{:S(2)}) %collective-permute-start.18) | collective-permute-done | bytes 786464 | tf_op jit(solution)/shard_map/ppermute | solution.py:731
  162.3 7.8 %collective-permute-done.21.refs_4_ = bf16[256,768]{1,0:T(8,128)(2,1)S(1)} collective-permute-done((bf16[256,768]{1,0:T(8,128)(2,1)S(1)}, bf16[256,768]{1,0:T(8,128)(2,1)S(1)}, u32[]{:S(2)}, u32[]{:S(2)}) %collective-permute-start.21) | collective-permute-done | bytes 393248 | tf_op jit(solution)/shard_map/ppermute | solution.py:725
  170.1 6.6 %shard_map.280 = (f32[256,768]{1,0:T(8,128)}, bf16[256,768]{1,0:T(8,128)(2,1)}, bf16[256,1536]{1,0:T(8,128)(2,1)}, bf16[256,1536]{1,0:T(8,128)(2,1)}, bf16[256,768]{1,0:T(8,128)(2,1)S(1)}) custom-call(s32[4]{0:T(128)S(1)} %pad_add_fusion.refs_0_, f32[16,768]{1,0:T(8,128)S(1)} %get-tuple-element.310.refs_1_, bf16[256,768]{1,0:T(8,128)(2,1)} %get-tuple-element.340.refs_2_, ...), custom_call_target="tpu_custom_call" | custom-call | flops 480000000 | bytes 800000 | tf_op jit(solution)/shard_map/pallas_call | solution.py:94
  184.0 6.6 %shard_map.283 = (f32[256,768]{1,0:T(8,128)}, bf16[256,768]{1,0:T(8,128)(2,1)}, bf16[256,1536]{1,0:T(8,128)(2,1)}, bf16[256,1536]{1,0:T(8,128)(2,1)}, bf16[256,768]{1,0:T(8,128)(2,1)S(1)}) custom-call(s32[4]{0:T(128)S(1)} %pad_add_fusion.refs_0_, f32[16,768]{1,0:T(8,128)S(1)} %get-tuple-element.310.refs_1_, bf16[256,768]{1,0:T(8,128)(2,1)} %get-tuple-element.341.refs_2_, ...), custom_call_target="tpu_custom_call" | custom-call | flops 480000000 | bytes 800000 | tf_op jit(solution)/shard_map/pallas_call | solution.py:94
  196.9 7.4 %shard_map.285 = (bf16[2,768,768]{2,1,0:T(8,128)(2,1)}, bf16[2,768,768]{2,1,0:T(8,128)(2,1)}) custom-call(s32[4]{0:T(128)S(1)} %pad_add_fusion.refs_0_, bf16[256,1536]{1,0:T(8,128)(2,1)} %get-tuple-element.359.refs_1_, bf16[256,1536]{1,0:T(8,128)(2,1)} %get-tuple-element.360.refs_2_, bf16[256,768]{1,0:T(8,128)(2,1)S(1)} %get-tuple-element.652.refs_1_.refs_3_.refs_5_, ...), custom_call_target="tpu_custom_call" | custom-call | flops 444000000 | bytes 740000 | tf_op jit(solution)/shard_map/pallas_call | solution.py:94
  228.5 7.7 %collective-permute-done.28 = bf16[384,768]{1,0:T(8,128)(2,1)S(1)} collective-permute-done((bf16[384,768]{1,0:T(8,128)(2,1)S(1)}, bf16[384,768]{1,0:T(8,128)(2,1)S(1)}, u32[]{:S(2)}, u32[]{:S(2)}) %collective-permute-start.28) | collective-permute-done | bytes 589856 | tf_op jit(solution)/shard_map/ppermute | solution.py:725
  243.1 7.8 %collective-permute-done.29 = bf16[384,768]{1,0:T(8,128)(2,1)} collective-permute-done((bf16[384,768]{1,0:T(8,128)(2,1)}, bf16[384,768]{1,0:T(8,128)(2,1)}, u32[]{:S(2)}, u32[]{:S(2)}) %collective-permute-start.29) | collective-permute-done | bytes 589856 | tf_op jit(solution)/shard_map/ppermute | solution.py:725
  253.0 8.7 %collective-permute-start.33 = (bf16[384,768]{1,0:T(8,128)(2,1)S(1)}, bf16[384,768]{1,0:T(8,128)(2,1)S(1)}, u32[]{:S(2)}, u32[]{:S(2)}) collective-permute-start(bf16[384,768]{1,0:T(8,128)(2,1)S(1)} %get-tuple-element.630), channel_id=1, source_target_pairs={{0,2},{1,3},{2,0},{3,1},{4,6},{5,7},{6,4},{7,5},{8,10},{9,11},{10,... | collective-permute-start | bytes 1769480 | tf_op jit(solution)/shard_map/ppermute | solution.py:725
  276.8 6.9 %collective-permute-done.32.refs_4_ = bf16[256,768]{1,0:T(8,128)(2,1)S(1)} collective-permute-done((bf16[256,768]{1,0:T(8,128)(2,1)S(1)}, bf16[256,768]{1,0:T(8,128)(2,1)S(1)}, u32[]{:S(2)}, u32[]{:S(2)}) %collective-permute-start.32) | collective-permute-done | bytes 393248 | tf_op jit(solution)/shard_map/ppermute | solution.py:725
  284.0 7.0 %collective-permute-start.37 = (bf16[384,768]{1,0:T(8,128)(2,1)S(1)}, bf16[384,768]{1,0:T(8,128)(2,1)S(1)}, u32[]{:S(2)}, u32[]{:S(2)}) collective-permute-start(bf16[384,768]{1,0:T(8,128)(2,1)S(1)} %add_convert_fusion.9), channel_id=1, source_target_pairs={{0,4},{1,5},{2,6},{3,7},{4,0},{5,1},{6,2},{7,3},{8,12},{9,13},{10,... | collective-permute-start | bytes 1769480 | tf_op jit(solution)/shard_map/ppermute | solution.py:725
  303.4 14.0 %collective-permute-done.37 = bf16[384,768]{1,0:T(8,128)(2,1)S(1)} collective-permute-done((bf16[384,768]{1,0:T(8,128)(2,1)S(1)}, bf16[384,768]{1,0:T(8,128)(2,1)S(1)}, u32[]{:S(2)}, u32[]{:S(2)}) %collective-permute-start.37) | collective-permute-done | bytes 589856 | tf_op jit(solution)/shard_map/ppermute | solution.py:725
  325.7 7.4 %shard_map.298 = (bf16[2,768,768]{2,1,0:T(8,128)(2,1)}, bf16[2,768,768]{2,1,0:T(8,128)(2,1)}) custom-call(s32[4]{0:T(128)S(1)} %pad_add_fusion.refs_0_, bf16[256,1536]{1,0:T(8,128)(2,1)} %get-tuple-element.449.refs_1_, bf16[256,1536]{1,0:T(8,128)(2,1)} %get-tuple-element.450.refs_2_, bf16[256,768]{1,0:T(8,128)(2,1)S(1)} %get-tuple-element.433.refs_1_.refs_3_.refs_5_, ...), custom_call_target="tpu_custom_call" | custom-call | flops 444000000 | bytes 740000 | tf_op jit(solution)/shard_map/pallas_call | solution.py:94
  348.8 7.4 %collective-permute-done.41 = bf16[192,768]{1,0:T(8,128)(2,1)S(1)} collective-permute-done((bf16[192,768]{1,0:T(8,128)(2,1)S(1)}, bf16[192,768]{1,0:T(8,128)(2,1)S(1)}, u32[]{:S(2)}, u32[]{:S(2)}) %collective-permute-start.41) | collective-permute-done | bytes 294944 | tf_op jit(solution)/shard_map/ppermute | solution.py:725
  365.3 9.5 %collective-permute-done.44 = bf16[384,768]{1,0:T(8,128)(2,1)S(1)} collective-permute-done((bf16[384,768]{1,0:T(8,128)(2,1)S(1)}, bf16[384,768]{1,0:T(8,128)(2,1)S(1)}, u32[]{:S(2)}, u32[]{:S(2)}) %collective-permute-start.44) | collective-permute-done | bytes 589856 | tf_op jit(solution)/shard_map/ppermute | solution.py:725
  381.2 8.5 %collective-permute-done.45 = bf16[384,768]{1,0:T(8,128)(2,1)S(1)} collective-permute-done((bf16[384,768]{1,0:T(8,128)(2,1)S(1)}, bf16[384,768]{1,0:T(8,128)(2,1)S(1)}, u32[]{:S(2)}, u32[]{:S(2)}) %collective-permute-start.45) | collective-permute-done | bytes 589856 | tf_op jit(solution)/shard_map/ppermute | solution.py:725
  418.1 11.0 %collective-permute-start.50 = (bf16[384,768]{1,0:T(8,128)(2,1)}, bf16[384,768]{1,0:T(8,128)(2,1)}, u32[]{:S(2)}, u32[]{:S(2)}) collective-permute-start(bf16[384,768]{1,0:T(8,128)(2,1)} %add_convert_fusion.4), channel_id=1, source_target_pairs={{0,4},{1,5},{2,6},{3,7},{4,0},{5,1},{6,2},{7,3},{8,12},{9,13},{10,... | collective-permute-start | bytes 1769480 | tf_op jit(solution)/shard_map/ppermute | solution.py:725
  445.3 9.9 %collective-permute-done.50 = bf16[384,768]{1,0:T(8,128)(2,1)} collective-permute-done((bf16[384,768]{1,0:T(8,128)(2,1)}, bf16[384,768]{1,0:T(8,128)(2,1)}, u32[]{:S(2)}, u32[]{:S(2)}) %collective-permute-start.50) | collective-permute-done | bytes 589856 | tf_op jit(solution)/shard_map/ppermute | solution.py:725
  462.2 16.5 %collective-permute-done.56 = bf16[576,768]{1,0:T(8,128)(2,1)S(1)} collective-permute-done((bf16[576,768]{1,0:T(8,128)(2,1)S(1)}, bf16[576,768]{1,0:T(8,128)(2,1)S(1)}, u32[]{:S(2)}, u32[]{:S(2)}) %collective-permute-start.56) | collective-permute-done | bytes 884768 | tf_op jit(solution)/shard_map/ppermute | solution.py:725
  489.1 8.3 %collective-permute-done.60 = bf16[192,768]{1,0:T(8,128)(2,1)S(1)} collective-permute-done((bf16[192,768]{1,0:T(8,128)(2,1)S(1)}, bf16[192,768]{1,0:T(8,128)(2,1)S(1)}, u32[]{:S(2)}, u32[]{:S(2)}) %collective-permute-start.60) | collective-permute-done | bytes 294944 | tf_op jit(solution)/shard_map/ppermute | solution.py:725
  516.5 7.2 %shard_map.309 = (f32[1536,768]{1,0:T(8,128)}, f32[768,1536]{1,0:T(8,128)}, f32[8,128]{1,0:T(8,128)S(1)}) custom-call(s32[4]{0:T(128)S(1)} %pad_add_fusion.refs_0_, bf16[768,768]{1,0:T(8,128)(2,1)} %copy-done.36, bf16[384,768]{1,0:T(8,128)(2,1)} %copy-done.65, bf16[384,768]{1,0:T(8,128)(2,1)} %copy-done.66, bf16[768,768]{1,0:T(8,128)(2,1)} %copy-done.54, ...), custom_call_target="tpu_custom_call" | custom-call | flops 600000000 | bytes 1000000 | tf_op jit(solution)/shard_map/pallas_call | solution.py:94
  (437 shorter events, 316.5 us)
Async XLA Ops:
  7.7 29.6 %collective-permute-start = (bf16[384,1152]{1,0:T(8,128)(2,1)}, bf16[384,1152]{1,0:T(8,128)(2,1)S(1)}, u32[]{:S(2)}, u32[]{:S(2)}) collective-permute-start(bf16[384,1152]{1,0:T(8,128)(2,1)} %concatenate.41), channel_id=1, source_target_pairs={{0,16},{16,0},{1,17},{17,1},{2,18},{18,2},{3,19},{19,3},{4,20},{20... | collective-permute-start | bytes 2654216 | tf_op jit(solution)/shard_map/ppermute | solution.py:725
  9.9 21.5 %collective-permute-start.2 = (f32[16,768]{1,0:T(8,128)S(1)}, f32[16,768]{1,0:T(8,128)S(1)}, u32[]{:S(2)}, u32[]{:S(2)}) collective-permute-start(f32[16,768]{1,0:T(8,128)S(1)} %concatenate.44), channel_id=1, source_target_pairs={{0,16},{16,0},{1,17},{17,1},{2,18},{18,2},{3,19},{19,3},{4,20},{20... | collective-permute-start | bytes 147464 | tf_op jit(solution)/shard_map/ppermute | solution.py:725
  10.8 20.6 %collective-permute-start.3 = (bf16[256,768]{1,0:T(8,128)(2,1)}, bf16[256,768]{1,0:T(8,128)(2,1)}, u32[]{:S(2)}, u32[]{:S(2)}) collective-permute-start(bf16[256,768]{1,0:T(8,128)(2,1)} %dynamic-slice_bitcast_fusion.4), channel_id=1, source_target_pairs={{0,8},{8,0},{1,9},{9,1},{2,10},{10,2},{3,11},{11,3},{4,12},{12,4},... | collective-permute-start | bytes 1179656 | tf_op jit(solution)/shard_map/ppermute | solution.py:725
  14.5 22.8 %collective-permute-start.1 = (bf16[192,768]{1,0:T(8,128)(2,1)}, bf16[192,768]{1,0:T(8,128)(2,1)S(1)}, u32[]{:S(2)}, u32[]{:S(2)}) collective-permute-start(bf16[192,768]{1,0:T(8,128)(2,1)} %dynamic-slice_bitcast_fusion.5), channel_id=1, source_target_pairs={{0,16},{16,0},{1,17},{17,1},{2,18},{18,2},{3,19},{19,3},{4,20},{20... | collective-permute-start | bytes 884744 | tf_op jit(solution)/shard_map/ppermute | solution.py:725
  39.1 28.1 %collective-permute-start.7 = (bf16[384,1536]{1,0:T(8,128)(2,1)S(1)}, bf16[384,1536]{1,0:T(8,128)(2,1)S(1)}, u32[]{:S(2)}, u32[]{:S(2)}) collective-permute-start(bf16[384,1536]{1,0:T(8,128)(2,1)S(1)} %dynamic-slice_bitcast_fusion.1), channel_id=1, source_target_pairs={{0,16},{16,0},{1,17},{17,1},{2,18},{18,2},{3,19},{19,3},{4,20},{20... | collective-permute-start | bytes 3538952 | tf_op jit(solution)/shard_map/ppermute | solution.py:725
  45.7 21.0 %collective-permute-start.5 = (bf16[512,768]{1,0:T(8,128)(2,1)S(1)}, bf16[512,768]{1,0:T(8,128)(2,1)S(1)}, u32[]{:S(2)}, u32[]{:S(2)}) collective-permute-start(bf16[512,768]{1,0:T(8,128)(2,1)S(1)} %get-tuple-element.317.refs_3_.refs_9_), channel_id=1, source_target_pairs={{0,2},{1,3},{2,4},{3,5},{4,6},{5,7},{8,10},{9,11},{10,12},{11,13},... | collective-permute-start | bytes 2359304 | tf_op jit(solution)/shard_map/ppermute | solution.py:731
  67.4 28.4 %collective-permute-start.13 = (bf16[768,768]{1,0:T(8,128)(2,1)S(1)}, bf16[768,768]{1,0:T(8,128)(2,1)S(1)}, u32[]{:S(2)}, u32[]{:S(2)}) collective-permute-start(bf16[768,768]{1,0:T(8,128)(2,1)S(1)} %dynamic-slice_bitcast_fusion), channel_id=1, source_target_pairs={{0,16},{16,0},{1,17},{17,1},{2,18},{18,2},{3,19},{19,3},{4,20},{20... | collective-permute-start | bytes 3538952 | tf_op jit(solution)/shard_map/ppermute | solution.py:725
  73.1 22.7 %collective-permute-start.12 = (bf16[256,768]{1,0:T(8,128)(2,1)S(1)}, bf16[256,768]{1,0:T(8,128)(2,1)S(1)}, u32[]{:S(2)}, u32[]{:S(2)}) collective-permute-start(bf16[256,768]{1,0:T(8,128)(2,1)S(1)} %get-tuple-element.330.refs_3_), channel_id=1, source_target_pairs={{0,8},{8,0},{1,9},{9,1},{2,10},{10,2},{3,11},{11,3},{4,12},{12,4},... | collective-permute-start | bytes 1179656 | tf_op jit(solution)/shard_map/ppermute | solution.py:725
  132.6 21.1 %collective-permute-start.18 = (bf16[512,768]{1,0:T(8,128)(2,1)S(1)}, bf16[512,768]{1,0:T(8,128)(2,1)S(1)}, u32[]{:S(2)}, u32[]{:S(2)}) collective-permute-start(bf16[512,768]{1,0:T(8,128)(2,1)S(1)} %get-tuple-element.343.refs_3_.refs_9_), channel_id=1, source_target_pairs={{0,2},{1,3},{2,4},{3,5},{4,6},{5,7},{8,10},{9,11},{10,12},{11,13},... | collective-permute-start | bytes 2359304 | tf_op jit(solution)/shard_map/ppermute | solution.py:731
  161.7 22.3 %collective-permute-start.23 = (bf16[256,768]{1,0:T(8,128)(2,1)S(1)}, bf16[256,768]{1,0:T(8,128)(2,1)S(1)}, u32[]{:S(2)}, u32[]{:S(2)}) collective-permute-start(bf16[256,768]{1,0:T(8,128)(2,1)S(1)} %get-tuple-element.356.refs_3_), channel_id=1, source_target_pairs={{0,8},{8,0},{1,9},{9,1},{2,10},{10,2},{3,11},{11,3},{4,12},{12,4},... | collective-permute-start | bytes 1179656 | tf_op jit(solution)/shard_map/ppermute | solution.py:725
  182.4 21.9 %collective-permute-start.22 = (bf16[256,768]{1,0:T(8,128)(2,1)S(1)}, bf16[256,768]{1,0:T(8,128)(2,1)S(1)}, u32[]{:S(2)}, u32[]{:S(2)}) collective-permute-start(bf16[256,768]{1,0:T(8,128)(2,1)S(1)} %get-tuple-element.366.refs_3_), channel_id=1, source_target_pairs={{0,8},{8,0},{1,9},{9,1},{2,10},{10,2},{3,11},{11,3},{4,12},{12,4},... | collective-permute-start | bytes 1179656 | tf_op jit(solution)/shard_map/ppermute | solution.py:725
  223.8 27.1 %collective-permute-start.27 = (bf16[512,768]{1,0:T(8,128)(2,1)}, bf16[512,768]{1,0:T(8,128)(2,1)S(1)}, u32[]{:S(2)}, u32[]{:S(2)}) collective-permute-start(bf16[512,768]{1,0:T(8,128)(2,1)} %add_convert_fusion.1), channel_id=1, source_target_pairs={{2,0},{3,1},{4,2},{5,3},{6,4},{7,5},{10,8},{11,9},{12,10},{13,11},... | collective-permute-start | bytes 2359304 | tf_op jit(solution)/shard_map/ppermute | solution.py:731
  237.0 24.8 %collective-permute-start.30 = (bf16[512,768]{1,0:T(8,128)(2,1)}, bf16[512,768]{1,0:T(8,128)(2,1)S(1)}, u32[]{:S(2)}, u32[]{:S(2)}) collective-permute-start(bf16[512,768]{1,0:T(8,128)(2,1)} %get-tuple-element.399), channel_id=1, source_target_pairs={{0,1},{1,0},{2,3},{3,2},{4,5},{5,4},{6,7},{7,6},{8,9},{9,8},{10,11... | collective-permute-start | bytes 2359304 | tf_op jit(solution)/shard_map/ppermute | solution.py:725
  253.0 30.7 %collective-permute-start.33 = (bf16[384,768]{1,0:T(8,128)(2,1)S(1)}, bf16[384,768]{1,0:T(8,128)(2,1)S(1)}, u32[]{:S(2)}, u32[]{:S(2)}) collective-permute-start(bf16[384,768]{1,0:T(8,128)(2,1)S(1)} %get-tuple-element.630), channel_id=1, source_target_pairs={{0,2},{1,3},{2,0},{3,1},{4,6},{5,7},{6,4},{7,5},{8,10},{9,11},{10,... | collective-permute-start | bytes 1769480 | tf_op jit(solution)/shard_map/ppermute | solution.py:725
  284.0 33.4 %collective-permute-start.37 = (bf16[384,768]{1,0:T(8,128)(2,1)S(1)}, bf16[384,768]{1,0:T(8,128)(2,1)S(1)}, u32[]{:S(2)}, u32[]{:S(2)}) collective-permute-start(bf16[384,768]{1,0:T(8,128)(2,1)S(1)} %add_convert_fusion.9), channel_id=1, source_target_pairs={{0,4},{1,5},{2,6},{3,7},{4,0},{5,1},{6,2},{7,3},{8,12},{9,13},{10,... | collective-permute-start | bytes 1769480 | tf_op jit(solution)/shard_map/ppermute | solution.py:725
  291.2 26.2 %collective-permute-start.36 = (bf16[384,768]{1,0:T(8,128)(2,1)S(1)}, bf16[384,768]{1,0:T(8,128)(2,1)S(1)}, u32[]{:S(2)}, u32[]{:S(2)}) collective-permute-start(bf16[384,768]{1,0:T(8,128)(2,1)S(1)} %fusion.8), channel_id=1, source_target_pairs={{0,16},{16,0},{1,17},{17,1},{2,18},{18,2},{3,19},{19,3},{4,20},{20... | collective-permute-start | bytes 1769480 | tf_op jit(solution)/shard_map/ppermute | solution.py:725
  317.9 21.7 %collective-permute-start.39 = (bf16[576,768]{1,0:T(8,128)(2,1)S(1)}, bf16[576,768]{1,0:T(8,128)(2,1)S(1)}, u32[]{:S(2)}, u32[]{:S(2)}) collective-permute-start(bf16[576,768]{1,0:T(8,128)(2,1)S(1)} %pad_maximum_fusion.2), channel_id=1, source_target_pairs={{0,2},{1,3},{2,0},{3,1},{4,6},{5,7},{6,4},{7,5},{8,10},{9,11},{10,... | collective-permute-start | bytes 2654216 | tf_op jit(solution)/shard_map/ppermute | solution.py:725
  318.0 21.7 %collective-permute-start.35 = (bf16[256,768]{1,0:T(8,128)(2,1)S(1)}, bf16[256,768]{1,0:T(8,128)(2,1)S(1)}, u32[]{:S(2)}, u32[]{:S(2)}) collective-permute-start(bf16[256,768]{1,0:T(8,128)(2,1)S(1)} %get-tuple-element.463.refs_3_), channel_id=1, source_target_pairs={{0,8},{8,0},{1,9},{9,1},{2,10},{10,2},{3,11},{11,3},{4,12},{12,4},... | collective-permute-start | bytes 1179656 | tf_op jit(solution)/shard_map/ppermute | solution.py:725
  361.5 28.1 %collective-permute-start.43 = (bf16[512,768]{1,0:T(8,128)(2,1)S(1)}, bf16[512,768]{1,0:T(8,128)(2,1)S(1)}, u32[]{:S(2)}, u32[]{:S(2)}) collective-permute-start(bf16[512,768]{1,0:T(8,128)(2,1)S(1)} %add_convert_fusion), channel_id=1, source_target_pairs={{2,0},{3,1},{4,2},{5,3},{6,4},{7,5},{10,8},{11,9},{12,10},{13,11},... | collective-permute-start | bytes 2359304 | tf_op jit(solution)/shard_map/ppermute | solution.py:731
  418.1 37.1 %collective-permute-start.50 = (bf16[384,768]{1,0:T(8,128)(2,1)}, bf16[384,768]{1,0:T(8,128)(2,1)}, u32[]{:S(2)}, u32[]{:S(2)}) collective-permute-start(bf16[384,768]{1,0:T(8,128)(2,1)} %add_convert_fusion.4), channel_id=1, source_target_pairs={{0,4},{1,5},{2,6},{3,7},{4,0},{5,1},{6,2},{7,3},{8,12},{9,13},{10,... | collective-permute-start | bytes 1769480 | tf_op jit(solution)/shard_map/ppermute | solution.py:725
  429.1 26.1 %collective-permute-start.54 = (bf16[256,768]{1,0:T(8,128)(2,1)S(1)}, bf16[256,768]{1,0:T(8,128)(2,1)}, u32[]{:S(2)}, u32[]{:S(2)}) collective-permute-start(bf16[256,768]{1,0:T(8,128)(2,1)S(1)} %get-tuple-element.558), channel_id=1, source_target_pairs={{0,8},{8,0},{1,9},{9,1},{2,10},{10,2},{3,11},{11,3},{4,12},{12,4},... | collective-permute-start | bytes 1179656 | tf_op jit(solution)/shard_map/ppermute | solution.py:725
  430.1 25.1 %collective-permute-start.55 = (bf16[256,768]{1,0:T(8,128)(2,1)S(1)}, bf16[256,768]{1,0:T(8,128)(2,1)}, u32[]{:S(2)}, u32[]{:S(2)}) collective-permute-start(bf16[256,768]{1,0:T(8,128)(2,1)S(1)} %copy-done.17), channel_id=1, source_target_pairs={{0,8},{8,0},{1,9},{9,1},{2,10},{10,2},{3,11},{11,3},{4,12},{12,4},... | collective-permute-start | bytes 1179656 | tf_op jit(solution)/shard_map/ppermute | solution.py:725
  457.3 21.4 %collective-permute-start.56 = (bf16[576,768]{1,0:T(8,128)(2,1)S(1)}, bf16[576,768]{1,0:T(8,128)(2,1)S(1)}, u32[]{:S(2)}, u32[]{:S(2)}) collective-permute-start(bf16[576,768]{1,0:T(8,128)(2,1)S(1)} %pad_maximum_fusion.4), channel_id=1, source_target_pairs={{0,2},{1,3},{2,0},{3,1},{4,6},{5,7},{6,4},{7,5},{8,10},{9,11},{10,... | collective-permute-start | bytes 2654216 | tf_op jit(solution)/shard_map/ppermute | solution.py:725
  457.6 21.1 %collective-permute-start.58 = (bf16[256,768]{1,0:T(8,128)(2,1)S(1)}, bf16[256,768]{1,0:T(8,128)(2,1)S(1)}, u32[]{:S(2)}, u32[]{:S(2)}) collective-permute-start(bf16[256,768]{1,0:T(8,128)(2,1)S(1)} %select_convert_fusion), channel_id=1, source_target_pairs={{0,16},{16,0},{1,17},{17,1},{2,18},{18,2},{3,19},{19,3},{4,20},{20... | collective-permute-start | bytes 1179656 | tf_op jit(solution)/shard_map/ppermute | solution.py:725
  (137 other events, 1140.6 us)

commit v5 on v4

--- a/solution.py
+++ b/solution.py
@@ -117,6 +117,24 @@
         pltpu.make_async_copy(other, held.at[pl.ds(rest, half)], sem).start()
 
 
+def fetch_parts(scalars, layer, own, got, other, held, sem):
+    half = held.shape[0] // 2
+
+    @pl.when(scalars[2] == layer)
+    def _():
+        pltpu.make_async_copy(own, held, sem).start()
+
+    @pl.when(scalars[2] != layer)
+    def _():
+        for side, refs in ((scalars[3], got), (1 - scalars[3], other)):
+            at = pl.ds(pl.multiple_of(side * half, half), half)
+            start = 0
+            for ref in refs:
+                end = start + ref.shape[1]
+                pltpu.make_async_copy(ref, held.at[at, start:end], sem).start()
+                start = end
+
+
 def fetch_wait(own, held, sem):
     pltpu.make_async_copy(own, held, sem).wait()
 
@@ -161,10 +179,10 @@
 
     def body(scal, tab, *refs):
         given = refs[: len(blocks) - 1]
-        own, got, other = refs[len(blocks) - 1 : len(blocks) + 2]
-        outs = refs[len(blocks) + 2 : -2]
+        own, *parts = refs[len(blocks) - 1 : len(blocks) + 4]
+        outs = refs[len(blocks) + 4 : -2]
         held, sem = refs[-2:]
-        fetch_start(scal, layer, own, got, other, held, sem)
+        fetch_parts(scal, layer, own, parts[:2], parts[2:], held, sem)
         for c in range(CHUNKS):
             at = slice(c * rows, (c + 1) * rows)
             if ahead is None:
@@ -491,40 +509,55 @@
     return call(body, outs, scalars, [dy, Late(slope)], [*up, *down], held_like(up, down), us=1.0)
 
 
-def middle_back(scalars, layer, table, hidden, mine, came, dy, attended, weights):
-    rows, features = hidden.shape
-    width = attended.shape[1]
-
-    def body(scal, tab, hid, mine_ref, came_ref, dy_ref, att, own, got, other, dh_ref, low_ref, da_ref, delta, sums, stats, held, sem):
+def middle_back(scalars, layer, table, hidden, parts, dy, attended, weights):
+    rows, features = hidden[0].shape
+    width = attended[0].shape[1]
+
+    def body(scal, tab, *refs):
+        given, (own, got, other) = refs[: 5 * CHUNKS], refs[5 * CHUNKS : 5 * CHUNKS + 3]
+        outs = refs[5 * CHUNKS + 3 : 9 * CHUNKS + 4]
+        stats, held, sem = refs[9 * CHUNKS + 4 :]
         fetch_start(scal, layer, own, got, other, held, sem)
-        grad = mine_ref[...].astype(F32) + came_ref[...].astype(F32)
-        back, d_gain, d_bias = norm_grad(hid[...], tab[GAIN1 : GAIN1 + 1], grad)
-        up = dy_ref[...].astype(F32)
-        dh = up + back
-        dh_ref[...] = dh
-        low = dh.astype(BF)
-        low_ref[...] = low
-        flush(dh_ref, low_ref)
+        sums = outs[-1]
         sums[...] = jnp.zeros_like(sums)
-        sums[0:1, :] = d_gain
-        sums[1:2, :] = d_bias
-        sums[2:3, :] = jnp.sum(dh, axis=0, keepdims=True)
-        sums[3:4, :] = jnp.sum(up, axis=0, keepdims=True)
         stats[...] = jnp.zeros_like(stats)
+        lows = []
+        for c in range(CHUNKS):
+            hid, mine, came, dy_ref, att = given[5 * c : 5 * c + 5]
+            dh_ref, low_ref, da_ref, delta = outs[4 * c : 4 * c + 4]
+            grad = mine[...].astype(F32) + came[...].astype(F32)
+            back, d_gain, d_bias = norm_grad(hid[...], tab[GAIN1 : GAIN1 + 1], grad)
+            up = dy_ref[...].astype(F32)
+            dh = up + back
+            dh_ref[...] = dh
+            low = dh.astype(BF)
+            low_ref[...] = low
+            flush(dh_ref, low_ref)
+            added = (d_gain, d_bias, jnp.sum(dh, axis=0, keepdims=True), jnp.sum(up, axis=0, keepdims=True))
+            for k, value in enumerate(added):
+                sums[k : k + 1, :] += value
+            lows.append(low)
         fetch_wait(own, held, sem)
-        da = dot_nt(low, held[...]).astype(BF)
-        da_ref[...] = da
-        for p in range(width // 128):
-            span = slice(p * 128, (p + 1) * 128)
-            product = da[:, span].astype(F32) * att[:, span].astype(F32)
-            first = low_lanes(product.shape)
-            stats[:, 2 * p : 2 * p + 1] = jnp.sum(jnp.where(first, product, 0.0), axis=1, keepdims=True)
-            stats[:, 2 * p + 1 : 2 * p + 2] = jnp.sum(jnp.where(first, 0.0, product), axis=1, keepdims=True)
-        delta[...] = jnp.transpose(stats[...])[0:8, :]
-
-    outs = [((rows, features), F32, LATER), ((rows, features), BF, LATER), ((rows, width), BF), ((8, rows), F32), ((8, features), F32)]
+        for c in range(CHUNKS):
+            att = given[5 * c + 4]
+            da_ref, delta = outs[4 * c + 2 : 4 * c + 4]
+            da = dot_nt(lows[c], held[...]).astype(BF)
+            da_ref[...] = da
+            for p in range(width // 128):
+                span = slice(p * 128, (p + 1) * 128)
+                product = da[:, span].astype(F32) * att[:, span].astype(F32)
+                first = low_lanes(product.shape)
+                stats[:, 2 * p : 2 * p + 1] = jnp.sum(jnp.where(first, product, 0.0), axis=1, keepdims=True)
+                stats[:, 2 * p + 1 : 2 * p + 2] = jnp.sum(jnp.where(first, 0.0, product), axis=1, keepdims=True)
+            delta[...] = jnp.transpose(stats[...])[0:8, :]
+
+    one = [((rows, features), F32, LATER), ((rows, features), BF, LATER), ((rows, width), BF), ((8, rows), F32)]
     scratch = [pltpu.VMEM((rows, 128), F32)] + held_like(weights)
-    return call(body, outs, scalars, [table, Late(hidden), mine, came, dy, Late(attended)], weights, scratch, us=2.8)
+    blocks = [table]
+    for c in range(CHUNKS):
+        blocks += [Late(hidden[c]), *parts[c], dy[c], Late(attended[c])]
+    r = call(body, one * CHUNKS + [((8, features), F32)], scalars, blocks, weights, scratch, us=2.8)
+    return [list(r[k : 4 * CHUNKS : 4]) for k in range(4)] + [r[-1]]
 
 
 def project_back(scalars, layer, c, dq, dkv, near, far, returned, weights):
@@ -533,10 +566,10 @@
 
     def body(scal, dq_ref, dkv_ref, near_ref, far_ref, *rest):
         back_ref = rest[0] if returned is not None else None
-        own, got, other = rest[-9:-6] if returned is None else rest[-8:-5]
         outs = rest[-6:-2] if returned is None else rest[-5:-2]
+        own, *parts = rest[-11:-6] if returned is None else rest[-10:-5]
         held, sem = rest[-2:]
-        fetch_start(scal, layer, own, got, other, held, sem)
+        fetch_parts(scal, layer, own, parts[:2], parts[2:], held, sem)
         at = slice(c * rows, (c + 1) * rows)
         total = dkv_ref[...] + near_ref[at, :].astype(F32) + far_ref[at, :].astype(F32)
         if returned is None:
@@ -563,21 +596,31 @@
     return call(body, outs, scalars, blocks, weights, held_like(weights), us=2.7)
 
 
-def last_back(scalars, table, x, mine, came, dh):
-    rows, features = x.shape
-
-    def body(scal, tab, x_ref, mine_ref, came_ref, dh_ref, dx_ref, low_ref, sums):
-        grad = mine_ref[...].astype(F32) + came_ref[...].astype(F32)
-        back, d_gain, d_bias = norm_grad(x_ref[...].astype(F32), tab[GAIN0 : GAIN0 + 1], grad)
-        dx = dh_ref[...] + back
-        dx_ref[...] = dx
-        low_ref[...] = dx.astype(BF)
+def last_back(scalars, table, x, parts, dh):
+    rows, features = x[0].shape
+
+    def body(scal, tab, *refs):
+        given, outs = refs[: 4 * CHUNKS], refs[4 * CHUNKS :]
+        sums = outs[-1]
         sums[...] = jnp.zeros_like(sums)
-        sums[0:1, :] = d_gain
-        sums[1:2, :] = d_bias
-
-    outs = [((rows, features), F32, LATER), ((rows, features), BF), ((8, features), F32)]
-    return call(body, outs, scalars, [table, Late(x), mine, came, Late(dh)], us=0.5)
+        for c in range(CHUNKS):
+            x_ref, mine, came, dh_ref = given[4 * c : 4 * c + 4]
+            dx_ref, low_ref = outs[2 * c : 2 * c + 2]
+            grad = mine[...].astype(F32) + came[...].astype(F32)
+            back, d_gain, d_bias = norm_grad(x_ref[...].astype(F32), tab[GAIN0 : GAIN0 + 1], grad)
+            dx = dh_ref[...] + back
+            dx_ref[...] = dx
+            flush(dx_ref)
+            low_ref[...] = dx.astype(BF)
+            sums[0:1, :] += d_gain
+            sums[1:2, :] += d_bias
+
+    outs = [((rows, features), F32, LATER), ((rows, features), BF)] * CHUNKS + [((8, features), F32)]
+    blocks = [table]
+    for c in range(CHUNKS):
+        blocks += [Late(x[c]), *parts[c], Late(dh[c])]
+    r = call(body, outs, scalars, blocks, us=0.5)
+    return list(r[0 : 2 * CHUNKS : 2]), list(r[1 : 2 * CHUNKS : 2]), r[-1]
 
 
 def both_chunks(left, left_span, right, right_span):
@@ -687,7 +730,7 @@
     rows = features // 4
     half, c, own = rows // 2, width // 4, width // 2
 
-    def body(scal, _, p0, p1, p2, p3, e0, e1, query, key, value, extra, out, held, pair, sem, pair_sem):
+    def body(scal, _, p0, p1, p2, p3, e0, e1, pairs, value, extra, out, held, pair, sem, pair_sem):
         last = [pltpu.make_async_copy(e, pair.at[i if i == 0 else 1], pair_sem.at[i]) for i, e in enumerate((e0, e1))]
         for copy in last:
             copy.start()
@@ -697,8 +740,8 @@
         for x in range(2):
             for core in range(2):
                 k, at = 2 * core + x, (2 * x + core) * rows
-                query[at : at + rows, :] = held[k, :rows, :width].astype(F32)
-                key[at : at + rows, :] = held[k, :rows, width:].astype(F32)
+                pairs[at : at + rows, 0, :] = held[k, :rows, :width].astype(F32)
+                pairs[at : at + rows, 1, :] = held[k, :rows, width:].astype(F32)
                 value[at : at + half, :] = held[k, rows : rows + half, :own].astype(F32)
                 value[at + half : at + rows, :] = held[k, rows : rows + half, width : width + own].astype(F32)
         for k in range(4):
@@ -712,7 +755,7 @@
             extra[pl.ds(at, half), :] = left[:, :own]
             extra[pl.ds(pl.multiple_of(at + half, 8), half), :] = right[:, :own]
 
-    outs = [((features, width), F32)] * 2 + [((features, own), F32), ((2 * rows, own), F32), ((width, features), F32)]
+    outs = [((features, 2, width), F32)] + [((features, own), F32), ((2 * rows, own), F32), ((width, features), F32)]
     scratch = [
         pltpu.VMEM((4, size, features), BF), pltpu.VMEM((2, half, features), BF),
         pltpu.SemaphoreType.DMA((4,)), pltpu.SemaphoreType.DMA((2,)),
@@ -855,11 +898,9 @@
         parts.append((part, swap(part, "tensor")))
     wide = Reduction(wide_grads(scalars, kept["active"], dy, kept["mlp_in"], d_up), 2)
     parts = steps("fed", parts, wide)
-    dh, dh_low, d_att, delta, mid_sums = [], [], [], [], []
-    for c in range(CHUNKS):
-        r = middle_back(scalars, layer, table, kept["hidden"][c], *parts[c], dy[c], kept["att"][c], w["out"])
-        for held, value in zip((dh, dh_low, d_att, delta, mid_sums), r):
-            held.append(value)
+    dh, dh_low, d_att, delta, mid = middle_back(
+        scalars, layer, table, kept["hidden"], parts, dy, kept["att"], w["out"]
+    )
     d_att = steps("mid", d_att, wide)
     dq, mine, others = attend_far_back(scalars, kept["q"], d_att, kept["lse"], delta, kept["far"])
     total = (mine.astype(F32) + swap(others, "batch").astype(F32)).astype(BF)
@@ -882,13 +923,8 @@
     narrow = Reduction(narrow_grads(scalars, kept["normed"], dq, dkv_low, kept["att"], dh_low), 1)
     parts = steps("proj", parts, wide, narrow)
     parts = steps("last", parts, wide, narrow)
-    dx, dx_low, last_sums = [], [], []
-    for c in range(CHUNKS):
-        r = last_back(scalars, table, kept["x"][c], *parts[c], dh[c])
-        dx.append(r[0])
-        dx_low.append(r[1])
-        last_sums.append(r[2])
-    up, mid, last, inn = [a + b for a, b in (up_sums, mid_sums, last_sums, in_sums)]
+    dx, dx_low, last = last_back(scalars, table, kept["x"], parts, dh)
+    up, inn = [a + b for a, b in (up_sums, in_sums)]
     blank = jnp.zeros((TABLE - BUP - 2, up.shape[1]), F32)
     small = jnp.concatenate(
         [last[0:1], mid[0:1], last[1:2], mid[1:2], mid[2:4], inn[0:2], up[0:2], blank], axis=0
@@ -925,26 +961,23 @@
         [norm_gains[0], norm_biases[0], out_bias, down_bias, row(query_bias[0]), row(blank, value_bias[0]),
          up_bias[0].reshape(2, features), jnp.zeros((TABLE - BUP - 2, features), F32)], axis=0
     )
-    extra = jnp.where(section == 0, value_extra, jnp.zeros_like(value_extra))
-    pieces = [query_key[0].reshape(features, 2 * width), value_own[0], extra]
-
     def half_of(weight):
         return take(weight.reshape((2, weight.shape[0] // 2) + weight.shape[1:]), core)
 
-    qkv_half = jnp.concatenate([half_of(p) for p in pieces], axis=1)
-    qkv = jnp.concatenate(pieces, axis=1)
+    query_keys = query_key[0].reshape(features, 2 * width)
+    extra = jnp.where(section == 0, value_extra, jnp.zeros_like(value_extra))
+    halves = [half_of(query_keys), jnp.concatenate([half_of(value_own[0]), half_of(extra)], axis=1)]
+    qkv = jnp.concatenate([query_keys, value_own[0], extra], axis=1)
+    qkv_got = [swap(h, "section") for h in halves]
     other_table = swap(own_table, "section")
-    qkv_got = swap(qkv_half, "section")
     out_got = swap(half_of(out_weight[0]), "section")
+    up_got = swap(after(half_of(up_weight[0]), x[0]), "section")
+    down_got = swap(after(half_of(down_weight[0]), x[0]), "section")
     tables = paired(own_table, other_table, section)
-    qkv_got, out_got, qkv, scalars, *rest = tie(qkv_got, out_got, qkv, scalars, *tables, *x)
+    qkv_got[0], qkv_got[1], out_got, qkv, scalars, *rest = tie(*qkv_got, out_got, qkv, scalars, *tables, *x)
     tables, x = rest[:2], rest[2:]
-    qkv_other = swap(qkv_got, "batch")
-    w = dict(qkv=(qkv, qkv_got, qkv_other))
-    late = dict(
-        up=swap(after(half_of(up_weight[0]), qkv_got), "section"),
-        down=swap(after(half_of(down_weight[0]), qkv_got), "section"),
-    )
+    w = dict(qkv=(qkv, *qkv_got, *[swap(g, "batch") for g in qkv_got]))
+    late = dict(up=up_got, down=down_got)
 
     def on_projected(kv, q):
         mine, kv = tie(take(cotangent, section)[0], kv)
@@ -1105,10 +1138,10 @@
     rows = features // 4
     extra = narrow0.quarter[rows : rows + rows // 2]
     extras = (extra, swap(extra, "batch"))
-    d_q, d_k, d_v, d_extra, d_out = narrow_unpack(
+    token, *extras = tie(token, *extras)
+    d_qk, d_v, d_extra, d_out = narrow_unpack(
         scalars, gathered(narrow0.quarter, narrow1.quarter), extras, width, token
     )
-    d_qk = jnp.stack([d_q, d_k], axis=1)
     return (
         outputs.reshape(1, micros, 1, half_rows, features),
         input_grads.reshape(1, micros, 1, half_rows, features),

time: 554 us -> 544 us (0.982)
  Pallas kernels: 176 us -> 168 us
  waiting for transfers between devices: 226 us -> 233 us
    pallas_call x40 -> x36, Pallas kernels: 176 us -> 168 us  [call(): pl.pallas_call(body, out_shape=shapes, in_specs=[SCALARS] + [FAR_OFF if i...]
    ppermute x4, waiting for transfers between devices: 25.4 us -> 31.7 us  [shift(): lax.ppermute(value, 'batch', [(i, i + steps) for i in range(first, last)])]
    unnamed x175 -> x160, local copies, waits for them, and re-layouts: 23.5 us -> 18.3 us
    ppermute x69 -> x71, starting transfers between devices: 68.3 us -> 63.5 us  [swap(): return lax.ppermute(value, axis, [(i, i ^ bits) for i in range(count)])]
    ppermute x69 -> x71, waiting for transfers between devices: 201 us -> 201 us  [swap(): return lax.ppermute(value, axis, [(i, i ^ bits) for i in range(count)])]
  transfers between devices with their start and end apart: 73 -> 75, of which waited for: 38 -> 37; matrix products, arithmetic and copies ran while one was open for 6% -> 6% of each run, Pallas kernels for 28% -> 27%
where the time goes in v5:
time: 544 us; the launch traced here: 536 us
  waiting for transfers between devices  233 us (43%)
  Pallas kernels  168 us (31%)
  starting transfers between devices  74.1 us (14%)
  local copies, waits for them, and re-layouts  32.4 us (6%)
  other arithmetic  25.4 us (5%)
    ppermute x71, waiting for transfers between devices, swap(): return lax.ppermute(value, axis, [(i, i ^ bits) for i in range(count)])  201 us
    pallas_call x36, Pallas kernels, call(): pl.pallas_call(body, out_shape=shapes, in_specs=[SCALARS] + [FAR_OFF if i...  168 us
    ppermute x71, starting transfers between devices, swap(): return lax.ppermute(value, axis, [(i, i ^ bits) for i in range(count)])  63.5 us
    ppermute x4, waiting for transfers between devices, shift(): lax.ppermute(value, 'batch', [(i, i + steps) for i in range(first, last)])  31.7 us
    unnamed x160, local copies, waits for them, and re-layouts  18.3 us
  transfers between devices with their start and end apart: 75, of which 37 were waited for; matrix products, arithmetic and copies ran while one was open for 6% of the time, Pallas kernels for 27%

profile of v5, /device:TPU:0, one launch (start us, length us, event | category | flops | bytes accessed | tf_op | source)
XLA Modules:
  0.0 535.8 jit_solution(18374584515857377960)
XLA Ops:
  27.3 8.9 %collective-permute-done.refs_5_.refs_11_.refs_6_.refs_7_ = bf16[384,768]{1,0:T(8,128)(2,1)} collective-permute-done((bf16[384,768]{1,0:T(8,128)(2,1)}, bf16[384,768]{1,0:T(8,128)(2,1)}, u32[]{:S(2)}, u32[]{:S(2)}) %collective-permute-start) | collective-permute-done | bytes 589856 | tf_op jit(solution)/shard_map/ppermute | solution.py:768
  53.6 11.9 %collective-permute-done.7.refs_2_.refs_9_ = bf16[512,768]{1,0:T(8,128)(2,1)S(1)} collective-permute-done((bf16[512,768]{1,0:T(8,128)(2,1)S(1)}, bf16[512,768]{1,0:T(8,128)(2,1)S(1)}, u32[]{:S(2)}, u32[]{:S(2)}) %collective-permute-start.7) | collective-permute-done | bytes 786464 | tf_op jit(solution)/shard_map/ppermute | solution.py:774
  75.6 18.5 %collective-permute-done.15.refs_9_.refs_7_ = bf16[768,768]{1,0:T(8,128)(2,1)S(1)} collective-permute-done((bf16[768,768]{1,0:T(8,128)(2,1)S(1)}, bf16[768,768]{1,0:T(8,128)(2,1)S(1)}, u32[]{:S(2)}, u32[]{:S(2)}) %collective-permute-start.15) | collective-permute-done | bytes 1179680 | tf_op jit(solution)/shard_map/ppermute | solution.py:768
  116.4 7.6 %collective-permute-done.18.refs_6_ = bf16[256,768]{1,0:T(8,128)(2,1)S(1)} collective-permute-done((bf16[256,768]{1,0:T(8,128)(2,1)S(1)}, bf16[256,768]{1,0:T(8,128)(2,1)S(1)}, u32[]{:S(2)}, u32[]{:S(2)}) %collective-permute-start.18) | collective-permute-done | bytes 393248 | tf_op jit(solution)/shard_map/ppermute | solution.py:768
  138.2 13.7 %collective-permute-done.20.refs_2_.refs_9_ = bf16[512,768]{1,0:T(8,128)(2,1)S(1)} collective-permute-done((bf16[512,768]{1,0:T(8,128)(2,1)S(1)}, bf16[512,768]{1,0:T(8,128)(2,1)S(1)}, u32[]{:S(2)}, u32[]{:S(2)}) %collective-permute-start.20) | collective-permute-done | bytes 786464 | tf_op jit(solution)/shard_map/ppermute | solution.py:774
  160.5 7.8 %collective-permute-done.23.refs_4_ = bf16[256,768]{1,0:T(8,128)(2,1)S(1)} collective-permute-done((bf16[256,768]{1,0:T(8,128)(2,1)S(1)}, bf16[256,768]{1,0:T(8,128)(2,1)S(1)}, u32[]{:S(2)}, u32[]{:S(2)}) %collective-permute-start.23) | collective-permute-done | bytes 393248 | tf_op jit(solution)/shard_map/ppermute | solution.py:768
  168.2 6.6 %shard_map.280 = (f32[256,768]{1,0:T(8,128)}, bf16[256,768]{1,0:T(8,128)(2,1)}, bf16[256,1536]{1,0:T(8,128)(2,1)}, bf16[256,1536]{1,0:T(8,128)(2,1)}, bf16[256,768]{1,0:T(8,128)(2,1)S(1)}) custom-call(s32[4]{0:T(128)S(1)} %pad_add_fusion.refs_0_, f32[16,768]{1,0:T(8,128)S(1)} %get-tuple-element.309.refs_1_, bf16[256,768]{1,0:T(8,128)(2,1)} %get-tuple-element.340.refs_2_, ...), custom_call_target="tpu_custom_call" | custom-call | flops 480000000 | bytes 800000 | tf_op jit(solution)/shard_map/pallas_call | solution.py:94
  182.9 6.6 %shard_map.283 = (f32[256,768]{1,0:T(8,128)}, bf16[256,768]{1,0:T(8,128)(2,1)}, bf16[256,1536]{1,0:T(8,128)(2,1)}, bf16[256,1536]{1,0:T(8,128)(2,1)}, bf16[256,768]{1,0:T(8,128)(2,1)S(1)}) custom-call(s32[4]{0:T(128)S(1)} %pad_add_fusion.refs_0_, f32[16,768]{1,0:T(8,128)S(1)} %get-tuple-element.309.refs_1_, ...), custom_call_target="tpu_custom_call" | custom-call | flops 480000000 | bytes 800000 | tf_op jit(solution)/shard_map/pallas_call | solution.py:94
  195.9 7.4 %shard_map.285 = (bf16[2,768,768]{2,1,0:T(8,128)(2,1)}, bf16[2,768,768]{2,1,0:T(8,128)(2,1)}) custom-call(s32[4]{0:T(128)S(1)} %pad_add_fusion.refs_0_, bf16[256,1536]{1,0:T(8,128)(2,1)} %get-tuple-element.359.refs_1_, bf16[256,1536]{1,0:T(8,128)(2,1)} %get-tuple-element.360.refs_2_, bf16[256,768]{1,0:T(8,128)(2,1)S(1)} %get-tuple-element.650.refs_1_.refs_3_.refs_5_, ...), custom_call_target="tpu_custom_call" | custom-call | flops 444000000 | bytes 740000 | tf_op jit(solution)/shard_map/pallas_call | solution.py:94
  204.6 6.3 %shard_map.286 = (f32[256,768]{1,0:T(8,128)}, bf16[256,768]{1,0:T(8,128)(2,1)}, bf16[256,384]{1,0:T(8,128)(2,1)S(1)}, f32[8,256]{1,0:T(8,128)S(1)}, f32[256,768]...) custom-call(s32[4]{0:T(128)S(1)} %pad_add_fusion.refs_0_, ...), custom_call_target="tpu_custom_call" | custom-call | flops 336000000 | bytes 560000 | tf_op jit(solution)/shard_map/pallas_call | solution.py:94
  223.9 7.6 %collective-permute-done.30 = bf16[384,768]{1,0:T(8,128)(2,1)S(1)} collective-permute-done((bf16[384,768]{1,0:T(8,128)(2,1)S(1)}, bf16[384,768]{1,0:T(8,128)(2,1)S(1)}, u32[]{:S(2)}, u32[]{:S(2)}) %collective-permute-start.30) | collective-permute-done | bytes 589856 | tf_op jit(solution)/shard_map/ppermute | solution.py:768
  254.5 8.1 %collective-permute-start.35 = (bf16[384,768]{1,0:T(8,128)(2,1)S(1)}, bf16[384,768]{1,0:T(8,128)(2,1)S(1)}, u32[]{:S(2)}, u32[]{:S(2)}) collective-permute-start(bf16[384,768]{1,0:T(8,128)(2,1)S(1)} %get-tuple-element.628), channel_id=1, source_target_pairs={{0,2},{1,3},{2,0},{3,1},{4,6},{5,7},{6,4},{7,5},{8,10},{9,11},{10,... | collective-permute-start | bytes 1769480 | tf_op jit(solution)/shard_map/ppermute | solution.py:768
  297.2 15.2 %collective-permute-done.39 = bf16[384,768]{1,0:T(8,128)(2,1)S(1)} collective-permute-done((bf16[384,768]{1,0:T(8,128)(2,1)S(1)}, bf16[384,768]{1,0:T(8,128)(2,1)S(1)}, u32[]{:S(2)}, u32[]{:S(2)}) %collective-permute-start.39) | collective-permute-done | bytes 589856 | tf_op jit(solution)/shard_map/ppermute | solution.py:768
  320.7 7.4 %shard_map.296 = (bf16[2,768,768]{2,1,0:T(8,128)(2,1)}, bf16[2,768,768]{2,1,0:T(8,128)(2,1)}) custom-call(s32[4]{0:T(128)S(1)} %pad_add_fusion.refs_0_, bf16[256,1536]{1,0:T(8,128)(2,1)} %get-tuple-element.449.refs_1_, bf16[256,1536]{1,0:T(8,128)(2,1)} %get-tuple-element.450.refs_2_, bf16[256,768]{1,0:T(8,128)(2,1)S(1)} %get-tuple-element.436.refs_1_.refs_3_.refs_5_, ...), custom_call_target="tpu_custom_call" | custom-call | flops 444000000 | bytes 740000 | tf_op jit(solution)/shard_map/pallas_call | solution.py:94
  328.1 6.4 %collective-permute-done.41 = bf16[576,768]{1,0:T(8,128)(2,1)S(1)} collective-permute-done((bf16[576,768]{1,0:T(8,128)(2,1)S(1)}, bf16[576,768]{1,0:T(8,128)(2,1)S(1)}, u32[]{:S(2)}, u32[]{:S(2)}) %collective-permute-start.41) | collective-permute-done | bytes 884768 | tf_op jit(solution)/shard_map/ppermute | solution.py:768
  340.6 10.5 %collective-permute-done.43 = bf16[192,768]{1,0:T(8,128)(2,1)S(1)} collective-permute-done((bf16[192,768]{1,0:T(8,128)(2,1)S(1)}, bf16[192,768]{1,0:T(8,128)(2,1)S(1)}, u32[]{:S(2)}, u32[]{:S(2)}) %collective-permute-start.43) | collective-permute-done | bytes 294944 | tf_op jit(solution)/shard_map/ppermute | solution.py:768
  360.2 9.5 %collective-permute-done.46 = bf16[384,768]{1,0:T(8,128)(2,1)S(1)} collective-permute-done((bf16[384,768]{1,0:T(8,128)(2,1)S(1)}, bf16[384,768]{1,0:T(8,128)(2,1)S(1)}, u32[]{:S(2)}, u32[]{:S(2)}) %collective-permute-start.46) | collective-permute-done | bytes 589856 | tf_op jit(solution)/shard_map/ppermute | solution.py:768
  376.9 7.7 %collective-permute-done.47 = bf16[384,768]{1,0:T(8,128)(2,1)S(1)} collective-permute-done((bf16[384,768]{1,0:T(8,128)(2,1)S(1)}, bf16[384,768]{1,0:T(8,128)(2,1)S(1)}, u32[]{:S(2)}, u32[]{:S(2)}) %collective-permute-start.47) | collective-permute-done | bytes 589856 | tf_op jit(solution)/shard_map/ppermute | solution.py:768
  385.2 6.8 %collective-permute-start.51 = (bf16[576,768]{1,0:T(8,128)(2,1)S(1)}, bf16[576,768]{1,0:T(8,128)(2,1)S(1)}, u32[]{:S(2)}, u32[]{:S(2)}) collective-permute-start(bf16[576,768]{1,0:T(8,128)(2,1)S(1)} %pad_maximum_fusion.3), channel_id=1, source_target_pairs={{0,2},{1,3},{2,0},{3,1},{4,6},{5,7},{6,4},{7,5},{8,10},{9,11},{10,... | collective-permute-start | bytes 2654216 | tf_op jit(solution)/shard_map/ppermute | solution.py:768
  424.8 9.0 %collective-permute-done.54 = bf16[384,768]{1,0:T(8,128)(2,1)} collective-permute-done((bf16[384,768]{1,0:T(8,128)(2,1)}, bf16[384,768]{1,0:T(8,128)(2,1)}, u32[]{:S(2)}, u32[]{:S(2)}) %collective-permute-start.54) | collective-permute-done | bytes 589856 | tf_op jit(solution)/shard_map/ppermute | solution.py:768
  442.6 6.3 %collective-permute-done.52 = bf16[384,768]{1,0:T(8,128)(2,1)} collective-permute-done((bf16[384,768]{1,0:T(8,128)(2,1)}, bf16[384,768]{1,0:T(8,128)(2,1)}, u32[]{:S(2)}, u32[]{:S(2)}) %collective-permute-start.52) | collective-permute-done | bytes 589856 | tf_op jit(solution)/shard_map/ppermute | solution.py:768
  455.8 16.6 %collective-permute-done.58 = bf16[576,768]{1,0:T(8,128)(2,1)S(1)} collective-permute-done((bf16[576,768]{1,0:T(8,128)(2,1)S(1)}, bf16[576,768]{1,0:T(8,128)(2,1)S(1)}, u32[]{:S(2)}, u32[]{:S(2)}) %collective-permute-start.58) | collective-permute-done | bytes 884768 | tf_op jit(solution)/shard_map/ppermute | solution.py:768
  482.8 8.3 %collective-permute-done.62 = bf16[192,768]{1,0:T(8,128)(2,1)S(1)} collective-permute-done((bf16[192,768]{1,0:T(8,128)(2,1)S(1)}, bf16[192,768]{1,0:T(8,128)(2,1)S(1)}, u32[]{:S(2)}, u32[]{:S(2)}) %collective-permute-start.62) | collective-permute-done | bytes 294944 | tf_op jit(solution)/shard_map/ppermute | solution.py:768
  510.6 7.2 %shard_map.305 = (f32[1536,768]{1,0:T(8,128)}, f32[768,1536]{1,0:T(8,128)}, f32[8,128]{1,0:T(8,128)S(1)}) custom-call(s32[4]{0:T(128)S(1)} %pad_add_fusion.refs_0_, bf16[768,768]{1,0:T(8,128)(2,1)} %copy-done.35, bf16[384,768]{1,0:T(8,128)(2,1)} %copy-done.62, bf16[384,768]{1,0:T(8,128)(2,1)} %copy-done.63, bf16[768,768]{1,0:T(8,128)(2,1)} %copy-done.51, ...), custom_call_target="tpu_custom_call" | custom-call | flops 600000000 | bytes 1000000 | tf_op jit(solution)/shard_map/pallas_call | solution.py:94
  (416 shorter events, 311.0 us)
Async XLA Ops:
  3.7 21.5 %collective-permute-start.3 = (f32[16,768]{1,0:T(8,128)S(1)}, f32[16,768]{1,0:T(8,128)}, u32[]{:S(2)}, u32[]{:S(2)}) collective-permute-start(f32[16,768]{1,0:T(8,128)S(1)} %concatenate.44), channel_id=1, source_target_pairs={{0,16},{16,0},{1,17},{17,1},{2,18},{18,2},{3,19},{19,3},{4,20},{20... | collective-permute-start | bytes 147464 | tf_op jit(solution)/shard_map/ppermute | solution.py:768
  36.3 29.3 %collective-permute-start.9 = (bf16[384,1536]{1,0:T(8,128)(2,1)S(1)}, bf16[384,1536]{1,0:T(8,128)(2,1)S(1)}, u32[]{:S(2)}, u32[]{:S(2)}) collective-permute-start(bf16[384,1536]{1,0:T(8,128)(2,1)S(1)} %dynamic-slice_bitcast_fusion.1), channel_id=1, source_target_pairs={{0,16},{16,0},{1,17},{17,1},{2,18},{18,2},{3,19},{19,3},{4,20},{20... | collective-permute-start | bytes 3538952 | tf_op jit(solution)/shard_map/ppermute | solution.py:768
  44.7 20.8 %collective-permute-start.7 = (bf16[512,768]{1,0:T(8,128)(2,1)S(1)}, bf16[512,768]{1,0:T(8,128)(2,1)S(1)}, u32[]{:S(2)}, u32[]{:S(2)}) collective-permute-start(bf16[512,768]{1,0:T(8,128)(2,1)S(1)} %get-tuple-element.317.refs_3_.refs_9_), channel_id=1, source_target_pairs={{0,2},{1,3},{2,4},{3,5},{4,6},{5,7},{8,10},{9,11},{10,12},{11,13},... | collective-permute-start | bytes 2359304 | tf_op jit(solution)/shard_map/ppermute | solution.py:774
  65.7 28.4 %collective-permute-start.15 = (bf16[768,768]{1,0:T(8,128)(2,1)S(1)}, bf16[768,768]{1,0:T(8,128)(2,1)S(1)}, u32[]{:S(2)}, u32[]{:S(2)}) collective-permute-start(bf16[768,768]{1,0:T(8,128)(2,1)S(1)} %dynamic-slice_bitcast_fusion), channel_id=1, source_target_pairs={{0,16},{16,0},{1,17},{17,1},{2,18},{18,2},{3,19},{19,3},{4,20},{20... | collective-permute-start | bytes 3538952 | tf_op jit(solution)/shard_map/ppermute | solution.py:768
  71.4 22.8 %collective-permute-start.14 = (bf16[256,768]{1,0:T(8,128)(2,1)S(1)}, bf16[256,768]{1,0:T(8,128)(2,1)S(1)}, u32[]{:S(2)}, u32[]{:S(2)}) collective-permute-start(bf16[256,768]{1,0:T(8,128)(2,1)S(1)} %get-tuple-element.330.refs_3_), channel_id=1, source_target_pairs={{0,8},{8,0},{1,9},{9,1},{2,10},{10,2},{3,11},{11,3},{4,12},{12,4},... | collective-permute-start | bytes 1179656 | tf_op jit(solution)/shard_map/ppermute | solution.py:768
  75.0 19.1 %collective-permute-start.13 = (bf16[256,768]{1,0:T(8,128)(2,1)S(1)}, bf16[256,768]{1,0:T(8,128)(2,1)S(1)}, u32[]{:S(2)}, u32[]{:S(2)}) collective-permute-start(bf16[256,768]{1,0:T(8,128)(2,1)S(1)} %get-tuple-element.329.refs_3_), channel_id=1, source_target_pairs={{0,8},{8,0},{1,9},{9,1},{2,10},{10,2},{3,11},{11,3},{4,12},{12,4},... | collective-permute-start | bytes 1179656 | tf_op jit(solution)/shard_map/ppermute | solution.py:768
  130.1 21.8 %collective-permute-start.20 = (bf16[512,768]{1,0:T(8,128)(2,1)S(1)}, bf16[512,768]{1,0:T(8,128)(2,1)S(1)}, u32[]{:S(2)}, u32[]{:S(2)}) collective-permute-start(bf16[512,768]{1,0:T(8,128)(2,1)S(1)} %get-tuple-element.343.refs_3_.refs_9_), channel_id=1, source_target_pairs={{0,2},{1,3},{2,4},{3,5},{4,6},{5,7},{8,10},{9,11},{10,12},{11,13},... | collective-permute-start | bytes 2359304 | tf_op jit(solution)/shard_map/ppermute | solution.py:774
  159.8 23.1 %collective-permute-start.25 = (bf16[256,768]{1,0:T(8,128)(2,1)S(1)}, bf16[256,768]{1,0:T(8,128)(2,1)S(1)}, u32[]{:S(2)}, u32[]{:S(2)}) collective-permute-start(bf16[256,768]{1,0:T(8,128)(2,1)S(1)} %get-tuple-element.356.refs_3_), channel_id=1, source_target_pairs={{0,8},{8,0},{1,9},{9,1},{2,10},{10,2},{3,11},{11,3},{4,12},{12,4},... | collective-permute-start | bytes 1179656 | tf_op jit(solution)/shard_map/ppermute | solution.py:768
  181.3 22.0 %collective-permute-start.24 = (bf16[256,768]{1,0:T(8,128)(2,1)S(1)}, bf16[256,768]{1,0:T(8,128)(2,1)S(1)}, u32[]{:S(2)}, u32[]{:S(2)}) collective-permute-start(bf16[256,768]{1,0:T(8,128)(2,1)S(1)} %get-tuple-element.366.refs_3_), channel_id=1, source_target_pairs={{0,8},{8,0},{1,9},{9,1},{2,10},{10,2},{3,11},{11,3},{4,12},{12,4},... | collective-permute-start | bytes 1179656 | tf_op jit(solution)/shard_map/ppermute | solution.py:768
  218.4 34.0 %collective-permute-start.29 = (bf16[512,768]{1,0:T(8,128)(2,1)S(1)}, bf16[512,768]{1,0:T(8,128)(2,1)S(1)}, u32[]{:S(2)}, u32[]{:S(2)}) collective-permute-start(bf16[512,768]{1,0:T(8,128)(2,1)S(1)} %add_convert_fusion.1), channel_id=1, source_target_pairs={{2,0},{3,1},{4,2},{5,3},{6,4},{7,5},{10,8},{11,9},{12,10},{13,11},... | collective-permute-start | bytes 2359304 | tf_op jit(solution)/shard_map/ppermute | solution.py:774
  232.4 30.2 %collective-permute-start.32 = (bf16[512,768]{1,0:T(8,128)(2,1)}, bf16[512,768]{1,0:T(8,128)(2,1)S(1)}, u32[]{:S(2)}, u32[]{:S(2)}) collective-permute-start(bf16[512,768]{1,0:T(8,128)(2,1)} %get-tuple-element.399), channel_id=1, source_target_pairs={{0,1},{1,0},{2,3},{3,2},{4,5},{5,4},{6,7},{7,6},{8,9},{9,8},{10,11... | collective-permute-start | bytes 2359304 | tf_op jit(solution)/shard_map/ppermute | solution.py:768
  254.5 28.5 %collective-permute-start.35 = (bf16[384,768]{1,0:T(8,128)(2,1)S(1)}, bf16[384,768]{1,0:T(8,128)(2,1)S(1)}, u32[]{:S(2)}, u32[]{:S(2)}) collective-permute-start(bf16[384,768]{1,0:T(8,128)(2,1)S(1)} %get-tuple-element.628), channel_id=1, source_target_pairs={{0,2},{1,3},{2,0},{3,1},{4,6},{5,7},{6,4},{7,5},{8,10},{9,11},{10,... | collective-permute-start | bytes 1769480 | tf_op jit(solution)/shard_map/ppermute | solution.py:768
  283.3 29.1 %collective-permute-start.39 = (bf16[384,768]{1,0:T(8,128)(2,1)S(1)}, bf16[384,768]{1,0:T(8,128)(2,1)S(1)}, u32[]{:S(2)}, u32[]{:S(2)}) collective-permute-start(bf16[384,768]{1,0:T(8,128)(2,1)S(1)} %add_convert_fusion.9), channel_id=1, source_target_pairs={{0,4},{1,5},{2,6},{3,7},{4,0},{5,1},{6,2},{7,3},{8,12},{9,13},{10,... | collective-permute-start | bytes 1769480 | tf_op jit(solution)/shard_map/ppermute | solution.py:768
  286.2 26.1 %collective-permute-start.38 = (bf16[384,768]{1,0:T(8,128)(2,1)S(1)}, bf16[384,768]{1,0:T(8,128)(2,1)S(1)}, u32[]{:S(2)}, u32[]{:S(2)}) collective-permute-start(bf16[384,768]{1,0:T(8,128)(2,1)S(1)} %fusion.8), channel_id=1, source_target_pairs={{0,16},{16,0},{1,17},{17,1},{2,18},{18,2},{3,19},{19,3},{4,20},{20... | collective-permute-start | bytes 1769480 | tf_op jit(solution)/shard_map/ppermute | solution.py:768
  312.8 21.7 %collective-permute-start.41 = (bf16[576,768]{1,0:T(8,128)(2,1)S(1)}, bf16[576,768]{1,0:T(8,128)(2,1)S(1)}, u32[]{:S(2)}, u32[]{:S(2)}) collective-permute-start(bf16[576,768]{1,0:T(8,128)(2,1)S(1)} %pad_maximum_fusion.2), channel_id=1, source_target_pairs={{0,2},{1,3},{2,0},{3,1},{4,6},{5,7},{6,4},{7,5},{8,10},{9,11},{10,... | collective-permute-start | bytes 2654216 | tf_op jit(solution)/shard_map/ppermute | solution.py:768
  312.9 21.6 %collective-permute-start.37 = (bf16[256,768]{1,0:T(8,128)(2,1)S(1)}, bf16[256,768]{1,0:T(8,128)(2,1)S(1)}, u32[]{:S(2)}, u32[]{:S(2)}) collective-permute-start(bf16[256,768]{1,0:T(8,128)(2,1)S(1)} %get-tuple-element.463.refs_3_), channel_id=1, source_target_pairs={{0,8},{8,0},{1,9},{9,1},{2,10},{10,2},{3,11},{11,3},{4,12},{12,4},... | collective-permute-start | bytes 1179656 | tf_op jit(solution)/shard_map/ppermute | solution.py:768
  356.4 28.1 %collective-permute-start.45 = (bf16[512,768]{1,0:T(8,128)(2,1)S(1)}, bf16[512,768]{1,0:T(8,128)(2,1)S(1)}, u32[]{:S(2)}, u32[]{:S(2)}) collective-permute-start(bf16[512,768]{1,0:T(8,128)(2,1)S(1)} %add_convert_fusion), channel_id=1, source_target_pairs={{2,0},{3,1},{4,2},{5,3},{6,4},{7,5},{10,8},{11,9},{12,10},{13,11},... | collective-permute-start | bytes 2359304 | tf_op jit(solution)/shard_map/ppermute | solution.py:774
  370.8 21.2 %collective-permute-start.48 = (bf16[512,768]{1,0:T(8,128)(2,1)S(1)}, bf16[512,768]{1,0:T(8,128)(2,1)S(1)}, u32[]{:S(2)}, u32[]{:S(2)}) collective-permute-start(bf16[512,768]{1,0:T(8,128)(2,1)S(1)} %get-tuple-element.496), channel_id=1, source_target_pairs={{0,1},{1,0},{2,3},{3,2},{4,5},{5,4},{6,7},{7,6},{8,9},{9,8},{10,11... | collective-permute-start | bytes 2359304 | tf_op jit(solution)/shard_map/ppermute | solution.py:768
  385.2 25.4 %collective-permute-start.51 = (bf16[576,768]{1,0:T(8,128)(2,1)S(1)}, bf16[576,768]{1,0:T(8,128)(2,1)S(1)}, u32[]{:S(2)}, u32[]{:S(2)}) collective-permute-start(bf16[576,768]{1,0:T(8,128)(2,1)S(1)} %pad_maximum_fusion.3), channel_id=1, source_target_pairs={{0,2},{1,3},{2,0},{3,1},{4,6},{5,7},{6,4},{7,5},{8,10},{9,11},{10,... | collective-permute-start | bytes 2654216 | tf_op jit(solution)/shard_map/ppermute | solution.py:768
  418.9 30.0 %collective-permute-start.52 = (bf16[384,768]{1,0:T(8,128)(2,1)}, bf16[384,768]{1,0:T(8,128)(2,1)}, u32[]{:S(2)}, u32[]{:S(2)}) collective-permute-start(bf16[384,768]{1,0:T(8,128)(2,1)} %add_convert_fusion.4), channel_id=1, source_target_pairs={{0,4},{1,5},{2,6},{3,7},{4,0},{5,1},{6,2},{7,3},{8,12},{9,13},{10,... | collective-permute-start | bytes 1769480 | tf_op jit(solution)/shard_map/ppermute | solution.py:768
  422.8 26.1 %collective-permute-start.56 = (bf16[256,768]{1,0:T(8,128)(2,1)S(1)}, bf16[256,768]{1,0:T(8,128)(2,1)}, u32[]{:S(2)}, u32[]{:S(2)}) collective-permute-start(bf16[256,768]{1,0:T(8,128)(2,1)S(1)} %copy-done.21), channel_id=1, source_target_pairs={{0,8},{8,0},{1,9},{9,1},{2,10},{10,2},{3,11},{11,3},{4,12},{12,4},... | collective-permute-start | bytes 1179656 | tf_op jit(solution)/shard_map/ppermute | solution.py:768
  423.3 25.5 %collective-permute-start.57 = (bf16[256,768]{1,0:T(8,128)(2,1)S(1)}, bf16[256,768]{1,0:T(8,128)(2,1)}, u32[]{:S(2)}, u32[]{:S(2)}) collective-permute-start(bf16[256,768]{1,0:T(8,128)(2,1)S(1)} %copy-done.23), channel_id=1, source_target_pairs={{0,8},{8,0},{1,9},{9,1},{2,10},{10,2},{3,11},{11,3},{4,12},{12,4},... | collective-permute-start | bytes 1179656 | tf_op jit(solution)/shard_map/ppermute | solution.py:768
  451.0 21.4 %collective-permute-start.58 = (bf16[576,768]{1,0:T(8,128)(2,1)S(1)}, bf16[576,768]{1,0:T(8,128)(2,1)S(1)}, u32[]{:S(2)}, u32[]{:S(2)}) collective-permute-start(bf16[576,768]{1,0:T(8,128)(2,1)S(1)} %pad_maximum_fusion.4), channel_id=1, source_target_pairs={{0,2},{1,3},{2,0},{3,1},{4,6},{5,7},{6,4},{7,5},{8,10},{9,11},{10,... | collective-permute-start | bytes 2654216 | tf_op jit(solution)/shard_map/ppermute | solution.py:768
  451.3 21.1 %collective-permute-start.60 = (bf16[256,768]{1,0:T(8,128)(2,1)S(1)}, bf16[256,768]{1,0:T(8,128)(2,1)S(1)}, u32[]{:S(2)}, u32[]{:S(2)}) collective-permute-start(bf16[256,768]{1,0:T(8,128)(2,1)S(1)} %select_convert_fusion), channel_id=1, source_target_pairs={{0,16},{16,0},{1,17},{17,1},{2,18},{18,2},{3,19},{19,3},{4,20},{20... | collective-permute-start | bytes 1179656 | tf_op jit(solution)/shard_map/ppermute | solution.py:768
  (131 other events, 1189.2 us)

commit v6 on v5

--- a/solution.py
+++ b/solution.py
@@ -351,7 +351,7 @@
         d_score = (weight * (d_weight - delta[h : h + 1, :])).astype(BF)
         dvs.append(dot_nn(weight.astype(BF), do))
         dks.append(dot_nn(d_score, q))
-        d = dot_tn(d_score, key)
+        d = dot_tn(key, d_score)
         dq = d if dq is None else dq + d
     low = low_lanes(dks[0].shape)
     return dq, jnp.where(low, dks[0], dks[1]), jnp.where(low, dvs[0], dvs[1])
@@ -376,16 +376,16 @@
     q, do, lse, delta = held
     for p in range(width // 128):
         ks, vs = spans(p, width)
-        total = dq_ref[:, ks]
+        total = None
         for source, ref, start in sources:
             for i in range(CHUNKS):
                 at = slice(start + i * size, start + (i + 1) * size)
                 tile = source.at[i * size : (i + 1) * size]
                 dq, dk, dv = back_tile(p, width, q[:, ks], do[:, ks], lse, delta, tile, None)
-                total = total + dq
+                total = dq if total is None else total + dq
                 ref[at, ks] = dk.astype(BF)
                 ref[at, vs] = dv.astype(BF)
-        dq_ref[:, ks] = total
+        dq_ref[:, ks] += jnp.transpose(total)
 
 
 def attend_far_back(scalars, q, do, lse, delta, far):
@@ -451,8 +451,9 @@
             second, dk, dv = back_tile(p, width, qs[size:, ks], dos[size:, ks], *late, k1, causal[:, :size])
             dk1[:, ks] = dk
             dk1[:, vs] = dv
-            dq0[:, ks] = ((before[:size, ks] + first[:size]) * 0.125).astype(BF)
-            dq1[:, ks] = ((before[size:, ks] + first[size:] + second) * 0.125).astype(BF)
+            first, second = jnp.transpose(first[:, :size]), jnp.transpose(first[:, size:] + second)
+            dq0[:, ks] = ((before[:size, ks] + first) * 0.125).astype(BF)
+            dq1[:, ks] = ((before[size:, ks] + second) * 0.125).astype(BF)
 
     outs = [((size, width), BF)] * 2 + [((size, 2 * width), F32)] * 2
     blocks = [*map(Late, q), *do, *map(Late, lse), *delta, Late(kv), dq_before]
@@ -507,6 +508,41 @@
 
     outs = [((rows, inner), BF), ((rows, features), BF), ((8, features), F32)]
     return call(body, outs, scalars, [dy, Late(slope)], [*up, *down], held_like(up, down), us=1.0)
+
+
+def feed_both(scalars, layer, table, x, mine, came, dy, up, down):
+    rows, features = x.shape
+    inner = up[0].shape[1]
+
+    def body(scal, tab, x_ref, mine_ref, came_ref, dy_ref, u_own, u_got, u_other, d_own, d_got, d_other,
+             hidden, mlp_in, active, result, d_up, part, sums, up_held, down_held, up_sem, down_sem):
+        fetch_start(scal, layer, u_own, u_got, u_other, up_held, up_sem)
+        fetch_start(scal, layer, d_own, d_got, d_other, down_held, down_sem)
+        h = x_ref[...].astype(F32) + (mine_ref[...].astype(F32) + came_ref[...].astype(F32)) + tab[BO : BO + 1]
+        hidden[...] = h
+        unit, _ = norm_parts(h)
+        low = (unit * tab[GAIN1 : GAIN1 + 1] + tab[BIAS1 : BIAS1 + 1]).astype(BF)
+        mlp_in[...] = low
+        flush(hidden, mlp_in)
+        sums[...] = jnp.zeros_like(sums)
+        fetch_wait(u_own, up_held, up_sem)
+        fetch_wait(d_own, down_held, down_sem)
+        for j in range(inner // features):
+            cols = slice(j * features, (j + 1) * features)
+            value, slope = gelu_both(dot_nn(low, up_held[:, cols]) + tab[BUP + j : BUP + j + 1])
+            active[:, cols] = value.astype(BF)
+            grad = (dot_nt(dy_ref[...], down_held[cols, :]) * slope).astype(BF)
+            d_up[:, cols] = grad
+            sums[j : j + 1, :] = jnp.sum(grad.astype(F32), axis=0, keepdims=True)
+        flush(active)
+        part[...] = dot_nt(d_up[...], up_held[...]).astype(BF)
+        result[...] = dot_nn(active[...], down_held[...]).astype(BF)
+
+    outs = [
+        ((rows, features), F32, LATER), ((rows, features), BF, LATER), ((rows, inner), BF, LATER), ((rows, features), BF, LATER),
+        ((rows, inner), BF), ((rows, features), BF), ((8, features), F32),
+    ]
+    return call(body, outs, scalars, [table, Late(x), mine, came, dy], [*up, *down], held_like(up, down), us=1.0)
 
 
 def middle_back(scalars, layer, table, hidden, parts, dy, attended, weights):
@@ -873,7 +909,7 @@
         came.append(swap(part, "tensor"))
     came = hooks.get("far", nothing)(came)
     hidden, mlp_in, active, slope, results = [], [], [], [], []
-    for c in range(CHUNKS):
+    for c in range(CHUNKS if layer == 0 else 0):
         h, m, a, s, part = feed_forward(scalars, layer, table, x[c], parts[c], came[c], w["up"], w["down"])
         hidden.append(h)
         mlp_in.append(m)
@@ -881,7 +917,7 @@
         slope.append(s)
         results.append((table, h, part))
     kept = dict(x=x, normed=normed, q=q, kv=kv, near=near, far=far, att=att, lse=lse, hidden=hidden,
-                mlp_in=mlp_in, active=active, slope=slope)
+                mlp_in=mlp_in, active=active, slope=slope, attention=(parts, came), results=results)
     return results, kept
 
 
@@ -892,11 +928,19 @@
     for c in range(CHUNKS):
         if c == 1:
             dy[1] = steps("half", after(dy[1], parts[0][0]))
-        grad, part, sums = feed_back(scalars, layer, dy[c], kept["slope"][c], w["up"], w["down"])
+        if layer == 0:
+            grad, part, sums = feed_back(scalars, layer, dy[c], kept["slope"][c], w["up"], w["down"])
+        else:
+            mine, came = [a[c] for a in kept["attention"]]
+            h, m, a, y, grad, part, sums = feed_both(scalars, layer, table, kept["x"][c], mine, came, dy[c], w["up"], w["down"])
+            kept["hidden"].append(h)
+            kept["mlp_in"].append(m)
+            kept["active"].append(a)
+            kept["results"].append((table, h, y))
         d_up.append(grad)
         up_sums.append(sums)
         parts.append((part, swap(part, "tensor")))
-    wide = Reduction(wide_grads(scalars, kept["active"], dy, kept["mlp_in"], d_up), 2)
+    wide = Reduction(wide_grads(scalars, kept["active"], dy, kept["mlp_in"], d_up), 1)
     parts = steps("fed", parts, wide)
     dh, dh_low, d_att, delta, mid = middle_back(
         scalars, layer, table, kept["hidden"], parts, dy, kept["att"], w["out"]
@@ -1001,7 +1045,7 @@
         scalars, 0, tables[0], w, x=x, hooks=dict(projected=on_projected, arrived=on_arrived, far=on_far)
     )
     first = [r + (swap(r[2], "tensor"),) for r in first]
-    second, kept1 = forward_layer(scalars, 1, tables[1], w, ahead=first, carried=kept0["kv"])
+    _, kept1 = forward_layer(scalars, 1, tables[1], w, ahead=first, carried=kept0["kv"])
     y0 = kept1["x"]
 
     def my_half(chunks):
@@ -1020,13 +1064,10 @@
         if number == "mid":
             *leaves, wide.near = tie(*leaves, wide.near)
             wide.prepare()
-            *leaves, wide.sent[0], wide.sent[1] = tie(*leaves, *wide.sent)
+            *leaves, wide.sent[0] = tie(*leaves, *wide.sent)
             wide.over_sections(0)
-        if number == "between":
-            *leaves, wide.came[0], wide.sent[1] = tie(*leaves, wide.came[0], wide.sent[1])
-            wide.over_sections(1)
         if number == "near":
-            *leaves, wide.came[1] = tie(*leaves, wide.came[1])
+            *leaves, wide.came[0] = tie(*leaves, wide.came[0])
             late["a1"] = swap_all([wide.scatter_send()], -2)[0]
         if number == "proj":
             *leaves, narrow.send, got = tie(*leaves, narrow.send, late["a1"])
@@ -1060,14 +1101,11 @@
         if number == "mid":
             *leaves, wide.near, got = tie(*leaves, wide.near, late["d1"])
             wide.prepare()
-            *leaves, wide.sent[0], wide.sent[1] = tie(*leaves, *wide.sent)
+            *leaves, wide.sent[0] = tie(*leaves, *wide.sent)
             wide.over_sections(0)
             late["e1"] = narrow1.gather_send(got)
-        if number == "between":
-            *leaves, wide.came[0], wide.sent[1] = tie(*leaves, wide.came[0], wide.sent[1])
-            wide.over_sections(1)
         if number == "near":
-            *leaves, wide.came[1] = tie(*leaves, wide.came[1])
+            *leaves, wide.came[0] = tie(*leaves, wide.came[0])
             late["a0"] = swap_all([wide.scatter_send(), late["e1"]], -2)
         if number == "proj":
             *leaves, narrow.send, got, narrow_got = tie(*leaves, narrow.send, *late["a0"])
@@ -1080,7 +1118,7 @@
             narrow.prepare()
             *leaves, narrow.sent[0] = tie(*leaves, narrow.sent[0])
             narrow.over_sections()
-            late["y1"] = [swap(after(r[2], leaves[0]), "tensor") for r in second]
+            late["y1"] = [swap(after(r[2], leaves[0]), "tensor") for r in kept1["results"]]
         if number == "last":
             *leaves, narrow.came[0] = tie(*leaves, narrow.came[0])
         return jax.tree.unflatten(tree, leaves)
@@ -1096,7 +1134,7 @@
     table = take(sums, section) + swap(take(sums, 1 - section), "section")
     mine_grads, other_grads = by_section(*grads, BF)
     y1 = my_half(
-        [(r[1] + r[0][BDOWN : BDOWN + 1] + r[2].astype(F32) + c.astype(F32)).astype(BF) for r, c in zip(second, y_came)]
+        [(r[1] + r[0][BDOWN : BDOWN + 1] + r[2].astype(F32) + c.astype(F32)).astype(BF) for r, c in zip(kept1["results"], y_came)]
     )
     mine_out, other_out = by_section(my_half(y0), y1, BF)
 

time: 544 us -> 531 us (0.976)
  Pallas kernels: 168 us -> 161 us
  waiting for transfers between devices: 233 us -> 226 us
    ppermute x71 -> x69, waiting for transfers between devices: 201 us -> 193 us  [swap(): return lax.ppermute(value, axis, [(i, i ^ bits) for i in range(count)])]
    pallas_call x36 -> x34, Pallas kernels: 168 us -> 161 us  [call(): pl.pallas_call(body, out_shape=shapes, in_specs=[SCALARS] + [FAR_OFF if i...]
    ppermute x71 -> x69, starting transfers between devices: 63.5 us -> 65.3 us  [swap(): return lax.ppermute(value, axis, [(i, i ^ bits) for i in range(count)])]
    unnamed x160 -> x152, local copies, waits for them, and re-layouts: 18.3 us -> 17.3 us
  transfers between devices with their start and end apart: 75 -> 73, of which waited for: 37 -> 36; matrix products, arithmetic and copies ran while one was open for 6% -> 6% of each run, Pallas kernels for 27% -> 26%
where the time goes in v6:
time: 531 us; the launch traced here: 522 us
  waiting for transfers between devices  226 us (43%)
  Pallas kernels  161 us (30%)
  starting transfers between devices  75.8 us (14%)
  local copies, waits for them, and re-layouts  31.5 us (6%)
  other arithmetic  25 us (5%)
    ppermute x69, waiting for transfers between devices, swap(): return lax.ppermute(value, axis, [(i, i ^ bits) for i in range(count)])  193 us
    pallas_call x34, Pallas kernels, call(): pl.pallas_call(body, out_shape=shapes, in_specs=[SCALARS] + [FAR_OFF if i...  161 us
    ppermute x69, starting transfers between devices, swap(): return lax.ppermute(value, axis, [(i, i ^ bits) for i in range(count)])  65.3 us
    ppermute x4, waiting for transfers between devices, shift(): lax.ppermute(value, 'batch', [(i, i + steps) for i in range(first, last)])  32.7 us
    unnamed x152, local copies, waits for them, and re-layouts  17.3 us
  transfers between devices with their start and end apart: 73, of which 36 were waited for; matrix products, arithmetic and copies ran while one was open for 6% of the time, Pallas kernels for 26%

profile of v6, /device:TPU:0, one launch (start us, length us, event | category | flops | bytes accessed | tf_op | source)
XLA Modules:
  0.0 522.2 jit_solution(4640241625986585831)
XLA Ops:
  27.3 8.9 %collective-permute-done.refs_5_.refs_11_.refs_6_.refs_7_ = bf16[384,768]{1,0:T(8,128)(2,1)} collective-permute-done((bf16[384,768]{1,0:T(8,128)(2,1)}, bf16[384,768]{1,0:T(8,128)(2,1)}, u32[]{:S(2)}, u32[]{:S(2)}) %collective-permute-start) | collective-permute-done | bytes 589856 | tf_op jit(solution)/shard_map/ppermute | solution.py:804
  53.6 11.9 %collective-permute-done.7.refs_2_.refs_9_ = bf16[512,768]{1,0:T(8,128)(2,1)S(1)} collective-permute-done((bf16[512,768]{1,0:T(8,128)(2,1)S(1)}, bf16[512,768]{1,0:T(8,128)(2,1)S(1)}, u32[]{:S(2)}, u32[]{:S(2)}) %collective-permute-start.7) | collective-permute-done | bytes 786464 | tf_op jit(solution)/shard_map/ppermute | solution.py:810
  75.6 18.6 %collective-permute-done.15.refs_9_.refs_10_.refs_7_ = bf16[768,768]{1,0:T(8,128)(2,1)S(1)} collective-permute-done((bf16[768,768]{1,0:T(8,128)(2,1)S(1)}, bf16[768,768]{1,0:T(8,128)(2,1)S(1)}, u32[]{:S(2)}, u32[]{:S(2)}) %collective-permute-start.15) | collective-permute-done | bytes 1179680 | tf_op jit(solution)/shard_map/ppermute | solution.py:804
  98.1 6.2 %shard_map.276 = (f32[256,768]{1,0:T(8,128)}, bf16[256,768]{1,0:T(8,128)(2,1)}, bf16[256,1536]{1,0:T(8,128)(2,1)}, bf16[256,1536]{1,0:T(8,128)(2,1)}, bf16[256,768]{1,0:T(8,128)(2,1)S(1)}) custom-call(s32[4]{0:T(128)S(1)} %pad_add_fusion.refs_0_, f32[16,768]{1,0:T(8,128)S(1)} %get-tuple-element.300.refs_1_.refs_2_, bf16[256,768]{1,0:T(8,128)(2,1)} %copy-done.2, ...), custom_call_target="tpu_custom_call" | custom-call | flops 480000000 | bytes 800000 | tf_op jit(solution)/shard_map/pallas_call | solution.py:94
  116.4 7.6 %collective-permute-done.18.refs_6_ = bf16[256,768]{1,0:T(8,128)(2,1)S(1)} collective-permute-done((bf16[256,768]{1,0:T(8,128)(2,1)S(1)}, bf16[256,768]{1,0:T(8,128)(2,1)S(1)}, u32[]{:S(2)}, u32[]{:S(2)}) %collective-permute-start.18) | collective-permute-done | bytes 393248 | tf_op jit(solution)/shard_map/ppermute | solution.py:804
  138.2 13.7 %collective-permute-done.20.refs_2_.refs_9_ = bf16[512,768]{1,0:T(8,128)(2,1)S(1)} collective-permute-done((bf16[512,768]{1,0:T(8,128)(2,1)S(1)}, bf16[512,768]{1,0:T(8,128)(2,1)S(1)}, u32[]{:S(2)}, u32[]{:S(2)}) %collective-permute-start.20) | collective-permute-done | bytes 786464 | tf_op jit(solution)/shard_map/ppermute | solution.py:810
  160.4 7.8 %collective-permute-done.23.refs_4_ = bf16[256,768]{1,0:T(8,128)(2,1)S(1)} collective-permute-done((bf16[256,768]{1,0:T(8,128)(2,1)S(1)}, bf16[256,768]{1,0:T(8,128)(2,1)S(1)}, u32[]{:S(2)}, u32[]{:S(2)}) %collective-permute-start.23) | collective-permute-done | bytes 393248 | tf_op jit(solution)/shard_map/ppermute | solution.py:804
  168.2 8.3 %shard_map.280 = (f32[256,768]{1,0:T(8,128)}, bf16[256,768]{1,0:T(8,128)(2,1)}, bf16[256,1536]{1,0:T(8,128)(2,1)}, bf16[256,768]{1,0:T(8,128)(2,1)}, bf16[256,15...) custom-call(s32[4]{0:T(128)S(1)} %pad_add_fusion.refs_0_, ...), custom_call_target="tpu_custom_call" | custom-call | flops 120000000 | bytes 200000 | tf_op jit(solution)/shard_map/pallas_call | solution.py:94
  178.2 8.4 %shard_map.282 = (f32[256,768]{1,0:T(8,128)}, bf16[256,768]{1,0:T(8,128)(2,1)}, bf16[256,1536]{1,0:T(8,128)(2,1)}, bf16[256,768]{1,0:T(8,128)(2,1)}, bf16[256,15...) custom-call(s32[4]{0:T(128)S(1)} %pad_add_fusion.refs_0_, ...), custom_call_target="tpu_custom_call" | custom-call | flops 120000000 | bytes 200000 | tf_op jit(solution)/shard_map/pallas_call | solution.py:94
  187.1 7.4 %shard_map.283 = (bf16[2,768,768]{2,1,0:T(8,128)(2,1)}, bf16[2,768,768]{2,1,0:T(8,128)(2,1)}) custom-call(s32[4]{0:T(128)S(1)} %pad_add_fusion.refs_0_, bf16[256,1536]{1,0:T(8,128)(2,1)} %get-tuple-element.347.refs_1_, bf16[256,1536]{1,0:T(8,128)(2,1)} %get-tuple-element.348.refs_2_, bf16[256,768]{1,0:T(8,128)(2,1)S(1)} %get-tuple-element.626.refs_5_.refs_3_, ...), custom_call_target="tpu_custom_call" | custom-call | flops 444000000 | bytes 740000 | tf_op jit(solution)/shard_map/pallas_call | solution.py:94
  227.5 8.5 %collective-permute-done.30 = bf16[768,768]{1,0:T(8,128)(2,1)} collective-permute-done((bf16[768,768]{1,0:T(8,128)(2,1)}, bf16[768,768]{1,0:T(8,128)(2,1)}, u32[]{:S(2)}, u32[]{:S(2)}) %collective-permute-start.30) | collective-permute-done | bytes 1179680 | tf_op jit(solution)/shard_map/ppermute | solution.py:804
  236.0 6.8 %collective-permute-done.29.refs_4_ = bf16[512,768]{1,0:T(8,128)(2,1)S(1)} collective-permute-done((bf16[512,768]{1,0:T(8,128)(2,1)S(1)}, bf16[512,768]{1,0:T(8,128)(2,1)S(1)}, u32[]{:S(2)}, u32[]{:S(2)}) %collective-permute-start.29) | collective-permute-done | bytes 786464 | tf_op jit(solution)/shard_map/ppermute | solution.py:810
  244.9 6.3 %collective-permute-start.34 = (bf16[384,768]{1,0:T(8,128)(2,1)S(1)}, bf16[384,768]{1,0:T(8,128)(2,1)S(1)}, u32[]{:S(2)}, u32[]{:S(2)}) collective-permute-start(bf16[384,768]{1,0:T(8,128)(2,1)S(1)} %get-tuple-element.608), channel_id=1, source_target_pairs={{0,2},{1,3},{2,0},{3,1},{4,6},{5,7},{6,4},{7,5},{8,10},{9,11},{10,... | collective-permute-start | bytes 1769480 | tf_op jit(solution)/shard_map/ppermute | solution.py:804
  266.2 6.4 %collective-permute-done.33.refs_8_ = bf16[256,768]{1,0:T(8,128)(2,1)S(1)} collective-permute-done((bf16[256,768]{1,0:T(8,128)(2,1)S(1)}, bf16[256,768]{1,0:T(8,128)(2,1)S(1)}, u32[]{:S(2)}, u32[]{:S(2)}) %collective-permute-start.33) | collective-permute-done | bytes 393248 | tf_op jit(solution)/shard_map/ppermute | solution.py:804
  286.3 15.5 %collective-permute-done.38 = bf16[384,768]{1,0:T(8,128)(2,1)S(1)} collective-permute-done((bf16[384,768]{1,0:T(8,128)(2,1)S(1)}, bf16[384,768]{1,0:T(8,128)(2,1)S(1)}, u32[]{:S(2)}, u32[]{:S(2)}) %collective-permute-start.38) | collective-permute-done | bytes 589856 | tf_op jit(solution)/shard_map/ppermute | solution.py:804
  310.1 7.4 %shard_map.294 = (bf16[2,768,768]{2,1,0:T(8,128)(2,1)}, bf16[2,768,768]{2,1,0:T(8,128)(2,1)}) custom-call(s32[4]{0:T(128)S(1)} %pad_add_fusion.refs_0_, bf16[256,1536]{1,0:T(8,128)(2,1)} %get-tuple-element.433.refs_1_, bf16[256,1536]{1,0:T(8,128)(2,1)} %get-tuple-element.434.refs_2_, bf16[256,768]{1,0:T(8,128)(2,1)S(1)} %get-tuple-element.420.refs_1_.refs_3_.refs_5_, ...), custom_call_target="tpu_custom_call" | custom-call | flops 444000000 | bytes 740000 | tf_op jit(solution)/shard_map/pallas_call | solution.py:94
  317.5 6.4 %collective-permute-done.40 = bf16[576,768]{1,0:T(8,128)(2,1)S(1)} collective-permute-done((bf16[576,768]{1,0:T(8,128)(2,1)S(1)}, bf16[576,768]{1,0:T(8,128)(2,1)S(1)}, u32[]{:S(2)}, u32[]{:S(2)}) %collective-permute-start.40) | collective-permute-done | bytes 884768 | tf_op jit(solution)/shard_map/ppermute | solution.py:804
  330.5 10.2 %collective-permute-done.42 = bf16[192,768]{1,0:T(8,128)(2,1)S(1)} collective-permute-done((bf16[192,768]{1,0:T(8,128)(2,1)S(1)}, bf16[192,768]{1,0:T(8,128)(2,1)S(1)}, u32[]{:S(2)}, u32[]{:S(2)}) %collective-permute-start.42) | collective-permute-done | bytes 294944 | tf_op jit(solution)/shard_map/ppermute | solution.py:804
  359.3 12.5 %collective-permute-done.45 = bf16[768,768]{1,0:T(8,128)(2,1)S(1)} collective-permute-done((bf16[768,768]{1,0:T(8,128)(2,1)S(1)}, bf16[768,768]{1,0:T(8,128)(2,1)S(1)}, u32[]{:S(2)}, u32[]{:S(2)}) %collective-permute-start.45) | collective-permute-done | bytes 1179680 | tf_op jit(solution)/shard_map/ppermute | solution.py:804
  372.7 6.2 %collective-permute-start.49 = (bf16[576,768]{1,0:T(8,128)(2,1)S(1)}, bf16[576,768]{1,0:T(8,128)(2,1)S(1)}, u32[]{:S(2)}, u32[]{:S(2)}) collective-permute-start(bf16[576,768]{1,0:T(8,128)(2,1)S(1)} %pad_maximum_fusion.3), channel_id=1, source_target_pairs={{0,2},{1,3},{2,0},{3,1},{4,6},{5,7},{6,4},{7,5},{8,10},{9,11},{10,... | collective-permute-start | bytes 2654216 | tf_op jit(solution)/shard_map/ppermute | solution.py:804
  409.9 11.7 %collective-permute-done.52 = bf16[384,768]{1,0:T(8,128)(2,1)} collective-permute-done((bf16[384,768]{1,0:T(8,128)(2,1)}, bf16[384,768]{1,0:T(8,128)(2,1)}, u32[]{:S(2)}, u32[]{:S(2)}) %collective-permute-start.52) | collective-permute-done | bytes 589856 | tf_op jit(solution)/shard_map/ppermute | solution.py:804
  442.4 17.2 %collective-permute-done.56 = bf16[576,768]{1,0:T(8,128)(2,1)S(1)} collective-permute-done((bf16[576,768]{1,0:T(8,128)(2,1)S(1)}, bf16[576,768]{1,0:T(8,128)(2,1)S(1)}, u32[]{:S(2)}, u32[]{:S(2)}) %collective-permute-start.56) | collective-permute-done | bytes 884768 | tf_op jit(solution)/shard_map/ppermute | solution.py:804
  470.5 7.1 %collective-permute-done.60 = bf16[192,768]{1,0:T(8,128)(2,1)S(1)} collective-permute-done((bf16[192,768]{1,0:T(8,128)(2,1)S(1)}, bf16[192,768]{1,0:T(8,128)(2,1)S(1)}, u32[]{:S(2)}, u32[]{:S(2)}) %collective-permute-start.60) | collective-permute-done | bytes 294944 | tf_op jit(solution)/shard_map/ppermute | solution.py:804
  497.8 7.2 %shard_map.303 = (f32[1536,768]{1,0:T(8,128)}, f32[768,1536]{1,0:T(8,128)}, f32[8,128]{1,0:T(8,128)S(1)}) custom-call(s32[4]{0:T(128)S(1)} %pad_add_fusion.refs_0_, bf16[768,768]{1,0:T(8,128)(2,1)} %copy-done.30, bf16[384,768]{1,0:T(8,128)(2,1)} %copy-done.57, bf16[384,768]{1,0:T(8,128)(2,1)} %copy-done.58, bf16[768,768]{1,0:T(8,128)(2,1)} %copy-done.46, ...), custom_call_target="tpu_custom_call" | custom-call | flops 600000000 | bytes 1000000 | tf_op jit(solution)/shard_map/pallas_call | solution.py:94
  (402 shorter events, 291.1 us)
Async XLA Ops:
  3.7 21.5 %collective-permute-start.3 = (f32[16,768]{1,0:T(8,128)S(1)}, f32[16,768]{1,0:T(8,128)}, u32[]{:S(2)}, u32[]{:S(2)}) collective-permute-start(f32[16,768]{1,0:T(8,128)S(1)} %concatenate.44), channel_id=1, source_target_pairs={{0,16},{16,0},{1,17},{17,1},{2,18},{18,2},{3,19},{19,3},{4,20},{20... | collective-permute-start | bytes 147464 | tf_op jit(solution)/shard_map/ppermute | solution.py:804
  36.3 29.3 %collective-permute-start.9 = (bf16[384,1536]{1,0:T(8,128)(2,1)S(1)}, bf16[384,1536]{1,0:T(8,128)(2,1)S(1)}, u32[]{:S(2)}, u32[]{:S(2)}) collective-permute-start(bf16[384,1536]{1,0:T(8,128)(2,1)S(1)} %dynamic-slice_bitcast_fusion.1), channel_id=1, source_target_pairs={{0,16},{16,0},{1,17},{17,1},{2,18},{18,2},{3,19},{19,3},{4,20},{20... | collective-permute-start | bytes 3538952 | tf_op jit(solution)/shard_map/ppermute | solution.py:804
  44.7 20.8 %collective-permute-start.7 = (bf16[512,768]{1,0:T(8,128)(2,1)S(1)}, bf16[512,768]{1,0:T(8,128)(2,1)S(1)}, u32[]{:S(2)}, u32[]{:S(2)}) collective-permute-start(bf16[512,768]{1,0:T(8,128)(2,1)S(1)} %get-tuple-element.307.refs_3_.refs_9_), channel_id=1, source_target_pairs={{0,2},{1,3},{2,4},{3,5},{4,6},{5,7},{8,10},{9,11},{10,12},{11,13},... | collective-permute-start | bytes 2359304 | tf_op jit(solution)/shard_map/ppermute | solution.py:810
  65.7 28.4 %collective-permute-start.15 = (bf16[768,768]{1,0:T(8,128)(2,1)S(1)}, bf16[768,768]{1,0:T(8,128)(2,1)S(1)}, u32[]{:S(2)}, u32[]{:S(2)}) collective-permute-start(bf16[768,768]{1,0:T(8,128)(2,1)S(1)} %dynamic-slice_bitcast_fusion), channel_id=1, source_target_pairs={{0,16},{16,0},{1,17},{17,1},{2,18},{18,2},{3,19},{19,3},{4,20},{20... | collective-permute-start | bytes 3538952 | tf_op jit(solution)/shard_map/ppermute | solution.py:804
  71.4 22.8 %collective-permute-start.14 = (bf16[256,768]{1,0:T(8,128)(2,1)S(1)}, bf16[256,768]{1,0:T(8,128)(2,1)S(1)}, u32[]{:S(2)}, u32[]{:S(2)}) collective-permute-start(bf16[256,768]{1,0:T(8,128)(2,1)S(1)} %get-tuple-element.320.refs_3_), channel_id=1, source_target_pairs={{0,8},{8,0},{1,9},{9,1},{2,10},{10,2},{3,11},{11,3},{4,12},{12,4},... | collective-permute-start | bytes 1179656 | tf_op jit(solution)/shard_map/ppermute | solution.py:804
  75.0 19.1 %collective-permute-start.13 = (bf16[256,768]{1,0:T(8,128)(2,1)S(1)}, bf16[256,768]{1,0:T(8,128)(2,1)S(1)}, u32[]{:S(2)}, u32[]{:S(2)}) collective-permute-start(bf16[256,768]{1,0:T(8,128)(2,1)S(1)} %get-tuple-element.319.refs_3_), channel_id=1, source_target_pairs={{0,8},{8,0},{1,9},{9,1},{2,10},{10,2},{3,11},{11,3},{4,12},{12,4},... | collective-permute-start | bytes 1179656 | tf_op jit(solution)/shard_map/ppermute | solution.py:804
  130.0 21.8 %collective-permute-start.20 = (bf16[512,768]{1,0:T(8,128)(2,1)S(1)}, bf16[512,768]{1,0:T(8,128)(2,1)S(1)}, u32[]{:S(2)}, u32[]{:S(2)}) collective-permute-start(bf16[512,768]{1,0:T(8,128)(2,1)S(1)} %get-tuple-element.333.refs_3_.refs_9_), channel_id=1, source_target_pairs={{0,2},{1,3},{2,4},{3,5},{4,6},{5,7},{8,10},{9,11},{10,12},{11,13},... | collective-permute-start | bytes 2359304 | tf_op jit(solution)/shard_map/ppermute | solution.py:810
  207.7 28.3 %collective-permute-start.30 = (bf16[768,768]{1,0:T(8,128)(2,1)}, bf16[768,768]{1,0:T(8,128)(2,1)}, u32[]{:S(2)}, u32[]{:S(2)}) collective-permute-start(bf16[768,768]{1,0:T(8,128)(2,1)} %fusion), channel_id=1, source_target_pairs={{0,16},{16,0},{1,17},{17,1},{2,18},{18,2},{3,19},{19,3},{4,20},{20... | collective-permute-start | bytes 3538952 | tf_op jit(solution)/shard_map/ppermute | solution.py:804
  209.8 32.9 %collective-permute-start.29 = (bf16[512,768]{1,0:T(8,128)(2,1)S(1)}, bf16[512,768]{1,0:T(8,128)(2,1)S(1)}, u32[]{:S(2)}, u32[]{:S(2)}) collective-permute-start(bf16[512,768]{1,0:T(8,128)(2,1)S(1)} %add_convert_fusion.3), channel_id=1, source_target_pairs={{2,0},{3,1},{4,2},{5,3},{6,4},{7,5},{10,8},{11,9},{12,10},{13,11},... | collective-permute-start | bytes 2359304 | tf_op jit(solution)/shard_map/ppermute | solution.py:810
  217.6 33.6 %collective-permute-start.31 = (bf16[512,768]{1,0:T(8,128)(2,1)}, bf16[512,768]{1,0:T(8,128)(2,1)S(1)}, u32[]{:S(2)}, u32[]{:S(2)}) collective-permute-start(bf16[512,768]{1,0:T(8,128)(2,1)} %get-tuple-element.384), channel_id=1, source_target_pairs={{0,1},{1,0},{2,3},{3,2},{4,5},{5,4},{6,7},{7,6},{8,9},{9,8},{10,11... | collective-permute-start | bytes 2359304 | tf_op jit(solution)/shard_map/ppermute | solution.py:804
  244.9 27.6 %collective-permute-start.34 = (bf16[384,768]{1,0:T(8,128)(2,1)S(1)}, bf16[384,768]{1,0:T(8,128)(2,1)S(1)}, u32[]{:S(2)}, u32[]{:S(2)}) collective-permute-start(bf16[384,768]{1,0:T(8,128)(2,1)S(1)} %get-tuple-element.608), channel_id=1, source_target_pairs={{0,2},{1,3},{2,0},{3,1},{4,6},{5,7},{6,4},{7,5},{8,10},{9,11},{10,... | collective-permute-start | bytes 1769480 | tf_op jit(solution)/shard_map/ppermute | solution.py:804
  272.7 29.1 %collective-permute-start.38 = (bf16[384,768]{1,0:T(8,128)(2,1)S(1)}, bf16[384,768]{1,0:T(8,128)(2,1)S(1)}, u32[]{:S(2)}, u32[]{:S(2)}) collective-permute-start(bf16[384,768]{1,0:T(8,128)(2,1)S(1)} %add_convert_fusion.9), channel_id=1, source_target_pairs={{0,4},{1,5},{2,6},{3,7},{4,0},{5,1},{6,2},{7,3},{8,12},{9,13},{10,... | collective-permute-start | bytes 1769480 | tf_op jit(solution)/shard_map/ppermute | solution.py:804
  275.7 26.1 %collective-permute-start.37 = (bf16[384,768]{1,0:T(8,128)(2,1)S(1)}, bf16[384,768]{1,0:T(8,128)(2,1)S(1)}, u32[]{:S(2)}, u32[]{:S(2)}) collective-permute-start(bf16[384,768]{1,0:T(8,128)(2,1)S(1)} %fusion.8), channel_id=1, source_target_pairs={{0,16},{16,0},{1,17},{17,1},{2,18},{18,2},{3,19},{19,3},{4,20},{20... | collective-permute-start | bytes 1769480 | tf_op jit(solution)/shard_map/ppermute | solution.py:804
  302.3 21.7 %collective-permute-start.40 = (bf16[576,768]{1,0:T(8,128)(2,1)S(1)}, bf16[576,768]{1,0:T(8,128)(2,1)S(1)}, u32[]{:S(2)}, u32[]{:S(2)}) collective-permute-start(bf16[576,768]{1,0:T(8,128)(2,1)S(1)} %pad_maximum_fusion.2), channel_id=1, source_target_pairs={{0,2},{1,3},{2,0},{3,1},{4,6},{5,7},{6,4},{7,5},{8,10},{9,11},{10,... | collective-permute-start | bytes 2654216 | tf_op jit(solution)/shard_map/ppermute | solution.py:804
  302.4 21.6 %collective-permute-start.36 = (bf16[256,768]{1,0:T(8,128)(2,1)S(1)}, bf16[256,768]{1,0:T(8,128)(2,1)S(1)}, u32[]{:S(2)}, u32[]{:S(2)}) collective-permute-start(bf16[256,768]{1,0:T(8,128)(2,1)S(1)} %get-tuple-element.447.refs_3_), channel_id=1, source_target_pairs={{0,8},{8,0},{1,9},{9,1},{2,10},{10,2},{3,11},{11,3},{4,12},{12,4},... | collective-permute-start | bytes 1179656 | tf_op jit(solution)/shard_map/ppermute | solution.py:804
  343.4 28.4 %collective-permute-start.45 = (bf16[768,768]{1,0:T(8,128)(2,1)S(1)}, bf16[768,768]{1,0:T(8,128)(2,1)S(1)}, u32[]{:S(2)}, u32[]{:S(2)}) collective-permute-start(bf16[768,768]{1,0:T(8,128)(2,1)S(1)} %fusion.1), channel_id=1, source_target_pairs={{0,16},{16,0},{1,17},{17,1},{2,18},{18,2},{3,19},{19,3},{4,20},{20... | collective-permute-start | bytes 3538952 | tf_op jit(solution)/shard_map/ppermute | solution.py:804
  345.9 26.2 %collective-permute-start.44 = (bf16[512,768]{1,0:T(8,128)(2,1)S(1)}, bf16[512,768]{1,0:T(8,128)(2,1)S(1)}, u32[]{:S(2)}, u32[]{:S(2)}) collective-permute-start(bf16[512,768]{1,0:T(8,128)(2,1)S(1)} %add_convert_fusion.2), channel_id=1, source_target_pairs={{2,0},{3,1},{4,2},{5,3},{6,4},{7,5},{10,8},{11,9},{12,10},{13,11},... | collective-permute-start | bytes 2359304 | tf_op jit(solution)/shard_map/ppermute | solution.py:810
  349.6 29.4 %collective-permute-start.46 = (bf16[512,768]{1,0:T(8,128)(2,1)S(1)}, bf16[512,768]{1,0:T(8,128)(2,1)S(1)}, u32[]{:S(2)}, u32[]{:S(2)}) collective-permute-start(bf16[512,768]{1,0:T(8,128)(2,1)S(1)} %get-tuple-element.477), channel_id=1, source_target_pairs={{0,1},{1,0},{2,3},{3,2},{4,5},{5,4},{6,7},{7,6},{8,9},{9,8},{10,11... | collective-permute-start | bytes 2359304 | tf_op jit(solution)/shard_map/ppermute | solution.py:804
  372.7 25.7 %collective-permute-start.49 = (bf16[576,768]{1,0:T(8,128)(2,1)S(1)}, bf16[576,768]{1,0:T(8,128)(2,1)S(1)}, u32[]{:S(2)}, u32[]{:S(2)}) collective-permute-start(bf16[576,768]{1,0:T(8,128)(2,1)S(1)} %pad_maximum_fusion.3), channel_id=1, source_target_pairs={{0,2},{1,3},{2,0},{3,1},{4,6},{5,7},{6,4},{7,5},{8,10},{9,11},{10,... | collective-permute-start | bytes 2654216 | tf_op jit(solution)/shard_map/ppermute | solution.py:804
  406.5 28.9 %collective-permute-start.50 = (bf16[384,768]{1,0:T(8,128)(2,1)}, bf16[384,768]{1,0:T(8,128)(2,1)}, u32[]{:S(2)}, u32[]{:S(2)}) collective-permute-start(bf16[384,768]{1,0:T(8,128)(2,1)} %add_convert_fusion.6), channel_id=1, source_target_pairs={{0,4},{1,5},{2,6},{3,7},{4,0},{5,1},{6,2},{7,3},{8,12},{9,13},{10,... | collective-permute-start | bytes 1769480 | tf_op jit(solution)/shard_map/ppermute | solution.py:804
  407.9 27.5 %collective-permute-start.54 = (bf16[256,768]{1,0:T(8,128)(2,1)}, bf16[256,768]{1,0:T(8,128)(2,1)}, u32[]{:S(2)}, u32[]{:S(2)}) collective-permute-start(bf16[256,768]{1,0:T(8,128)(2,1)} %get-tuple-element.534), channel_id=1, source_target_pairs={{0,8},{8,0},{1,9},{9,1},{2,10},{10,2},{3,11},{11,3},{4,12},{12,4},... | collective-permute-start | bytes 1179656 | tf_op jit(solution)/shard_map/ppermute | solution.py:804
  408.4 27.0 %collective-permute-start.55 = (bf16[256,768]{1,0:T(8,128)(2,1)}, bf16[256,768]{1,0:T(8,128)(2,1)}, u32[]{:S(2)}, u32[]{:S(2)}) collective-permute-start(bf16[256,768]{1,0:T(8,128)(2,1)} %get-tuple-element.536), channel_id=1, source_target_pairs={{0,8},{8,0},{1,9},{9,1},{2,10},{10,2},{3,11},{11,3},{4,12},{12,4},... | collective-permute-start | bytes 1179656 | tf_op jit(solution)/shard_map/ppermute | solution.py:804
  438.2 21.4 %collective-permute-start.56 = (bf16[576,768]{1,0:T(8,128)(2,1)S(1)}, bf16[576,768]{1,0:T(8,128)(2,1)S(1)}, u32[]{:S(2)}, u32[]{:S(2)}) collective-permute-start(bf16[576,768]{1,0:T(8,128)(2,1)S(1)} %pad_maximum_fusion.4), channel_id=1, source_target_pairs={{0,2},{1,3},{2,0},{3,1},{4,6},{5,7},{6,4},{7,5},{8,10},{9,11},{10,... | collective-permute-start | bytes 2654216 | tf_op jit(solution)/shard_map/ppermute | solution.py:804
  438.4 21.2 %collective-permute-start.58 = (bf16[256,768]{1,0:T(8,128)(2,1)S(1)}, bf16[256,768]{1,0:T(8,128)(2,1)S(1)}, u32[]{:S(2)}, u32[]{:S(2)}) collective-permute-start(bf16[256,768]{1,0:T(8,128)(2,1)S(1)} %select_convert_fusion), channel_id=1, source_target_pairs={{0,16},{16,0},{1,17},{17,1},{2,18},{18,2},{3,19},{19,3},{4,20},{20... | collective-permute-start | bytes 1179656 | tf_op jit(solution)/shard_map/ppermute | solution.py:804
  (125 other events, 1161.5 us)

commit v7 on v6

--- a/solution.py
+++ b/solution.py
@@ -1010,9 +1010,11 @@
 
     query_keys = query_key[0].reshape(features, 2 * width)
     extra = jnp.where(section == 0, value_extra, jnp.zeros_like(value_extra))
-    halves = [half_of(query_keys), jnp.concatenate([half_of(value_own[0]), half_of(extra)], axis=1)]
+    halves = [half_of(query_keys), half_of(value_own[0])]
+    other_extra = half_of(jnp.where(section == 1, value_extra, jnp.zeros_like(value_extra)))
     qkv = jnp.concatenate([query_keys, value_own[0], extra], axis=1)
     qkv_got = [swap(h, "section") for h in halves]
+    qkv_got[1] = jnp.concatenate([qkv_got[1], other_extra], axis=1)
     other_table = swap(own_table, "section")
     out_got = swap(half_of(out_weight[0]), "section")
     up_got = swap(after(half_of(up_weight[0]), x[0]), "section")

time: 531 us -> 531 us (level)
  waiting for transfers between devices: 226 us -> 212 us
  starting transfers between devices: 75.8 us -> 87.2 us
    ppermute x69, starting transfers between devices: 65.3 us -> 76.4 us  [swap(): return lax.ppermute(value, axis, [(i, i ^ bits) for i in range(count)])]
    ppermute x69, waiting for transfers between devices: 193 us -> 186 us  [swap(): return lax.ppermute(value, axis, [(i, i ^ bits) for i in range(count)])]
    ppermute x4, waiting for transfers between devices: 32.7 us -> 25.6 us  [shift(): lax.ppermute(value, 'batch', [(i, i + steps) for i in range(first, last)])]
    unnamed x152 -> x156, local copies, waits for them, and re-layouts: 17.3 us -> 18.4 us
  transfers between devices with their start and end apart: 73 -> 73, of which waited for: 36 -> 33; matrix products, arithmetic and copies ran while one was open for 6% -> 6% of each run, Pallas kernels for 26% -> 26%
where the time goes in v7:
time: 531 us; the launch traced here: 522 us
  waiting for transfers between devices  212 us (40%)
  Pallas kernels  161 us (30%)
  starting transfers between devices  87.2 us (16%)
  local copies, waits for them, and re-layouts  33 us (6%)
  other arithmetic  26.2 us (5%)
    ppermute x69, waiting for transfers between devices, swap(): return lax.ppermute(value, axis, [(i, i ^ bits) for i in range(count)])  186 us
    pallas_call x34, Pallas kernels, call(): pl.pallas_call(body, out_shape=shapes, in_specs=[SCALARS] + [FAR_OFF if i...  161 us
    ppermute x69, starting transfers between devices, swap(): return lax.ppermute(value, axis, [(i, i ^ bits) for i in range(count)])  76.4 us
    ppermute x4, waiting for transfers between devices, shift(): lax.ppermute(value, 'batch', [(i, i + steps) for i in range(first, last)])  25.6 us
    unnamed x156, local copies, waits for them, and re-layouts  18.4 us
    ppermute x4, starting transfers between devices, shift(): lax.ppermute(value, 'batch', [(i, i + steps) for i in range(first, last)])  10.8 us
  transfers between devices with their start and end apart: 73, of which 33 were waited for; matrix products, arithmetic and copies ran while one was open for 6% of the time, Pallas kernels for 26%

profile of v7, /device:TPU:0, one launch (start us, length us, event | category | flops | bytes accessed | tf_op | source)
XLA Modules:
  0.0 522.2 jit_solution(12204649601036564472)
XLA Ops:
  51.8 11.9 %collective-permute-done.7.refs_2_.refs_9_ = bf16[512,768]{1,0:T(8,128)(2,1)S(1)} collective-permute-done((bf16[512,768]{1,0:T(8,128)(2,1)S(1)}, bf16[512,768]{1,0:T(8,128)(2,1)S(1)}, u32[]{:S(2)}, u32[]{:S(2)}) %collective-permute-start.7) | collective-permute-done | bytes 786464 | tf_op jit(solution)/shard_map/ppermute | solution.py:810
  74.0 18.4 %collective-permute-done.15.refs_9_.refs_10_.refs_7_ = bf16[768,768]{1,0:T(8,128)(2,1)S(1)} collective-permute-done((bf16[768,768]{1,0:T(8,128)(2,1)S(1)}, bf16[768,768]{1,0:T(8,128)(2,1)S(1)}, u32[]{:S(2)}, u32[]{:S(2)}) %collective-permute-start.15) | collective-permute-done | bytes 1179680 | tf_op jit(solution)/shard_map/ppermute | solution.py:804
  96.3 6.2 %shard_map.276 = (f32[256,768]{1,0:T(8,128)}, bf16[256,768]{1,0:T(8,128)(2,1)}, bf16[256,1536]{1,0:T(8,128)(2,1)}, bf16[256,1536]{1,0:T(8,128)(2,1)}, bf16[256,768]{1,0:T(8,128)(2,1)S(1)}) custom-call(s32[4]{0:T(128)S(1)} %pad_add_fusion.refs_0_, f32[16,768]{1,0:T(8,128)S(1)} %get-tuple-element.300.refs_1_.refs_2_, bf16[256,768]{1,0:T(8,128)(2,1)} %copy-done.2, ...), custom_call_target="tpu_custom_call" | custom-call | flops 480000000 | bytes 800000 | tf_op jit(solution)/shard_map/pallas_call | solution.py:94
  104.2 6.2 %shard_map.275 = (f32[256,768]{1,0:T(8,128)}, bf16[256,768]{1,0:T(8,128)(2,1)}, bf16[256,1536]{1,0:T(8,128)(2,1)}, bf16[256,1536]{1,0:T(8,128)(2,1)}, bf16[256,768]{1,0:T(8,128)(2,1)S(1)}) custom-call(s32[4]{0:T(128)S(1)} %pad_add_fusion.refs_0_, f32[16,768]{1,0:T(8,128)S(1)} %get-tuple-element.300.refs_1_.refs_2_, bf16[256,768]{1,0:T(8,128)(2,1)} %copy-done.3, ...), custom_call_target="tpu_custom_call" | custom-call | flops 480000000 | bytes 800000 | tf_op jit(solution)/shard_map/pallas_call | solution.py:94
  114.6 7.6 %collective-permute-done.18.refs_6_ = bf16[256,768]{1,0:T(8,128)(2,1)S(1)} collective-permute-done((bf16[256,768]{1,0:T(8,128)(2,1)S(1)}, bf16[256,768]{1,0:T(8,128)(2,1)S(1)}, u32[]{:S(2)}, u32[]{:S(2)}) %collective-permute-start.18) | collective-permute-done | bytes 393248 | tf_op jit(solution)/shard_map/ppermute | solution.py:804
  136.4 13.7 %collective-permute-done.20.refs_2_.refs_9_ = bf16[512,768]{1,0:T(8,128)(2,1)S(1)} collective-permute-done((bf16[512,768]{1,0:T(8,128)(2,1)S(1)}, bf16[512,768]{1,0:T(8,128)(2,1)S(1)}, u32[]{:S(2)}, u32[]{:S(2)}) %collective-permute-start.20) | collective-permute-done | bytes 786464 | tf_op jit(solution)/shard_map/ppermute | solution.py:810
  158.7 7.8 %collective-permute-done.23.refs_4_ = bf16[256,768]{1,0:T(8,128)(2,1)S(1)} collective-permute-done((bf16[256,768]{1,0:T(8,128)(2,1)S(1)}, bf16[256,768]{1,0:T(8,128)(2,1)S(1)}, u32[]{:S(2)}, u32[]{:S(2)}) %collective-permute-start.23) | collective-permute-done | bytes 393248 | tf_op jit(solution)/shard_map/ppermute | solution.py:804
  166.5 8.4 %shard_map.280 = (f32[256,768]{1,0:T(8,128)}, bf16[256,768]{1,0:T(8,128)(2,1)}, bf16[256,1536]{1,0:T(8,128)(2,1)}, bf16[256,768]{1,0:T(8,128)(2,1)}, bf16[256,15...) custom-call(s32[4]{0:T(128)S(1)} %pad_add_fusion.refs_0_, ...), custom_call_target="tpu_custom_call" | custom-call | flops 120000000 | bytes 200000 | tf_op jit(solution)/shard_map/pallas_call | solution.py:94
  176.4 8.4 %shard_map.282 = (f32[256,768]{1,0:T(8,128)}, bf16[256,768]{1,0:T(8,128)(2,1)}, bf16[256,1536]{1,0:T(8,128)(2,1)}, bf16[256,768]{1,0:T(8,128)(2,1)}, bf16[256,15...) custom-call(s32[4]{0:T(128)S(1)} %pad_add_fusion.refs_0_, ...), custom_call_target="tpu_custom_call" | custom-call | flops 120000000 | bytes 200000 | tf_op jit(solution)/shard_map/pallas_call | solution.py:94
  185.4 7.4 %shard_map.283 = (bf16[2,768,768]{2,1,0:T(8,128)(2,1)}, bf16[2,768,768]{2,1,0:T(8,128)(2,1)}) custom-call(s32[4]{0:T(128)S(1)} %pad_add_fusion.refs_0_, bf16[256,1536]{1,0:T(8,128)(2,1)} %get-tuple-element.347.refs_1_, bf16[256,1536]{1,0:T(8,128)(2,1)} %get-tuple-element.348.refs_2_, bf16[256,768]{1,0:T(8,128)(2,1)S(1)} %get-tuple-element.626.refs_5_.refs_3_, ...), custom_call_target="tpu_custom_call" | custom-call | flops 444000000 | bytes 740000 | tf_op jit(solution)/shard_map/pallas_call | solution.py:94
  225.8 8.5 %collective-permute-done.30 = bf16[768,768]{1,0:T(8,128)(2,1)} collective-permute-done((bf16[768,768]{1,0:T(8,128)(2,1)}, bf16[768,768]{1,0:T(8,128)(2,1)}, u32[]{:S(2)}, u32[]{:S(2)}) %collective-permute-start.30) | collective-permute-done | bytes 1179680 | tf_op jit(solution)/shard_map/ppermute | solution.py:804
  253.9 6.4 %collective-permute-done.33.refs_8_ = bf16[256,768]{1,0:T(8,128)(2,1)S(1)} collective-permute-done((bf16[256,768]{1,0:T(8,128)(2,1)S(1)}, bf16[256,768]{1,0:T(8,128)(2,1)S(1)}, u32[]{:S(2)}, u32[]{:S(2)}) %collective-permute-start.33) | collective-permute-done | bytes 393248 | tf_op jit(solution)/shard_map/ppermute | solution.py:804
  260.5 13.2 %collective-permute-start.38 = (bf16[384,768]{1,0:T(8,128)(2,1)S(1)}, bf16[384,768]{1,0:T(8,128)(2,1)S(1)}, u32[]{:S(2)}, u32[]{:S(2)}) collective-permute-start(bf16[384,768]{1,0:T(8,128)(2,1)S(1)} %add_convert_fusion.9), channel_id=1, source_target_pairs={{0,4},{1,5},{2,6},{3,7},{4,0},{5,1},{6,2},{7,3},{8,12},{9,13},{10,... | collective-permute-start | bytes 1769480 | tf_op jit(solution)/shard_map/ppermute | solution.py:804
  284.5 15.5 %collective-permute-done.38 = bf16[384,768]{1,0:T(8,128)(2,1)S(1)} collective-permute-done((bf16[384,768]{1,0:T(8,128)(2,1)S(1)}, bf16[384,768]{1,0:T(8,128)(2,1)S(1)}, u32[]{:S(2)}, u32[]{:S(2)}) %collective-permute-start.38) | collective-permute-done | bytes 589856 | tf_op jit(solution)/shard_map/ppermute | solution.py:804
  308.4 7.4 %shard_map.294 = (bf16[2,768,768]{2,1,0:T(8,128)(2,1)}, bf16[2,768,768]{2,1,0:T(8,128)(2,1)}) custom-call(s32[4]{0:T(128)S(1)} %pad_add_fusion.refs_0_, bf16[256,1536]{1,0:T(8,128)(2,1)} %get-tuple-element.433.refs_1_, bf16[256,1536]{1,0:T(8,128)(2,1)} %get-tuple-element.434.refs_2_, bf16[256,768]{1,0:T(8,128)(2,1)S(1)} %get-tuple-element.420.refs_1_.refs_3_.refs_5_, ...), custom_call_target="tpu_custom_call" | custom-call | flops 444000000 | bytes 740000 | tf_op jit(solution)/shard_map/pallas_call | solution.py:94
  315.8 6.5 %collective-permute-done.40 = bf16[576,768]{1,0:T(8,128)(2,1)S(1)} collective-permute-done((bf16[576,768]{1,0:T(8,128)(2,1)S(1)}, bf16[576,768]{1,0:T(8,128)(2,1)S(1)}, u32[]{:S(2)}, u32[]{:S(2)}) %collective-permute-start.40) | collective-permute-done | bytes 884768 | tf_op jit(solution)/shard_map/ppermute | solution.py:804
  329.4 9.5 %collective-permute-done.42 = bf16[192,768]{1,0:T(8,128)(2,1)S(1)} collective-permute-done((bf16[192,768]{1,0:T(8,128)(2,1)S(1)}, bf16[192,768]{1,0:T(8,128)(2,1)S(1)}, u32[]{:S(2)}, u32[]{:S(2)}) %collective-permute-start.42) | collective-permute-done | bytes 294944 | tf_op jit(solution)/shard_map/ppermute | solution.py:804
  357.6 12.5 %collective-permute-done.45 = bf16[768,768]{1,0:T(8,128)(2,1)S(1)} collective-permute-done((bf16[768,768]{1,0:T(8,128)(2,1)S(1)}, bf16[768,768]{1,0:T(8,128)(2,1)S(1)}, u32[]{:S(2)}, u32[]{:S(2)}) %collective-permute-start.45) | collective-permute-done | bytes 1179680 | tf_op jit(solution)/shard_map/ppermute | solution.py:804
  385.8 6.2 %collective-permute-done.49 = bf16[576,768]{1,0:T(8,128)(2,1)S(1)} collective-permute-done((bf16[576,768]{1,0:T(8,128)(2,1)S(1)}, bf16[576,768]{1,0:T(8,128)(2,1)S(1)}, u32[]{:S(2)}, u32[]{:S(2)}) %collective-permute-start.49) | collective-permute-done | bytes 884768 | tf_op jit(solution)/shard_map/ppermute | solution.py:804
  398.9 10.3 %collective-permute-start.50 = (bf16[384,768]{1,0:T(8,128)(2,1)}, bf16[384,768]{1,0:T(8,128)(2,1)}, u32[]{:S(2)}, u32[]{:S(2)}) collective-permute-start(bf16[384,768]{1,0:T(8,128)(2,1)} %add_convert_fusion.6), channel_id=1, source_target_pairs={{0,4},{1,5},{2,6},{3,7},{4,0},{5,1},{6,2},{7,3},{8,12},{9,13},{10,... | collective-permute-start | bytes 1769480 | tf_op jit(solution)/shard_map/ppermute | solution.py:804
  422.5 12.7 %collective-permute-done.50 = bf16[384,768]{1,0:T(8,128)(2,1)} collective-permute-done((bf16[384,768]{1,0:T(8,128)(2,1)}, bf16[384,768]{1,0:T(8,128)(2,1)}, u32[]{:S(2)}, u32[]{:S(2)}) %collective-permute-start.50) | collective-permute-done | bytes 589856 | tf_op jit(solution)/shard_map/ppermute | solution.py:804
  442.2 17.1 %collective-permute-done.56 = bf16[576,768]{1,0:T(8,128)(2,1)S(1)} collective-permute-done((bf16[576,768]{1,0:T(8,128)(2,1)S(1)}, bf16[576,768]{1,0:T(8,128)(2,1)S(1)}, u32[]{:S(2)}, u32[]{:S(2)}) %collective-permute-start.56) | collective-permute-done | bytes 884768 | tf_op jit(solution)/shard_map/ppermute | solution.py:804
  469.2 8.3 %collective-permute-done.60 = bf16[192,768]{1,0:T(8,128)(2,1)S(1)} collective-permute-done((bf16[192,768]{1,0:T(8,128)(2,1)S(1)}, bf16[192,768]{1,0:T(8,128)(2,1)S(1)}, u32[]{:S(2)}, u32[]{:S(2)}) %collective-permute-start.60) | collective-permute-done | bytes 294944 | tf_op jit(solution)/shard_map/ppermute | solution.py:804
  497.6 7.2 %shard_map.303 = (f32[1536,768]{1,0:T(8,128)}, f32[768,1536]{1,0:T(8,128)}, f32[8,128]{1,0:T(8,128)S(1)}) custom-call(s32[4]{0:T(128)S(1)} %pad_add_fusion.refs_0_, bf16[768,768]{1,0:T(8,128)(2,1)} %copy-done.35, bf16[384,768]{1,0:T(8,128)(2,1)} %copy-done.60, bf16[384,768]{1,0:T(8,128)(2,1)} %copy-done.61, bf16[768,768]{1,0:T(8,128)(2,1)} %copy-done.49, ...), custom_call_target="tpu_custom_call" | custom-call | flops 600000000 | bytes 1000000 | tf_op jit(solution)/shard_map/pallas_call | solution.py:94
  (407 shorter events, 282.0 us)
Async XLA Ops:
  3.8 22.4 %collective-permute-start.3 = (f32[16,768]{1,0:T(8,128)S(1)}, f32[16,768]{1,0:T(8,128)}, u32[]{:S(2)}, u32[]{:S(2)}) collective-permute-start(f32[16,768]{1,0:T(8,128)S(1)} %concatenate.44), channel_id=1, source_target_pairs={{0,16},{16,0},{1,17},{17,1},{2,18},{18,2},{3,19},{19,3},{4,20},{20... | collective-permute-start | bytes 147464 | tf_op jit(solution)/shard_map/ppermute | solution.py:804
  8.6 21.0 %collective-permute-start.2 = (bf16[192,768]{1,0:T(8,128)(2,1)}, bf16[192,768]{1,0:T(8,128)(2,1)S(1)}, u32[]{:S(2)}, u32[]{:S(2)}) collective-permute-start(bf16[192,768]{1,0:T(8,128)(2,1)} %dynamic-slice_bitcast_fusion.5), channel_id=1, source_target_pairs={{0,16},{16,0},{1,17},{17,1},{2,18},{18,2},{3,19},{19,3},{4,20},{20... | collective-permute-start | bytes 884744 | tf_op jit(solution)/shard_map/ppermute | solution.py:804
  34.9 28.9 %collective-permute-start.9 = (bf16[384,1536]{1,0:T(8,128)(2,1)S(1)}, bf16[384,1536]{1,0:T(8,128)(2,1)S(1)}, u32[]{:S(2)}, u32[]{:S(2)}) collective-permute-start(bf16[384,1536]{1,0:T(8,128)(2,1)S(1)} %dynamic-slice_bitcast_fusion.1), channel_id=1, source_target_pairs={{0,16},{16,0},{1,17},{17,1},{2,18},{18,2},{3,19},{19,3},{4,20},{20... | collective-permute-start | bytes 3538952 | tf_op jit(solution)/shard_map/ppermute | solution.py:804
  42.7 21.0 %collective-permute-start.7 = (bf16[512,768]{1,0:T(8,128)(2,1)S(1)}, bf16[512,768]{1,0:T(8,128)(2,1)S(1)}, u32[]{:S(2)}, u32[]{:S(2)}) collective-permute-start(bf16[512,768]{1,0:T(8,128)(2,1)S(1)} %get-tuple-element.307.refs_3_.refs_9_), channel_id=1, source_target_pairs={{0,2},{1,3},{2,4},{3,5},{4,6},{5,7},{8,10},{9,11},{10,12},{11,13},... | collective-permute-start | bytes 2359304 | tf_op jit(solution)/shard_map/ppermute | solution.py:810
  64.0 28.4 %collective-permute-start.15 = (bf16[768,768]{1,0:T(8,128)(2,1)S(1)}, bf16[768,768]{1,0:T(8,128)(2,1)S(1)}, u32[]{:S(2)}, u32[]{:S(2)}) collective-permute-start(bf16[768,768]{1,0:T(8,128)(2,1)S(1)} %dynamic-slice_bitcast_fusion), channel_id=1, source_target_pairs={{0,16},{16,0},{1,17},{17,1},{2,18},{18,2},{3,19},{19,3},{4,20},{20... | collective-permute-start | bytes 3538952 | tf_op jit(solution)/shard_map/ppermute | solution.py:804
  69.8 22.6 %collective-permute-start.14 = (bf16[256,768]{1,0:T(8,128)(2,1)S(1)}, bf16[256,768]{1,0:T(8,128)(2,1)S(1)}, u32[]{:S(2)}, u32[]{:S(2)}) collective-permute-start(bf16[256,768]{1,0:T(8,128)(2,1)S(1)} %get-tuple-element.320.refs_3_), channel_id=1, source_target_pairs={{0,8},{8,0},{1,9},{9,1},{2,10},{10,2},{3,11},{11,3},{4,12},{12,4},... | collective-permute-start | bytes 1179656 | tf_op jit(solution)/shard_map/ppermute | solution.py:804
  128.3 21.8 %collective-permute-start.20 = (bf16[512,768]{1,0:T(8,128)(2,1)S(1)}, bf16[512,768]{1,0:T(8,128)(2,1)S(1)}, u32[]{:S(2)}, u32[]{:S(2)}) collective-permute-start(bf16[512,768]{1,0:T(8,128)(2,1)S(1)} %get-tuple-element.333.refs_3_.refs_9_), channel_id=1, source_target_pairs={{0,2},{1,3},{2,4},{3,5},{4,6},{5,7},{8,10},{9,11},{10,12},{11,13},... | collective-permute-start | bytes 2359304 | tf_op jit(solution)/shard_map/ppermute | solution.py:810
  206.0 28.3 %collective-permute-start.30 = (bf16[768,768]{1,0:T(8,128)(2,1)}, bf16[768,768]{1,0:T(8,128)(2,1)}, u32[]{:S(2)}, u32[]{:S(2)}) collective-permute-start(bf16[768,768]{1,0:T(8,128)(2,1)} %fusion), channel_id=1, source_target_pairs={{0,16},{16,0},{1,17},{17,1},{2,18},{18,2},{3,19},{19,3},{4,20},{20... | collective-permute-start | bytes 3538952 | tf_op jit(solution)/shard_map/ppermute | solution.py:804
  208.1 26.2 %collective-permute-start.29 = (bf16[512,768]{1,0:T(8,128)(2,1)S(1)}, bf16[512,768]{1,0:T(8,128)(2,1)S(1)}, u32[]{:S(2)}, u32[]{:S(2)}) collective-permute-start(bf16[512,768]{1,0:T(8,128)(2,1)S(1)} %add_convert_fusion.3), channel_id=1, source_target_pairs={{2,0},{3,1},{4,2},{5,3},{6,4},{7,5},{10,8},{11,9},{12,10},{13,11},... | collective-permute-start | bytes 2359304 | tf_op jit(solution)/shard_map/ppermute | solution.py:810
  215.8 23.1 %collective-permute-start.31 = (bf16[512,768]{1,0:T(8,128)(2,1)}, bf16[512,768]{1,0:T(8,128)(2,1)S(1)}, u32[]{:S(2)}, u32[]{:S(2)}) collective-permute-start(bf16[512,768]{1,0:T(8,128)(2,1)} %get-tuple-element.384), channel_id=1, source_target_pairs={{0,1},{1,0},{2,3},{3,2},{4,5},{5,4},{6,7},{7,6},{8,9},{9,8},{10,11... | collective-permute-start | bytes 2359304 | tf_op jit(solution)/shard_map/ppermute | solution.py:804
  236.4 23.9 %collective-permute-start.34 = (bf16[384,768]{1,0:T(8,128)(2,1)S(1)}, bf16[384,768]{1,0:T(8,128)(2,1)S(1)}, u32[]{:S(2)}, u32[]{:S(2)}) collective-permute-start(bf16[384,768]{1,0:T(8,128)(2,1)S(1)} %get-tuple-element.608), channel_id=1, source_target_pairs={{0,2},{1,3},{2,0},{3,1},{4,6},{5,7},{6,4},{7,5},{8,10},{9,11},{10,... | collective-permute-start | bytes 1769480 | tf_op jit(solution)/shard_map/ppermute | solution.py:804
  260.5 39.5 %collective-permute-start.38 = (bf16[384,768]{1,0:T(8,128)(2,1)S(1)}, bf16[384,768]{1,0:T(8,128)(2,1)S(1)}, u32[]{:S(2)}, u32[]{:S(2)}) collective-permute-start(bf16[384,768]{1,0:T(8,128)(2,1)S(1)} %add_convert_fusion.9), channel_id=1, source_target_pairs={{0,4},{1,5},{2,6},{3,7},{4,0},{5,1},{6,2},{7,3},{8,12},{9,13},{10,... | collective-permute-start | bytes 1769480 | tf_op jit(solution)/shard_map/ppermute | solution.py:804
  273.8 26.2 %collective-permute-start.37 = (bf16[384,768]{1,0:T(8,128)(2,1)S(1)}, bf16[384,768]{1,0:T(8,128)(2,1)S(1)}, u32[]{:S(2)}, u32[]{:S(2)}) collective-permute-start(bf16[384,768]{1,0:T(8,128)(2,1)S(1)} %fusion.8), channel_id=1, source_target_pairs={{0,16},{16,0},{1,17},{17,1},{2,18},{18,2},{3,19},{19,3},{4,20},{20... | collective-permute-start | bytes 1769480 | tf_op jit(solution)/shard_map/ppermute | solution.py:804
  300.5 21.7 %collective-permute-start.40 = (bf16[576,768]{1,0:T(8,128)(2,1)S(1)}, bf16[576,768]{1,0:T(8,128)(2,1)S(1)}, u32[]{:S(2)}, u32[]{:S(2)}) collective-permute-start(bf16[576,768]{1,0:T(8,128)(2,1)S(1)} %pad_maximum_fusion.2), channel_id=1, source_target_pairs={{0,2},{1,3},{2,0},{3,1},{4,6},{5,7},{6,4},{7,5},{8,10},{9,11},{10,... | collective-permute-start | bytes 2654216 | tf_op jit(solution)/shard_map/ppermute | solution.py:804
  300.6 21.7 %collective-permute-start.36 = (bf16[256,768]{1,0:T(8,128)(2,1)S(1)}, bf16[256,768]{1,0:T(8,128)(2,1)S(1)}, u32[]{:S(2)}, u32[]{:S(2)}) collective-permute-start(bf16[256,768]{1,0:T(8,128)(2,1)S(1)} %get-tuple-element.447.refs_3_), channel_id=1, source_target_pairs={{0,8},{8,0},{1,9},{9,1},{2,10},{10,2},{3,11},{11,3},{4,12},{12,4},... | collective-permute-start | bytes 1179656 | tf_op jit(solution)/shard_map/ppermute | solution.py:804
  341.7 28.4 %collective-permute-start.45 = (bf16[768,768]{1,0:T(8,128)(2,1)S(1)}, bf16[768,768]{1,0:T(8,128)(2,1)S(1)}, u32[]{:S(2)}, u32[]{:S(2)}) collective-permute-start(bf16[768,768]{1,0:T(8,128)(2,1)S(1)} %fusion.1), channel_id=1, source_target_pairs={{0,16},{16,0},{1,17},{17,1},{2,18},{18,2},{3,19},{19,3},{4,20},{20... | collective-permute-start | bytes 3538952 | tf_op jit(solution)/shard_map/ppermute | solution.py:804
  344.2 25.9 %collective-permute-start.44 = (bf16[512,768]{1,0:T(8,128)(2,1)S(1)}, bf16[512,768]{1,0:T(8,128)(2,1)S(1)}, u32[]{:S(2)}, u32[]{:S(2)}) collective-permute-start(bf16[512,768]{1,0:T(8,128)(2,1)S(1)} %add_convert_fusion.2), channel_id=1, source_target_pairs={{2,0},{3,1},{4,2},{5,3},{6,4},{7,5},{10,8},{11,9},{12,10},{13,11},... | collective-permute-start | bytes 2359304 | tf_op jit(solution)/shard_map/ppermute | solution.py:810
  347.8 22.9 %collective-permute-start.46 = (bf16[512,768]{1,0:T(8,128)(2,1)S(1)}, bf16[512,768]{1,0:T(8,128)(2,1)S(1)}, u32[]{:S(2)}, u32[]{:S(2)}) collective-permute-start(bf16[512,768]{1,0:T(8,128)(2,1)S(1)} %get-tuple-element.477), channel_id=1, source_target_pairs={{0,1},{1,0},{2,3},{3,2},{4,5},{5,4},{6,7},{7,6},{8,9},{9,8},{10,11... | collective-permute-start | bytes 2359304 | tf_op jit(solution)/shard_map/ppermute | solution.py:804
  370.7 21.3 %collective-permute-start.49 = (bf16[576,768]{1,0:T(8,128)(2,1)S(1)}, bf16[576,768]{1,0:T(8,128)(2,1)S(1)}, u32[]{:S(2)}, u32[]{:S(2)}) collective-permute-start(bf16[576,768]{1,0:T(8,128)(2,1)S(1)} %pad_maximum_fusion.3), channel_id=1, source_target_pairs={{0,2},{1,3},{2,0},{3,1},{4,6},{5,7},{6,4},{7,5},{8,10},{9,11},{10,... | collective-permute-start | bytes 2654216 | tf_op jit(solution)/shard_map/ppermute | solution.py:804
  398.9 36.3 %collective-permute-start.50 = (bf16[384,768]{1,0:T(8,128)(2,1)}, bf16[384,768]{1,0:T(8,128)(2,1)}, u32[]{:S(2)}, u32[]{:S(2)}) collective-permute-start(bf16[384,768]{1,0:T(8,128)(2,1)} %add_convert_fusion.6), channel_id=1, source_target_pairs={{0,4},{1,5},{2,6},{3,7},{4,0},{5,1},{6,2},{7,3},{8,12},{9,13},{10,... | collective-permute-start | bytes 1769480 | tf_op jit(solution)/shard_map/ppermute | solution.py:804
  409.2 26.0 %collective-permute-start.54 = (bf16[256,768]{1,0:T(8,128)(2,1)}, bf16[256,768]{1,0:T(8,128)(2,1)}, u32[]{:S(2)}, u32[]{:S(2)}) collective-permute-start(bf16[256,768]{1,0:T(8,128)(2,1)} %get-tuple-element.534), channel_id=1, source_target_pairs={{0,8},{8,0},{1,9},{9,1},{2,10},{10,2},{3,11},{11,3},{4,12},{12,4},... | collective-permute-start | bytes 1179656 | tf_op jit(solution)/shard_map/ppermute | solution.py:804
  409.7 25.5 %collective-permute-start.55 = (bf16[256,768]{1,0:T(8,128)(2,1)}, bf16[256,768]{1,0:T(8,128)(2,1)}, u32[]{:S(2)}, u32[]{:S(2)}) collective-permute-start(bf16[256,768]{1,0:T(8,128)(2,1)} %get-tuple-element.536), channel_id=1, source_target_pairs={{0,8},{8,0},{1,9},{9,1},{2,10},{10,2},{3,11},{11,3},{4,12},{12,4},... | collective-permute-start | bytes 1179656 | tf_op jit(solution)/shard_map/ppermute | solution.py:804
  437.9 21.4 %collective-permute-start.56 = (bf16[576,768]{1,0:T(8,128)(2,1)S(1)}, bf16[576,768]{1,0:T(8,128)(2,1)S(1)}, u32[]{:S(2)}, u32[]{:S(2)}) collective-permute-start(bf16[576,768]{1,0:T(8,128)(2,1)S(1)} %pad_maximum_fusion.4), channel_id=1, source_target_pairs={{0,2},{1,3},{2,0},{3,1},{4,6},{5,7},{6,4},{7,5},{8,10},{9,11},{10,... | collective-permute-start | bytes 2654216 | tf_op jit(solution)/shard_map/ppermute | solution.py:804
  438.2 21.2 %collective-permute-start.58 = (bf16[256,768]{1,0:T(8,128)(2,1)S(1)}, bf16[256,768]{1,0:T(8,128)(2,1)S(1)}, u32[]{:S(2)}, u32[]{:S(2)}) collective-permute-start(bf16[256,768]{1,0:T(8,128)(2,1)S(1)} %select_convert_fusion), channel_id=1, source_target_pairs={{0,16},{16,0},{1,17},{17,1},{2,18},{18,2},{3,19},{19,3},{4,20},{20... | collective-permute-start | bytes 1179656 | tf_op jit(solution)/shard_map/ppermute | solution.py:804
  (127 other events, 1120.8 us)
